TPU v7x, 32 devices: a whole 2x2x4 slice. The times are simulated.
32 devices in a mesh: rows: 4 (over y, core), batch: 8 (over z, x).
Axes of the slice: x: 2, y: 2, z: 4, core: 2. Of those that a mesh axis runs over, the one named last changes fastest.
Arguments:
- tokens: bfloat16 [64, 16, 64, 128], P('batch', 'rows'), may hold values from -6 to 6
- valid_rows: int32 [64], P('batch'), may hold values from 8 to 16, as said below
- valid_cols: int32 [64], P('batch'), may hold values from 32 to 64, as said below
- ln1_gain: float32 [128], replicated, may hold values from 0.25 to 1.75
- q_weight: bfloat16 [128, 128], replicated, may hold values from -0.5 to 0.5
- sr_weight: bfloat16 [2048, 128], replicated, may hold values from -0.125 to 0.125
- sr_gain: float32 [128], replicated, may hold values from 0.25 to 1.75
- kv_weight: bfloat16 [128, 256], replicated, may hold values from -0.5 to 0.5
- out_weight: bfloat16 [128, 128], replicated, may hold values from -1 to 1
- ln2_gain: float32 [128], replicated, may hold values from 0.25 to 1.75
- fc1_weight: bfloat16 [128, 1024], replicated, may hold values from -0.5 to 0.5
- dw_weight: bfloat16 [3, 3, 1024], replicated, may hold values from -2 to 2
- fc2_weight: bfloat16 [1024, 128], replicated, may hold values from -0.1875 to 0.1875
- cotangent: bfloat16 [64, 16, 64, 128], P('batch', 'rows'), may hold values from -6 to 6
Outputs:
- block_out: bfloat16 [64, 16, 64, 128], P('batch', 'rows')
- input_grad: bfloat16 [64, 16, 64, 128], P('batch', 'rows')
- ln1_gain_grad: float32 [128], replicated
- q_weight_grad: float32 [128, 128], replicated
- sr_weight_grad: float32 [2048, 128], replicated
- sr_gain_grad: float32 [128], replicated
- kv_weight_grad: float32 [128, 256], replicated
- out_weight_grad: float32 [128, 128], replicated
- ln2_gain_grad: float32 [128], replicated
- fc1_weight_grad: float32 [128, 1024], replicated
- dw_weight_grad: float32 [3, 3, 1024], replicated
- fc2_weight_grad: float32 [1024, 128], replicated
Inputs may be any that keep to these rules, and one draw needn't show every extreme that they name: `valid_rows`: a multiple of 4; on each index b of batch one of the images 8 * b to 8 * b + 7, drawn from the seed, has all rows and all columns valid. `valid_cols`: a multiple of 4.
All inputs are finite; a program needn't handle non-finite values.
Results may differ from a plain program's by a relative error of at most 0.017.
Values may be sent and summed in bfloat16 or wider, within the bound.
No kernel may reach another device: no remote copies, remote signals or barrier semaphores. Data moves between devices by JAX's collectives and lax.ppermute only.
A program may use at most 128 MiB of HBM per device.

v0:
```python
import jax
import jax.numpy as jnp
from jax import lax
from jax.sharding import PartitionSpec as P

D = 128
FF = 1024
HEADS = 2
POOL = 4
HEAD_DIM = 64


EPS = 1e-06
NEG = -1e30


def padded_2(value, sides, width):
    for axis, dim in sides:
        size, length = (lax.axis_size(axis), value.shape[dim])
        up = [(i, (i + 1) % size) for i in range(size - 1)]
        down = [(j, i) for i, j in up]
        last = lax.slice_in_dim(value, length - width, length, axis=dim)
        first = lax.slice_in_dim(value, 0, width, axis=dim)
        before = lax.ppermute(last, axis, up)
        after = lax.ppermute(first, axis, down)
        value = jnp.concatenate([before, value, after], axis=dim)
    return value


def layer_norm(source, gain):
    centered = source - jnp.mean(source, axis=-1, keepdims=True)
    spread = jnp.mean(centered * centered, axis=-1, keepdims=True)
    return centered * lax.rsqrt(spread + EPS) * gain


def activate(source):
    return jax.nn.gelu(source, approximate=False)


def outer_product(left, right):
    return lax.dot_general(
        left.reshape(-1, left.shape[-1]),
        right.reshape(-1, right.shape[-1]),
        (((0,), (0,)), ((), ())),
        preferred_element_type=jnp.float32,
    )


def back_product(grad, weight):
    return lax.dot_general(
        grad, weight, (((grad.ndim - 1,), (1,)), ((), ())), preferred_element_type=jnp.float32
    )


def pad_columns(source):
    return jnp.pad(source, ((0, 0), (0, 0), (1, 1), (0, 0)))


def depth_conv(padded, kernel, count, columns):
    summed = jnp.zeros((padded.shape[0], count, columns, padded.shape[3]), jnp.float32)
    for offset_row in range(3):
        for offset_col in range(3):
            summed = (
                summed
                + padded[:, offset_row : offset_row + count, offset_col : offset_col + columns]
                * kernel[offset_row, offset_col]
            )
    return summed


def shards(
    tokens,
    valid_rows,
    valid_cols,
    ln1_gain,
    q_weight,
    sr_weight,
    sr_gain,
    kv_weight,
    out_weight,
    ln2_gain,
    fc1_weight,
    dw_weight,
    fc2_weight,
    cotangent,
):
    images = tokens.shape[0]
    columns = tokens.shape[2]
    groups = lax.axis_size("rows")
    score_scale = HEAD_DIM ** (-0.5)
    first_row = lax.axis_index("rows") * POOL
    ids = first_row + jnp.arange(POOL, dtype=jnp.int32)
    inside = (
        (ids[None, :, None] >= 0)
        & (ids[None, :, None] < valid_rows[:, None, None])
        & (jnp.arange(columns)[None, None, :] < valid_cols[:, None, None])
    )
    inside_float = inside.astype(jnp.float32)[..., None]
    key_live = (
        (jnp.arange(groups)[None, :, None] * POOL < valid_rows[:, None, None])
        & (jnp.arange(columns // POOL)[None, None, :] * POOL < valid_cols[:, None, None])
    ).reshape(images, -1)
    picture = tokens.astype(jnp.float32)
    normed, ln1_back = jax.vjp(layer_norm, picture, ln1_gain)
    normed_low = normed.astype(jnp.bfloat16)
    queries = jnp.dot(normed_low, q_weight, preferred_element_type=jnp.float32).astype(jnp.bfloat16)
    masked = jnp.where(inside[..., None], normed_low, 0)
    patches = (
        masked.reshape(images, POOL, columns // POOL, POOL, D)
        .transpose(0, 2, 1, 3, 4)
        .reshape(images, columns // POOL, POOL * POOL * D)
    )
    pooled = jnp.dot(patches, sr_weight, preferred_element_type=jnp.float32)
    reduced, sr_back = jax.vjp(layer_norm, pooled, sr_gain)
    reduced_low = reduced.astype(jnp.bfloat16)
    key_value = jnp.dot(reduced_low, kv_weight, preferred_element_type=jnp.float32).astype(
        jnp.bfloat16
    )
    gathered = lax.all_gather(key_value[:, None], "rows", axis=1, tiled=True).reshape(
        images, -1, 2 * D
    )
    key_part = gathered[..., :D].reshape(images, -1, HEADS, HEAD_DIM)
    value_part = gathered[..., D:].reshape(images, -1, HEADS, HEAD_DIM)
    head_queries = queries.reshape(images, -1, HEADS, HEAD_DIM)
    scores = (
        jnp.einsum("inhe,iphe->ihnp", head_queries, key_part, preferred_element_type=jnp.float32)
        * score_scale
    )
    scores = jnp.where(key_live[:, None, None, :], scores, NEG)
    probabilities = jax.nn.softmax(scores, axis=-1)
    probs_low = probabilities.astype(jnp.bfloat16)
    attended = jnp.einsum(
        "ihnp,iphe->inhe", probs_low, value_part, preferred_element_type=jnp.float32
    ).reshape(images, POOL, columns, D)
    attended_low = (attended * inside_float).astype(jnp.bfloat16)
    middle = picture + jnp.dot(attended_low, out_weight, preferred_element_type=jnp.float32)
    normed2, ln2_back = jax.vjp(layer_norm, middle, ln2_gain)
    normed2_low = normed2.astype(jnp.bfloat16)
    kernel = dw_weight.astype(jnp.float32)
    hidden_shape = (images, POOL, columns, FF)
    hidden = jnp.where(
        inside[..., None],
        jnp.dot(normed2_low, fc1_weight, preferred_element_type=jnp.float32).astype(jnp.bfloat16),
        0,
    )
    padded = pad_columns(padded_2(hidden, (("rows", 1),), 1))
    convolved = depth_conv(padded, kernel, POOL, columns)
    active, gelu_back = jax.vjp(activate, convolved)
    active_low = active.astype(jnp.bfloat16)
    block_out = (
        middle + jnp.dot(active_low, fc2_weight, preferred_element_type=jnp.float32) * inside_float
    ).astype(jnp.bfloat16)
    branch_grad = jnp.where(inside[..., None], cotangent, 0)
    fc2_grad = outer_product(active_low, branch_grad)
    active_grad = back_product(branch_grad, fc2_weight)
    (conv_grad,) = gelu_back(active_grad)
    conv_low = conv_grad.astype(jnp.bfloat16)
    grad_padded = pad_columns(padded_2(conv_low, (("rows", 1),), 1))
    hidden_grad = jnp.zeros(hidden_shape, jnp.float32)
    for offset_row in range(3):
        for offset_col in range(3):
            hidden_grad = (
                hidden_grad
                + grad_padded[
                    :,
                    2 - offset_row : 2 - offset_row + POOL,
                    2 - offset_col : 2 - offset_col + columns,
                ]
                * kernel[offset_row, offset_col]
            )
    dw_grad = jnp.stack(
        [
            jnp.stack(
                [
                    jnp.sum(
                        padded[:, offset_row : offset_row + POOL, offset_col : offset_col + columns]
                        * conv_low.astype(jnp.float32),
                        axis=(0, 1, 2),
                    )
                    for offset_col in range(3)
                ]
            )
            for offset_row in range(3)
        ]
    )
    hidden_low_grad = jnp.where(inside[..., None], hidden_grad, 0.0).astype(jnp.bfloat16)
    fc1_grad = outer_product(normed2_low, hidden_low_grad)
    normed2_grad = back_product(hidden_low_grad, fc1_weight)
    middle_back, ln2_gain_grad = ln2_back(normed2_grad)
    middle_grad = cotangent.astype(jnp.float32) + middle_back
    branch_low = middle_grad.astype(jnp.bfloat16)
    out_grad = outer_product(attended_low, branch_low)
    attended_grad = (
        jnp.where(inside[..., None], back_product(branch_low, out_weight), 0.0)
        .astype(jnp.bfloat16)
        .reshape(images, -1, HEADS, HEAD_DIM)
    )
    value_grad = jnp.einsum(
        "ihnp,inhe->iphe", probs_low, attended_grad, preferred_element_type=jnp.float32
    )
    prob_grad = jnp.einsum(
        "inhe,iphe->ihnp", attended_grad, value_part, preferred_element_type=jnp.float32
    )
    score_grad = (
        probabilities
        * (prob_grad - jnp.sum(probabilities * prob_grad, axis=-1, keepdims=True))
        * score_scale
    ).astype(jnp.bfloat16)
    query_grad = (
        jnp.einsum("ihnp,iphe->inhe", score_grad, key_part, preferred_element_type=jnp.float32)
        .astype(jnp.bfloat16)
        .reshape(images, POOL, columns, D)
    )
    key_grad = jnp.einsum(
        "ihnp,inhe->iphe", score_grad, head_queries, preferred_element_type=jnp.float32
    )
    pair_partial = jnp.concatenate(
        [key_grad.reshape(images, -1, D), value_grad.reshape(images, -1, D)], axis=-1
    ).reshape(images, groups, columns // POOL, 2 * D)
    pair_owned = lax.psum_scatter(pair_partial, "rows", scatter_dimension=1, tiled=True)
    pair_low = pair_owned[:, 0].astype(jnp.bfloat16)
    pair_weight_grad = outer_product(reduced_low, pair_low)
    reduced_grad = back_product(pair_low, kv_weight)
    pooled_grad, sr_gain_grad = sr_back(reduced_grad)
    pooled_low = pooled_grad.astype(jnp.bfloat16)
    sr_grad = outer_product(patches, pooled_low)
    patch_grad = (
        back_product(pooled_low, sr_weight)
        .reshape(images, columns // POOL, POOL, POOL, D)
        .transpose(0, 2, 1, 3, 4)
        .reshape(images, POOL, columns, D)
    )
    normed_grad = back_product(query_grad, q_weight) + jnp.where(inside[..., None], patch_grad, 0.0)
    q_grad = outer_product(normed_low, query_grad)
    picture_back, ln1_gain_grad = ln1_back(normed_grad)
    input_grad = (middle_grad + picture_back).astype(jnp.bfloat16)
    ln1_sum, q_sum, sr_sum, srg_sum, pair_sum, out_sum, ln2_sum, fc1_sum, dw_sum, fc2_sum = (
        lax.psum(
            (
                ln1_gain_grad,
                q_grad,
                sr_grad,
                sr_gain_grad,
                pair_weight_grad,
                out_grad,
                ln2_gain_grad,
                fc1_grad,
                dw_grad,
                fc2_grad,
            ),
            ("rows", "batch"),
        )
    )
    return (
        block_out,
        input_grad,
        ln1_sum,
        q_sum,
        sr_sum,
        srg_sum,
        pair_sum,
        out_sum,
        ln2_sum,
        fc1_sum,
        dw_sum,
        fc2_sum,
    )


def solution(mesh):
    placed = (
        P("batch", "rows", None, None),
        P("batch"),
        P("batch"),
        P(),
        P(),
        P(),
        P(),
        P(),
        P(),
        P(),
        P(),
        P(),
        P(),
        P("batch", "rows", None, None),
    )
    return jax.shard_map(
        shards,
        mesh=mesh,
        in_specs=placed,
        out_specs=(
            P("batch", "rows", None, None),
            P("batch", "rows", None, None),
            P(),
            P(),
            P(),
            P(),
            P(),
            P(),
            P(),
            P(),
            P(),
            P(),
        ),
        check_vma=False,
    )
```

profile of v0, /device:TPU:0, one launch (start us, length us, event | category | flops | bytes accessed | tf_op | source)
XLA Modules:
  0.0 374.6 jit_solution(12874337041095830819)
XLA Ops:
  9.5 1.7 fusion.53
  12.1 1.9 broadcast_select_fusion.1
  16.3 7.2 %all-gather = bf16[8,64,256]{2,1,0:T(8,128)(2,1)S(1)} all-gather(bf16[8,16,256]{2,1,0:T(8,128)(2,1)S(1)} %convolution_convert_fusion.2), channel_id=2, replica_groups=mesh['rows'=4,'batch'=8] {'rows'}, dimensions={1}, use_global_device_ids=true | all-gather | bytes 327680 | tf_op jit(solution)/shard_map/all_gather | solution.py:119
  28.5 2.5 fusion.115
  31.0 1.7 convolution_bitcast_fusion
  32.7 2.2 reshape.361
  34.9 1.9 copy.77
  36.8 1.4 fusion.116
  39.6 2.6 convert_select_fusion
  42.2 1.9 copy-done.1
  44.1 1.5 fusion.111
  45.6 3.3 collective-permute-start
  48.8 1.5 collective-permute-start.1
  50.3 2.2 reshape_reshape.7
  54.9 4.8 %select_maximum_fusion.2 = bf16[8,6,66,1024]{3,2,1,0:T(8,128)(2,1)S(1)} fusion(bf16[8,1,64,1024]{3,2,1,0:T(8,128)(2,1)} %collective-permute-done.1, bf16[8,4,64,1024]{3,2,1,0:T(8,128)(2,1)} %copy-done.1, bf16[8,1,64,1024]{3,2,1,0:T(8,128)(2,1)} %collective-permute-done), kind=kLoop, calls=%fused_computation.67 | loop fusion | flops 38928384 | bytes 12779520 | tf_op jit(solution)/shard_map/concatenate | solution.py:26
  59.7 30.9 %multiply_convert_fusion = (bf16[8,4,64,1024]{3,2,1,0:T(8,128)(2,1)S(1)}, f32[8,4,64,1024]{3,2,1,0:T(8,128)}, f32[8,4,64,1024]{3,2,1,0:T(8,128)}) fusion(f32[1024]{0:T(1024)S(1)} %bitcast.183, bf16[8,6,66,1024]{3,2,1,0:T(8,128)(2,1)S(1)} %select_maximum_fusion.2, f32[1024]{0:T(1024)S(1)} %bitcast.181, bf16[8,1,64,1024]{3,2,1,0:T(8,128)(2,1)} %collective-permute-done.1, ...), kind=kLoop, calls=%fused_computation.51 | loop fusion | flops 195035136 | bytes 52465664 | tf_op jit(solution)/shard_map/convert_element_type | solution.py:149
  90.6 17.6 %fusion.19 = (f32[1024]{0:T(1024)S(1)}, f32[1024]{0:T(1024)S(1)}, f32[1024]{0:T(1024)S(1)}, f32[1024]{0:T(1024)S(1)}, f32[1024]{0:T(1024)S(1)}, /*index=5*/f32[1...) fusion(bf16[8,6,66,1024]{3,2,1,0:T(8,128)(2,1)S(1)} %select_maximum_fus, ...), kind=kOutput, calls=%fused_computation.41 | convolution fusion | flops 629398528 | bytes 53254144 | tf_op jit(solution)/shard_map/dot_general | solution.py:50
  108.2 1.8 fusion.110
  110.0 12.7 %collective-permute-start.2 = (bf16[8,1,64,1024]{3,2,1,0:T(8,128)(2,1)S(1)}, bf16[8,1,64,1024]{3,2,1,0:T(8,128)(2,1)S(1)}, u32[]{:S(2)}, u32[]{:S(2)}) collective-permute-start(bf16[8,1,64,1024]{3,2,1,0:T(8,128)(2,1)S(1)} %get-tuple-element.47), channel_id=1, source_target_pairs={{0,8},{8,16},{16,24},{1,9},{9,17},{17,25},{2,10},{10,18},{18,26},{... | collective-permute-start | bytes 3145736 | tf_op jit(solution)/shard_map/ppermute | solution.py:24
  124.7 2.1 fusion.45
  126.8 2.4 convolution_bitcast_fusion.1
  129.2 3.0 select_maximum_fusion
  132.2 9.0 %fusion.18 = bf16[8,4,64,1024]{3,2,1,0:T(8,128)(2,1)S(1)} fusion(bf16[8,4,64,1024]{3,2,1,0:T(8,128)(2,1)S(1)} %copy-done.3, bf16[8,6,66,1024]{3,2,1,0:T(8,128)(2,1)S(1)} %select_maximum_fusion, bf16[8,1,64,1024]{3,2,1,0:T(8,128)(2,1)S(1)} %collective-permute-done.2, bf16[8,1,64,1024]{3,2,1,0:T(8,128)(2,1)S(1)} %collective-permute-done.3, ...), kind=kLoop, calls=%fused_computation.40 | loop fusion | flops 62914560 | bytes 35690496 | tf_op jit(solution)/shard_map/convert_element_type | solution.py:186
  141.2 2.7 convolution_bitcast_fusion.2
  143.9 1.9 multiply_reduce_fusion
  150.5 2.4 reshape.343
  152.9 1.8 copy.60
  154.7 2.4 fusion.78
  157.1 2.9 convolution_bitcast_fusion.3
  160.0 3.7 convolution_bitcast_fusion.4
  163.6 3.6 fusion.48
  171.9 25.0 %all-reduce.9 = bf16[8,4,16,256]{3,2,1,0:T(8,128)(2,1)S(1)} all-reduce(f32[8,4,16,256]{3,2,1,0:T(8,128)S(1)} %pad_maximum_fusion.4), channel_id=3, replica_groups=mesh['rows'=4,'batch'=8] {'rows'}, use_global_device_ids=true, to_apply=%region_11.12.clone | all-reduce | flops 131072 | bytes 786432
  196.9 1.6 convolution_bitcast_fusion.5
  198.5 2.3 multiply_reduce_fusion.5
  202.2 2.8 reshape.362
  209.7 2.9 reshape.345
  212.6 2.5 copy.68
  215.1 2.0 fusion.117
  218.4 2.7 fusion.54
  222.6 41.1 %all-reduce.3 = (f32[128]{0:T(128)}, f32[128]{0:T(128)}, f32[128]{0:T(128)}, f32[3,3,1024]{2,1,0:T(4,128)}) all-reduce(f32[128]{0:T(128)S(1)} %get-tuple-element.26, f32[128]{0:T(128)S(1)} %get-tuple-element.28, f32[128]{0:T(128)S(1)} %copy-done.35, ...), channel_id=1, replica_groups=mesh['rows'=4,'batch'=8] {'rows','batch'}, use_global_device_ids=true, to_apply=%region_17.18 | all-reduce | flops 9600 | bytes 76800 | tf_op jit(solution)/shard_map/psum | solution.py:238
  263.7 4.0 %add_convert_fusion.1 = bf16[8,4,64,128]{3,2,1,0:T(8,128)(2,1)} fusion(f32[8,4,64,128]{3,2,1,0:T(8,128)S(1)} %copy-done.6, bf16[8,4,64,128]{3,2,1,0:T(8,128)(2,1)} %param.27, f32[8,4,64]{2,1,0:T(4,128)S(1)} %negate_multiply_fusion.1, f32[8,4,64]{2,1,0:T(4,128)S(1)} %copy-done.22, f32[8,4,64]{2,1,0:T(4,128)S(1)} %multiply_multiply_fusion.5, ...), kind=kLoop, calls=%fused_computation.117 | loop fusion | flops 3407872 | bytes 3711488 | tf_op jit(solution)/shard_map/convert_element_type | solution.py:236
  267.6 89.6 %all-reduce.8.cloned.1.call-done = (f32[128,128]{1,0:T(8,128)}, f32[2048,128]{1,0:T(8,128)}, f32[128,256]{1,0:T(8,128)}, f32[128,128]{1,0:T(8,128)}, f32[128,1024]{1,0:T(8,128)}, /*index=5*/f32[1024,128]{1,0:T(8,128)}) async-done(((f32[128,128]{1,0:T(8,128)}, f32[2048,128]{1,0:T(8,128)}, f32[128,256]{1,0:T(8,128)}, f32[128,128]{1,0:T(8,128)}, f32[128,1024]{1,0:T(8,128)}, /*index=5*/f32[1024,128]{1,0:T(8,128)}), ...) | async-done | bytes 2359312 | tf_op jit(solution)/shard_map/psum | solution.py:238
  357.2 1.5 copy.101
  358.7 2.3 copy.102
  361.0 1.6 copy.103
  362.5 1.5 copy.104
  364.0 1.9 copy.105
  365.9 1.9 copy.106
  (140 shorter events, 33.8 us)
Async XLA Ops:
  7.2 7.5 %copy-start = (bf16[2048,128]{1,0:T(8,128)(2,1)S(1)}, bf16[2048,128]{1,0:T(8,128)(2,1)}, u32[]{:S(2)}) copy-start(bf16[2048,128]{1,0:T(8,128)(2,1)} %param.19) | copy-start | bytes 1572868
  7.2 20.0 %copy-start.36 = (s32[8]{0:T(128)S(1)}, s32[8]{0:T(128)}, u32[]{:S(2)}) copy-start(s32[8]{0:T(128)} %param.16) | copy-start | bytes 100
  7.2 350.0 %all-reduce.8.cloned.1.call-start = ((), (), s32[]{:S(2)}) async-start(), calls=%async_computation | async-start | bytes 4718592 | tf_op jit(solution)/shard_map/psum | solution.py:238
  11.2 2.8 copy-start.25
  11.2 2.8 copy-start.15
  12.0 136.4 %copy-start.28 = (pred[8,4,64]{2,1,0:T(4,128)(4,1)}, pred[8,4,64]{2,1,0:T(4,128)(4,1)S(1)}, u32[]{:S(2)}) copy-start(pred[8,4,64]{2,1,0:T(4,128)(4,1)S(1)} %get-tuple-element.63) | copy-start | bytes 6148
  14.0 11.1 %copy-start.7 = (bf16[8,4,64,128]{3,2,1,0:T(8,128)(2,1)}, bf16[8,4,64,128]{3,2,1,0:T(8,128)(2,1)S(1)}, u32[]{:S(2)}) copy-start(bf16[8,4,64,128]{3,2,1,0:T(8,128)(2,1)S(1)} %get-tuple-element.46) | copy-start | bytes 1572868
  14.2 18.5 %copy-start.9 = (bf16[8,4,16,4,128]{4,3,1,2,0:T(4,128)(2,1)}, bf16[8,4,16,4,128]{4,3,1,2,0:T(4,128)(2,1)S(1)}, u32[]{:S(2)}) copy-start(bf16[8,4,16,4,128]{4,3,1,2,0:T(4,128)(2,1)S(1)} %copy.92) | copy-start | bytes 1572868
  15.0 181.9 %copy-start.19 = (f32[8,16]{1,0:T(8,128)}, f32[8,16]{1,0:T(8,128)S(1)}, u32[]{:S(2)}) copy-start(f32[8,16]{1,0:T(8,128)S(1)} %broadcast_multiply_fusion.2) | copy-start | bytes 1540
  15.2 21.6 %copy-start.29 = (f32[8,16]{1,0:T(8,128)}, f32[8,16]{1,0:T(8,128)S(1)}, u32[]{:S(2)}) copy-start(f32[8,16]{1,0:T(8,128)S(1)} %multiply_reduce_fusion.6) | copy-start | bytes 1540
  15.2 181.7 %copy-start.27 = (f32[8,16]{1,0:T(8,128)}, f32[8,16]{1,0:T(8,128)S(1)}, u32[]{:S(2)}) copy-start(f32[8,16]{1,0:T(8,128)S(1)} %fusion.92) | copy-start | bytes 1540
  26.1 10.7 %copy-start.4 = (bf16[8,4,64,128]{3,2,1,0:T(8,128)(2,1)S(1)}, bf16[8,4,64,128]{3,2,1,0:T(8,128)(2,1)}, u32[]{:S(2)}) copy-start(bf16[8,4,64,128]{3,2,1,0:T(8,128)(2,1)} %param.14) | copy-start | bytes 1572868
  27.2 9.6 %copy-start.14 = (bf16[8,256,2,64]{1,3,2,0:T(8,128)(2,1)}, bf16[8,256,2,64]{1,3,2,0:T(8,128)(2,1)S(1)}, u32[]{:S(2)}) copy-start(bf16[8,256,2,64]{1,3,2,0:T(8,128)(2,1)S(1)} %copy.56) | copy-start | bytes 1572868
  27.5 10.8 %copy-start.34 = (pred[8,64]{1,0:T(8,128)(4,1)}, pred[8,64]{1,0:T(8,128)(4,1)S(1)}, u32[]{:S(2)}) copy-start(pred[8,64]{1,0:T(8,128)(4,1)S(1)} %and.62) | copy-start | bytes 1540
  28.5 11.0 %copy-start.33 = (f32[128]{0:T(128)S(1)}, f32[128]{0:T(128)}, u32[]{:S(2)}) copy-start(f32[128]{0:T(128)} %param.23) | copy-start | bytes 1540
  31.0 5.8 %copy-start.38 = (f32[8,2,256]{2,1,0:T(2,128)}, f32[8,2,256]{2,1,0:T(2,128)S(1)}, u32[]{:S(2)}) copy-start(f32[8,2,256]{2,1,0:T(2,128)S(1)} %get-tuple-element.68) | copy-start | bytes 49156
  38.9 0.6 copy-start.23
  42.2 1.9 copy-start.1
  45.6 9.3 %collective-permute-start = (bf16[8,1,64,1024]{3,2,1,0:T(8,128)(2,1)}, bf16[8,1,64,1024]{3,2,1,0:T(8,128)(2,1)}, u32[]{:S(2)}, u32[]{:S(2)}) collective-permute-start(bf16[8,1,64,1024]{3,2,1,0:T(8,128)(2,1)} %get-tuple-element.49), channel_id=1, source_target_pairs={{0,8},{8,16},{16,24},{1,9},{9,17},{17,25},{2,10},{10,18},{18,26},{... | collective-permute-start | bytes 3145736 | tf_op jit(solution)/shard_map/ppermute | solution.py:24
  48.8 6.0 %collective-permute-start.1 = (bf16[8,1,64,1024]{3,2,1,0:T(8,128)(2,1)}, bf16[8,1,64,1024]{3,2,1,0:T(8,128)(2,1)}, u32[]{:S(2)}, u32[]{:S(2)}) collective-permute-start(bf16[8,1,64,1024]{3,2,1,0:T(8,128)(2,1)} %get-tuple-element.50), channel_id=1, source_target_pairs={{8,0},{16,8},{24,16},{9,1},{17,9},{25,17},{10,2},{18,10},{26,18},{... | collective-permute-start | bytes 3145736 | tf_op jit(solution)/shard_map/ppermute | solution.py:25
  52.6 7.1 %copy-start.2 = (bf16[8,4,64,1024]{3,2,1,0:T(8,128)(2,1)S(1)}, bf16[8,4,64,1024]{3,2,1,0:T(8,128)(2,1)}, u32[]{:S(2)}) copy-start(bf16[8,4,64,1024]{3,2,1,0:T(8,128)(2,1)} %copy-done.1) | copy-start | bytes 12582916
  59.7 30.9 %copy-start.13 = (bf16[8,4,64,128]{3,2,1,0:T(8,128)(2,1)S(1)}, bf16[8,4,64,128]{3,2,1,0:T(8,128)(2,1)}, u32[]{:S(2)}) copy-start(bf16[8,4,64,128]{3,2,1,0:T(8,128)(2,1)} %param.27) | copy-start | bytes 1572868
  59.7 30.9 %copy-start.17 = (bf16[1024,128]{1,0:T(8,128)(2,1)S(1)}, bf16[1024,128]{1,0:T(8,128)(2,1)}, u32[]{:S(2)}) copy-start(bf16[1024,128]{1,0:T(8,128)(2,1)} %param.26) | copy-start | bytes 786436
  110.0 19.2 %collective-permute-start.2 = (bf16[8,1,64,1024]{3,2,1,0:T(8,128)(2,1)S(1)}, bf16[8,1,64,1024]{3,2,1,0:T(8,128)(2,1)S(1)}, u32[]{:S(2)}, u32[]{:S(2)}) collective-permute-start(bf16[8,1,64,1024]{3,2,1,0:T(8,128)(2,1)S(1)} %get-tuple-element.47), channel_id=1, source_target_pairs={{0,8},{8,16},{16,24},{1,9},{9,17},{17,25},{2,10},{10,18},{18,26},{... | collective-permute-start | bytes 3145736 | tf_op jit(solution)/shard_map/ppermute | solution.py:24
  122.7 6.6 %collective-permute-start.3 = (bf16[8,1,64,1024]{3,2,1,0:T(8,128)(2,1)S(1)}, bf16[8,1,64,1024]{3,2,1,0:T(8,128)(2,1)S(1)}, u32[]{:S(2)}, u32[]{:S(2)}) collective-permute-start(bf16[8,1,64,1024]{3,2,1,0:T(8,128)(2,1)S(1)} %get-tuple-element.48), channel_id=1, source_target_pairs={{8,0},{16,8},{24,16},{9,1},{17,9},{25,17},{10,2},{18,10},{26,18},{... | collective-permute-start | bytes 3145736 | tf_op jit(solution)/shard_map/ppermute | solution.py:25
  124.7 4.6 %copy-start.3 = (bf16[8,4,64,1024]{3,2,1,0:T(8,128)(2,1)S(1)}, bf16[8,4,64,1024]{3,2,1,0:T(8,128)(2,1)}, u32[]{:S(2)}) copy-start(bf16[8,4,64,1024]{3,2,1,0:T(8,128)(2,1)} %get-tuple-element.77) | copy-start | bytes 12582916
  132.2 11.7 %copy-start.37 = (bf16[128,1024]{1,0:T(8,128)(2,1)S(1)}, bf16[128,1024]{1,0:T(8,128)(2,1)}, u32[]{:S(2)}) copy-start(bf16[128,1024]{1,0:T(8,128)(2,1)} %param.24) | copy-start | bytes 786436
  141.2 4.6 %copy-start.24 = (f32[8,4,64]{2,1,0:T(4,128)S(1)}, f32[8,4,64]{2,1,0:T(4,128)}, u32[]{:S(2)}) copy-start(f32[8,4,64]{2,1,0:T(4,128)} %copy-done.23) | copy-start | bytes 24580
  141.2 8.1 %copy-start.30 = (bf16[128,128]{1,0:T(8,128)(2,1)S(1)}, bf16[128,128]{1,0:T(8,128)(2,1)}, u32[]{:S(2)}) copy-start(bf16[128,128]{1,0:T(8,128)(2,1)} %param.22) | copy-start | bytes 98308
  147.1 1.0 copy-start.5
  147.1 16.5 %copy-start.21 = (f32[8,4,64]{2,1,0:T(4,128)}, f32[8,4,64]{2,1,0:T(4,128)S(1)}, u32[]{:S(2)}) copy-start(f32[8,4,64]{2,1,0:T(4,128)S(1)} %negate_multiply_fusion.2) | copy-start | bytes 24580
  148.5 0.8 copy-start.11
  154.7 9.0 %copy-start.18 = (bf16[8,64,128]{1,2,0:T(8,128)(2,1)S(1)}, bf16[8,64,128]{1,2,0:T(8,128)(2,1)}, u32[]{:S(2)}) copy-start(bf16[8,64,128]{1,2,0:T(8,128)(2,1)} %copy.81) | copy-start | bytes 393220
  157.1 10.1 %copy-start.12 = (bf16[8,4,64,128]{3,2,1,0:T(8,128)(2,1)S(1)}, bf16[8,4,64,128]{3,2,1,0:T(8,128)(2,1)}, u32[]{:S(2)}) copy-start(bf16[8,4,64,128]{3,2,1,0:T(8,128)(2,1)} %copy-done.11) | copy-start | bytes 1572868
  160.0 37.0 %copy-start.31 = (f32[128]{0:T(128)S(1)}, f32[128]{0:T(128)}, u32[]{:S(2)}) copy-start(f32[128]{0:T(128)} %param.20) | copy-start | bytes 1540
  167.2 47.9 %copy-start.8 = (bf16[8,4,64,128]{3,2,1,0:T(8,128)(2,1)S(1)}, bf16[8,4,64,128]{3,2,1,0:T(8,128)(2,1)}, u32[]{:S(2)}) copy-start(bf16[8,4,64,128]{3,2,1,0:T(8,128)(2,1)} %copy-done.7) | copy-start | bytes 1572868
  168.5 48.5 %copy-start.10 = (bf16[128,2048]{1,0:T(8,128)(2,1)S(1)}, bf16[128,2048]{1,0:T(8,128)(2,1)}, u32[]{:S(2)}) copy-start(bf16[128,2048]{1,0:T(8,128)(2,1)} %reshape_reshape.7) | copy-start | bytes 1572868
  205.0 16.2 %copy-start.26 = (f32[8,4,64]{2,1,0:T(4,128)S(1)}, f32[8,4,64]{2,1,0:T(4,128)}, u32[]{:S(2)}) copy-start(f32[8,4,64]{2,1,0:T(4,128)} %copy-done.25) | copy-start | bytes 24580
  205.0 16.2 %copy-start.16 = (f32[8,4,64]{2,1,0:T(4,128)S(1)}, f32[8,4,64]{2,1,0:T(4,128)}, u32[]{:S(2)}) copy-start(f32[8,4,64]{2,1,0:T(4,128)} %copy-done.15) | copy-start | bytes 24580
  205.0 16.2 %copy-start.32 = (f32[128]{0:T(128)S(1)}, f32[128]{0:T(128)}, u32[]{:S(2)}) copy-start(f32[128]{0:T(128)} %param.17) | copy-start | bytes 1540
  205.9 16.7 %copy-start.20 = (f32[3,3,1024]{2,1,0:T(4,128)S(1)}, f32[3,3,1024]{2,1,0:T(4,128)}, u32[]{:S(2)}) copy-start(f32[3,3,1024]{2,1,0:T(4,128)} %pad_maximum_fusion.5) | copy-start | bytes 110596
  205.9 16.7 %copy-start.35 = (f32[128]{0:T(128)S(1)}, f32[128]{0:T(128)}, u32[]{:S(2)}) copy-start(f32[128]{0:T(128)} %get-tuple-element.24) | copy-start | bytes 1540
  205.9 57.8 %copy-start.6 = (f32[8,4,64,128]{3,2,1,0:T(8,128)S(1)}, f32[8,4,64,128]{3,2,1,0:T(8,128)}, u32[]{:S(2)}) copy-start(f32[8,4,64,128]{3,2,1,0:T(8,128)} %copy-done.5) | copy-start | bytes 3145732
  205.9 57.8 %copy-start.22 = (f32[8,4,64]{2,1,0:T(4,128)S(1)}, f32[8,4,64]{2,1,0:T(4,128)}, u32[]{:S(2)}) copy-start(f32[8,4,64]{2,1,0:T(4,128)} %copy-done.21) | copy-start | bytes 24580
Sparse Core Ops, SparseCore 0:
  218.6 138.6 all-reduce.7
where the time goes:
time: 376 us; the launch traced here: 375 us
  waiting for transfers between devices  89.6 us (24%)
  blocking collectives  73.3 us (19%)
  other arithmetic  65.5 us (17%)
  matrix products  63.6 us (17%)
  local copies, waits for them, and re-layouts  49 us (13%)
  starting transfers between devices  18.7 us (5%)
  between operations  14.9 us (4%)
    psum x1, waiting for transfers between devices, shards(): lax.psum((ln1_gain_grad, q_grad, sr_grad, sr_gain_grad, pair_weight_grad,...  89.6 us
    psum x1, blocking collectives, shards(): lax.psum((ln1_gain_grad, q_grad, sr_grad, sr_gain_grad, pair_weight_grad,...  41.1 us
    convert_element_type x1, other arithmetic, shards(): active_low = active.astype(jnp.bfloat16)  30.9 us
    dot_general x6, matrix products, back_product(): lax.dot_general(grad, weight, (((grad.ndim - 1,), (1,)), ((), ())), prefe...  27 us
    unnamed x1, blocking collectives  25 us
    unnamed x86, local copies, waits for them, and re-layouts  17.3 us
    ppermute x2, starting transfers between devices, padded_2(): before = lax.ppermute(last, axis, up)  15.9 us
    dot_general x6, matrix products, outer_product(): lax.dot_general(left.reshape(-1, left.shape[-1]), right.reshape(-1, right...  11.3 us
  transfers between devices with their start and end apart: 5, of which 1 were waited for; matrix products, arithmetic and copies ran while one was open for 5% of the time, Pallas kernels for 0%

commit v1 on v0

--- a/solution.py
+++ b/solution.py
@@ -1,6 +1,8 @@
 import jax
 import jax.numpy as jnp
 from jax import lax
+from jax.experimental import pallas as pl
+from jax.experimental.pallas import tpu as pltpu
 from jax.sharding import PartitionSpec as P
 
 D = 128
@@ -68,7 +70,7 @@
     return summed
 
 
-def shards(
+def row_shards(
     tokens,
     valid_rows,
     valid_cols,
@@ -267,6 +269,491 @@
     )
 
 
+VMEM = pltpu.VMEM
+NT = (((1,), (1,)), ((), ()))
+TN = (((0,), (0,)), ((), ()))
+
+
+def mm(left, right):
+    return jnp.dot(left, right, preferred_element_type=jnp.float32)
+
+
+def mm_nt(left, right):
+    return lax.dot_general(left, right, NT, preferred_element_type=jnp.float32)
+
+
+def mm_tn(left, right):
+    return lax.dot_general(left, right, TN, preferred_element_type=jnp.float32)
+
+
+def norm_parts(source):
+    centered = source - jnp.mean(source, axis=-1, keepdims=True)
+    scale = lax.rsqrt(jnp.mean(centered * centered, axis=-1, keepdims=True) + EPS)
+    return centered * scale, scale
+
+
+def norm_back(grad, gain, unit, scale):
+    scaled = grad * gain
+    inner = jnp.mean(scaled * unit, axis=-1, keepdims=True)
+    return scale * (scaled - jnp.mean(scaled, axis=-1, keepdims=True) - unit * inner)
+
+
+def block_inside(first_row, rows, cols):
+    row = first_row + lax.broadcasted_iota(jnp.int32, (4, 64, D), 0)
+    col = lax.broadcasted_iota(jnp.int32, (4, 64, D), 1)
+    return ((row < rows) & (col < cols)).reshape(256, D)
+
+
+def halves(shape):
+    return lax.broadcasted_iota(jnp.int32, shape, len(shape) - 1) < HEAD_DIM
+
+
+def block_pair(source):
+    left = halves(source.shape)
+    zero = jnp.zeros_like(source)
+    return jnp.concatenate([jnp.where(left, source, zero), jnp.where(left, zero, source)], axis=0)
+
+
+def half_reduce(reducer, value, empty):
+    left = halves(value.shape)
+    first = reducer(jnp.where(left, value, empty), axis=-1, keepdims=True)
+    second = reducer(jnp.where(left, empty, value), axis=-1, keepdims=True)
+    return jnp.where(left, first, second)
+
+
+def attend_kernel(
+    place, vrows, vcols, own, near1, near2, near3, ln1, wq, wsr, srg, wkv, wout,
+    x_out, normed_out, q_out, prob_out, att_out, mid_out, pat_out, pooled_out, kv_out, masked,
+):
+    me = place[0]
+    for k, chunk in enumerate((own, near1, near2, near3)):
+        block = me ^ k
+        for i in range(2):
+            raw = own[2 * me + i] if k == 0 else chunk[i]
+            x_out[pl.ds(block * 4, 4), i] = raw
+            unit, _ = norm_parts(raw.astype(jnp.float32).reshape(256, D))
+            normed = (unit * ln1[...]).astype(jnp.bfloat16)
+            normed_out[pl.ds(block * 4, 4), i] = normed.reshape(4, 64, D)
+            inside = block_inside(block * 4, vrows[2 * me + i], vcols[2 * me + i])
+            start = pl.multiple_of(i * 1024 + block * 256, 256)
+            masked[pl.ds(start, 256), :] = jnp.where(inside, normed.astype(jnp.float32), 0.0)
+    for i in range(2):
+        for a in range(4):
+            for u in range(4):
+                for t in range(4):
+                    piece = masked[pl.ds(i * 1024 + (4 * a + u) * 64 + t, 16, stride=4), :]
+                    pat_out[pl.ds(i * 64 + a * 16, 16), pl.ds((u * 4 + t) * D, D)] = piece.astype(
+                        jnp.bfloat16
+                    )
+    pooled = mm(pat_out[...], wsr[...])
+    pooled_out[...] = pooled
+    unit, _ = norm_parts(pooled)
+    pairs = mm((unit * srg[...]).astype(jnp.bfloat16), wkv[...]).astype(jnp.bfloat16)
+    kv_out[...] = pairs
+    lane = lax.broadcasted_iota(jnp.int32, (1, D), 1) % 64
+    for i in range(2):
+        rows, cols = vrows[2 * me + i], vcols[2 * me + i]
+        live = ((lane // 16) * 4 < rows) & ((lane % 16) * 4 < cols)
+        keys = block_pair(pairs[i * 64 : i * 64 + 64, :D].astype(jnp.float32)).astype(jnp.bfloat16)
+        values = block_pair(pairs[i * 64 : i * 64 + 64, D:].astype(jnp.float32)).astype(jnp.bfloat16)
+        for b in range(4):
+            part = pl.ds(b * 4, 4)
+            query = mm(normed_out[part, i].reshape(256, D), wq[...]).astype(jnp.bfloat16)
+            q_out[part, i] = query.reshape(4, 64, D)
+            scores = jnp.where(live, mm_nt(query, keys) * SCORE_SCALE, NEG)
+            weights = jnp.exp(scores - half_reduce(jnp.max, scores, -jnp.inf))
+            probs = weights / half_reduce(jnp.sum, weights, 0.0)
+            prob_out[part, i] = probs.reshape(4, 64, D)
+            mixed = mm(probs.astype(jnp.bfloat16), values)
+            mixed = jnp.where(block_inside(b * 4, rows, cols), mixed, 0.0).astype(jnp.bfloat16)
+            att_out[part, i] = mixed.reshape(4, 64, D)
+            middle = x_out[part, i].astype(jnp.float32).reshape(256, D) + mm(mixed, wout[...])
+            mid_out[part, i] = middle.reshape(4, 64, D)
+
+
+def gelu_parts(x):
+    density = jnp.exp(x * x * -0.5) * 0.3989422804014327
+    phi = 0.5 + 0.5 * lax.erf(x * 0.7071067811865476)
+    return x * phi, phi + x * density
+
+
+def feed_kernel(
+    place, vrows, vcols, mid, cot, cot1, cot2, cot3, ln2, wfc1, wdw, wfc2,
+    bo0, bo1, bo2, bo3, mg_out, send_out, keep_out,
+    cj, br, br_t, wide, x_t, xcol, w9, cg, act, acc, stage, mask,
+):
+    me = place[0]
+    zeros = jnp.zeros((128, 3 * D), jnp.bfloat16)
+    wide[pl.ds(0, 128), :] = zeros
+    wide[pl.ds(2176, 128), :] = zeros
+    x_t[:, pl.ds(0, 128)] = jnp.zeros((3 * D, 128), jnp.bfloat16)
+    x_t[:, pl.ds(2176, 128)] = jnp.zeros((3 * D, 128), jnp.bfloat16)
+    cg[pl.ds(0, 128), :] = jnp.zeros((128, FF), jnp.bfloat16)
+    cg[pl.ds(2176, 128), :] = jnp.zeros((128, FF), jnp.bfloat16)
+    col = lax.broadcasted_iota(jnp.int32, (512, D), 0) % 64
+    for k, chunk in enumerate((cot, cot1, cot2, cot3)):
+        block = me ^ k
+        for i in range(2):
+            raw = cot[2 * me + i] if k == 0 else chunk[i]
+            inside = block_inside(block * 4, vrows[2 * me + i], vcols[2 * me + i]).reshape(4, 64, D)
+            for r in range(4):
+                at = pl.ds(pl.multiple_of(block * 512 + r * 128 + i * 64, 64), 64)
+                cj[at, :] = raw[r]
+                mask[at, :] = jnp.where(inside[r], 1.0, 0.0)
+    fc1_wide = wfc1[...].astype(jnp.float32)
+    for tap in range(9):
+        w9[pl.ds(tap * D, D), :] = (fc1_wide * wdw[pl.ds(tap, 1), :]).astype(jnp.bfloat16)
+    for b in range(4):
+        part = pl.ds(b * 512, 512)
+        inside = mask[part, :]
+        branch = cj[part, :].astype(jnp.float32) * inside
+        br[part, :] = branch.astype(jnp.bfloat16)
+        br_t[:, part] = branch.T.astype(jnp.bfloat16)
+        unit, _ = norm_parts(mid[part, :])
+        normed = ((unit * ln2[...]).astype(jnp.bfloat16)).astype(jnp.float32) * inside
+        before = jnp.where(col == 0, 0.0, pltpu.roll(normed, 1, 0))
+        after = jnp.where(col == 63, 0.0, pltpu.roll(normed, 511, 0))
+        for s, value in enumerate((before, normed, after)):
+            wide[pl.ds(b * 512 + 128, 512), pl.ds(s * D, D)] = value.astype(jnp.bfloat16)
+            x_t[pl.ds(s * D, D), pl.ds(b * 512 + 128, 512)] = value.T.astype(jnp.bfloat16)
+    for p in range(3):
+        xcol[:, pl.ds(p * 3 * D, 3 * D)] = wide[pl.ds(p * 128, 2048), :]
+    for f in range(FF // FC):
+        chan = pl.ds(f * FC, FC)
+        for b in range(2048 // TB):
+            part = pl.ds(b * TB, TB)
+            conv = mm(xcol[part, :], w9[:, chan])
+            value, slope = gelu_parts(conv)
+            low = value.astype(jnp.bfloat16)
+            act[part, :] = low
+            grad = mm_nt(br[part, :], wfc2[chan, :]) * slope
+            cg[pl.ds(b * TB + 128, TB), chan] = grad.astype(jnp.bfloat16)
+            if f == 0:
+                acc[part, :] = mm(low, wfc2[chan, :])
+            else:
+                acc[part, :] += mm(low, wfc2[chan, :])
+        fc2_grad = mm(br_t[...], act[...])
+        stage[pl.ds(FF + f * FC, FC), :] = fc2_grad.T
+        fc1_grad = jnp.zeros((D, FC), jnp.float32)
+        grads = cg[pl.ds(128, 2048), chan]
+        for p in range(3):
+            outer = mm(x_t[:, pl.ds(p * 128, 2048)], grads)
+            for s in range(3):
+                tap = p * 3 + s
+                here = outer[s * D : (s + 1) * D]
+                fc1_grad += here * wdw[pl.ds(tap, 1), chan]
+                dw_grad = jnp.sum(here * wfc1[:, chan].astype(jnp.float32), axis=0, keepdims=True)
+                for j in range(FC // D):
+                    stage[pl.ds(2 * FF + tap * 8 + f * (FC // D) + j, 1), :] = dw_grad[:, j * D : (j + 1) * D]
+        for j in range(FC // D):
+            stage[pl.ds((f * (FC // D) + j) * D, D), :] = fc1_grad[:, j * D : (j + 1) * D]
+    gain_grad = jnp.zeros((1, D), jnp.float32)
+    for k, bo in enumerate((bo0, bo1, bo2, bo3)):
+        base = pl.multiple_of((me ^ k) * 512, 512)
+        part = pl.ds(base, 512)
+        inside = mask[part, :]
+        middle = mid[part, :]
+        result = (middle + acc[part, :] * inside).astype(jnp.bfloat16).reshape(4, 2, 64, D)
+        for i in range(2):
+            bo[i] = result[:, i]
+        spread = jnp.zeros((512, 3 * D), jnp.float32)
+        for p in range(3):
+            rows = pl.ds(pl.multiple_of(base + (2 - p) * 128, 128), 512)
+            spread += mm_nt(cg[rows, :], w9[pl.ds(p * 3 * D, 3 * D), :])
+        after = jnp.where(col == 63, 0.0, pltpu.roll(spread[:, :D], 511, 0))
+        before = jnp.where(col == 0, 0.0, pltpu.roll(spread[:, 2 * D :], 1, 0))
+        normed_grad = (spread[:, D : 2 * D] + before + after) * inside
+        unit, scale = norm_parts(middle)
+        gain_grad += jnp.sum(normed_grad * unit, axis=0, keepdims=True)
+        mg_out[part, :] = cj[part, :].astype(jnp.float32) + norm_back(normed_grad, ln2[...], unit, scale)
+    stage[pl.ds(2 * FF + 72, 1), :] = gain_grad
+    stage[pl.ds(2 * FF + 73, 55), :] = jnp.zeros((55, D), jnp.float32)
+    split_pack(place, stage, send_out, keep_out)
+
+
+def split_pack(place, stage, send_out, keep_out):
+    rows = stage.shape[0] // 8
+    for k in range(4):
+        at = pl.ds(k * rows, rows)
+        for out, core in ((send_out, 1 - place[1]), (keep_out, place[1])):
+            start = pl.multiple_of((core * 4 + (place[2] ^ k)) * rows, 16)
+            out[at, :] = stage[pl.ds(start, rows), :].astype(jnp.bfloat16)
+
+
+def back_kernel(
+    place, vrows, vcols, x, normed, query, prob, att, mgrad, pat, pooled, kv,
+    ln1, wq, wsr, srg, wkv, wout,
+    ig0, ig1, ig2, ig3, send_out, keep_out,
+    stage, probs_low, att_grad, score_grad, query_grad, unfold,
+):
+    me = place[0]
+    zero = jnp.zeros((D, D), jnp.float32)
+    out_grad = zero
+    key_rows = []
+    for i in range(2):
+        rows, cols = vrows[2 * me + i], vcols[2 * me + i]
+        keys = block_pair(kv[pl.ds(i * 64, 64), pl.ds(0, D)].astype(jnp.float32)).astype(jnp.bfloat16)
+        values = block_pair(kv[pl.ds(i * 64, 64), pl.ds(D, D)].astype(jnp.float32)).astype(jnp.bfloat16)
+        for b in range(4):
+            part = pl.ds(b * 4, 4)
+            at = pl.ds(b * 256, 256)
+            low = mgrad[part, i].reshape(256, D).astype(jnp.bfloat16)
+            out_grad += mm_tn(att[part, i].reshape(256, D), low)
+            mixed = jnp.where(block_inside(b * 4, rows, cols), mm_nt(low, wout[...]), 0.0).astype(jnp.bfloat16)
+            att_grad[at, :] = mixed
+            weights = prob[part, i].reshape(256, D)
+            probs_low[at, :] = weights.astype(jnp.bfloat16)
+            back = mm_nt(mixed, values)
+            back = weights * (back - half_reduce(jnp.sum, weights * back, 0.0)) * SCORE_SCALE
+            back = back.astype(jnp.bfloat16)
+            score_grad[at, :] = back
+            query_grad[pl.ds(i * 1024 + b * 256, 256), :] = mm(back, keys).astype(jnp.bfloat16)
+        value_full = mm_tn(probs_low[...], att_grad[...])
+        key_full = mm_tn(score_grad[...], query[:, i].reshape(1024, D))
+        left = halves((64, D))
+        key_rows.append(
+            jnp.concatenate(
+                [
+                    jnp.where(left, key_full[:64], key_full[64:]),
+                    jnp.where(left, value_full[:64], value_full[64:]),
+                ],
+                axis=1,
+            )
+        )
+    pair = jnp.concatenate(key_rows, axis=0).astype(jnp.bfloat16)
+    unit, scale = norm_parts(pooled[...])
+    reduced = (unit * srg[...]).astype(jnp.bfloat16)
+    kv_grad = mm_tn(reduced, pair)
+    reduced_grad = mm_nt(pair, wkv[...])
+    srg_grad = jnp.sum(reduced_grad * unit, axis=0, keepdims=True)
+    pooled_low = norm_back(reduced_grad, srg[...], unit, scale).astype(jnp.bfloat16)
+    stage[pl.ds(0, 2048), :] = mm_tn(pat[...], pooled_low)
+    patch_grad = mm_nt(pooled_low, wsr[...])
+    for i in range(2):
+        for a in range(4):
+            for u in range(4):
+                for t in range(4):
+                    unfold[pl.ds(i * 1024 + (4 * a + u) * 64 + t, 16, stride=4), :] = patch_grad[
+                        i * 64 + a * 16 : i * 64 + a * 16 + 16, (u * 4 + t) * D : (u * 4 + t + 1) * D
+                    ]
+    stage[pl.ds(2048, D), :] = kv_grad[:, :D]
+    stage[pl.ds(2176, D), :] = kv_grad[:, D:]
+    stage[pl.ds(2432, D), :] = out_grad
+    q_grad = zero
+    gain_grad = jnp.zeros((1, D), jnp.float32)
+    for k, ig in enumerate((ig0, ig1, ig2, ig3)):
+        block = me ^ k
+        part = pl.ds(block * 4, 4)
+        for i in range(2):
+            at = pl.ds(pl.multiple_of(i * 1024 + block * 256, 256), 256)
+            inside = block_inside(block * 4, vrows[2 * me + i], vcols[2 * me + i])
+            back = query_grad[at, :]
+            q_grad += mm_tn(normed[part, i].reshape(256, D), back)
+            grad = mm_nt(back, wq[...]) + jnp.where(inside, unfold[at, :], 0.0)
+            unit, scale = norm_parts(x[part, i].astype(jnp.float32).reshape(256, D))
+            gain_grad += jnp.sum(grad * unit, axis=0, keepdims=True)
+            total = mgrad[part, i].reshape(256, D) + norm_back(grad, ln1[...], unit, scale)
+            ig[i] = total.astype(jnp.bfloat16).reshape(4, 64, D)
+    stage[pl.ds(2304, D), :] = q_grad
+    stage[pl.ds(2560, 1), :] = gain_grad
+    stage[pl.ds(2561, 1), :] = srg_grad
+    stage[pl.ds(2562, 126), :] = jnp.zeros((126, D), jnp.float32)
+    split_pack(place, stage, send_out, keep_out)
+
+
+def call(kernel, scalars, arrays, outs, scratch, flops=0, name=None):
+    spec = pl.BlockSpec(memory_space=VMEM)
+    return pl.pallas_call(
+        kernel,
+        out_shape=[jax.ShapeDtypeStruct(shape, kind) for shape, kind in outs],
+        in_specs=[pl.BlockSpec(memory_space=pltpu.SMEM)] * len(scalars) + [spec] * len(arrays),
+        out_specs=[spec] * len(outs),
+        scratch_shapes=scratch,
+        compiler_params=pltpu.CompilerParams(vmem_limit_bytes=56 * 2**20),
+        cost_estimate=pl.CostEstimate(flops=flops, bytes_accessed=4 * 2**20, transcendentals=0),
+        name=name,
+    )(*scalars, *arrays)
+
+
+BF, F32 = jnp.bfloat16, jnp.float32
+JOINT = (16, 2, 64, D)
+CHUNK = (2, 4, 64, D)
+PACK1, PACK2 = 2176, 2688
+FC, TB = 256, 512
+SCORE_SCALE = HEAD_DIM ** (-0.5)
+
+
+def attend(place, vrows, vcols, chunks, ln1, wq, wsr, srg, wkv, wout):
+    return call(
+        attend_kernel,
+        (place, vrows, vcols),
+        (*chunks, ln1, wq, wsr, srg, wkv, wout),
+        [
+            (JOINT, BF), (JOINT, BF), (JOINT, BF), (JOINT, F32), (JOINT, BF), (JOINT, F32),
+            ((128, 2048), BF), ((128, D), F32), ((128, 2 * D), BF),
+        ],
+        [VMEM((2048, D), F32)],
+        flops=10**9, name="attend",
+    )
+
+
+def feed(place, vrows, vcols, middle, chunks, ln2, wfc1, wdw, wfc2):
+    return call(
+        feed_kernel,
+        (place, vrows, vcols),
+        (middle, *chunks, ln2, wfc1, wdw, wfc2),
+        [(CHUNK, BF)] * 4 + [((2048, D), F32), ((PACK1 // 2, D), BF), ((PACK1 // 2, D), BF)],
+        [
+            VMEM((2048, D), BF), VMEM((2048, D), BF), VMEM((D, 2048), BF),
+            VMEM((2304, 3 * D), BF), VMEM((3 * D, 2304), BF), VMEM((2048, 9 * D), BF),
+            VMEM((9 * D, FF), BF), VMEM((2304, FF), BF), VMEM((2048, FC), BF),
+            VMEM((2048, D), F32), VMEM((PACK1, D), F32), VMEM((2048, D), F32),
+        ],
+        flops=16 * 10**9, name="feed",
+    )
+
+
+def back(place, vrows, vcols, kept, mgrad, ln1, wq, wsr, srg, wkv, wout):
+    x, normed, query, prob, att, _, pat, pooled, kv = kept
+    return call(
+        back_kernel,
+        (place, vrows, vcols),
+        (x, normed, query, prob, att, mgrad, pat, pooled, kv, ln1, wq, wsr, srg, wkv, wout),
+        [(CHUNK, BF)] * 4 + [((PACK2 // 2, D), BF), ((PACK2 // 2, D), BF)],
+        [
+            VMEM((PACK2, D), F32), VMEM((1024, D), BF), VMEM((1024, D), BF), VMEM((1024, D), BF),
+            VMEM((2048, D), BF), VMEM((2048, D), F32),
+        ],
+        flops=2 * 10**9, name="back",
+    )
+
+
+def swap(value, axes, partner):
+    size = lax.axis_size(axes)
+    return lax.ppermute(value, axes, [(i, partner(i)) for i in range(size)])
+
+
+def over_rows(value, k):
+    return swap(value, "rows", lambda i: i ^ k)
+
+
+def over_plane(value, k):
+    size = lax.axis_size("batch")
+    return swap(value, ("rows", "batch"), lambda i: i ^ ((k >> 1) * 2 * size) ^ (k & 1))
+
+
+def over_line(value, k):
+    return swap(value, "batch", lambda i: i ^ (2 * k))
+
+
+def plus(*values):
+    return sum(v.astype(F32) for v in values).astype(BF)
+
+
+def summed(send, keep):
+    rows = send.shape[0] // 4
+    both = plus(keep, over_rows(send, 1))
+    parts = [both[k * rows : (k + 1) * rows] for k in range(4)]
+    mine = plus(parts[0], *(over_plane(parts[k], k) for k in (1, 2, 3)))
+    near, far, last = (over_line(mine, k).astype(F32) for k in (1, 2, 3))
+    total = ((mine.astype(F32) + near) + (far + last)).astype(BF)
+    pieces = [total] + [over_plane(total, k) for k in (1, 2, 3)]
+    return pieces + [over_rows(piece, 1) for piece in pieces]
+
+
+def finish_kernel(place, *refs):
+    first, second = refs[:8], refs[8:16]
+    q, sr, kv, out, fc1, dw, fc2, gains, stage1, stage2 = refs[16:]
+    for pieces, stage in ((first, stage1), (second, stage2)):
+        rows = stage.shape[0] // 8
+        for j, piece in enumerate(pieces):
+            core = place[1] if j < 4 else 1 - place[1]
+            start = pl.multiple_of((core * 4 + (place[2] ^ (j % 4))) * rows, 16)
+            stage[pl.ds(start, rows), :] = piece[...].astype(F32)
+    for j in range(8):
+        fc1[:, pl.ds(j * D, D)] = stage1[pl.ds(j * D, D), :]
+    fc2[...] = stage1[pl.ds(FF, FF), :]
+    dw[...] = stage1[pl.ds(2 * FF, 72), :]
+    sr[...] = stage2[pl.ds(0, 2048), :]
+    for j in range(2):
+        kv[:, pl.ds(j * D, D)] = stage2[pl.ds(2048 + j * D, D), :]
+    q[...] = stage2[pl.ds(2304, D), :]
+    out[...] = stage2[pl.ds(2432, D), :]
+    gains[pl.ds(0, 1), :] = stage1[pl.ds(2 * FF + 72, 1), :]
+    gains[pl.ds(1, 1), :] = stage2[pl.ds(2560, 1), :]
+    gains[pl.ds(2, 1), :] = stage2[pl.ds(2561, 1), :]
+    gains[pl.ds(3, 5), :] = jnp.zeros((5, D), F32)
+
+
+def finish(place, first, second):
+    return call(
+        finish_kernel,
+        (place,),
+        (*first, *second),
+        [
+            ((D, D), F32), ((2048, D), F32), ((D, 2 * D), F32), ((D, D), F32),
+            ((D, FF), F32), ((72, D), F32), ((FF, D), F32), ((8, D), F32),
+        ],
+        [VMEM((PACK1, D), F32), VMEM((PACK2, D), F32)],
+        name="finish",
+    )
+
+
+def gather_kernel(place, part0, part1, part2, part3, out):
+    for k, part in enumerate((part0, part1, part2, part3)):
+        out[pl.ds(2 * (place[0] ^ k), 2)] = part[...]
+
+
+def gather_rows(place, parts, shape):
+    (out,) = call(gather_kernel, (place,), parts, [(shape, BF)], [], name="gather_rows")
+    return out
+
+
+def image_shards(
+    tokens, valid_rows, valid_cols, ln1_gain, q_weight, sr_weight, sr_gain, kv_weight, out_weight,
+    ln2_gain, fc1_weight, dw_weight, fc2_weight, cotangent,
+):
+    me, lane = lax.axis_index("rows"), lax.axis_index("batch")
+    place = jnp.stack([me, me & 1, (me >> 1) * 2 + (lane & 1), lane >> 1]).astype(jnp.int32)
+
+    def spread(source):
+        near = [
+            over_rows(lax.dynamic_slice_in_dim(source, 2 * (me ^ k), 2, 0), k) for k in (1, 2, 3)
+        ]
+        return (source, *near)
+
+    def returned(parts):
+        return gather_rows(place, (parts[0], *(over_rows(parts[k], k) for k in (1, 2, 3))), tokens.shape)
+
+    ln1, ln2, srg = (g.reshape(1, D) for g in (ln1_gain, ln2_gain, sr_gain))
+    taps = jnp.pad(dw_weight.astype(F32).reshape(9, FF), ((0, 7), (0, 0)))
+    kept = attend(
+        place, valid_rows, valid_cols, spread(tokens), ln1, q_weight, sr_weight, srg, kv_weight, out_weight
+    )
+    *block_parts, mgrad, send1, keep1 = feed(
+        place, valid_rows, valid_cols, kept[5].reshape(2048, D), spread(cotangent), ln2, fc1_weight, taps, fc2_weight
+    )
+    *input_parts, send2, keep2 = back(
+        place, valid_rows, valid_cols, kept, mgrad.reshape(JOINT), ln1, q_weight, sr_weight, srg, kv_weight, out_weight
+    )
+    block_out = returned(block_parts)
+    input_grad = returned(input_parts)
+    q, sr, kv, out, fc1, dw, fc2, gains = finish(place, summed(send1, keep1), summed(send2, keep2))
+    return (
+        block_out, input_grad, gains[1], q, sr, gains[2], kv, out, gains[0], fc1, dw.reshape(3, 3, FF), fc2,
+    )
+
+
+def shards(*arrays):
+    tokens = arrays[0]
+    fits = (
+        lax.axis_size("rows") == 4
+        and lax.axis_size("batch") == 8
+        and tokens.shape == (8, 4, 64, D)
+    )
+    return image_shards(*arrays) if fits else row_shards(*arrays)
+
+
 def solution(mesh):
     placed = (
         P("batch", "rows", None, None),

time: 376 us -> 110 us (0.29)
  waiting for transfers between devices: 89.6 us -> 10.8 us
  blocking collectives: 73.3 us -> 0 us
  other arithmetic: 65.5 us -> 1.64 us
  matrix products: 63.6 us -> 0 us
  Pallas kernels: 0 us -> 50.8 us
  local copies, waits for them, and re-layouts: 49 us -> 6.99 us
  starting transfers between devices: 18.7 us -> 37.7 us
  between operations: 14.9 us -> 1.19 us
    psum x1 -> x0, waiting for transfers between devices: 89.6 us -> none  [shards(): lax.psum((ln1_gain_grad, q_grad, sr_grad, sr_gain_grad, pair_weight_grad,...]
    dot_general x23 -> x0, matrix products: 61.1 us -> none  [the longest x6 27 us: back_product(): lax.dot_general(grad, weight, (((grad.ndim - 1,), (1,)), ((), ())), prefe...]
    pallas_call x0 -> x6, Pallas kernels: none -> 50.8 us  [call(): pl.pallas_call(kernel, out_shape=[jax.ShapeDtypeStruct(shape, kind) for s...]
    convert_element_type x6, other arithmetic: 45.1 us -> 0.36 us  [the longest x4 0.26 us: plus(): return sum((v.astype(F32) for v in values)).astype(BF)]
    psum x1 -> x0, blocking collectives: 41.1 us -> none  [shards(): lax.psum((ln1_gain_grad, q_grad, sr_grad, sr_gain_grad, pair_weight_grad,...]
    unnamed x1 -> x0, blocking collectives: 25 us -> none
    ppermute x4 -> x40, starting transfers between devices: 18.7 us -> 37.7 us  [swap(): return lax.ppermute(value, axes, [(i, partner(i)) for i in range(size)])]
    reshape x13 -> x2, local copies, waits for them, and re-layouts: 20 us -> 1.43 us  [the longest x1 1.4 us: image_shards(): dw.reshape(3, 3, FF)]
  transfers between devices with their start and end apart: 5 -> 40, of which waited for: 1 -> 12; matrix products, arithmetic and copies ran while one was open for 5% -> 2% of each run, Pallas kernels for 0% -> 19%
where the time goes in v1:
time: 110 us; the launch traced here: 109 us
  Pallas kernels  50.8 us (46%)
  starting transfers between devices  37.7 us (34%)
  waiting for transfers between devices  10.8 us (10%)
  local copies, waits for them, and re-layouts  6.99 us (6%)
  other arithmetic  1.64 us (1%)
  between operations  1.19 us (1%)
    pallas_call x6, Pallas kernels, call(): pl.pallas_call(kernel, out_shape=[jax.ShapeDtypeStruct(shape, kind) for s...  50.8 us
    ppermute x40, starting transfers between devices, swap(): return lax.ppermute(value, axes, [(i, partner(i)) for i in range(size)])  37.7 us
    ppermute x40, waiting for transfers between devices, swap(): return lax.ppermute(value, axes, [(i, partner(i)) for i in range(size)])  10.8 us
    unnamed x72, local copies, waits for them, and re-layouts  3.06 us
  transfers between devices with their start and end apart: 40, of which 12 were waited for; matrix products, arithmetic and copies ran while one was open for 2% of the time, Pallas kernels for 19%

profile of v1, /device:TPU:0, one launch (start us, length us, event | category | flops | bytes accessed | tf_op | source)
XLA Modules:
  0.0 109.1 jit_solution(4185518125263328630)
XLA Ops:
  0.7 1.1 %constant_dynamic-slice_fusion.3 = (bf16[2,4,64,128]{3,2,1,0:T(8,128)(2,1)S(1)}, bf16[2,4,64,128]{3,2,1,0:T(8,128)(2,1)S(1)}, bf16[2,4,64,128]{3,2,1,0:T(8,128)(2,1)S(1)}) fusion(bf16[8,4,64,128]{3,2,1,0:T(8,128)(2,1)} %own.1, s32[]{:T(128)S(6)} %select_n.14, s32[]{:T(128)S(6)} %select_n.13, s32[]{:T(128)S(6)} %select_n.12), kind=kLoop, calls=%fused_computation.10 | loop fusion | bytes 786444 | tf_op jit(solution)/shard_map/dynamic_slice | solution.py:721
  1.8 2.5 %collective-permute-start.2 = (bf16[2,4,64,128]{3,2,1,0:T(8,128)(2,1)S(1)}, bf16[2,4,64,128]{3,2,1,0:T(8,128)(2,1)S(1)}, u32[]{:S(2)}, u32[]{:S(2)}) collective-permute-start(bf16[2,4,64,128]{3,2,1,0:T(8,128)(2,1)S(1)} %get-tuple-element.75), channel_id=1, source_target_pairs={{0,24},{8,16},{16,8},{24,0},{1,25},{9,17},{17,9},{25,1},{2,26},{10... | collective-permute-start | bytes 393224 | tf_op jit(solution)/shard_map/ppermute | solution.py:633
  4.3 0.6 collective-permute-start.1
  5.0 1.5 %collective-permute-start.5 = (bf16[2,4,64,128]{3,2,1,0:T(8,128)(2,1)S(1)}, bf16[2,4,64,128]{3,2,1,0:T(8,128)(2,1)S(1)}, u32[]{:S(2)}, u32[]{:S(2)}) collective-permute-start(bf16[2,4,64,128]{3,2,1,0:T(8,128)(2,1)S(1)} %get-tuple-element.72), channel_id=1, source_target_pairs={{0,24},{8,16},{16,8},{24,0},{1,25},{9,17},{17,9},{25,1},{2,26},{10... | collective-permute-start | bytes 393224 | tf_op jit(solution)/shard_map/ppermute | solution.py:633
  6.5 0.6 collective-permute-start.4
  7.2 0.6 pad_convert_fusion.wdw
  8.2 0.8 collective-permute-start.3
  8.9 0.7 pad_add_fusion.place
  9.6 2.3 %collective-permute-done.1.near2 = bf16[2,4,64,128]{3,2,1,0:T(8,128)(2,1)S(1)} collective-permute-done((bf16[2,4,64,128]{3,2,1,0:T(8,128)(2,1)S(1)}, bf16[2,4,64,128]{3,2,1,0:T(8,128)(2,1)S(1)}, u32[]{:S(2)}, u32[]{:S(2)}) %collective-permute-start.1) | collective-permute-done | bytes 131104 | tf_op jit(solution)/shard_map/ppermute | solution.py:633
  11.9 0.6 copy-done.33
  12.6 8.4 %attend.1 = (bf16[16,2,64,128]{3,2,1,0:T(8,128)(2,1)}, bf16[16,2,64,128]{3,2,1,0:T(8,128)(2,1)}, bf16[16,2,64,128]{3,2,1,0:T(8,128)(2,1)}, f32[16,2,64,128]{3,2,...) custom-call(s32[4]{0:T(128)} %pad_add_fusion.place, ...), custom_call_target="tpu_custom_call" | custom-call | flops 1000000000 | bytes 4194304 | tf_op jit(solution)/shard_map/attend/pallas_call | solution.py:566
  21.0 0.6 copy-done.30
  21.7 26.6 %feed.1 = (bf16[2,4,64,128]{3,2,1,0:T(8,128)(2,1)}, bf16[2,4,64,128]{3,2,1,0:T(8,128)(2,1)}, bf16[2,4,64,128]{3,2,1,0:T(8,128)(2,1)}, bf16[2,4,64,128]{3,2,1,0:T...) custom-call(s32[4]{0:T(128)} %pad_add_fusion.place, s32[8]{0:T(128)} %vrows.5, ...), custom_call_target="tpu_custom_call" | custom-call | flops 16000000000 | bytes 4194304 | tf_op jit(solution)/shard_map/feed/pallas_call | solution.py:566
  48.3 0.5 collective-permute-start.6
  48.8 1.6 %collective-permute-start.7 = (bf16[2,4,64,128]{3,2,1,0:T(8,128)(2,1)}, bf16[2,4,64,128]{3,2,1,0:T(8,128)(2,1)S(1)}, u32[]{:S(2)}, u32[]{:S(2)}) collective-permute-start(bf16[2,4,64,128]{3,2,1,0:T(8,128)(2,1)} %get-tuple-element.45), channel_id=1, source_target_pairs={{0,16},{8,24},{16,0},{24,8},{1,17},{9,25},{17,1},{25,9},{2,18},{10... | collective-permute-start | bytes 393224 | tf_op jit(solution)/shard_map/ppermute | solution.py:633
  50.4 9.0 %back.1 = (bf16[2,4,64,128]{3,2,1,0:T(8,128)(2,1)}, bf16[2,4,64,128]{3,2,1,0:T(8,128)(2,1)}, bf16[2,4,64,128]{3,2,1,0:T(8,128)(2,1)}, bf16[2,4,64,128]{3,2,1,0:T...) custom-call(s32[4]{0:T(128)} %pad_add_fusion.place, s32[8]{0:T(128)} %vrows.5, s32[8]{0:T(128)} %vcols.5, ...), custom_call_target="tpu_custom_call" | custom-call | flops 2000000000 | bytes 4194304 | tf_op jit(solution)/shard_map/back/pallas_call | solution.py:566
  59.6 1.5 %collective-permute-start.13 = (bf16[272,128]{1,0:T(8,128)(2,1)S(1)}, bf16[272,128]{1,0:T(8,128)(2,1)S(1)}, u32[]{:S(2)}, u32[]{:S(2)}) collective-permute-start(bf16[272,128]{1,0:T(8,128)(2,1)S(1)} %get-tuple-element.81), channel_id=1, source_target_pairs={{0,1},{1,0},{2,3},{3,2},{4,5},{5,4},{6,7},{7,6},{8,9},{9,8},{10,11... | collective-permute-start | bytes 208904 | tf_op jit(solution)/shard_map/ppermute | solution.py:633
  61.6 1.6 %collective-permute-start.14 = (bf16[272,128]{1,0:T(8,128)(2,1)S(1)}, bf16[272,128]{1,0:T(8,128)(2,1)S(1)}, u32[]{:S(2)}, u32[]{:S(2)}) collective-permute-start(bf16[272,128]{1,0:T(8,128)(2,1)S(1)} %get-tuple-element.83), channel_id=1, source_target_pairs={{0,16},{1,17},{2,18},{3,19},{4,20},{5,21},{6,22},{7,23},{8,24},{9,... | collective-permute-start | bytes 208904 | tf_op jit(solution)/shard_map/ppermute | solution.py:633
  63.2 1.3 %collective-permute-done.13 = bf16[272,128]{1,0:T(8,128)(2,1)S(1)} collective-permute-done((bf16[272,128]{1,0:T(8,128)(2,1)S(1)}, bf16[272,128]{1,0:T(8,128)(2,1)S(1)}, u32[]{:S(2)}, u32[]{:S(2)}) %collective-permute-start.13) | collective-permute-done | bytes 69664 | tf_op jit(solution)/shard_map/ppermute | solution.py:633
  64.5 1.6 %collective-permute-start.27 = (bf16[336,128]{1,0:T(8,128)(2,1)S(1)}, bf16[336,128]{1,0:T(8,128)(2,1)S(1)}, u32[]{:S(2)}, u32[]{:S(2)}) collective-permute-start(bf16[336,128]{1,0:T(8,128)(2,1)S(1)} %get-tuple-element.78), channel_id=1, source_target_pairs={{0,1},{1,0},{2,3},{3,2},{4,5},{5,4},{6,7},{7,6},{8,9},{9,8},{10,11... | collective-permute-start | bytes 258056 | tf_op jit(solution)/shard_map/ppermute | solution.py:633
  66.4 1.8 %collective-permute-start.29 = (bf16[336,128]{1,0:T(8,128)(2,1)S(1)}, bf16[336,128]{1,0:T(8,128)(2,1)S(1)}, u32[]{:S(2)}, u32[]{:S(2)}) collective-permute-start(bf16[336,128]{1,0:T(8,128)(2,1)S(1)} %get-tuple-element.79), channel_id=1, source_target_pairs={{0,17},{1,16},{2,19},{3,18},{4,21},{5,20},{6,23},{7,22},{8,25},{9,... | collective-permute-start | bytes 258056 | tf_op jit(solution)/shard_map/ppermute | solution.py:633
  68.2 0.6 collective-permute-start.28
  69.2 3.6 %collective-permute-start.18 = (bf16[272,128]{1,0:T(8,128)(2,1)S(1)}, bf16[272,128]{1,0:T(8,128)(2,1)S(1)}, u32[]{:S(2)}, u32[]{:S(2)}) collective-permute-start(bf16[272,128]{1,0:T(8,128)(2,1)S(1)} %add_convert_fusion.5), channel_id=1, source_target_pairs={{0,6},{1,7},{2,4},{3,5},{4,2},{5,3},{6,0},{7,1},{8,14},{9,15},{10,... | collective-permute-start | bytes 208904 | tf_op jit(solution)/shard_map/ppermute | solution.py:633
  72.8 1.7 %collective-permute-start.17 = (bf16[272,128]{1,0:T(8,128)(2,1)S(1)}, bf16[272,128]{1,0:T(8,128)(2,1)S(1)}, u32[]{:S(2)}, u32[]{:S(2)}) collective-permute-start(bf16[272,128]{1,0:T(8,128)(2,1)S(1)} %add_convert_fusion.5), channel_id=1, source_target_pairs={{0,4},{1,5},{2,6},{3,7},{4,0},{5,1},{6,2},{7,3},{8,12},{9,13},{10,... | collective-permute-start | bytes 208904 | tf_op jit(solution)/shard_map/ppermute | solution.py:633
  74.5 1.6 %collective-permute-start.16 = (bf16[272,128]{1,0:T(8,128)(2,1)S(1)}, bf16[272,128]{1,0:T(8,128)(2,1)S(1)}, u32[]{:S(2)}, u32[]{:S(2)}) collective-permute-start(bf16[272,128]{1,0:T(8,128)(2,1)S(1)} %add_convert_fusion.5), channel_id=1, source_target_pairs={{0,2},{1,3},{2,0},{3,1},{4,6},{5,7},{6,4},{7,5},{8,10},{9,11},{10,... | collective-permute-start | bytes 208904 | tf_op jit(solution)/shard_map/ppermute | solution.py:633
  76.3 0.9 collective-permute-start.10
  77.1 3.0 %collective-permute-start.32 = (bf16[336,128]{1,0:T(8,128)(2,1)S(1)}, bf16[336,128]{1,0:T(8,128)(2,1)S(1)}, u32[]{:S(2)}, u32[]{:S(2)}) collective-permute-start(bf16[336,128]{1,0:T(8,128)(2,1)S(1)} %add_convert_fusion.3), channel_id=1, source_target_pairs={{0,6},{1,7},{2,4},{3,5},{4,2},{5,3},{6,0},{7,1},{8,14},{9,15},{10,... | collective-permute-start | bytes 258056 | tf_op jit(solution)/shard_map/ppermute | solution.py:633
  80.5 2.4 %collective-permute-start.30 = (bf16[336,128]{1,0:T(8,128)(2,1)S(1)}, bf16[336,128]{1,0:T(8,128)(2,1)S(1)}, u32[]{:S(2)}, u32[]{:S(2)}) collective-permute-start(bf16[336,128]{1,0:T(8,128)(2,1)S(1)} %add_convert_fusion.3), channel_id=1, source_target_pairs={{0,2},{1,3},{2,0},{3,1},{4,6},{5,7},{6,4},{7,5},{8,10},{9,11},{10,... | collective-permute-start | bytes 258056 | tf_op jit(solution)/shard_map/ppermute | solution.py:633
  83.1 1.2 %collective-permute-start.22 = (bf16[272,128]{1,0:T(8,128)(2,1)S(1)}, bf16[272,128]{1,0:T(8,128)(2,1)S(1)}, u32[]{:S(2)}, u32[]{:S(2)}) collective-permute-start(bf16[272,128]{1,0:T(8,128)(2,1)S(1)} %add_convert_fusion.4.refs_0_), channel_id=1, source_target_pairs={{0,8},{8,0},{16,24},{24,16},{1,9},{9,1},{17,25},{25,17},{2,10},{10... | collective-permute-start | bytes 208904 | tf_op jit(solution)/shard_map/ppermute | solution.py:633
  84.4 1.4 %collective-permute-start.21 = (bf16[272,128]{1,0:T(8,128)(2,1)S(1)}, bf16[272,128]{1,0:T(8,128)(2,1)S(1)}, u32[]{:S(2)}, u32[]{:S(2)}) collective-permute-start(bf16[272,128]{1,0:T(8,128)(2,1)S(1)} %add_convert_fusion.4.refs_0_), channel_id=1, source_target_pairs={{0,17},{1,16},{2,19},{3,18},{4,21},{5,20},{6,23},{7,22},{8,25},{9,... | collective-permute-start | bytes 208904 | tf_op jit(solution)/shard_map/ppermute | solution.py:633
  85.8 2.4 %collective-permute-done.31 = bf16[336,128]{1,0:T(8,128)(2,1)S(1)} collective-permute-done((bf16[336,128]{1,0:T(8,128)(2,1)S(1)}, bf16[336,128]{1,0:T(8,128)(2,1)S(1)}, u32[]{:S(2)}, u32[]{:S(2)}) %collective-permute-start.31) | collective-permute-done | bytes 86048 | tf_op jit(solution)/shard_map/ppermute | solution.py:633
  88.2 1.2 %collective-permute-start.20 = (bf16[272,128]{1,0:T(8,128)(2,1)S(1)}, bf16[272,128]{1,0:T(8,128)(2,1)S(1)}, u32[]{:S(2)}, u32[]{:S(2)}) collective-permute-start(bf16[272,128]{1,0:T(8,128)(2,1)S(1)} %add_convert_fusion.4.refs_0_), channel_id=1, source_target_pairs={{0,16},{1,17},{2,18},{3,19},{4,20},{5,21},{6,22},{7,23},{8,24},{9,... | collective-permute-start | bytes 208904 | tf_op jit(solution)/shard_map/ppermute | solution.py:633
  89.4 0.5 collective-permute-start.19
  90.0 1.9 %collective-permute-start.35 = (bf16[336,128]{1,0:T(8,128)(2,1)S(1)}, bf16[336,128]{1,0:T(8,128)(2,1)S(1)}, u32[]{:S(2)}, u32[]{:S(2)}) collective-permute-start(bf16[336,128]{1,0:T(8,128)(2,1)S(1)} %add_convert_fusion.2.refs_8_), channel_id=1, source_target_pairs={{0,17},{1,16},{2,19},{3,18},{4,21},{5,20},{6,23},{7,22},{8,25},{9,... | collective-permute-start | bytes 258056 | tf_op jit(solution)/shard_map/ppermute | solution.py:633
  91.9 1.2 %collective-permute-start.34 = (bf16[336,128]{1,0:T(8,128)(2,1)S(1)}, bf16[336,128]{1,0:T(8,128)(2,1)S(1)}, u32[]{:S(2)}, u32[]{:S(2)}) collective-permute-start(bf16[336,128]{1,0:T(8,128)(2,1)S(1)} %add_convert_fusion.2.refs_8_), channel_id=1, source_target_pairs={{0,16},{1,17},{2,18},{3,19},{4,20},{5,21},{6,22},{7,23},{8,24},{9,... | collective-permute-start | bytes 258056 | tf_op jit(solution)/shard_map/ppermute | solution.py:633
  93.1 0.5 collective-permute-start.33
  93.6 0.8 collective-permute-done.19.refs_1_
  95.0 1.5 %collective-permute-done.35.refs_11_ = bf16[336,128]{1,0:T(8,128)(2,1)S(1)} collective-permute-done((bf16[336,128]{1,0:T(8,128)(2,1)S(1)}, bf16[336,128]{1,0:T(8,128)(2,1)S(1)}, u32[]{:S(2)}, u32[]{:S(2)}) %collective-permute-start.35) | collective-permute-done | bytes 86048 | tf_op jit(solution)/shard_map/ppermute | solution.py:633
  96.5 0.5 collective-permute-done.34.refs_10_
  97.1 0.5 collective-permute-done.33.refs_9_
  97.6 0.5 collective-permute-start.23
  98.1 1.9 %gather_rows.2 = bf16[8,4,64,128]{3,2,1,0:T(8,128)(2,1)} custom-call(s32[4]{0:T(128)} %pad_add_fusion.place, bf16[2,4,64,128]{3,2,1,0:T(8,128)(2,1)} %get-tuple-element.43.part0, bf16[2,4,64,128]{3,2,1,0:T(8,128)(2,1)} %copy-done.5, bf16[2,4,64,128]{3,2,1,0:T(8,128)(2,1)} %copy-done.6, bf16[2,4,64,128]{3,2,1,0:T(8,128)(2,1)} %copy-done.7), custom_call_target="tpu_custom_call" | custom-call | bytes 4194304 | tf_op jit(solution)/shard_map/gather_rows/pallas_call | solution.py:566
  100.1 1.9 %gather_rows.3 = bf16[8,4,64,128]{3,2,1,0:T(8,128)(2,1)} custom-call(s32[4]{0:T(128)} %pad_add_fusion.place, bf16[2,4,64,128]{3,2,1,0:T(8,128)(2,1)} %get-tuple-element.56.part0, bf16[2,4,64,128]{3,2,1,0:T(8,128)(2,1)} %copy-done.8, bf16[2,4,64,128]{3,2,1,0:T(8,128)(2,1)} %copy-done.9, bf16[2,4,64,128]{3,2,1,0:T(8,128)(2,1)} %copy-done.10), custom_call_target="tpu_custom_call" | custom-call | bytes 4194304 | tf_op jit(solution)/shard_map/gather_rows/pallas_call | solution.py:566
  102.1 0.6 copy-done.24
  102.8 0.6 copy-done.17
  103.4 3.0 %finish.1 = (f32[128,128]{1,0:T(8,128)}, f32[2048,128]{1,0:T(8,128)}, f32[128,256]{1,0:T(8,128)}, f32[128,128]{1,0:T(8,128)}, f32[128,1024]{1,0:T(8,128)}, /*ind...) custom-call(s32[4]{0:T(128)} %pad_add_fusion.place, bf16[272,128]{1,0:T(8,128)(2,1)} %copy-done.3, ...), custom_call_target="tpu_custom_call" | custom-call | bytes 4194304 | tf_op jit(solution)/shard_map/finish/pallas_call | solution.py:566
  106.4 1.3 %slice_bitcast_fusion = (f32[128]{0:T(128)}, f32[128]{0:T(128)}, f32[128]{0:T(128)}) fusion(f32[8,128]{1,0:T(8,128)} %get-tuple-element.64), kind=kLoop, calls=%fused_computation.14 | loop fusion | bytes 3072 | tf_op jit(solution)/shard_map/squeeze | solution.py:743
  107.7 1.4 %reshape.52 = f32[3,3,1024]{2,1,0:T(4,128)} reshape(f32[72,128]{1,0:T(8,128)} %get-tuple-element.70) | data formatting | bytes 73728 | tf_op jit(solution)/shard_map/reshape | solution.py:743
  (125 shorter events, 3.8 us)
Async XLA Ops:
  1.8 6.4 %collective-permute-start.2 = (bf16[2,4,64,128]{3,2,1,0:T(8,128)(2,1)S(1)}, bf16[2,4,64,128]{3,2,1,0:T(8,128)(2,1)S(1)}, u32[]{:S(2)}, u32[]{:S(2)}) collective-permute-start(bf16[2,4,64,128]{3,2,1,0:T(8,128)(2,1)S(1)} %get-tuple-element.75), channel_id=1, source_target_pairs={{0,24},{8,16},{16,8},{24,0},{1,25},{9,17},{17,9},{25,1},{2,26},{10... | collective-permute-start | bytes 393224 | tf_op jit(solution)/shard_map/ppermute | solution.py:633
  4.3 7.6 %collective-permute-start.1 = (bf16[2,4,64,128]{3,2,1,0:T(8,128)(2,1)S(1)}, bf16[2,4,64,128]{3,2,1,0:T(8,128)(2,1)S(1)}, u32[]{:S(2)}, u32[]{:S(2)}) collective-permute-start(bf16[2,4,64,128]{3,2,1,0:T(8,128)(2,1)S(1)} %get-tuple-element.76), channel_id=1, source_target_pairs={{0,16},{8,24},{16,0},{24,8},{1,17},{9,25},{17,1},{25,9},{2,18},{10... | collective-permute-start | bytes 393224 | tf_op jit(solution)/shard_map/ppermute | solution.py:633
  4.9 7.0 %collective-permute-start = (bf16[2,4,64,128]{3,2,1,0:T(8,128)(2,1)S(1)}, bf16[2,4,64,128]{3,2,1,0:T(8,128)(2,1)S(1)}, u32[]{:S(2)}, u32[]{:S(2)}) collective-permute-start(bf16[2,4,64,128]{3,2,1,0:T(8,128)(2,1)S(1)} %get-tuple-element.77), channel_id=1, source_target_pairs={{0,8},{8,0},{16,24},{24,16},{1,9},{9,1},{17,25},{25,17},{2,10},{10... | collective-permute-start | bytes 393224 | tf_op jit(solution)/shard_map/ppermute | solution.py:633
  5.0 16.0 %collective-permute-start.5 = (bf16[2,4,64,128]{3,2,1,0:T(8,128)(2,1)S(1)}, bf16[2,4,64,128]{3,2,1,0:T(8,128)(2,1)S(1)}, u32[]{:S(2)}, u32[]{:S(2)}) collective-permute-start(bf16[2,4,64,128]{3,2,1,0:T(8,128)(2,1)S(1)} %get-tuple-element.72), channel_id=1, source_target_pairs={{0,24},{8,16},{16,8},{24,0},{1,25},{9,17},{17,9},{25,1},{2,26},{10... | collective-permute-start | bytes 393224 | tf_op jit(solution)/shard_map/ppermute | solution.py:633
  6.5 14.5 %collective-permute-start.4 = (bf16[2,4,64,128]{3,2,1,0:T(8,128)(2,1)S(1)}, bf16[2,4,64,128]{3,2,1,0:T(8,128)(2,1)S(1)}, u32[]{:S(2)}, u32[]{:S(2)}) collective-permute-start(bf16[2,4,64,128]{3,2,1,0:T(8,128)(2,1)S(1)} %get-tuple-element.73), channel_id=1, source_target_pairs={{0,16},{8,24},{16,0},{24,8},{1,17},{9,25},{17,1},{25,9},{2,18},{10... | collective-permute-start | bytes 393224 | tf_op jit(solution)/shard_map/ppermute | solution.py:633
  8.2 12.8 %collective-permute-start.3 = (bf16[2,4,64,128]{3,2,1,0:T(8,128)(2,1)S(1)}, bf16[2,4,64,128]{3,2,1,0:T(8,128)(2,1)S(1)}, u32[]{:S(2)}, u32[]{:S(2)}) collective-permute-start(bf16[2,4,64,128]{3,2,1,0:T(8,128)(2,1)S(1)} %get-tuple-element.74), channel_id=1, source_target_pairs={{0,8},{8,0},{16,24},{24,16},{1,9},{9,1},{17,25},{25,17},{2,10},{10... | collective-permute-start | bytes 393224 | tf_op jit(solution)/shard_map/ppermute | solution.py:633
  48.3 11.1 %collective-permute-start.12 = (bf16[1088,128]{1,0:T(8,128)(2,1)}, bf16[1088,128]{1,0:T(8,128)(2,1)S(1)}, u32[]{:S(2)}, u32[]{:S(2)}) collective-permute-start(bf16[1088,128]{1,0:T(8,128)(2,1)} %get-tuple-element.61), channel_id=1, source_target_pairs={{0,8},{8,0},{16,24},{24,16},{1,9},{9,1},{17,25},{25,17},{2,10},{10... | collective-permute-start | bytes 835592 | tf_op jit(solution)/shard_map/ppermute | solution.py:633
  48.3 20.5 %collective-permute-start.6 = (bf16[2,4,64,128]{3,2,1,0:T(8,128)(2,1)}, bf16[2,4,64,128]{3,2,1,0:T(8,128)(2,1)S(1)}, u32[]{:S(2)}, u32[]{:S(2)}) collective-permute-start(bf16[2,4,64,128]{3,2,1,0:T(8,128)(2,1)} %get-tuple-element.44), channel_id=1, source_target_pairs={{0,8},{8,0},{16,24},{24,16},{1,9},{9,1},{17,25},{25,17},{2,10},{10... | collective-permute-start | bytes 393224 | tf_op jit(solution)/shard_map/ppermute | solution.py:633
  48.8 27.3 %collective-permute-start.7 = (bf16[2,4,64,128]{3,2,1,0:T(8,128)(2,1)}, bf16[2,4,64,128]{3,2,1,0:T(8,128)(2,1)S(1)}, u32[]{:S(2)}, u32[]{:S(2)}) collective-permute-start(bf16[2,4,64,128]{3,2,1,0:T(8,128)(2,1)} %get-tuple-element.45), channel_id=1, source_target_pairs={{0,16},{8,24},{16,0},{24,8},{1,17},{9,25},{17,1},{25,9},{2,18},{10... | collective-permute-start | bytes 393224 | tf_op jit(solution)/shard_map/ppermute | solution.py:633
  50.4 9.1 %copy-start.4 = (bf16[1088,128]{1,0:T(8,128)(2,1)S(1)}, bf16[1088,128]{1,0:T(8,128)(2,1)}, u32[]{:S(2)}) copy-start(bf16[1088,128]{1,0:T(8,128)(2,1)} %get-tuple-element.60) | copy-start | bytes 835588
  59.3 2.2 %collective-permute-start.26 = (bf16[1344,128]{1,0:T(8,128)(2,1)}, bf16[1344,128]{1,0:T(8,128)(2,1)S(1)}, u32[]{:S(2)}, u32[]{:S(2)}) collective-permute-start(bf16[1344,128]{1,0:T(8,128)(2,1)} %get-tuple-element.63), channel_id=1, source_target_pairs={{0,8},{8,0},{16,24},{24,16},{1,9},{9,1},{17,25},{25,17},{2,10},{10... | collective-permute-start | bytes 1032200 | tf_op jit(solution)/shard_map/ppermute | solution.py:633
  59.6 5.0 %collective-permute-start.13 = (bf16[272,128]{1,0:T(8,128)(2,1)S(1)}, bf16[272,128]{1,0:T(8,128)(2,1)S(1)}, u32[]{:S(2)}, u32[]{:S(2)}) collective-permute-start(bf16[272,128]{1,0:T(8,128)(2,1)S(1)} %get-tuple-element.81), channel_id=1, source_target_pairs={{0,1},{1,0},{2,3},{3,2},{4,5},{5,4},{6,7},{7,6},{8,9},{9,8},{10,11... | collective-permute-start | bytes 208904 | tf_op jit(solution)/shard_map/ppermute | solution.py:633
  61.1 5.3 %collective-permute-start.15 = (bf16[272,128]{1,0:T(8,128)(2,1)S(1)}, bf16[272,128]{1,0:T(8,128)(2,1)S(1)}, u32[]{:S(2)}, u32[]{:S(2)}) collective-permute-start(bf16[272,128]{1,0:T(8,128)(2,1)S(1)} %get-tuple-element.82), channel_id=1, source_target_pairs={{0,17},{1,16},{2,19},{3,18},{4,21},{5,20},{6,23},{7,22},{8,25},{9,... | collective-permute-start | bytes 208904 | tf_op jit(solution)/shard_map/ppermute | solution.py:633
  61.6 6.6 %collective-permute-start.14 = (bf16[272,128]{1,0:T(8,128)(2,1)S(1)}, bf16[272,128]{1,0:T(8,128)(2,1)S(1)}, u32[]{:S(2)}, u32[]{:S(2)}) collective-permute-start(bf16[272,128]{1,0:T(8,128)(2,1)S(1)} %get-tuple-element.83), channel_id=1, source_target_pairs={{0,16},{1,17},{2,18},{3,19},{4,20},{5,21},{6,22},{7,23},{8,24},{9,... | collective-permute-start | bytes 208904 | tf_op jit(solution)/shard_map/ppermute | solution.py:633
  64.5 4.7 %collective-permute-start.27 = (bf16[336,128]{1,0:T(8,128)(2,1)S(1)}, bf16[336,128]{1,0:T(8,128)(2,1)S(1)}, u32[]{:S(2)}, u32[]{:S(2)}) collective-permute-start(bf16[336,128]{1,0:T(8,128)(2,1)S(1)} %get-tuple-element.78), channel_id=1, source_target_pairs={{0,1},{1,0},{2,3},{3,2},{4,5},{5,4},{6,7},{7,6},{8,9},{9,8},{10,11... | collective-permute-start | bytes 258056 | tf_op jit(solution)/shard_map/ppermute | solution.py:633
  66.4 6.4 %collective-permute-start.29 = (bf16[336,128]{1,0:T(8,128)(2,1)S(1)}, bf16[336,128]{1,0:T(8,128)(2,1)S(1)}, u32[]{:S(2)}, u32[]{:S(2)}) collective-permute-start(bf16[336,128]{1,0:T(8,128)(2,1)S(1)} %get-tuple-element.79), channel_id=1, source_target_pairs={{0,17},{1,16},{2,19},{3,18},{4,21},{5,20},{6,23},{7,22},{8,25},{9,... | collective-permute-start | bytes 258056 | tf_op jit(solution)/shard_map/ppermute | solution.py:633
  68.2 6.3 %collective-permute-start.28 = (bf16[336,128]{1,0:T(8,128)(2,1)S(1)}, bf16[336,128]{1,0:T(8,128)(2,1)S(1)}, u32[]{:S(2)}, u32[]{:S(2)}) collective-permute-start(bf16[336,128]{1,0:T(8,128)(2,1)S(1)} %get-tuple-element.80), channel_id=1, source_target_pairs={{0,16},{1,17},{2,18},{3,19},{4,20},{5,21},{6,22},{7,23},{8,24},{9,... | collective-permute-start | bytes 258056 | tf_op jit(solution)/shard_map/ppermute | solution.py:633
  68.8 7.3 %copy-start.5 = (bf16[2,4,64,128]{3,2,1,0:T(8,128)(2,1)}, bf16[2,4,64,128]{3,2,1,0:T(8,128)(2,1)S(1)}, u32[]{:S(2)}) copy-start(bf16[2,4,64,128]{3,2,1,0:T(8,128)(2,1)S(1)} %collective-permute-done.6.part1) | copy-start | bytes 393220
  69.1 7.1 %copy-start.28 = (bf16[2,4,64,128]{3,2,1,0:T(8,128)(2,1)S(1)}, bf16[2,4,64,128]{3,2,1,0:T(8,128)(2,1)}, u32[]{:S(2)}) copy-start(bf16[2,4,64,128]{3,2,1,0:T(8,128)(2,1)} %get-tuple-element.57) | copy-start | bytes 393220
  69.1 7.2 %copy-start.27 = (bf16[2,4,64,128]{3,2,1,0:T(8,128)(2,1)S(1)}, bf16[2,4,64,128]{3,2,1,0:T(8,128)(2,1)}, u32[]{:S(2)}) copy-start(bf16[2,4,64,128]{3,2,1,0:T(8,128)(2,1)} %get-tuple-element.58) | copy-start | bytes 393220
  69.1 7.2 %collective-permute-start.8 = (bf16[2,4,64,128]{3,2,1,0:T(8,128)(2,1)S(1)}, bf16[2,4,64,128]{3,2,1,0:T(8,128)(2,1)S(1)}, u32[]{:S(2)}, u32[]{:S(2)}) collective-permute-start(bf16[2,4,64,128]{3,2,1,0:T(8,128)(2,1)S(1)} %copy-done.29), channel_id=1, source_target_pairs={{0,24},{8,16},{16,8},{24,0},{1,25},{9,17},{17,9},{25,1},{2,26},{10... | collective-permute-start | bytes 393224 | tf_op jit(solution)/shard_map/ppermute | solution.py:633
  69.2 7.9 %collective-permute-start.18 = (bf16[272,128]{1,0:T(8,128)(2,1)S(1)}, bf16[272,128]{1,0:T(8,128)(2,1)S(1)}, u32[]{:S(2)}, u32[]{:S(2)}) collective-permute-start(bf16[272,128]{1,0:T(8,128)(2,1)S(1)} %add_convert_fusion.5), channel_id=1, source_target_pairs={{0,6},{1,7},{2,4},{3,5},{4,2},{5,3},{6,0},{7,1},{8,14},{9,15},{10,... | collective-permute-start | bytes 208904 | tf_op jit(solution)/shard_map/ppermute | solution.py:633
  72.8 7.3 %collective-permute-start.17 = (bf16[272,128]{1,0:T(8,128)(2,1)S(1)}, bf16[272,128]{1,0:T(8,128)(2,1)S(1)}, u32[]{:S(2)}, u32[]{:S(2)}) collective-permute-start(bf16[272,128]{1,0:T(8,128)(2,1)S(1)} %add_convert_fusion.5), channel_id=1, source_target_pairs={{0,4},{1,5},{2,6},{3,7},{4,0},{5,1},{6,2},{7,3},{8,12},{9,13},{10,... | collective-permute-start | bytes 208904 | tf_op jit(solution)/shard_map/ppermute | solution.py:633
  74.5 6.0 %collective-permute-start.16 = (bf16[272,128]{1,0:T(8,128)(2,1)S(1)}, bf16[272,128]{1,0:T(8,128)(2,1)S(1)}, u32[]{:S(2)}, u32[]{:S(2)}) collective-permute-start(bf16[272,128]{1,0:T(8,128)(2,1)S(1)} %add_convert_fusion.5), channel_id=1, source_target_pairs={{0,2},{1,3},{2,0},{3,1},{4,6},{5,7},{6,4},{7,5},{8,10},{9,11},{10,... | collective-permute-start | bytes 208904 | tf_op jit(solution)/shard_map/ppermute | solution.py:633
  76.2 6.8 %collective-permute-start.9 = (bf16[2,4,64,128]{3,2,1,0:T(8,128)(2,1)S(1)}, bf16[2,4,64,128]{3,2,1,0:T(8,128)(2,1)S(1)}, u32[]{:S(2)}, u32[]{:S(2)}) collective-permute-start(bf16[2,4,64,128]{3,2,1,0:T(8,128)(2,1)S(1)} %copy-done.28), channel_id=1, source_target_pairs={{0,8},{8,0},{16,24},{24,16},{1,9},{9,1},{17,25},{25,17},{2,10},{10... | collective-permute-start | bytes 393224 | tf_op jit(solution)/shard_map/ppermute | solution.py:633
  76.3 6.8 %collective-permute-start.10 = (bf16[2,4,64,128]{3,2,1,0:T(8,128)(2,1)S(1)}, bf16[2,4,64,128]{3,2,1,0:T(8,128)(2,1)S(1)}, u32[]{:S(2)}, u32[]{:S(2)}) collective-permute-start(bf16[2,4,64,128]{3,2,1,0:T(8,128)(2,1)S(1)} %copy-done.27), channel_id=1, source_target_pairs={{0,16},{8,24},{16,0},{24,8},{1,17},{9,25},{17,1},{25,9},{2,18},{10... | collective-permute-start | bytes 393224 | tf_op jit(solution)/shard_map/ppermute | solution.py:633
  77.1 7.3 %collective-permute-start.32 = (bf16[336,128]{1,0:T(8,128)(2,1)S(1)}, bf16[336,128]{1,0:T(8,128)(2,1)S(1)}, u32[]{:S(2)}, u32[]{:S(2)}) collective-permute-start(bf16[336,128]{1,0:T(8,128)(2,1)S(1)} %add_convert_fusion.3), channel_id=1, source_target_pairs={{0,6},{1,7},{2,4},{3,5},{4,2},{5,3},{6,0},{7,1},{8,14},{9,15},{10,... | collective-permute-start | bytes 258056 | tf_op jit(solution)/shard_map/ppermute | solution.py:633
  80.1 8.1 %collective-permute-start.31 = (bf16[336,128]{1,0:T(8,128)(2,1)S(1)}, bf16[336,128]{1,0:T(8,128)(2,1)S(1)}, u32[]{:S(2)}, u32[]{:S(2)}) collective-permute-start(bf16[336,128]{1,0:T(8,128)(2,1)S(1)} %add_convert_fusion.3), channel_id=1, source_target_pairs={{0,4},{1,5},{2,6},{3,7},{4,0},{5,1},{6,2},{7,3},{8,12},{9,13},{10,... | collective-permute-start | bytes 258056 | tf_op jit(solution)/shard_map/ppermute | solution.py:633
  80.5 8.9 %collective-permute-start.30 = (bf16[336,128]{1,0:T(8,128)(2,1)S(1)}, bf16[336,128]{1,0:T(8,128)(2,1)S(1)}, u32[]{:S(2)}, u32[]{:S(2)}) collective-permute-start(bf16[336,128]{1,0:T(8,128)(2,1)S(1)} %add_convert_fusion.3), channel_id=1, source_target_pairs={{0,2},{1,3},{2,0},{3,1},{4,6},{5,7},{6,4},{7,5},{8,10},{9,11},{10,... | collective-permute-start | bytes 258056 | tf_op jit(solution)/shard_map/ppermute | solution.py:633
  83.0 7.0 %copy-start.3 = (bf16[272,128]{1,0:T(8,128)(2,1)}, bf16[272,128]{1,0:T(8,128)(2,1)S(1)}, u32[]{:S(2)}) copy-start(bf16[272,128]{1,0:T(8,128)(2,1)S(1)} %add_convert_fusion.4.refs_0_) | copy-start | bytes 208900
  83.0 7.0 %collective-permute-start.11 = (bf16[2,4,64,128]{3,2,1,0:T(8,128)(2,1)S(1)}, bf16[2,4,64,128]{3,2,1,0:T(8,128)(2,1)S(1)}, u32[]{:S(2)}, u32[]{:S(2)}) collective-permute-start(bf16[2,4,64,128]{3,2,1,0:T(8,128)(2,1)S(1)} %copy-done.26), channel_id=1, source_target_pairs={{0,24},{8,16},{16,8},{24,0},{1,25},{9,17},{17,9},{25,1},{2,26},{10... | collective-permute-start | bytes 393224 | tf_op jit(solution)/shard_map/ppermute | solution.py:633
  83.1 8.8 %collective-permute-start.22 = (bf16[272,128]{1,0:T(8,128)(2,1)S(1)}, bf16[272,128]{1,0:T(8,128)(2,1)S(1)}, u32[]{:S(2)}, u32[]{:S(2)}) collective-permute-start(bf16[272,128]{1,0:T(8,128)(2,1)S(1)} %add_convert_fusion.4.refs_0_), channel_id=1, source_target_pairs={{0,8},{8,0},{16,24},{24,16},{1,9},{9,1},{17,25},{25,17},{2,10},{10... | collective-permute-start | bytes 208904 | tf_op jit(solution)/shard_map/ppermute | solution.py:633
  84.4 8.7 %collective-permute-start.21 = (bf16[272,128]{1,0:T(8,128)(2,1)S(1)}, bf16[272,128]{1,0:T(8,128)(2,1)S(1)}, u32[]{:S(2)}, u32[]{:S(2)}) collective-permute-start(bf16[272,128]{1,0:T(8,128)(2,1)S(1)} %add_convert_fusion.4.refs_0_), channel_id=1, source_target_pairs={{0,17},{1,16},{2,19},{3,18},{4,21},{5,20},{6,23},{7,22},{8,25},{9,... | collective-permute-start | bytes 208904 | tf_op jit(solution)/shard_map/ppermute | solution.py:633
  88.2 5.4 %collective-permute-start.20 = (bf16[272,128]{1,0:T(8,128)(2,1)S(1)}, bf16[272,128]{1,0:T(8,128)(2,1)S(1)}, u32[]{:S(2)}, u32[]{:S(2)}) collective-permute-start(bf16[272,128]{1,0:T(8,128)(2,1)S(1)} %add_convert_fusion.4.refs_0_), channel_id=1, source_target_pairs={{0,16},{1,17},{2,18},{3,19},{4,20},{5,21},{6,22},{7,23},{8,24},{9,... | collective-permute-start | bytes 208904 | tf_op jit(solution)/shard_map/ppermute | solution.py:633
  89.4 5.0 %collective-permute-start.19 = (bf16[272,128]{1,0:T(8,128)(2,1)S(1)}, bf16[272,128]{1,0:T(8,128)(2,1)S(1)}, u32[]{:S(2)}, u32[]{:S(2)}) collective-permute-start(bf16[272,128]{1,0:T(8,128)(2,1)S(1)} %add_convert_fusion.4.refs_0_), channel_id=1, source_target_pairs={{0,1},{1,0},{2,3},{3,2},{4,5},{5,4},{6,7},{7,6},{8,9},{9,8},{10,11... | collective-permute-start | bytes 208904 | tf_op jit(solution)/shard_map/ppermute | solution.py:633
  90.0 10.0 %copy-start.1 = (bf16[336,128]{1,0:T(8,128)(2,1)}, bf16[336,128]{1,0:T(8,128)(2,1)S(1)}, u32[]{:S(2)}) copy-start(bf16[336,128]{1,0:T(8,128)(2,1)S(1)} %add_convert_fusion.2.refs_8_) | copy-start | bytes 258052
  90.0 10.0 %copy-start.10 = (bf16[2,4,64,128]{3,2,1,0:T(8,128)(2,1)}, bf16[2,4,64,128]{3,2,1,0:T(8,128)(2,1)S(1)}, u32[]{:S(2)}) copy-start(bf16[2,4,64,128]{3,2,1,0:T(8,128)(2,1)S(1)} %collective-permute-done.11.part3) | copy-start | bytes 393220
  90.0 6.5 %collective-permute-start.35 = (bf16[336,128]{1,0:T(8,128)(2,1)S(1)}, bf16[336,128]{1,0:T(8,128)(2,1)S(1)}, u32[]{:S(2)}, u32[]{:S(2)}) collective-permute-start(bf16[336,128]{1,0:T(8,128)(2,1)S(1)} %add_convert_fusion.2.refs_8_), channel_id=1, source_target_pairs={{0,17},{1,16},{2,19},{3,18},{4,21},{5,20},{6,23},{7,22},{8,25},{9,... | collective-permute-start | bytes 258056 | tf_op jit(solution)/shard_map/ppermute | solution.py:633
  91.9 8.1 %copy-start.18 = (bf16[272,128]{1,0:T(8,128)(2,1)}, bf16[272,128]{1,0:T(8,128)(2,1)S(1)}, u32[]{:S(2)}) copy-start(bf16[272,128]{1,0:T(8,128)(2,1)S(1)} %collective-permute-done.22.refs_4_) | copy-start | bytes 208900
  91.9 5.2 %collective-permute-start.34 = (bf16[336,128]{1,0:T(8,128)(2,1)S(1)}, bf16[336,128]{1,0:T(8,128)(2,1)S(1)}, u32[]{:S(2)}, u32[]{:S(2)}) collective-permute-start(bf16[336,128]{1,0:T(8,128)(2,1)S(1)} %add_convert_fusion.2.refs_8_), channel_id=1, source_target_pairs={{0,16},{1,17},{2,18},{3,19},{4,20},{5,21},{6,22},{7,23},{8,24},{9,... | collective-permute-start | bytes 258056 | tf_op jit(solution)/shard_map/ppermute | solution.py:633
  93.1 4.5 %collective-permute-start.33 = (bf16[336,128]{1,0:T(8,128)(2,1)S(1)}, bf16[336,128]{1,0:T(8,128)(2,1)S(1)}, u32[]{:S(2)}, u32[]{:S(2)}) collective-permute-start(bf16[336,128]{1,0:T(8,128)(2,1)S(1)} %add_convert_fusion.2.refs_8_), channel_id=1, source_target_pairs={{0,1},{1,0},{2,3},{3,2},{4,5},{5,4},{6,7},{7,6},{8,9},{9,8},{10,11... | collective-permute-start | bytes 258056 | tf_op jit(solution)/shard_map/ppermute | solution.py:633
  93.6 1.3 %collective-permute-start.25 = (bf16[272,128]{1,0:T(8,128)(2,1)S(1)}, bf16[272,128]{1,0:T(8,128)(2,1)S(1)}, u32[]{:S(2)}, u32[]{:S(2)}) collective-permute-start(bf16[272,128]{1,0:T(8,128)(2,1)S(1)} %collective-permute-done.21.refs_3_), channel_id=1, source_target_pairs={{0,8},{8,0},{16,24},{24,16},{1,9},{9,1},{17,25},{25,17},{2,10},{10... | collective-permute-start | bytes 208904 | tf_op jit(solution)/shard_map/ppermute | solution.py:633
  94.4 3.2 %collective-permute-start.24 = (bf16[272,128]{1,0:T(8,128)(2,1)S(1)}, bf16[272,128]{1,0:T(8,128)(2,1)S(1)}, u32[]{:S(2)}, u32[]{:S(2)}) collective-permute-start(bf16[272,128]{1,0:T(8,128)(2,1)S(1)} %collective-permute-done.20.refs_2_), channel_id=1, source_target_pairs={{0,8},{8,0},{16,24},{24,16},{1,9},{9,1},{17,25},{25,17},{2,10},{10... | collective-permute-start | bytes 208904 | tf_op jit(solution)/shard_map/ppermute | solution.py:633
  94.9 7.2 %collective-permute-start.36 = (bf16[336,128]{1,0:T(8,128)(2,1)S(1)}, bf16[336,128]{1,0:T(8,128)(2,1)S(1)}, u32[]{:S(2)}, u32[]{:S(2)}) collective-permute-start(bf16[336,128]{1,0:T(8,128)(2,1)S(1)} %add_convert_fusion.2.refs_8_), channel_id=1, source_target_pairs={{0,8},{8,0},{16,24},{24,16},{1,9},{9,1},{17,25},{25,17},{2,10},{10... | collective-permute-start | bytes 258056 | tf_op jit(solution)/shard_map/ppermute | solution.py:633
  96.5 5.6 %collective-permute-start.39 = (bf16[336,128]{1,0:T(8,128)(2,1)S(1)}, bf16[336,128]{1,0:T(8,128)(2,1)S(1)}, u32[]{:S(2)}, u32[]{:S(2)}) collective-permute-start(bf16[336,128]{1,0:T(8,128)(2,1)S(1)} %collective-permute-done.35.refs_11_), channel_id=1, source_target_pairs={{0,8},{8,0},{16,24},{24,16},{1,9},{9,1},{17,25},{25,17},{2,10},{10... | collective-permute-start | bytes 258056 | tf_op jit(solution)/shard_map/ppermute | solution.py:633
  97.1 5.0 %collective-permute-start.38 = (bf16[336,128]{1,0:T(8,128)(2,1)S(1)}, bf16[336,128]{1,0:T(8,128)(2,1)S(1)}, u32[]{:S(2)}, u32[]{:S(2)}) collective-permute-start(bf16[336,128]{1,0:T(8,128)(2,1)S(1)} %collective-permute-done.34.refs_10_), channel_id=1, source_target_pairs={{0,8},{8,0},{16,24},{24,16},{1,9},{9,1},{17,25},{25,17},{2,10},{10... | collective-permute-start | bytes 258056 | tf_op jit(solution)/shard_map/ppermute | solution.py:633
  97.6 4.5 %collective-permute-start.37 = (bf16[336,128]{1,0:T(8,128)(2,1)S(1)}, bf16[336,128]{1,0:T(8,128)(2,1)S(1)}, u32[]{:S(2)}, u32[]{:S(2)}) collective-permute-start(bf16[336,128]{1,0:T(8,128)(2,1)S(1)} %collective-permute-done.33.refs_9_), channel_id=1, source_target_pairs={{0,8},{8,0},{16,24},{24,16},{1,9},{9,1},{17,25},{25,17},{2,10},{10... | collective-permute-start | bytes 258056 | tf_op jit(solution)/shard_map/ppermute | solution.py:633
  97.6 4.5 %collective-permute-start.23 = (bf16[272,128]{1,0:T(8,128)(2,1)S(1)}, bf16[272,128]{1,0:T(8,128)(2,1)S(1)}, u32[]{:S(2)}, u32[]{:S(2)}) collective-permute-start(bf16[272,128]{1,0:T(8,128)(2,1)S(1)} %collective-permute-done.19.refs_1_), channel_id=1, source_target_pairs={{0,8},{8,0},{16,24},{24,16},{1,9},{9,1},{17,25},{25,17},{2,10},{10... | collective-permute-start | bytes 208904 | tf_op jit(solution)/shard_map/ppermute | solution.py:633
  (28 other events, 91.5 us)

commit v2 on v1

--- a/solution.py
+++ b/solution.py
@@ -322,7 +322,7 @@
 
 
 def attend_kernel(
-    place, vrows, vcols, own, near1, near2, near3, ln1, wq, wsr, srg, wkv, wout,
+    place, own, near1, near2, near3, gains, wq, wsr, wkv, wout,
     x_out, normed_out, q_out, prob_out, att_out, mid_out, pat_out, pooled_out, kv_out, masked,
 ):
     me = place[0]
@@ -332,9 +332,9 @@
             raw = own[2 * me + i] if k == 0 else chunk[i]
             x_out[pl.ds(block * 4, 4), i] = raw
             unit, _ = norm_parts(raw.astype(jnp.float32).reshape(256, D))
-            normed = (unit * ln1[...]).astype(jnp.bfloat16)
+            normed = (unit * gains[pl.ds(0, 1), :]).astype(jnp.bfloat16)
             normed_out[pl.ds(block * 4, 4), i] = normed.reshape(4, 64, D)
-            inside = block_inside(block * 4, vrows[2 * me + i], vcols[2 * me + i])
+            inside = block_inside(block * 4, place[4 + i], place[6 + i])
             start = pl.multiple_of(i * 1024 + block * 256, 256)
             masked[pl.ds(start, 256), :] = jnp.where(inside, normed.astype(jnp.float32), 0.0)
     for i in range(2):
@@ -348,11 +348,11 @@
     pooled = mm(pat_out[...], wsr[...])
     pooled_out[...] = pooled
     unit, _ = norm_parts(pooled)
-    pairs = mm((unit * srg[...]).astype(jnp.bfloat16), wkv[...]).astype(jnp.bfloat16)
+    pairs = mm((unit * gains[pl.ds(1, 1), :]).astype(jnp.bfloat16), wkv[...]).astype(jnp.bfloat16)
     kv_out[...] = pairs
     lane = lax.broadcasted_iota(jnp.int32, (1, D), 1) % 64
     for i in range(2):
-        rows, cols = vrows[2 * me + i], vcols[2 * me + i]
+        rows, cols = place[4 + i], place[6 + i]
         live = ((lane // 16) * 4 < rows) & ((lane % 16) * 4 < cols)
         keys = block_pair(pairs[i * 64 : i * 64 + 64, :D].astype(jnp.float32)).astype(jnp.bfloat16)
         values = block_pair(pairs[i * 64 : i * 64 + 64, D:].astype(jnp.float32)).astype(jnp.bfloat16)
@@ -378,94 +378,122 @@
 
 
 def feed_kernel(
-    place, vrows, vcols, mid, cot, cot1, cot2, cot3, ln2, wfc1, wdw, wfc2,
+    place, mid, cot, cot1, cot2, cot3, gains, wfc1, taps, wfc2,
     bo0, bo1, bo2, bo3, mg_out, send_out, keep_out,
-    cj, br, br_t, wide, x_t, xcol, w9, cg, act, acc, stage, mask,
+    cj, br, br_t, mask, even, odd, mix, pairs, pairs_t, cg, act, acc, back, stage,
 ):
     me = place[0]
-    zeros = jnp.zeros((128, 3 * D), jnp.bfloat16)
-    wide[pl.ds(0, 128), :] = zeros
-    wide[pl.ds(2176, 128), :] = zeros
-    x_t[:, pl.ds(0, 128)] = jnp.zeros((3 * D, 128), jnp.bfloat16)
-    x_t[:, pl.ds(2176, 128)] = jnp.zeros((3 * D, 128), jnp.bfloat16)
-    cg[pl.ds(0, 128), :] = jnp.zeros((128, FF), jnp.bfloat16)
-    cg[pl.ds(2176, 128), :] = jnp.zeros((128, FF), jnp.bfloat16)
-    col = lax.broadcasted_iota(jnp.int32, (512, D), 0) % 64
+    edge = jnp.zeros((128, 3 * D), jnp.bfloat16)
+    even[pl.ds(1024, 128), :] = edge
+    odd[pl.ds(0, 128), :] = edge
+    col = lax.broadcasted_iota(jnp.int32, (256, D), 0) % 64
     for k, chunk in enumerate((cot, cot1, cot2, cot3)):
         block = me ^ k
         for i in range(2):
             raw = cot[2 * me + i] if k == 0 else chunk[i]
-            inside = block_inside(block * 4, vrows[2 * me + i], vcols[2 * me + i]).reshape(4, 64, D)
+            inside = block_inside(block * 4, place[4 + i], place[6 + i]).reshape(4, 64, D)
             for r in range(4):
-                at = pl.ds(pl.multiple_of(block * 512 + r * 128 + i * 64, 64), 64)
+                at = pl.ds(pl.multiple_of((r % 2) * 1024 + block * 256 + (r // 2) * 128 + i * 64, 64), 64)
                 cj[at, :] = raw[r]
                 mask[at, :] = jnp.where(inside[r], 1.0, 0.0)
     fc1_wide = wfc1[...].astype(jnp.float32)
-    for tap in range(9):
-        w9[pl.ds(tap * D, D), :] = (fc1_wide * wdw[pl.ds(tap, 1), :]).astype(jnp.bfloat16)
-    for b in range(4):
-        part = pl.ds(b * 512, 512)
-        inside = mask[part, :]
-        branch = cj[part, :].astype(jnp.float32) * inside
-        br[part, :] = branch.astype(jnp.bfloat16)
-        br_t[:, part] = branch.T.astype(jnp.bfloat16)
-        unit, _ = norm_parts(mid[part, :])
-        normed = ((unit * ln2[...]).astype(jnp.bfloat16)).astype(jnp.float32) * inside
-        before = jnp.where(col == 0, 0.0, pltpu.roll(normed, 1, 0))
-        after = jnp.where(col == 63, 0.0, pltpu.roll(normed, 511, 0))
-        for s, value in enumerate((before, normed, after)):
-            wide[pl.ds(b * 512 + 128, 512), pl.ds(s * D, D)] = value.astype(jnp.bfloat16)
-            x_t[pl.ds(s * D, D), pl.ds(b * 512 + 128, 512)] = value.T.astype(jnp.bfloat16)
-    for p in range(3):
-        xcol[:, pl.ds(p * 3 * D, 3 * D)] = wide[pl.ds(p * 128, 2048), :]
+    for k in range(4):
+        for s in range(3):
+            mix[k, pl.ds(s * D, D), :] = (fc1_wide * taps[pl.ds(3 * k + s, 1), :]).astype(jnp.bfloat16)
+    for e, side in enumerate((even, odd)):
+        for j in range(0, 8, 2):
+            part = pl.ds(e * 1024 + j * 128, 256)
+            inside = mask[part, :]
+            branch = cj[part, :].astype(jnp.float32) * inside
+            br[part, :] = branch.astype(jnp.bfloat16)
+            br_t[:, part] = branch.T.astype(jnp.bfloat16)
+            source = jnp.concatenate([mid[pl.ds((2 * (j + h) + e) * 128, 128), :] for h in range(2)], axis=0)
+            unit, _ = norm_parts(source)
+            normed = ((unit * gains[pl.ds(2, 1), :]).astype(jnp.bfloat16)).astype(jnp.float32) * inside
+            before = jnp.where(col == 0, 0.0, pltpu.roll(normed, 1, 0))
+            after = jnp.where(col == 63, 0.0, pltpu.roll(normed, 255, 0))
+            for s, value in enumerate((before, normed, after)):
+                side[pl.ds((j + e) * 128, 256), pl.ds(s * D, D)] = value.astype(jnp.bfloat16)
+    for k in range(4):
+        for j in range(0, 8, 2):
+            for s in range(3):
+                lanes = pl.ds(s * D, D)
+                ev, ev_next = (even[pl.ds((j + h) * 128, 256), lanes].astype(jnp.float32) for h in (0, 1))
+                od_last, od = (odd[pl.ds((j + h) * 128, 256), lanes].astype(jnp.float32) for h in (0, 1))
+                value = (od_last - od, ev + od, od - ev, ev - ev_next)[k]
+                pairs[k, pl.ds(j * 128, 256), lanes] = value.astype(jnp.bfloat16)
+                pairs_t[k, lanes, pl.ds(j * 128, 256)] = value.T.astype(jnp.bfloat16)
     for f in range(FF // FC):
         chan = pl.ds(f * FC, FC)
-        for b in range(2048 // TB):
+        for b in range(1024 // TB):
             part = pl.ds(b * TB, TB)
-            conv = mm(xcol[part, :], w9[:, chan])
-            value, slope = gelu_parts(conv)
-            low = value.astype(jnp.bfloat16)
-            act[part, :] = low
-            grad = mm_nt(br[part, :], wfc2[chan, :]) * slope
-            cg[pl.ds(b * TB + 128, TB), chan] = grad.astype(jnp.bfloat16)
-            if f == 0:
-                acc[part, :] = mm(low, wfc2[chan, :])
-            else:
-                acc[part, :] += mm(low, wfc2[chan, :])
+            m0, m1, m2, m3 = (mm(pairs[k, part, :], mix[k, :, chan]) for k in range(4))
+            grads = []
+            for e, conv in enumerate((m0 + (m1 + m2), (m1 - m2) - m3)):
+                here = pl.ds(e * 1024 + b * TB, TB)
+                value, slope = gelu_parts(conv)
+                low = value.astype(jnp.bfloat16)
+                act[here, :] = low
+                grads.append(mm_nt(br[here, :], wfc2[chan, :]) * slope)
+                if f == 0:
+                    acc[here, :] = mm(low, wfc2[chan, :])
+                else:
+                    acc[here, :] += mm(low, wfc2[chan, :])
+            for k, value in enumerate((grads[0], grads[0] + grads[1], grads[0] - grads[1], grads[1])):
+                cg[k, part, chan] = value.astype(jnp.bfloat16)
         fc2_grad = mm(br_t[...], act[...])
         stage[pl.ds(FF + f * FC, FC), :] = fc2_grad.T
         fc1_grad = jnp.zeros((D, FC), jnp.float32)
-        grads = cg[pl.ds(128, 2048), chan]
-        for p in range(3):
-            outer = mm(x_t[:, pl.ds(p * 128, 2048)], grads)
+        tap_grads = []
+        for k in range(4):
+            outer = mm(pairs_t[k], cg[k, :, chan])
             for s in range(3):
-                tap = p * 3 + s
                 here = outer[s * D : (s + 1) * D]
-                fc1_grad += here * wdw[pl.ds(tap, 1), chan]
-                dw_grad = jnp.sum(here * wfc1[:, chan].astype(jnp.float32), axis=0, keepdims=True)
+                if k == 3:
+                    here = -here
+                fc1_grad += here * taps[pl.ds(3 * k + s, 1), chan]
+                tap_grads.append(jnp.sum(here * wfc1[:, chan].astype(jnp.float32), axis=0, keepdims=True))
+        for s in range(3):
+            half_sum = 0.5 * (tap_grads[3 + s] + tap_grads[6 + s])
+            half_gap = 0.5 * (tap_grads[3 + s] - tap_grads[6 + s])
+            for p, value in enumerate((tap_grads[s] + half_sum, half_gap, half_sum + tap_grads[9 + s])):
                 for j in range(FC // D):
-                    stage[pl.ds(2 * FF + tap * 8 + f * (FC // D) + j, 1), :] = dw_grad[:, j * D : (j + 1) * D]
+                    at = 2 * FF + (3 * p + s) * 8 + f * (FC // D) + j
+                    stage[pl.ds(at, 1), :] = value[:, j * D : (j + 1) * D]
         for j in range(FC // D):
             stage[pl.ds((f * (FC // D) + j) * D, D), :] = fc1_grad[:, j * D : (j + 1) * D]
+    back[0, pl.ds(1024, 128), :] = jnp.zeros((128, 3 * D), jnp.float32)
+    back[3, pl.ds(0, 128), :] = jnp.zeros((128, 3 * D), jnp.float32)
+    for k in range(4):
+        for b in range(1024 // TB):
+            here = pl.ds(b * TB + (128 if k == 3 else 0), TB)
+            back[k, here, :] = mm_nt(cg[k, pl.ds(b * TB, TB), :], mix[k])
     gain_grad = jnp.zeros((1, D), jnp.float32)
     for k, bo in enumerate((bo0, bo1, bo2, bo3)):
-        base = pl.multiple_of((me ^ k) * 512, 512)
-        part = pl.ds(base, 512)
-        inside = mask[part, :]
-        middle = mid[part, :]
-        result = (middle + acc[part, :] * inside).astype(jnp.bfloat16).reshape(4, 2, 64, D)
-        for i in range(2):
-            bo[i] = result[:, i]
-        spread = jnp.zeros((512, 3 * D), jnp.float32)
-        for p in range(3):
-            rows = pl.ds(pl.multiple_of(base + (2 - p) * 128, 128), 512)
-            spread += mm_nt(cg[rows, :], w9[pl.ds(p * 3 * D, 3 * D), :])
-        after = jnp.where(col == 63, 0.0, pltpu.roll(spread[:, :D], 511, 0))
-        before = jnp.where(col == 0, 0.0, pltpu.roll(spread[:, 2 * D :], 1, 0))
-        normed_grad = (spread[:, D : 2 * D] + before + after) * inside
-        unit, scale = norm_parts(middle)
-        gain_grad += jnp.sum(normed_grad * unit, axis=0, keepdims=True)
-        mg_out[part, :] = cj[part, :].astype(jnp.float32) + norm_back(normed_grad, ln2[...], unit, scale)
+        block = me ^ k
+        for e in range(2):
+            start = pl.multiple_of(block * 256, 256)
+            here, later = pl.ds(start, 256), pl.ds(start + 128, 256)
+            part = pl.ds(pl.multiple_of(e * 1024 + block * 256, 256), 256)
+            rows = [pl.ds(pl.multiple_of(block * 512 + (2 * h + e) * 128, 128), 128) for h in range(2)]
+            inside = mask[part, :]
+            middle = jnp.concatenate([mid[row, :] for row in rows], axis=0)
+            result = (middle + acc[part, :] * inside).astype(jnp.bfloat16).reshape(2, 2, 64, D)
+            for i in range(2):
+                for h in range(2):
+                    bo[i, 2 * h + e] = result[h, i]
+            if e == 0:
+                spread = back[1, here, :] - back[2, here, :] + back[3, here, :] - back[3, later, :]
+            else:
+                spread = back[1, here, :] + back[2, here, :] - back[0, here, :] + back[0, later, :]
+            after = jnp.where(col == 63, 0.0, pltpu.roll(spread[:, :D], 255, 0))
+            before = jnp.where(col == 0, 0.0, pltpu.roll(spread[:, 2 * D :], 1, 0))
+            normed_grad = (spread[:, D : 2 * D] + before + after) * inside
+            unit, scale = norm_parts(middle)
+            gain_grad += jnp.sum(normed_grad * unit, axis=0, keepdims=True)
+            total = cj[part, :].astype(jnp.float32) + norm_back(normed_grad, gains[pl.ds(2, 1), :], unit, scale)
+            for h in range(2):
+                mg_out[rows[h], :] = total[h * 128 : (h + 1) * 128]
     stage[pl.ds(2 * FF + 72, 1), :] = gain_grad
     stage[pl.ds(2 * FF + 73, 55), :] = jnp.zeros((55, D), jnp.float32)
     split_pack(place, stage, send_out, keep_out)
@@ -475,14 +503,14 @@
     rows = stage.shape[0] // 8
     for k in range(4):
         at = pl.ds(k * rows, rows)
-        for out, core in ((send_out, 1 - place[1]), (keep_out, place[1])):
-            start = pl.multiple_of((core * 4 + (place[2] ^ k)) * rows, 16)
+        for out, core, first in ((send_out, 1 - place[1], place[3]), (keep_out, place[1], place[2])):
+            start = pl.multiple_of((core * 4 + (first ^ k)) * rows, 16)
             out[at, :] = stage[pl.ds(start, rows), :].astype(jnp.bfloat16)
 
 
 def back_kernel(
-    place, vrows, vcols, x, normed, query, prob, att, mgrad, pat, pooled, kv,
-    ln1, wq, wsr, srg, wkv, wout,
+    place, x, normed, query, prob, att, mgrad, pat, pooled, kv,
+    gains, wq, wsr, wkv, wout,
     ig0, ig1, ig2, ig3, send_out, keep_out,
     stage, probs_low, att_grad, score_grad, query_grad, unfold,
 ):
@@ -491,7 +519,7 @@
     out_grad = zero
     key_rows = []
     for i in range(2):
-        rows, cols = vrows[2 * me + i], vcols[2 * me + i]
+        rows, cols = place[4 + i], place[6 + i]
         keys = block_pair(kv[pl.ds(i * 64, 64), pl.ds(0, D)].astype(jnp.float32)).astype(jnp.bfloat16)
         values = block_pair(kv[pl.ds(i * 64, 64), pl.ds(D, D)].astype(jnp.float32)).astype(jnp.bfloat16)
         for b in range(4):
@@ -522,11 +550,11 @@
         )
     pair = jnp.concatenate(key_rows, axis=0).astype(jnp.bfloat16)
     unit, scale = norm_parts(pooled[...])
-    reduced = (unit * srg[...]).astype(jnp.bfloat16)
+    reduced = (unit * gains[pl.ds(1, 1), :]).astype(jnp.bfloat16)
     kv_grad = mm_tn(reduced, pair)
     reduced_grad = mm_nt(pair, wkv[...])
     srg_grad = jnp.sum(reduced_grad * unit, axis=0, keepdims=True)
-    pooled_low = norm_back(reduced_grad, srg[...], unit, scale).astype(jnp.bfloat16)
+    pooled_low = norm_back(reduced_grad, gains[pl.ds(1, 1), :], unit, scale).astype(jnp.bfloat16)
     stage[pl.ds(0, 2048), :] = mm_tn(pat[...], pooled_low)
     patch_grad = mm_nt(pooled_low, wsr[...])
     for i in range(2):
@@ -546,13 +574,13 @@
         part = pl.ds(block * 4, 4)
         for i in range(2):
             at = pl.ds(pl.multiple_of(i * 1024 + block * 256, 256), 256)
-            inside = block_inside(block * 4, vrows[2 * me + i], vcols[2 * me + i])
+            inside = block_inside(block * 4, place[4 + i], place[6 + i])
             back = query_grad[at, :]
             q_grad += mm_tn(normed[part, i].reshape(256, D), back)
             grad = mm_nt(back, wq[...]) + jnp.where(inside, unfold[at, :], 0.0)
             unit, scale = norm_parts(x[part, i].astype(jnp.float32).reshape(256, D))
             gain_grad += jnp.sum(grad * unit, axis=0, keepdims=True)
-            total = mgrad[part, i].reshape(256, D) + norm_back(grad, ln1[...], unit, scale)
+            total = mgrad[part, i].reshape(256, D) + norm_back(grad, gains[pl.ds(0, 1), :], unit, scale)
             ig[i] = total.astype(jnp.bfloat16).reshape(4, 64, D)
     stage[pl.ds(2304, D), :] = q_grad
     stage[pl.ds(2560, 1), :] = gain_grad
@@ -561,7 +589,7 @@
     split_pack(place, stage, send_out, keep_out)
 
 
-def call(kernel, scalars, arrays, outs, scratch, flops=0, name=None):
+def call(kernel, scalars, arrays, outs, scratch, flops=0, name=None, vmem=24):
     spec = pl.BlockSpec(memory_space=VMEM)
     return pl.pallas_call(
         kernel,
@@ -569,7 +597,7 @@
         in_specs=[pl.BlockSpec(memory_space=pltpu.SMEM)] * len(scalars) + [spec] * len(arrays),
         out_specs=[spec] * len(outs),
         scratch_shapes=scratch,
-        compiler_params=pltpu.CompilerParams(vmem_limit_bytes=56 * 2**20),
+        compiler_params=pltpu.CompilerParams(vmem_limit_bytes=vmem * 2**20),
         cost_estimate=pl.CostEstimate(flops=flops, bytes_accessed=4 * 2**20, transcendentals=0),
         name=name,
     )(*scalars, *arrays)
@@ -579,15 +607,15 @@
 JOINT = (16, 2, 64, D)
 CHUNK = (2, 4, 64, D)
 PACK1, PACK2 = 2176, 2688
-FC, TB = 256, 512
+FC, TB = 512, 1024
 SCORE_SCALE = HEAD_DIM ** (-0.5)
 
 
-def attend(place, vrows, vcols, chunks, ln1, wq, wsr, srg, wkv, wout):
+def attend(place, chunks, gains, wq, wsr, wkv, wout):
     return call(
         attend_kernel,
-        (place, vrows, vcols),
-        (*chunks, ln1, wq, wsr, srg, wkv, wout),
+        (place,),
+        (*chunks, gains, wq, wsr, wkv, wout),
         [
             (JOINT, BF), (JOINT, BF), (JOINT, BF), (JOINT, F32), (JOINT, BF), (JOINT, F32),
             ((128, 2048), BF), ((128, D), F32), ((128, 2 * D), BF),
@@ -597,28 +625,28 @@
     )
 
 
-def feed(place, vrows, vcols, middle, chunks, ln2, wfc1, wdw, wfc2):
+def feed(place, middle, chunks, gains, wfc1, taps, wfc2):
     return call(
         feed_kernel,
-        (place, vrows, vcols),
-        (middle, *chunks, ln2, wfc1, wdw, wfc2),
+        (place,),
+        (middle, *chunks, gains, wfc1, taps, wfc2),
         [(CHUNK, BF)] * 4 + [((2048, D), F32), ((PACK1 // 2, D), BF), ((PACK1 // 2, D), BF)],
         [
-            VMEM((2048, D), BF), VMEM((2048, D), BF), VMEM((D, 2048), BF),
-            VMEM((2304, 3 * D), BF), VMEM((3 * D, 2304), BF), VMEM((2048, 9 * D), BF),
-            VMEM((9 * D, FF), BF), VMEM((2304, FF), BF), VMEM((2048, FC), BF),
-            VMEM((2048, D), F32), VMEM((PACK1, D), F32), VMEM((2048, D), F32),
+            VMEM((2048, D), BF), VMEM((2048, D), BF), VMEM((D, 2048), BF), VMEM((2048, D), F32),
+            VMEM((1152, 3 * D), BF), VMEM((1152, 3 * D), BF), VMEM((4, 3 * D, FF), BF),
+            VMEM((4, 1024, 3 * D), BF), VMEM((4, 3 * D, 1024), BF), VMEM((4, 1024, FF), BF), VMEM((2048, FC), BF),
+            VMEM((2048, D), F32), VMEM((4, 1152, 3 * D), F32), VMEM((PACK1, D), F32),
         ],
-        flops=16 * 10**9, name="feed",
-    )
-
-
-def back(place, vrows, vcols, kept, mgrad, ln1, wq, wsr, srg, wkv, wout):
+        flops=16 * 10**9, name="feed", vmem=44,
+    )
+
+
+def back(place, kept, mgrad, gains, wq, wsr, wkv, wout):
     x, normed, query, prob, att, _, pat, pooled, kv = kept
     return call(
         back_kernel,
-        (place, vrows, vcols),
-        (x, normed, query, prob, att, mgrad, pat, pooled, kv, ln1, wq, wsr, srg, wkv, wout),
+        (place,),
+        (x, normed, query, prob, att, mgrad, pat, pooled, kv, gains, wq, wsr, wkv, wout),
         [(CHUNK, BF)] * 4 + [((PACK2 // 2, D), BF), ((PACK2 // 2, D), BF)],
         [
             VMEM((PACK2, D), F32), VMEM((1024, D), BF), VMEM((1024, D), BF), VMEM((1024, D), BF),
@@ -628,85 +656,108 @@
     )
 
 
-def swap(value, axes, partner):
-    size = lax.axis_size(axes)
-    return lax.ppermute(value, axes, [(i, partner(i)) for i in range(size)])
-
-
 def over_rows(value, k):
-    return swap(value, "rows", lambda i: i ^ k)
-
-
-def over_plane(value, k):
-    size = lax.axis_size("batch")
-    return swap(value, ("rows", "batch"), lambda i: i ^ ((k >> 1) * 2 * size) ^ (k & 1))
-
-
-def over_line(value, k):
-    return swap(value, "batch", lambda i: i ^ (2 * k))
+    return lax.ppermute(value, "rows", [(i, i ^ k) for i in range(4)])
+
+
+def over_four(value, k, phase):
+    plane, line = (k >> 1) * 16 + (k & 1), 2 * k
+    pairs = [(i, i ^ (plane if (i >> 3) & 1 == phase else line)) for i in range(32)]
+    return lax.ppermute(value, ("rows", "batch"), pairs)
 
 
 def plus(*values):
     return sum(v.astype(F32) for v in values).astype(BF)
 
 
-def summed(send, keep):
-    rows = send.shape[0] // 4
-    both = plus(keep, over_rows(send, 1))
-    parts = [both[k * rows : (k + 1) * rows] for k in range(4)]
-    mine = plus(parts[0], *(over_plane(parts[k], k) for k in (1, 2, 3)))
-    near, far, last = (over_line(mine, k).astype(F32) for k in (1, 2, 3))
-    total = ((mine.astype(F32) + near) + (far + last)).astype(BF)
-    pieces = [total] + [over_plane(total, k) for k in (1, 2, 3)]
-    return pieces + [over_rows(piece, 1) for piece in pieces]
+def plane_parts(packs):
+    halves_in = [plus(keep, over_rows(send, 1)) for send, keep in packs]
+    return [
+        jnp.concatenate([h[k * (h.shape[0] // 4) : (k + 1) * (h.shape[0] // 4)] for h in halves_in])
+        for k in range(4)
+    ]
+
+
+def first_sum(parts):
+    got = {k: over_four(parts[k], k, 0) for k in (3, 2, 1)}
+    return plus(parts[0], got[1], got[2], got[3])
+
+
+def second_sum(mine, got):
+    got = [g.astype(F32) for g in got]
+    return ((mine.astype(F32) + got[0]) + (got[1] + got[2])).astype(BF)
+
+
+def to_four(value, phase):
+    got = {k: over_four(value, k, phase) for k in (3, 2, 1)}
+    return got[1], got[2], got[3]
 
 
 def finish_kernel(place, *refs):
-    first, second = refs[:8], refs[8:16]
-    q, sr, kv, out, fc1, dw, fc2, gains, stage1, stage2 = refs[16:]
-    for pieces, stage in ((first, stage1), (second, stage2)):
-        rows = stage.shape[0] // 8
-        for j, piece in enumerate(pieces):
-            core = place[1] if j < 4 else 1 - place[1]
-            start = pl.multiple_of((core * 4 + (place[2] ^ (j % 4))) * rows, 16)
-            stage[pl.ds(start, rows), :] = piece[...].astype(F32)
-    for j in range(8):
-        fc1[:, pl.ds(j * D, D)] = stage1[pl.ds(j * D, D), :]
-    fc2[...] = stage1[pl.ds(FF, FF), :]
-    dw[...] = stage1[pl.ds(2 * FF, 72), :]
-    sr[...] = stage2[pl.ds(0, 2048), :]
-    for j in range(2):
-        kv[:, pl.ds(j * D, D)] = stage2[pl.ds(2048 + j * D, D), :]
-    q[...] = stage2[pl.ds(2304, D), :]
-    out[...] = stage2[pl.ds(2432, D), :]
-    gains[pl.ds(0, 1), :] = stage1[pl.ds(2 * FF + 72, 1), :]
-    gains[pl.ds(1, 1), :] = stage2[pl.ds(2560, 1), :]
-    gains[pl.ds(2, 1), :] = stage2[pl.ds(2561, 1), :]
-    gains[pl.ds(3, 5), :] = jnp.zeros((5, D), F32)
-
-
-def finish(place, first, second):
-    return call(
+    pieces, (q, sr, kv, out, fc1, fc2, dw, ln1, ln2, srg, stage1, stage2, sems) = refs[:8], refs[8:]
+    rows1, rows2 = PACK1 // 8, PACK2 // 8
+    for j, piece in enumerate(pieces):
+        core, first = (place[1], place[2]) if j < 4 else (1 - place[1], place[3])
+        spot = core * 4 + (first ^ (j % 4))
+        stage1[pl.ds(pl.multiple_of(spot * rows1, 16), rows1), :] = piece[pl.ds(0, rows1), :].astype(F32)
+        stage2[pl.ds(pl.multiple_of(spot * rows2, 16), rows2), :] = piece[pl.ds(rows1, rows2), :].astype(F32)
+    moves = [
+        (stage2.at[pl.ds(0, 2048)], sr),
+        (stage1.at[pl.ds(FF, FF)], fc2),
+        *((stage1.at[pl.ds(j * D, D)], fc1.at[:, pl.ds(j * D, D)]) for j in range(8)),
+        *((stage2.at[pl.ds(2048 + j * D, D)], kv.at[:, pl.ds(j * D, D)]) for j in range(2)),
+        (stage2.at[pl.ds(2304, D)], q),
+        (stage2.at[pl.ds(2432, D)], out),
+    ]
+    copies = [pltpu.make_async_copy(a, b, sems.at[n]) for n, (a, b) in enumerate(moves)]
+    for copy in copies:
+        copy.start()
+    for tap in range(9):
+        for j in range(8):
+            dw[tap // 3, pl.ds(tap % 3, 1), pl.ds(j * D, D)] = stage1[pl.ds(2 * FF + tap * 8 + j, 1), :]
+    ln2[...] = stage1[pl.ds(2 * FF + 72, 1), :].reshape(D)
+    ln1[...] = stage2[pl.ds(2560, 1), :].reshape(D)
+    srg[...] = stage2[pl.ds(2561, 1), :].reshape(D)
+    for copy in copies:
+        copy.wait()
+
+
+def finish(place, pieces):
+    far, near = pl.BlockSpec(memory_space=pl.ANY), pl.BlockSpec(memory_space=VMEM)
+    shapes = [(D, D), (2048, D), (D, 2 * D), (D, D), (D, FF), (FF, D), (3, 3, FF), (D,), (D,), (D,)]
+    return pl.pallas_call(
         finish_kernel,
-        (place,),
-        (*first, *second),
-        [
-            ((D, D), F32), ((2048, D), F32), ((D, 2 * D), F32), ((D, D), F32),
-            ((D, FF), F32), ((72, D), F32), ((FF, D), F32), ((8, D), F32),
-        ],
-        [VMEM((PACK1, D), F32), VMEM((PACK2, D), F32)],
+        out_shape=[jax.ShapeDtypeStruct(shape, F32) for shape in shapes],
+        in_specs=[pl.BlockSpec(memory_space=pltpu.SMEM)] + [near] * 8,
+        out_specs=[far] * 6 + [near] * 4,
+        scratch_shapes=[VMEM((PACK1, D), F32), VMEM((PACK2, D), F32), pltpu.SemaphoreType.DMA((14,))],
+        compiler_params=pltpu.CompilerParams(vmem_limit_bytes=12 * 2**20),
         name="finish",
-    )
-
-
-def gather_kernel(place, part0, part1, part2, part3, out):
-    for k, part in enumerate((part0, part1, part2, part3)):
-        out[pl.ds(2 * (place[0] ^ k), 2)] = part[...]
+    )(place, *pieces)
+
+
+def gather_kernel(place, part0, part1, part2, part3, out, sems):
+    copies = [
+        pltpu.make_async_copy(part, out.at[pl.ds(2 * (place[0] ^ k), 2)], sems.at[k])
+        for k, part in enumerate((part0, part1, part2, part3))
+    ]
+    for copy in copies:
+        copy.start()
+    for copy in copies:
+        copy.wait()
 
 
 def gather_rows(place, parts, shape):
-    (out,) = call(gather_kernel, (place,), parts, [(shape, BF)], [], name="gather_rows")
-    return out
+    far = pl.BlockSpec(memory_space=pl.ANY)
+    return pl.pallas_call(
+        gather_kernel,
+        out_shape=jax.ShapeDtypeStruct(shape, BF),
+        in_specs=[pl.BlockSpec(memory_space=pltpu.SMEM)] + [pl.BlockSpec(memory_space=VMEM)] * 4,
+        out_specs=far,
+        scratch_shapes=[pltpu.SemaphoreType.DMA((4,))],
+        compiler_params=pltpu.CompilerParams(vmem_limit_bytes=4 * 2**20),
+        name="gather_rows",
+    )(place, *parts)
 
 
 def image_shards(
@@ -714,34 +765,52 @@
     ln2_gain, fc1_weight, dw_weight, fc2_weight, cotangent,
 ):
     me, lane = lax.axis_index("rows"), lax.axis_index("batch")
-    place = jnp.stack([me, me & 1, (me >> 1) * 2 + (lane & 1), lane >> 1]).astype(jnp.int32)
+    core = me & 1
+    plane, line = (me >> 1) * 2 + (lane & 1), lane >> 1
+    first, second = jnp.where(core == 0, plane, line), jnp.where(core == 0, line, plane)
+    sizes = [lax.dynamic_slice_in_dim(v, 2 * me, 2) for v in (valid_rows, valid_cols)]
+    place = jnp.concatenate([jnp.stack([me, core, first, second]), *sizes]).astype(jnp.int32)
 
     def spread(source):
-        near = [
-            over_rows(lax.dynamic_slice_in_dim(source, 2 * (me ^ k), 2, 0), k) for k in (1, 2, 3)
-        ]
-        return (source, *near)
+        near = {
+            k: over_rows(lax.dynamic_slice_in_dim(source, 2 * (me ^ k), 2, 0), k) for k in (3, 2, 1)
+        }
+        return source, near[1], near[2], near[3]
 
     def returned(parts):
-        return gather_rows(place, (parts[0], *(over_rows(parts[k], k) for k in (1, 2, 3))), tokens.shape)
-
-    ln1, ln2, srg = (g.reshape(1, D) for g in (ln1_gain, ln2_gain, sr_gain))
-    taps = jnp.pad(dw_weight.astype(F32).reshape(9, FF), ((0, 7), (0, 0)))
+        near = {k: over_rows(parts[k], k) for k in (3, 2, 1)}
+        return parts[0], near[1], near[2], near[3]
+
+    gains = jnp.stack([ln1_gain, sr_gain, ln2_gain])
+    row0, row1, row2 = dw_weight.astype(F32)
+    taps = jnp.concatenate(
+        [row0, 0.5 * (row0 + row1 + row2), 0.5 * (row0 - row1 + row2), row2, jnp.zeros((4, FF), F32)]
+    )
+    token_parts = spread(tokens)
+    cotangent, _ = lax.optimization_barrier((cotangent, token_parts[3]))
     kept = attend(
-        place, valid_rows, valid_cols, spread(tokens), ln1, q_weight, sr_weight, srg, kv_weight, out_weight
+        place, token_parts, gains, q_weight, sr_weight, kv_weight, out_weight
     )
     *block_parts, mgrad, send1, keep1 = feed(
-        place, valid_rows, valid_cols, kept[5].reshape(2048, D), spread(cotangent), ln2, fc1_weight, taps, fc2_weight
+        place, kept[5].reshape(2048, D), spread(cotangent), gains, fc1_weight, taps, fc2_weight
     )
     *input_parts, send2, keep2 = back(
-        place, valid_rows, valid_cols, kept, mgrad.reshape(JOINT), ln1, q_weight, sr_weight, srg, kv_weight, out_weight
-    )
-    block_out = returned(block_parts)
-    input_grad = returned(input_parts)
-    q, sr, kv, out, fc1, dw, fc2, gains = finish(place, summed(send1, keep1), summed(send2, keep2))
-    return (
-        block_out, input_grad, gains[1], q, sr, gains[2], kv, out, gains[0], fc1, dw.reshape(3, 3, FF), fc2,
-    )
+        place, kept, mgrad.reshape(JOINT), gains, q_weight, sr_weight, kv_weight, out_weight
+    )
+    parts = plane_parts([(send1, keep1), (send2, keep2)])
+    parts, block_parts = lax.optimization_barrier((parts, returned(block_parts)))
+    mine = first_sum(parts)
+    got, block_out, input_parts = lax.optimization_barrier(
+        (to_four(mine, 1), gather_rows(place, block_parts, tokens.shape), returned(input_parts))
+    )
+    total = second_sum(mine, got)
+    got, input_grad = lax.optimization_barrier(
+        (to_four(total, 0), gather_rows(place, input_parts, tokens.shape))
+    )
+    pieces = [total, *got]
+    pieces += [over_rows(piece, 1) for piece in pieces]
+    q, sr, kv, out, fc1, fc2, dw, ln1_sum, ln2_sum, srg_sum = finish(place, pieces)
+    return block_out, input_grad, ln1_sum, q, sr, srg_sum, kv, out, ln2_sum, fc1, dw, fc2
 
 
 def shards(*arrays):

time: 110 us -> 87.7 us (0.80)
  starting transfers between devices: 37.7 us -> 24.5 us
  Pallas kernels: 50.8 us -> 39 us
  waiting for transfers between devices: 10.8 us -> 20.3 us
  local copies, waits for them, and re-layouts: 6.99 us -> 2.12 us
  other arithmetic: 1.64 us -> 0.42 us
    pallas_call x6 -> x3, Pallas kernels: 50.8 us -> 33.4 us  [call(): pl.pallas_call(kernel, out_shape=[jax.ShapeDtypeStruct(shape, kind) for s...]
    ppermute x40 -> x27, starting transfers between devices: 37.7 us -> 24.5 us  [the longest x18 12.9 us: over_rows(): return lax.ppermute(value, 'rows', [(i, i ^ k) for i in range(4)])]
    ppermute x40 -> x27, waiting for transfers between devices: 10.8 us -> 20.3 us  [the longest x18 11.6 us: over_rows(): return lax.ppermute(value, 'rows', [(i, i ^ k) for i in range(4)])]
    pallas_call x0 -> x3, Pallas kernels: none -> 5.56 us  [the longest x1 2.84 us: finish(): pl.pallas_call(finish_kernel, out_shape=[jax.ShapeDtypeStruct(shape, F32)...]
    unnamed x72 -> x28, local copies, waits for them, and re-layouts: 3.06 us -> 0.52 us
    reshape x2 -> x0, local copies, waits for them, and re-layouts: 1.43 us -> none  [the longest x1 1.4 us: image_shards(): dw.reshape(3, 3, FF)]
    squeeze x1 -> x0, local copies, waits for them, and re-layouts: 1.32 us -> none  [image_shards(): gains[0]]
  transfers between devices with their start and end apart: 40 -> 27, of which waited for: 12 -> 13; matrix products, arithmetic and copies ran while one was open for 2% -> 1% of each run, Pallas kernels for 19% -> 17%
where the time goes in v2:
time: 87.7 us; the launch traced here: 87.5 us
  Pallas kernels  39 us (44%)
  starting transfers between devices  24.5 us (28%)
  waiting for transfers between devices  20.3 us (23%)
  local copies, waits for them, and re-layouts  2.12 us (2%)
  between operations  1.2 us (1%)
    pallas_call x3, Pallas kernels, call(): pl.pallas_call(kernel, out_shape=[jax.ShapeDtypeStruct(shape, kind) for s...  33.4 us
    ppermute x18, starting transfers between devices, over_rows(): return lax.ppermute(value, 'rows', [(i, i ^ k) for i in range(4)])  12.9 us
    ppermute x18, waiting for transfers between devices, over_rows(): return lax.ppermute(value, 'rows', [(i, i ^ k) for i in range(4)])  11.6 us
    ppermute x9, starting transfers between devices, over_four(): return lax.ppermute(value, ('rows', 'batch'), pairs)  11.6 us
    ppermute x9, waiting for transfers between devices, over_four(): return lax.ppermute(value, ('rows', 'batch'), pairs)  8.68 us
    pallas_call x1, Pallas kernels, finish(): pl.pallas_call(finish_kernel, out_shape=[jax.ShapeDtypeStruct(shape, F32)...  2.84 us
    pallas_call x2, Pallas kernels, gather_rows(): pl.pallas_call(gather_kernel, out_shape=jax.ShapeDtypeStruct(shape, BF),...  2.72 us
  transfers between devices with their start and end apart: 27, of which 13 were waited for; matrix products, arithmetic and copies ran while one was open for 1% of the time, Pallas kernels for 17%

profile of v2, /device:TPU:0, one launch (start us, length us, event | category | flops | bytes accessed | tf_op | source)
XLA Modules:
  0.0 87.5 jit_solution(10200869822797120989)
XLA Ops:
  0.7 1.1 %constant_dynamic-slice_fusion.3 = (bf16[2,4,64,128]{3,2,1,0:T(8,128)(2,1)S(1)}, bf16[2,4,64,128]{3,2,1,0:T(8,128)(2,1)S(1)}, bf16[2,4,64,128]{3,2,1,0:T(8,128)(2,1)S(1)}) fusion(bf16[8,4,64,128]{3,2,1,0:T(8,128)(2,1)} %own.1, s32[]{:T(128)S(6)} %select_n.28, s32[]{:T(128)S(6)} %select_n.27, s32[]{:T(128)S(6)} %select_n.26), kind=kLoop, calls=%fused_computation.17 | loop fusion | bytes 786444 | tf_op jit(solution)/shard_map/dynamic_slice | solution.py:776
  1.8 2.5 %collective-permute-start.2 = (bf16[2,4,64,128]{3,2,1,0:T(8,128)(2,1)S(1)}, bf16[2,4,64,128]{3,2,1,0:T(8,128)(2,1)S(1)}, u32[]{:S(2)}, u32[]{:S(2)}) collective-permute-start(bf16[2,4,64,128]{3,2,1,0:T(8,128)(2,1)S(1)} %get-tuple-element.121), channel_id=1, source_target_pairs={{0,24},{8,16},{16,8},{24,0},{1,25},{9,17},{17,9},{25,1},{2,26},{10... | collective-permute-start | bytes 393224 | tf_op jit(solution)/shard_map/ppermute | solution.py:660
  4.3 0.6 collective-permute-start.1
  5.1 3.1 %collective-permute-done.2.near3 = bf16[2,4,64,128]{3,2,1,0:T(8,128)(2,1)S(1)} collective-permute-done((bf16[2,4,64,128]{3,2,1,0:T(8,128)(2,1)S(1)}, bf16[2,4,64,128]{3,2,1,0:T(8,128)(2,1)S(1)}, u32[]{:S(2)}, u32[]{:S(2)}) %collective-permute-start.2) | collective-permute-done | bytes 131104 | tf_op jit(solution)/shard_map/ppermute | solution.py:660
  8.2 2.2 %collective-permute-start.5 = (bf16[2,4,64,128]{3,2,1,0:T(8,128)(2,1)S(1)}, bf16[2,4,64,128]{3,2,1,0:T(8,128)(2,1)S(1)}, u32[]{:S(2)}, u32[]{:S(2)}) collective-permute-start(bf16[2,4,64,128]{3,2,1,0:T(8,128)(2,1)S(1)} %get-tuple-element.118), channel_id=1, source_target_pairs={{0,24},{8,16},{16,8},{24,0},{1,25},{9,17},{17,9},{25,1},{2,26},{10... | collective-permute-start | bytes 393224 | tf_op jit(solution)/shard_map/ppermute | solution.py:660
  10.4 0.4 collective-permute-start.4
  10.9 0.1 dynamic_slice.24
  11.0 0.2 concatenate.19.taps
  11.2 0.1 concatenate.18.place
  11.4 0.4 copy-done.6
  11.8 5.8 %attend.1 = (bf16[16,2,64,128]{3,2,1,0:T(8,128)(2,1)S(1)}, bf16[16,2,64,128]{3,2,1,0:T(8,128)(2,1)S(1)}, bf16[16,2,64,128]{3,2,1,0:T(8,128)(2,1)S(1)}, f32[16,2,...) custom-call(s32[8]{0:T(128)S(1)} %concatenate.18.place, ...), custom_call_target="tpu_custom_call" | custom-call | flops 1000000000 | bytes 4194304 | tf_op jit(solution)/shard_map/attend/pallas_call | solution.py:594
  17.7 20.9 %feed.1 = (bf16[2,4,64,128]{3,2,1,0:T(8,128)(2,1)S(1)}, bf16[2,4,64,128]{3,2,1,0:T(8,128)(2,1)S(1)}, bf16[2,4,64,128]{3,2,1,0:T(8,128)(2,1)S(1)}, bf16[2,4,64,12...) custom-call(s32[8]{0:T(128)S(1)} %concatenate.18.place, ...), custom_call_target="tpu_custom_call" | custom-call | flops 16000000000 | bytes 4194304 | tf_op jit(solution)/shard_map/feed/pallas_call | solution.py:594
  38.6 0.6 collective-permute-start.6
  39.2 0.1 collective-permute-start.8
  39.3 1.7 %collective-permute-start.9 = (bf16[2,4,64,128]{3,2,1,0:T(8,128)(2,1)S(1)}, bf16[2,4,64,128]{3,2,1,0:T(8,128)(2,1)S(1)}, u32[]{:S(2)}, u32[]{:S(2)}) collective-permute-start(bf16[2,4,64,128]{3,2,1,0:T(8,128)(2,1)S(1)} %get-tuple-element.82), channel_id=1, source_target_pairs={{0,16},{8,24},{16,0},{24,8},{1,17},{9,25},{17,1},{25,9},{2,18},{10... | collective-permute-start | bytes 393224 | tf_op jit(solution)/shard_map/ppermute | solution.py:660
  41.1 6.7 %back.1 = (bf16[2,4,64,128]{3,2,1,0:T(8,128)(2,1)S(1)}, bf16[2,4,64,128]{3,2,1,0:T(8,128)(2,1)S(1)}, bf16[2,4,64,128]{3,2,1,0:T(8,128)(2,1)S(1)}, bf16[2,4,64,12...) custom-call(s32[8]{0:T(128)S(1)} %concatenate.18.place, ...), custom_call_target="tpu_custom_call" | custom-call | flops 2000000000 | bytes 4194304 | tf_op jit(solution)/shard_map/back/pallas_call | solution.py:594
  47.7 0.4 collective-permute-start.7
  48.3 1.2 %collective-permute-done.7 = bf16[1344,128]{1,0:T(8,128)(2,1)S(1)} collective-permute-done((bf16[1344,128]{1,0:T(8,128)(2,1)S(1)}, bf16[1344,128]{1,0:T(8,128)(2,1)S(1)}, u32[]{:S(2)}, u32[]{:S(2)}) %collective-permute-start.7) | collective-permute-done | bytes 344096 | tf_op jit(solution)/shard_map/ppermute | solution.py:660
  49.4 0.1 add_convert_fusion
  49.7 1.7 %collective-permute-start.11 = (bf16[608,128]{1,0:T(8,128)(2,1)S(1)}, bf16[608,128]{1,0:T(8,128)(2,1)S(1)}, u32[]{:S(2)}, u32[]{:S(2)}) collective-permute-start(bf16[608,128]{1,0:T(8,128)(2,1)S(1)} %get-tuple-element.85), channel_id=1, source_target_pairs={{0,1},{1,0},{2,3},{3,2},{4,5},{5,4},{6,7},{7,6},{8,10},{9,11},{10,... | collective-permute-start | bytes 466952 | tf_op jit(solution)/shard_map/ppermute | solution.py:666
  51.3 1.6 %collective-permute-start.12 = (bf16[608,128]{1,0:T(8,128)(2,1)S(1)}, bf16[608,128]{1,0:T(8,128)(2,1)S(1)}, u32[]{:S(2)}, u32[]{:S(2)}) collective-permute-start(bf16[608,128]{1,0:T(8,128)(2,1)S(1)} %get-tuple-element.86), channel_id=1, source_target_pairs={{0,16},{1,17},{2,18},{3,19},{4,20},{5,21},{6,22},{7,23},{8,12},{9,... | collective-permute-start | bytes 466952 | tf_op jit(solution)/shard_map/ppermute | solution.py:666
  52.9 0.3 collective-permute-start.13
  53.2 0.6 collective-permute-start.17
  53.8 1.1 %collective-permute-done.11 = bf16[608,128]{1,0:T(8,128)(2,1)S(1)} collective-permute-done((bf16[608,128]{1,0:T(8,128)(2,1)S(1)}, bf16[608,128]{1,0:T(8,128)(2,1)S(1)}, u32[]{:S(2)}, u32[]{:S(2)}) %collective-permute-start.11) | collective-permute-done | bytes 155680 | tf_op jit(solution)/shard_map/ppermute | solution.py:666
  55.0 2.4 %collective-permute-done.12 = bf16[608,128]{1,0:T(8,128)(2,1)S(1)} collective-permute-done((bf16[608,128]{1,0:T(8,128)(2,1)S(1)}, bf16[608,128]{1,0:T(8,128)(2,1)S(1)}, u32[]{:S(2)}, u32[]{:S(2)}) %collective-permute-start.12) | collective-permute-done | bytes 155680 | tf_op jit(solution)/shard_map/ppermute | solution.py:666
  57.4 1.7 %collective-permute-done.13 = bf16[608,128]{1,0:T(8,128)(2,1)S(1)} collective-permute-done((bf16[608,128]{1,0:T(8,128)(2,1)S(1)}, bf16[608,128]{1,0:T(8,128)(2,1)S(1)}, u32[]{:S(2)}, u32[]{:S(2)}) %collective-permute-start.13) | collective-permute-done | bytes 155680 | tf_op jit(solution)/shard_map/ppermute | solution.py:666
  59.1 0.1 add_convert_fusion.3
  59.2 3.7 %collective-permute-start.16 = (bf16[608,128]{1,0:T(8,128)(2,1)S(1)}, bf16[608,128]{1,0:T(8,128)(2,1)S(1)}, u32[]{:S(2)}, u32[]{:S(2)}) collective-permute-start(bf16[608,128]{1,0:T(8,128)(2,1)S(1)} %add_convert_fusion.3), channel_id=1, source_target_pairs={{0,6},{1,7},{2,4},{3,5},{4,2},{5,3},{6,0},{7,1},{8,25},{9,24},{10,... | collective-permute-start | bytes 466952 | tf_op jit(solution)/shard_map/ppermute | solution.py:666
  62.8 0.8 collective-permute-start.14
  63.6 0.8 collective-permute-start.18
  64.4 1.4 %gather_rows.2 = bf16[8,4,64,128]{3,2,1,0:T(8,128)(2,1)} custom-call(s32[8]{0:T(128)S(1)} %concatenate.18.place, bf16[2,4,64,128]{3,2,1,0:T(8,128)(2,1)S(1)} %get-tuple-element.88.part0, bf16[2,4,64,128]{3,2,1,0:T(8,128)(2,1)S(1)} %collective-permute-done.8.part1, bf16[2,4,64,128]{3,2,1,0:T(8,128)(2,1)S(1)} %collective-permute-done.9.part2, ...), custom_call_target="tpu_custom_call" | custom-call | tf_op jit(solution)/shard_map/gather_rows/pallas_call | solution.py:752
  65.8 4.3 %collective-permute-done.18.part2 = bf16[2,4,64,128]{3,2,1,0:T(8,128)(2,1)S(1)} collective-permute-done((bf16[2,4,64,128]{3,2,1,0:T(8,128)(2,1)S(1)}, bf16[2,4,64,128]{3,2,1,0:T(8,128)(2,1)S(1)}, u32[]{:S(2)}, u32[]{:S(2)}) %collective-permute-start.18) | collective-permute-done | bytes 131104 | tf_op jit(solution)/shard_map/ppermute | solution.py:660
  70.1 2.0 %collective-permute-done.19.part3 = bf16[2,4,64,128]{3,2,1,0:T(8,128)(2,1)S(1)} collective-permute-done((bf16[2,4,64,128]{3,2,1,0:T(8,128)(2,1)S(1)}, bf16[2,4,64,128]{3,2,1,0:T(8,128)(2,1)S(1)}, u32[]{:S(2)}, u32[]{:S(2)}) %collective-permute-start.19) | collective-permute-done | bytes 131104 | tf_op jit(solution)/shard_map/ppermute | solution.py:660
  72.0 0.1 add_convert_fusion.2.refs_0_
  72.1 2.2 %collective-permute-start.22 = (bf16[608,128]{1,0:T(8,128)(2,1)S(1)}, bf16[608,128]{1,0:T(8,128)(2,1)S(1)}, u32[]{:S(2)}, u32[]{:S(2)}) collective-permute-start(bf16[608,128]{1,0:T(8,128)(2,1)S(1)} %add_convert_fusion.2.refs_0_), channel_id=1, source_target_pairs={{0,17},{1,16},{2,19},{3,18},{4,21},{5,20},{6,23},{7,22},{8,14},{9,... | collective-permute-start | bytes 466952 | tf_op jit(solution)/shard_map/ppermute | solution.py:666
  74.4 1.2 %collective-permute-start.21 = (bf16[608,128]{1,0:T(8,128)(2,1)S(1)}, bf16[608,128]{1,0:T(8,128)(2,1)S(1)}, u32[]{:S(2)}, u32[]{:S(2)}) collective-permute-start(bf16[608,128]{1,0:T(8,128)(2,1)S(1)} %add_convert_fusion.2.refs_0_), channel_id=1, source_target_pairs={{0,16},{1,17},{2,18},{3,19},{4,20},{5,21},{6,22},{7,23},{8,12},{9,... | collective-permute-start | bytes 466952 | tf_op jit(solution)/shard_map/ppermute | solution.py:666
  75.6 0.1 collective-permute-start.20
  75.7 0.3 collective-permute-start.23
  76.0 1.4 %gather_rows.3 = bf16[8,4,64,128]{3,2,1,0:T(8,128)(2,1)} custom-call(s32[8]{0:T(128)S(1)} %concatenate.18.place, bf16[2,4,64,128]{3,2,1,0:T(8,128)(2,1)S(1)} %get-tuple-element.100.part0, bf16[2,4,64,128]{3,2,1,0:T(8,128)(2,1)S(1)} %collective-permute-done.17.part1, bf16[2,4,64,128]{3,2,1,0:T(8,128)(2,1)S(1)} %collective-permute-done.18.part2, ...), custom_call_target="tpu_custom_call" | custom-call | tf_op jit(solution)/shard_map/gather_rows/pallas_call | solution.py:752
  77.4 1.0 %collective-permute-done.22.refs_3_ = bf16[608,128]{1,0:T(8,128)(2,1)S(1)} collective-permute-done((bf16[608,128]{1,0:T(8,128)(2,1)S(1)}, bf16[608,128]{1,0:T(8,128)(2,1)S(1)}, u32[]{:S(2)}, u32[]{:S(2)}) %collective-permute-start.22) | collective-permute-done | bytes 155680 | tf_op jit(solution)/shard_map/ppermute | solution.py:666
  78.4 1.6 %collective-permute-done.21.refs_2_ = bf16[608,128]{1,0:T(8,128)(2,1)S(1)} collective-permute-done((bf16[608,128]{1,0:T(8,128)(2,1)S(1)}, bf16[608,128]{1,0:T(8,128)(2,1)S(1)}, u32[]{:S(2)}, u32[]{:S(2)}) %collective-permute-start.21) | collective-permute-done | bytes 155680 | tf_op jit(solution)/shard_map/ppermute | solution.py:666
  80.0 0.8 collective-permute-done.20.refs_1_
  80.8 2.1 %collective-permute-start.24 = (bf16[608,128]{1,0:T(8,128)(2,1)S(1)}, bf16[608,128]{1,0:T(8,128)(2,1)S(1)}, u32[]{:S(2)}, u32[]{:S(2)}) collective-permute-start(bf16[608,128]{1,0:T(8,128)(2,1)S(1)} %collective-permute-done.20.refs_1_), channel_id=1, source_target_pairs={{0,8},{8,0},{16,24},{24,16},{1,9},{9,1},{17,25},{25,17},{2,10},{10... | collective-permute-start | bytes 466952 | tf_op jit(solution)/shard_map/ppermute | solution.py:660
  82.9 0.5 collective-permute-start.26
  83.4 0.5 collective-permute-done.24.refs_5_
  83.9 0.4 collective-permute-done.25.refs_6_
  84.3 0.2 collective-permute-done.26.refs_7_
  84.5 2.8 %finish.1 = (f32[128,128]{1,0:T(8,128)}, f32[2048,128]{1,0:T(8,128)}, f32[128,256]{1,0:T(8,128)}, f32[128,128]{1,0:T(8,128)}, f32[128,1024]{1,0:T(8,128)}, /*ind...) custom-call(s32[8]{0:T(128)S(1)} %concatenate.18.place, ...), custom_call_target="tpu_custom_call" | custom-call | tf_op jit(solution)/shard_map/finish/pallas_call | solution.py:728
  (59 shorter events, 0.6 us)
Async XLA Ops:
  0.6 7.5 %copy-start.1 = (bf16[8,4,64,128]{3,2,1,0:T(8,128)(2,1)S(1)}, bf16[8,4,64,128]{3,2,1,0:T(8,128)(2,1)}, u32[]{:S(2)}) copy-start(bf16[8,4,64,128]{3,2,1,0:T(8,128)(2,1)} %cot) | copy-start | bytes 1572868
  0.7 4.3 %copy-start.8 = (bf16[3,3,1024]{2,1,0:T(4,128)(2,1)S(1)}, bf16[3,3,1024]{2,1,0:T(4,128)(2,1)}, u32[]{:S(2)}) copy-start(bf16[3,3,1024]{2,1,0:T(4,128)(2,1)} %param.25) | copy-start | bytes 55300
  1.8 6.4 %collective-permute-start.2 = (bf16[2,4,64,128]{3,2,1,0:T(8,128)(2,1)S(1)}, bf16[2,4,64,128]{3,2,1,0:T(8,128)(2,1)S(1)}, u32[]{:S(2)}, u32[]{:S(2)}) collective-permute-start(bf16[2,4,64,128]{3,2,1,0:T(8,128)(2,1)S(1)} %get-tuple-element.121), channel_id=1, source_target_pairs={{0,24},{8,16},{16,8},{24,0},{1,25},{9,17},{17,9},{25,1},{2,26},{10... | collective-permute-start | bytes 393224 | tf_op jit(solution)/shard_map/ppermute | solution.py:660
  4.3 7.0 %collective-permute-start.1 = (bf16[2,4,64,128]{3,2,1,0:T(8,128)(2,1)S(1)}, bf16[2,4,64,128]{3,2,1,0:T(8,128)(2,1)S(1)}, u32[]{:S(2)}, u32[]{:S(2)}) collective-permute-start(bf16[2,4,64,128]{3,2,1,0:T(8,128)(2,1)S(1)} %get-tuple-element.122), channel_id=1, source_target_pairs={{0,16},{8,24},{16,0},{24,8},{1,17},{9,25},{17,1},{25,9},{2,18},{10... | collective-permute-start | bytes 393224 | tf_op jit(solution)/shard_map/ppermute | solution.py:660
  4.9 6.4 %collective-permute-start = (bf16[2,4,64,128]{3,2,1,0:T(8,128)(2,1)S(1)}, bf16[2,4,64,128]{3,2,1,0:T(8,128)(2,1)S(1)}, u32[]{:S(2)}, u32[]{:S(2)}) collective-permute-start(bf16[2,4,64,128]{3,2,1,0:T(8,128)(2,1)S(1)} %get-tuple-element.123), channel_id=1, source_target_pairs={{0,8},{8,0},{16,24},{24,16},{1,9},{9,1},{17,25},{25,17},{2,10},{10... | collective-permute-start | bytes 393224 | tf_op jit(solution)/shard_map/ppermute | solution.py:660
  5.0 6.4 %copy-start.7 = (bf16[128,128]{1,0:T(8,128)(2,1)S(1)}, bf16[128,128]{1,0:T(8,128)(2,1)}, u32[]{:S(2)}) copy-start(bf16[128,128]{1,0:T(8,128)(2,1)} %wout.3) | copy-start | bytes 98308
  5.0 6.4 %copy-start.5 = (bf16[128,256]{1,0:T(8,128)(2,1)S(1)}, bf16[128,256]{1,0:T(8,128)(2,1)}, u32[]{:S(2)}) copy-start(bf16[128,256]{1,0:T(8,128)(2,1)} %wkv.3) | copy-start | bytes 196612
  5.0 5.8 %copy-start.9 = (f32[128]{0:T(128)S(1)}, f32[128]{0:T(128)}, u32[]{:S(2)}) copy-start(f32[128]{0:T(128)} %param.23) | copy-start | bytes 1540
  5.0 5.8 %copy-start.10 = (f32[128]{0:T(128)S(1)}, f32[128]{0:T(128)}, u32[]{:S(2)}) copy-start(f32[128]{0:T(128)} %param.20) | copy-start | bytes 1540
  5.0 5.8 %copy-start.11 = (f32[128]{0:T(128)S(1)}, f32[128]{0:T(128)}, u32[]{:S(2)}) copy-start(f32[128]{0:T(128)} %param.17) | copy-start | bytes 1540
  5.0 5.8 %copy-start.12 = (s32[8]{0:T(128)S(1)}, s32[8]{0:T(128)}, u32[]{:S(2)}) copy-start(s32[8]{0:T(128)} %param.15) | copy-start | bytes 100
  5.0 5.9 %copy-start.13 = (s32[8]{0:T(128)S(1)}, s32[8]{0:T(128)}, u32[]{:S(2)}) copy-start(s32[8]{0:T(128)} %param.16) | copy-start | bytes 100
  5.1 6.3 %copy-start.2 = (bf16[2048,128]{1,0:T(8,128)(2,1)S(1)}, bf16[2048,128]{1,0:T(8,128)(2,1)}, u32[]{:S(2)}) copy-start(bf16[2048,128]{1,0:T(8,128)(2,1)} %wsr.3) | copy-start | bytes 1572868
  5.1 6.3 %copy-start = (bf16[8,4,64,128]{3,2,1,0:T(8,128)(2,1)S(1)}, bf16[8,4,64,128]{3,2,1,0:T(8,128)(2,1)}, u32[]{:S(2)}) copy-start(bf16[8,4,64,128]{3,2,1,0:T(8,128)(2,1)} %own.1) | copy-start | bytes 1572868
  8.2 9.4 %collective-permute-start.5 = (bf16[2,4,64,128]{3,2,1,0:T(8,128)(2,1)S(1)}, bf16[2,4,64,128]{3,2,1,0:T(8,128)(2,1)S(1)}, u32[]{:S(2)}, u32[]{:S(2)}) collective-permute-start(bf16[2,4,64,128]{3,2,1,0:T(8,128)(2,1)S(1)} %get-tuple-element.118), channel_id=1, source_target_pairs={{0,24},{8,16},{16,8},{24,0},{1,25},{9,17},{17,9},{25,1},{2,26},{10... | collective-permute-start | bytes 393224 | tf_op jit(solution)/shard_map/ppermute | solution.py:660
  10.4 7.2 %collective-permute-start.4 = (bf16[2,4,64,128]{3,2,1,0:T(8,128)(2,1)S(1)}, bf16[2,4,64,128]{3,2,1,0:T(8,128)(2,1)S(1)}, u32[]{:S(2)}, u32[]{:S(2)}) collective-permute-start(bf16[2,4,64,128]{3,2,1,0:T(8,128)(2,1)S(1)} %get-tuple-element.119), channel_id=1, source_target_pairs={{0,16},{8,24},{16,0},{24,8},{1,17},{9,25},{17,1},{25,9},{2,18},{10... | collective-permute-start | bytes 393224 | tf_op jit(solution)/shard_map/ppermute | solution.py:660
  10.8 6.9 %collective-permute-start.3 = (bf16[2,4,64,128]{3,2,1,0:T(8,128)(2,1)S(1)}, bf16[2,4,64,128]{3,2,1,0:T(8,128)(2,1)S(1)}, u32[]{:S(2)}, u32[]{:S(2)}) collective-permute-start(bf16[2,4,64,128]{3,2,1,0:T(8,128)(2,1)S(1)} %get-tuple-element.120), channel_id=1, source_target_pairs={{0,8},{8,0},{16,24},{24,16},{1,9},{9,1},{17,25},{25,17},{2,10},{10... | collective-permute-start | bytes 393224 | tf_op jit(solution)/shard_map/ppermute | solution.py:660
  11.0 0.8 copy-start.6
  11.3 6.4 %copy-start.3 = (bf16[128,1024]{1,0:T(8,128)(2,1)S(1)}, bf16[128,1024]{1,0:T(8,128)(2,1)}, u32[]{:S(2)}) copy-start(bf16[128,1024]{1,0:T(8,128)(2,1)} %wfc1.1) | copy-start | bytes 786436
  11.3 6.4 %copy-start.4 = (bf16[1024,128]{1,0:T(8,128)(2,1)S(1)}, bf16[1024,128]{1,0:T(8,128)(2,1)}, u32[]{:S(2)}) copy-start(bf16[1024,128]{1,0:T(8,128)(2,1)} %wfc2.1) | copy-start | bytes 786436
  38.6 9.5 %collective-permute-start.6 = (bf16[1088,128]{1,0:T(8,128)(2,1)S(1)}, bf16[1088,128]{1,0:T(8,128)(2,1)S(1)}, u32[]{:S(2)}, u32[]{:S(2)}) collective-permute-start(bf16[1088,128]{1,0:T(8,128)(2,1)S(1)} %get-tuple-element.68), channel_id=1, source_target_pairs={{0,8},{8,0},{16,24},{24,16},{1,9},{9,1},{17,25},{25,17},{2,10},{10... | collective-permute-start | bytes 835592 | tf_op jit(solution)/shard_map/ppermute | solution.py:660
  39.2 10.4 %collective-permute-start.8 = (bf16[2,4,64,128]{3,2,1,0:T(8,128)(2,1)S(1)}, bf16[2,4,64,128]{3,2,1,0:T(8,128)(2,1)S(1)}, u32[]{:S(2)}, u32[]{:S(2)}) collective-permute-start(bf16[2,4,64,128]{3,2,1,0:T(8,128)(2,1)S(1)} %get-tuple-element.81), channel_id=1, source_target_pairs={{0,8},{8,0},{16,24},{24,16},{1,9},{9,1},{17,25},{25,17},{2,10},{10... | collective-permute-start | bytes 393224 | tf_op jit(solution)/shard_map/ppermute | solution.py:660
  39.3 10.4 %collective-permute-start.9 = (bf16[2,4,64,128]{3,2,1,0:T(8,128)(2,1)S(1)}, bf16[2,4,64,128]{3,2,1,0:T(8,128)(2,1)S(1)}, u32[]{:S(2)}, u32[]{:S(2)}) collective-permute-start(bf16[2,4,64,128]{3,2,1,0:T(8,128)(2,1)S(1)} %get-tuple-element.82), channel_id=1, source_target_pairs={{0,16},{8,24},{16,0},{24,8},{1,17},{9,25},{17,1},{25,9},{2,18},{10... | collective-permute-start | bytes 393224 | tf_op jit(solution)/shard_map/ppermute | solution.py:660
  41.0 8.7 %collective-permute-start.10 = (bf16[2,4,64,128]{3,2,1,0:T(8,128)(2,1)S(1)}, bf16[2,4,64,128]{3,2,1,0:T(8,128)(2,1)S(1)}, u32[]{:S(2)}, u32[]{:S(2)}) collective-permute-start(bf16[2,4,64,128]{3,2,1,0:T(8,128)(2,1)S(1)} %get-tuple-element.83), channel_id=1, source_target_pairs={{0,24},{8,16},{16,8},{24,0},{1,25},{9,17},{17,9},{25,1},{2,26},{10... | collective-permute-start | bytes 393224 | tf_op jit(solution)/shard_map/ppermute | solution.py:660
  47.7 1.7 %collective-permute-start.7 = (bf16[1344,128]{1,0:T(8,128)(2,1)S(1)}, bf16[1344,128]{1,0:T(8,128)(2,1)S(1)}, u32[]{:S(2)}, u32[]{:S(2)}) collective-permute-start(bf16[1344,128]{1,0:T(8,128)(2,1)S(1)} %get-tuple-element.79), channel_id=1, source_target_pairs={{0,8},{8,0},{16,24},{24,16},{1,9},{9,1},{17,25},{25,17},{2,10},{10... | collective-permute-start | bytes 1032200 | tf_op jit(solution)/shard_map/ppermute | solution.py:660
  49.7 5.3 %collective-permute-start.11 = (bf16[608,128]{1,0:T(8,128)(2,1)S(1)}, bf16[608,128]{1,0:T(8,128)(2,1)S(1)}, u32[]{:S(2)}, u32[]{:S(2)}) collective-permute-start(bf16[608,128]{1,0:T(8,128)(2,1)S(1)} %get-tuple-element.85), channel_id=1, source_target_pairs={{0,1},{1,0},{2,3},{3,2},{4,5},{5,4},{6,7},{7,6},{8,10},{9,11},{10,... | collective-permute-start | bytes 466952 | tf_op jit(solution)/shard_map/ppermute | solution.py:666
  51.3 6.0 %collective-permute-start.12 = (bf16[608,128]{1,0:T(8,128)(2,1)S(1)}, bf16[608,128]{1,0:T(8,128)(2,1)S(1)}, u32[]{:S(2)}, u32[]{:S(2)}) collective-permute-start(bf16[608,128]{1,0:T(8,128)(2,1)S(1)} %get-tuple-element.86), channel_id=1, source_target_pairs={{0,16},{1,17},{2,18},{3,19},{4,20},{5,21},{6,22},{7,23},{8,12},{9,... | collective-permute-start | bytes 466952 | tf_op jit(solution)/shard_map/ppermute | solution.py:666
  52.9 6.1 %collective-permute-start.13 = (bf16[608,128]{1,0:T(8,128)(2,1)S(1)}, bf16[608,128]{1,0:T(8,128)(2,1)S(1)}, u32[]{:S(2)}, u32[]{:S(2)}) collective-permute-start(bf16[608,128]{1,0:T(8,128)(2,1)S(1)} %get-tuple-element.87), channel_id=1, source_target_pairs={{0,17},{1,16},{2,19},{3,18},{4,21},{5,20},{6,23},{7,22},{8,14},{9,... | collective-permute-start | bytes 466952 | tf_op jit(solution)/shard_map/ppermute | solution.py:666
  53.2 11.2 %collective-permute-start.17 = (bf16[2,4,64,128]{3,2,1,0:T(8,128)(2,1)S(1)}, bf16[2,4,64,128]{3,2,1,0:T(8,128)(2,1)S(1)}, u32[]{:S(2)}, u32[]{:S(2)}) collective-permute-start(bf16[2,4,64,128]{3,2,1,0:T(8,128)(2,1)S(1)} %get-tuple-element.93), channel_id=1, source_target_pairs={{0,8},{8,0},{16,24},{24,16},{1,9},{9,1},{17,25},{25,17},{2,10},{10... | collective-permute-start | bytes 393224 | tf_op jit(solution)/shard_map/ppermute | solution.py:660
  59.2 12.9 %collective-permute-start.16 = (bf16[608,128]{1,0:T(8,128)(2,1)S(1)}, bf16[608,128]{1,0:T(8,128)(2,1)S(1)}, u32[]{:S(2)}, u32[]{:S(2)}) collective-permute-start(bf16[608,128]{1,0:T(8,128)(2,1)S(1)} %add_convert_fusion.3), channel_id=1, source_target_pairs={{0,6},{1,7},{2,4},{3,5},{4,2},{5,3},{6,0},{7,1},{8,25},{9,24},{10,... | collective-permute-start | bytes 466952 | tf_op jit(solution)/shard_map/ppermute | solution.py:666
  62.8 9.2 %collective-permute-start.15 = (bf16[608,128]{1,0:T(8,128)(2,1)S(1)}, bf16[608,128]{1,0:T(8,128)(2,1)S(1)}, u32[]{:S(2)}, u32[]{:S(2)}) collective-permute-start(bf16[608,128]{1,0:T(8,128)(2,1)S(1)} %add_convert_fusion.3), channel_id=1, source_target_pairs={{0,4},{1,5},{2,6},{3,7},{4,0},{5,1},{6,2},{7,3},{8,24},{9,25},{10,... | collective-permute-start | bytes 466952 | tf_op jit(solution)/shard_map/ppermute | solution.py:666
  62.8 9.2 %collective-permute-start.14 = (bf16[608,128]{1,0:T(8,128)(2,1)S(1)}, bf16[608,128]{1,0:T(8,128)(2,1)S(1)}, u32[]{:S(2)}, u32[]{:S(2)}) collective-permute-start(bf16[608,128]{1,0:T(8,128)(2,1)S(1)} %add_convert_fusion.3), channel_id=1, source_target_pairs={{0,2},{1,3},{2,0},{3,1},{4,6},{5,7},{6,4},{7,5},{8,9},{9,8},{10,11... | collective-permute-start | bytes 466952 | tf_op jit(solution)/shard_map/ppermute | solution.py:666
  63.6 6.4 %collective-permute-start.18 = (bf16[2,4,64,128]{3,2,1,0:T(8,128)(2,1)S(1)}, bf16[2,4,64,128]{3,2,1,0:T(8,128)(2,1)S(1)}, u32[]{:S(2)}, u32[]{:S(2)}) collective-permute-start(bf16[2,4,64,128]{3,2,1,0:T(8,128)(2,1)S(1)} %get-tuple-element.94), channel_id=1, source_target_pairs={{0,16},{8,24},{16,0},{24,8},{1,17},{9,25},{17,1},{25,9},{2,18},{10... | collective-permute-start | bytes 393224 | tf_op jit(solution)/shard_map/ppermute | solution.py:660
  64.4 7.6 %collective-permute-start.19 = (bf16[2,4,64,128]{3,2,1,0:T(8,128)(2,1)S(1)}, bf16[2,4,64,128]{3,2,1,0:T(8,128)(2,1)S(1)}, u32[]{:S(2)}, u32[]{:S(2)}) collective-permute-start(bf16[2,4,64,128]{3,2,1,0:T(8,128)(2,1)S(1)} %get-tuple-element.95), channel_id=1, source_target_pairs={{0,24},{8,16},{16,8},{24,0},{1,25},{9,17},{17,9},{25,1},{2,26},{10... | collective-permute-start | bytes 393224 | tf_op jit(solution)/shard_map/ppermute | solution.py:660
  72.1 6.2 %collective-permute-start.22 = (bf16[608,128]{1,0:T(8,128)(2,1)S(1)}, bf16[608,128]{1,0:T(8,128)(2,1)S(1)}, u32[]{:S(2)}, u32[]{:S(2)}) collective-permute-start(bf16[608,128]{1,0:T(8,128)(2,1)S(1)} %add_convert_fusion.2.refs_0_), channel_id=1, source_target_pairs={{0,17},{1,16},{2,19},{3,18},{4,21},{5,20},{6,23},{7,22},{8,14},{9,... | collective-permute-start | bytes 466952 | tf_op jit(solution)/shard_map/ppermute | solution.py:666
  74.4 5.6 %collective-permute-start.21 = (bf16[608,128]{1,0:T(8,128)(2,1)S(1)}, bf16[608,128]{1,0:T(8,128)(2,1)S(1)}, u32[]{:S(2)}, u32[]{:S(2)}) collective-permute-start(bf16[608,128]{1,0:T(8,128)(2,1)S(1)} %add_convert_fusion.2.refs_0_), channel_id=1, source_target_pairs={{0,16},{1,17},{2,18},{3,19},{4,20},{5,21},{6,22},{7,23},{8,12},{9,... | collective-permute-start | bytes 466952 | tf_op jit(solution)/shard_map/ppermute | solution.py:666
  75.6 5.2 %collective-permute-start.20 = (bf16[608,128]{1,0:T(8,128)(2,1)S(1)}, bf16[608,128]{1,0:T(8,128)(2,1)S(1)}, u32[]{:S(2)}, u32[]{:S(2)}) collective-permute-start(bf16[608,128]{1,0:T(8,128)(2,1)S(1)} %add_convert_fusion.2.refs_0_), channel_id=1, source_target_pairs={{0,1},{1,0},{2,3},{3,2},{4,5},{5,4},{6,7},{7,6},{8,10},{9,11},{10,... | collective-permute-start | bytes 466952 | tf_op jit(solution)/shard_map/ppermute | solution.py:666
  75.7 7.7 %collective-permute-start.23 = (bf16[608,128]{1,0:T(8,128)(2,1)S(1)}, bf16[608,128]{1,0:T(8,128)(2,1)S(1)}, u32[]{:S(2)}, u32[]{:S(2)}) collective-permute-start(bf16[608,128]{1,0:T(8,128)(2,1)S(1)} %add_convert_fusion.2.refs_0_), channel_id=1, source_target_pairs={{0,8},{8,0},{16,24},{24,16},{1,9},{9,1},{17,25},{25,17},{2,10},{10... | collective-permute-start | bytes 466952 | tf_op jit(solution)/shard_map/ppermute | solution.py:660
  80.8 3.1 %collective-permute-start.24 = (bf16[608,128]{1,0:T(8,128)(2,1)S(1)}, bf16[608,128]{1,0:T(8,128)(2,1)S(1)}, u32[]{:S(2)}, u32[]{:S(2)}) collective-permute-start(bf16[608,128]{1,0:T(8,128)(2,1)S(1)} %collective-permute-done.20.refs_1_), channel_id=1, source_target_pairs={{0,8},{8,0},{16,24},{24,16},{1,9},{9,1},{17,25},{25,17},{2,10},{10... | collective-permute-start | bytes 466952 | tf_op jit(solution)/shard_map/ppermute | solution.py:660
  82.9 1.4 %collective-permute-start.25 = (bf16[608,128]{1,0:T(8,128)(2,1)S(1)}, bf16[608,128]{1,0:T(8,128)(2,1)S(1)}, u32[]{:S(2)}, u32[]{:S(2)}) collective-permute-start(bf16[608,128]{1,0:T(8,128)(2,1)S(1)} %collective-permute-done.21.refs_2_), channel_id=1, source_target_pairs={{0,8},{8,0},{16,24},{24,16},{1,9},{9,1},{17,25},{25,17},{2,10},{10... | collective-permute-start | bytes 466952 | tf_op jit(solution)/shard_map/ppermute | solution.py:660
  82.9 1.6 %collective-permute-start.26 = (bf16[608,128]{1,0:T(8,128)(2,1)S(1)}, bf16[608,128]{1,0:T(8,128)(2,1)S(1)}, u32[]{:S(2)}, u32[]{:S(2)}) collective-permute-start(bf16[608,128]{1,0:T(8,128)(2,1)S(1)} %collective-permute-done.22.refs_3_), channel_id=1, source_target_pairs={{0,8},{8,0},{16,24},{24,16},{1,9},{9,1},{17,25},{25,17},{2,10},{10... | collective-permute-start | bytes 466952 | tf_op jit(solution)/shard_map/ppermute | solution.py:660

commit v3 on v2

--- a/solution.py
+++ b/solution.py
@@ -1,3 +1,5 @@
+import functools
+
 import jax
 import jax.numpy as jnp
 from jax import lax
@@ -298,10 +300,15 @@
     return scale * (scaled - jnp.mean(scaled, axis=-1, keepdims=True) - unit * inner)
 
 
-def block_inside(first_row, rows, cols):
-    row = first_row + lax.broadcasted_iota(jnp.int32, (4, 64, D), 0)
-    col = lax.broadcasted_iota(jnp.int32, (4, 64, D), 1)
-    return ((row < rows) & (col < cols)).reshape(256, D)
+def inside_mask(place, shape, image, row):
+    at = [lax.broadcasted_iota(jnp.int32, shape, d) for d in range(len(shape) - 1)]
+    first = image(at) == 0
+    rows, cols = (jnp.where(first, place[n], place[n + 1]) for n in (4, 6))
+    return ((row(at) < rows) & (at[-1] < cols)).reshape(-1, D)
+
+
+def image_mask(place):
+    return inside_mask(place, (2, 16, 64, D), lambda at: at[0], lambda at: at[1])
 
 
 def halves(shape):
@@ -327,16 +334,17 @@
 ):
     me = place[0]
     for k, chunk in enumerate((own, near1, near2, near3)):
-        block = me ^ k
         for i in range(2):
             raw = own[2 * me + i] if k == 0 else chunk[i]
-            x_out[pl.ds(block * 4, 4), i] = raw
-            unit, _ = norm_parts(raw.astype(jnp.float32).reshape(256, D))
-            normed = (unit * gains[pl.ds(0, 1), :]).astype(jnp.bfloat16)
-            normed_out[pl.ds(block * 4, 4), i] = normed.reshape(4, 64, D)
-            inside = block_inside(block * 4, place[4 + i], place[6 + i])
-            start = pl.multiple_of(i * 1024 + block * 256, 256)
-            masked[pl.ds(start, 256), :] = jnp.where(inside, normed.astype(jnp.float32), 0.0)
+            x_out[pl.ds(pl.multiple_of(i * 1024 + (me ^ k) * 256, 256), 256), :] = raw.reshape(256, D)
+    picture = x_out[...].astype(jnp.float32)
+    unit, _ = norm_parts(picture)
+    normed = (unit * gains[pl.ds(0, 1), :]).astype(jnp.bfloat16)
+    normed_out[...] = normed
+    inside = image_mask(place)
+    masked[...] = jnp.where(inside, normed.astype(jnp.float32), 0.0)
+    query = mm(normed, wq[...]).astype(jnp.bfloat16)
+    q_out[...] = query
     for i in range(2):
         for a in range(4):
             for u in range(4):
@@ -350,25 +358,23 @@
     unit, _ = norm_parts(pooled)
     pairs = mm((unit * gains[pl.ds(1, 1), :]).astype(jnp.bfloat16), wkv[...]).astype(jnp.bfloat16)
     kv_out[...] = pairs
-    lane = lax.broadcasted_iota(jnp.int32, (1, D), 1) % 64
+    lane = lax.broadcasted_iota(jnp.int32, (1024, D), 1) % 64
+    scores, values = [], []
     for i in range(2):
-        rows, cols = place[4 + i], place[6 + i]
-        live = ((lane // 16) * 4 < rows) & ((lane % 16) * 4 < cols)
+        live = ((lane // 16) * 4 < place[4 + i]) & ((lane % 16) * 4 < place[6 + i])
         keys = block_pair(pairs[i * 64 : i * 64 + 64, :D].astype(jnp.float32)).astype(jnp.bfloat16)
-        values = block_pair(pairs[i * 64 : i * 64 + 64, D:].astype(jnp.float32)).astype(jnp.bfloat16)
-        for b in range(4):
-            part = pl.ds(b * 4, 4)
-            query = mm(normed_out[part, i].reshape(256, D), wq[...]).astype(jnp.bfloat16)
-            q_out[part, i] = query.reshape(4, 64, D)
-            scores = jnp.where(live, mm_nt(query, keys) * SCORE_SCALE, NEG)
-            weights = jnp.exp(scores - half_reduce(jnp.max, scores, -jnp.inf))
-            probs = weights / half_reduce(jnp.sum, weights, 0.0)
-            prob_out[part, i] = probs.reshape(4, 64, D)
-            mixed = mm(probs.astype(jnp.bfloat16), values)
-            mixed = jnp.where(block_inside(b * 4, rows, cols), mixed, 0.0).astype(jnp.bfloat16)
-            att_out[part, i] = mixed.reshape(4, 64, D)
-            middle = x_out[part, i].astype(jnp.float32).reshape(256, D) + mm(mixed, wout[...])
-            mid_out[part, i] = middle.reshape(4, 64, D)
+        values.append(block_pair(pairs[i * 64 : i * 64 + 64, D:].astype(jnp.float32)).astype(jnp.bfloat16))
+        here = mm_nt(query[i * 1024 : (i + 1) * 1024], keys)
+        scores.append(jnp.where(live, here * SCORE_SCALE, NEG))
+    scores = jnp.concatenate(scores, axis=0)
+    weights = jnp.exp(scores - half_reduce(jnp.max, scores, -jnp.inf))
+    probs = weights / half_reduce(jnp.sum, weights, 0.0)
+    prob_out[...] = probs
+    low = probs.astype(jnp.bfloat16)
+    mixed = jnp.concatenate([mm(low[i * 1024 : (i + 1) * 1024], values[i]) for i in range(2)], axis=0)
+    mixed = jnp.where(inside, mixed, 0.0).astype(jnp.bfloat16)
+    att_out[...] = mixed
+    mid_out[...] = picture + mm(mixed, wout[...])
 
 
 def gelu_parts(x):
@@ -380,49 +386,53 @@
 def feed_kernel(
     place, mid, cot, cot1, cot2, cot3, gains, wfc1, taps, wfc2,
     bo0, bo1, bo2, bo3, mg_out, send_out, keep_out,
-    cj, br, br_t, mask, even, odd, mix, pairs, pairs_t, cg, act, acc, back, stage,
+    cj, br, br_t, mask, even, odd, mix, pairs, pairs_t, cg, act, acc, back, stage, result,
 ):
     me = place[0]
-    edge = jnp.zeros((128, 3 * D), jnp.bfloat16)
-    even[pl.ds(1024, 128), :] = edge
-    odd[pl.ds(0, 128), :] = edge
-    col = lax.broadcasted_iota(jnp.int32, (256, D), 0) % 64
+    edge = jnp.zeros((64, 3 * D), jnp.bfloat16)
+    for i in range(2):
+        even[pl.ds(i * 576 + 512, 64), :] = edge
+        odd[pl.ds(i * 576, 64), :] = edge
+    col = lax.broadcasted_iota(jnp.int32, (2048, D), 0) % 64
     for k, chunk in enumerate((cot, cot1, cot2, cot3)):
-        block = me ^ k
         for i in range(2):
             raw = cot[2 * me + i] if k == 0 else chunk[i]
-            inside = block_inside(block * 4, place[4 + i], place[6 + i]).reshape(4, 64, D)
             for r in range(4):
-                at = pl.ds(pl.multiple_of((r % 2) * 1024 + block * 256 + (r // 2) * 128 + i * 64, 64), 64)
-                cj[at, :] = raw[r]
-                mask[at, :] = jnp.where(inside[r], 1.0, 0.0)
+                at = (r % 2) * 1024 + i * 512 + (me ^ k) * 128 + (r // 2) * 64
+                cj[pl.ds(pl.multiple_of(at, 64), 64), :] = raw[r]
+    inside = inside_mask(place, (2, 2, 8, 64, D), lambda at: at[1], lambda at: 2 * at[2] + at[0])
+    mask[...] = jnp.where(inside, 1.0, 0.0)
     fc1_wide = wfc1[...].astype(jnp.float32)
     for k in range(4):
         for s in range(3):
             mix[k, pl.ds(s * D, D), :] = (fc1_wide * taps[pl.ds(3 * k + s, 1), :]).astype(jnp.bfloat16)
-    for e, side in enumerate((even, odd)):
-        for j in range(0, 8, 2):
-            part = pl.ds(e * 1024 + j * 128, 256)
-            inside = mask[part, :]
-            branch = cj[part, :].astype(jnp.float32) * inside
-            br[part, :] = branch.astype(jnp.bfloat16)
-            br_t[:, part] = branch.T.astype(jnp.bfloat16)
-            source = jnp.concatenate([mid[pl.ds((2 * (j + h) + e) * 128, 128), :] for h in range(2)], axis=0)
-            unit, _ = norm_parts(source)
-            normed = ((unit * gains[pl.ds(2, 1), :]).astype(jnp.bfloat16)).astype(jnp.float32) * inside
-            before = jnp.where(col == 0, 0.0, pltpu.roll(normed, 1, 0))
-            after = jnp.where(col == 63, 0.0, pltpu.roll(normed, 255, 0))
-            for s, value in enumerate((before, normed, after)):
-                side[pl.ds((j + e) * 128, 256), pl.ds(s * D, D)] = value.astype(jnp.bfloat16)
-    for k in range(4):
-        for j in range(0, 8, 2):
+    for c in range(8):
+        stage[pl.ds(c * (PACK1 // 8) + 2 * D, 16), :] = jnp.zeros((16, D), jnp.float32)
+    branch = cj[...].astype(jnp.float32) * mask[...]
+    br[...] = branch.astype(jnp.bfloat16)
+    br_t[...] = branch.T.astype(jnp.bfloat16)
+
+    def by_parity():
+        return jnp.concatenate([mid[:, :, e].reshape(1024, D) for e in range(2)], axis=0)
+
+    unit, _ = norm_parts(by_parity())
+    normed = ((unit * gains[pl.ds(2, 1), :]).astype(jnp.bfloat16)).astype(jnp.float32) * mask[...]
+    before = jnp.where(col == 0, 0.0, pltpu.roll(normed, 1, 0))
+    after = jnp.where(col == 63, 0.0, pltpu.roll(normed, 2047, 0))
+    for s, value in enumerate((before, normed, after)):
+        value = value.astype(jnp.bfloat16)
+        for e, side in enumerate((even, odd)):
+            for i in range(2):
+                at = e * 1024 + i * 512
+                side[pl.ds(i * 576 + e * 64, 512), pl.ds(s * D, D)] = value[at : at + 512]
+    for i in range(2):
+        ev, ev_next = (even[pl.ds(i * 576 + h * 64, 512), :].astype(jnp.float32) for h in (0, 1))
+        od_last, od = (odd[pl.ds(i * 576 + h * 64, 512), :].astype(jnp.float32) for h in (0, 1))
+        for k, value in enumerate((od_last - od, ev + od, od - ev, ev - ev_next)):
+            here = pl.ds(i * 512, 512)
+            pairs[k, here, :] = value.astype(jnp.bfloat16)
             for s in range(3):
-                lanes = pl.ds(s * D, D)
-                ev, ev_next = (even[pl.ds((j + h) * 128, 256), lanes].astype(jnp.float32) for h in (0, 1))
-                od_last, od = (odd[pl.ds((j + h) * 128, 256), lanes].astype(jnp.float32) for h in (0, 1))
-                value = (od_last - od, ev + od, od - ev, ev - ev_next)[k]
-                pairs[k, pl.ds(j * 128, 256), lanes] = value.astype(jnp.bfloat16)
-                pairs_t[k, lanes, pl.ds(j * 128, 256)] = value.T.astype(jnp.bfloat16)
+                pairs_t[k, pl.ds(s * D, D), here] = value[:, s * D : (s + 1) * D].T.astype(jnp.bfloat16)
     for f in range(FF // FC):
         chan = pl.ds(f * FC, FC)
         for b in range(1024 // TB):
@@ -442,7 +452,9 @@
             for k, value in enumerate((grads[0], grads[0] + grads[1], grads[0] - grads[1], grads[1])):
                 cg[k, part, chan] = value.astype(jnp.bfloat16)
         fc2_grad = mm(br_t[...], act[...])
-        stage[pl.ds(FF + f * FC, FC), :] = fc2_grad.T
+        fc2_grad = fc2_grad.T
+        for j in range(FC // D):
+            stage[pl.ds((f * (FC // D) + j) * (PACK1 // 8) + D, D), :] = fc2_grad[j * D : (j + 1) * D]
         fc1_grad = jnp.zeros((D, FC), jnp.float32)
         tap_grads = []
         for k in range(4):
@@ -458,44 +470,41 @@
             half_gap = 0.5 * (tap_grads[3 + s] - tap_grads[6 + s])
             for p, value in enumerate((tap_grads[s] + half_sum, half_gap, half_sum + tap_grads[9 + s])):
                 for j in range(FC // D):
-                    at = 2 * FF + (3 * p + s) * 8 + f * (FC // D) + j
+                    at = (f * (FC // D) + j) * (PACK1 // 8) + 2 * D + 3 * p + s
                     stage[pl.ds(at, 1), :] = value[:, j * D : (j + 1) * D]
         for j in range(FC // D):
-            stage[pl.ds((f * (FC // D) + j) * D, D), :] = fc1_grad[:, j * D : (j + 1) * D]
-    back[0, pl.ds(1024, 128), :] = jnp.zeros((128, 3 * D), jnp.float32)
-    back[3, pl.ds(0, 128), :] = jnp.zeros((128, 3 * D), jnp.float32)
+            stage[pl.ds((f * (FC // D) + j) * (PACK1 // 8), D), :] = fc1_grad[:, j * D : (j + 1) * D]
+    for i in range(2):
+        back[0, pl.ds(i * 576 + 512, 64), :] = jnp.zeros((64, 3 * D), jnp.float32)
+        back[3, pl.ds(i * 576, 64), :] = jnp.zeros((64, 3 * D), jnp.float32)
     for k in range(4):
-        for b in range(1024 // TB):
-            here = pl.ds(b * TB + (128 if k == 3 else 0), TB)
-            back[k, here, :] = mm_nt(cg[k, pl.ds(b * TB, TB), :], mix[k])
-    gain_grad = jnp.zeros((1, D), jnp.float32)
+        spread = mm_nt(cg[k], mix[k])
+        for i in range(2):
+            back[k, pl.ds(i * 576 + (64 if k == 3 else 0), 512), :] = spread[i * 512 : (i + 1) * 512]
+    spread = []
+    for e in range(2):
+        for i in range(2):
+            here, later = pl.ds(i * 576, 512), pl.ds(i * 576 + 64, 512)
+            if e == 0:
+                spread.append(back[1, here, :] - back[2, here, :] + (back[3, here, :] - back[3, later, :]))
+            else:
+                spread.append(back[1, here, :] + back[2, here, :] + (back[0, later, :] - back[0, here, :]))
+    spread = jnp.concatenate(spread, axis=0)
+    after = jnp.where(col == 63, 0.0, pltpu.roll(spread[:, :D], 2047, 0))
+    before = jnp.where(col == 0, 0.0, pltpu.roll(spread[:, 2 * D :], 1, 0))
+    normed_grad = (spread[:, D : 2 * D] + before + after) * mask[...]
+    middle = by_parity()
+    unit, scale = norm_parts(middle)
+    gain_grad = jnp.sum(normed_grad * unit, axis=0, keepdims=True)
+    total = cj[...].astype(jnp.float32) + norm_back(normed_grad, gains[pl.ds(2, 1), :], unit, scale)
+    final = (middle + acc[...] * mask[...]).astype(jnp.bfloat16)
+    for e in range(2):
+        mg_out[:, :, e] = total[e * 1024 : (e + 1) * 1024].reshape(2, 8, 64, D)
+        result[:, :, e] = final[e * 1024 : (e + 1) * 1024].reshape(2, 8, 64, D)
     for k, bo in enumerate((bo0, bo1, bo2, bo3)):
-        block = me ^ k
-        for e in range(2):
-            start = pl.multiple_of(block * 256, 256)
-            here, later = pl.ds(start, 256), pl.ds(start + 128, 256)
-            part = pl.ds(pl.multiple_of(e * 1024 + block * 256, 256), 256)
-            rows = [pl.ds(pl.multiple_of(block * 512 + (2 * h + e) * 128, 128), 128) for h in range(2)]
-            inside = mask[part, :]
-            middle = jnp.concatenate([mid[row, :] for row in rows], axis=0)
-            result = (middle + acc[part, :] * inside).astype(jnp.bfloat16).reshape(2, 2, 64, D)
-            for i in range(2):
-                for h in range(2):
-                    bo[i, 2 * h + e] = result[h, i]
-            if e == 0:
-                spread = back[1, here, :] - back[2, here, :] + back[3, here, :] - back[3, later, :]
-            else:
-                spread = back[1, here, :] + back[2, here, :] - back[0, here, :] + back[0, later, :]
-            after = jnp.where(col == 63, 0.0, pltpu.roll(spread[:, :D], 255, 0))
-            before = jnp.where(col == 0, 0.0, pltpu.roll(spread[:, 2 * D :], 1, 0))
-            normed_grad = (spread[:, D : 2 * D] + before + after) * inside
-            unit, scale = norm_parts(middle)
-            gain_grad += jnp.sum(normed_grad * unit, axis=0, keepdims=True)
-            total = cj[part, :].astype(jnp.float32) + norm_back(normed_grad, gains[pl.ds(2, 1), :], unit, scale)
-            for h in range(2):
-                mg_out[rows[h], :] = total[h * 128 : (h + 1) * 128]
-    stage[pl.ds(2 * FF + 72, 1), :] = gain_grad
-    stage[pl.ds(2 * FF + 73, 55), :] = jnp.zeros((55, D), jnp.float32)
+        for i in range(2):
+            bo[i] = result[i, pl.ds((me ^ k) * 2, 2)].reshape(4, 64, D)
+    stage[pl.ds(2 * D + 9, 1), :] = gain_grad
     split_pack(place, stage, send_out, keep_out)
 
 
@@ -509,36 +518,35 @@
 
 
 def back_kernel(
-    place, x, normed, query, prob, att, mgrad, pat, pooled, kv,
+    place, normed, query, prob, att, mgrad, pat, pooled, kv,
     gains, wq, wsr, wkv, wout,
-    ig0, ig1, ig2, ig3, send_out, keep_out,
-    stage, probs_low, att_grad, score_grad, query_grad, unfold,
+    query_grad, pooled_out, send_out, keep_out,
+    stage,
 ):
-    me = place[0]
-    zero = jnp.zeros((D, D), jnp.float32)
-    out_grad = zero
+    inside = image_mask(place)
+    low = mgrad[...].astype(jnp.bfloat16)
+    out_grad = mm_tn(att[...], low)
+    mixed = jnp.where(inside, mm_nt(low, wout[...]), 0.0).astype(jnp.bfloat16)
+    keys, values = (
+        [
+            block_pair(kv[pl.ds(i * 64, 64), pl.ds(n * D, D)].astype(jnp.float32)).astype(jnp.bfloat16)
+            for i in range(2)
+        ]
+        for n in range(2)
+    )
+    parts = [slice(i * 1024, (i + 1) * 1024) for i in range(2)]
+    weights = prob[...]
+    back = jnp.concatenate([mm_nt(mixed[parts[i]], values[i]) for i in range(2)], axis=0)
+    back = weights * (back - half_reduce(jnp.sum, weights * back, 0.0)) * SCORE_SCALE
+    back = back.astype(jnp.bfloat16)
+    grads = jnp.concatenate([mm(back[parts[i]], keys[i]) for i in range(2)], axis=0).astype(jnp.bfloat16)
+    query_grad[...] = grads
+    weights = weights.astype(jnp.bfloat16)
+    left = halves((64, D))
     key_rows = []
     for i in range(2):
-        rows, cols = place[4 + i], place[6 + i]
-        keys = block_pair(kv[pl.ds(i * 64, 64), pl.ds(0, D)].astype(jnp.float32)).astype(jnp.bfloat16)
-        values = block_pair(kv[pl.ds(i * 64, 64), pl.ds(D, D)].astype(jnp.float32)).astype(jnp.bfloat16)
-        for b in range(4):
-            part = pl.ds(b * 4, 4)
-            at = pl.ds(b * 256, 256)
-            low = mgrad[part, i].reshape(256, D).astype(jnp.bfloat16)
-            out_grad += mm_tn(att[part, i].reshape(256, D), low)
-            mixed = jnp.where(block_inside(b * 4, rows, cols), mm_nt(low, wout[...]), 0.0).astype(jnp.bfloat16)
-            att_grad[at, :] = mixed
-            weights = prob[part, i].reshape(256, D)
-            probs_low[at, :] = weights.astype(jnp.bfloat16)
-            back = mm_nt(mixed, values)
-            back = weights * (back - half_reduce(jnp.sum, weights * back, 0.0)) * SCORE_SCALE
-            back = back.astype(jnp.bfloat16)
-            score_grad[at, :] = back
-            query_grad[pl.ds(i * 1024 + b * 256, 256), :] = mm(back, keys).astype(jnp.bfloat16)
-        value_full = mm_tn(probs_low[...], att_grad[...])
-        key_full = mm_tn(score_grad[...], query[:, i].reshape(1024, D))
-        left = halves((64, D))
+        value_full = mm_tn(weights[parts[i]], mixed[parts[i]])
+        key_full = mm_tn(back[parts[i]], query[pl.ds(i * 1024, 1024), :])
         key_rows.append(
             jnp.concatenate(
                 [
@@ -555,8 +563,39 @@
     reduced_grad = mm_nt(pair, wkv[...])
     srg_grad = jnp.sum(reduced_grad * unit, axis=0, keepdims=True)
     pooled_low = norm_back(reduced_grad, gains[pl.ds(1, 1), :], unit, scale).astype(jnp.bfloat16)
-    stage[pl.ds(0, 2048), :] = mm_tn(pat[...], pooled_low)
-    patch_grad = mm_nt(pooled_low, wsr[...])
+    pooled_out[...] = pooled_low
+    sr_grad = mm_tn(pat[...], pooled_low)
+    each = PACK2 // 8
+    for c in range(8):
+        stage[pl.ds(c * each, 256), :] = sr_grad[c * 256 : (c + 1) * 256]
+    for c in range(8):
+        side, row = c // 4, (c % 4) * 32
+        stage[pl.ds(c * each + 256, 32), :] = kv_grad[row : row + 32, side * D : (side + 1) * D]
+        stage[pl.ds(c * each + 304, 16), :] = out_grad[c * 16 : (c + 1) * 16]
+        stage[pl.ds(c * each + 320, 16), :] = jnp.zeros((16, D), jnp.float32)
+    q_grad = mm_tn(normed[...], grads)
+    weighted = q_grad * wq[...].astype(jnp.float32)
+    for c in range(16):
+        at = slice(c * D, (c + 1) * D)
+        weighted += sr_grad[at] * wsr[pl.ds(c * D, D), :].astype(jnp.float32)
+    high = weighted.astype(jnp.bfloat16)
+    low = (weighted - high.astype(jnp.float32)).astype(jnp.bfloat16)
+    ones = jnp.ones((16, D), jnp.bfloat16)
+    gain_grad = (mm_nt(ones, high) + mm_nt(ones, low))[0:1] / gains[pl.ds(0, 1), :]
+    for c in range(8):
+        stage[pl.ds(c * each + 288, 16), :] = q_grad[c * 16 : (c + 1) * 16]
+    stage[pl.ds(320, 1), :] = gain_grad
+    stage[pl.ds(321, 1), :] = srg_grad
+    split_pack(place, stage, send_out, keep_out)
+
+
+def input_kernel(
+    place, x, query_grad, pooled_low, mgrad, gains, wq, wsr,
+    ig0, ig1, ig2, ig3,
+    unfold, result,
+):
+    me = place[0]
+    patch_grad = mm_nt(pooled_low[...], wsr[...])
     for i in range(2):
         for a in range(4):
             for u in range(4):
@@ -564,29 +603,13 @@
                     unfold[pl.ds(i * 1024 + (4 * a + u) * 64 + t, 16, stride=4), :] = patch_grad[
                         i * 64 + a * 16 : i * 64 + a * 16 + 16, (u * 4 + t) * D : (u * 4 + t + 1) * D
                     ]
-    stage[pl.ds(2048, D), :] = kv_grad[:, :D]
-    stage[pl.ds(2176, D), :] = kv_grad[:, D:]
-    stage[pl.ds(2432, D), :] = out_grad
-    q_grad = zero
-    gain_grad = jnp.zeros((1, D), jnp.float32)
+    grad = mm_nt(query_grad[...], wq[...]) + jnp.where(image_mask(place), unfold[...], 0.0)
+    unit, scale = norm_parts(x[...].astype(jnp.float32))
+    total = mgrad[...] + norm_back(grad, gains[pl.ds(0, 1), :], unit, scale)
+    result[...] = total.astype(jnp.bfloat16).reshape(2, 16, 64, D)
     for k, ig in enumerate((ig0, ig1, ig2, ig3)):
-        block = me ^ k
-        part = pl.ds(block * 4, 4)
         for i in range(2):
-            at = pl.ds(pl.multiple_of(i * 1024 + block * 256, 256), 256)
-            inside = block_inside(block * 4, place[4 + i], place[6 + i])
-            back = query_grad[at, :]
-            q_grad += mm_tn(normed[part, i].reshape(256, D), back)
-            grad = mm_nt(back, wq[...]) + jnp.where(inside, unfold[at, :], 0.0)
-            unit, scale = norm_parts(x[part, i].astype(jnp.float32).reshape(256, D))
-            gain_grad += jnp.sum(grad * unit, axis=0, keepdims=True)
-            total = mgrad[part, i].reshape(256, D) + norm_back(grad, gains[pl.ds(0, 1), :], unit, scale)
-            ig[i] = total.astype(jnp.bfloat16).reshape(4, 64, D)
-    stage[pl.ds(2304, D), :] = q_grad
-    stage[pl.ds(2560, 1), :] = gain_grad
-    stage[pl.ds(2561, 1), :] = srg_grad
-    stage[pl.ds(2562, 126), :] = jnp.zeros((126, D), jnp.float32)
-    split_pack(place, stage, send_out, keep_out)
+            ig[i] = result[i, pl.ds((me ^ k) * 4, 4)]
 
 
 def call(kernel, scalars, arrays, outs, scratch, flops=0, name=None, vmem=24):
@@ -604,7 +627,8 @@
 
 
 BF, F32 = jnp.bfloat16, jnp.float32
-JOINT = (16, 2, 64, D)
+FLAT = (2048, D)
+SPLIT = (2, 8, 2, 64, D)
 CHUNK = (2, 4, 64, D)
 PACK1, PACK2 = 2176, 2688
 FC, TB = 512, 1024
@@ -617,7 +641,7 @@
         (place,),
         (*chunks, gains, wq, wsr, wkv, wout),
         [
-            (JOINT, BF), (JOINT, BF), (JOINT, BF), (JOINT, F32), (JOINT, BF), (JOINT, F32),
+            (FLAT, BF), (FLAT, BF), (FLAT, BF), (FLAT, F32), (FLAT, BF), (FLAT, F32),
             ((128, 2048), BF), ((128, D), F32), ((128, 2 * D), BF),
         ],
         [VMEM((2048, D), F32)],
@@ -630,29 +654,37 @@
         feed_kernel,
         (place,),
         (middle, *chunks, gains, wfc1, taps, wfc2),
-        [(CHUNK, BF)] * 4 + [((2048, D), F32), ((PACK1 // 2, D), BF), ((PACK1 // 2, D), BF)],
+        [(CHUNK, BF)] * 4 + [(SPLIT, F32), ((PACK1 // 2, D), BF), ((PACK1 // 2, D), BF)],
         [
             VMEM((2048, D), BF), VMEM((2048, D), BF), VMEM((D, 2048), BF), VMEM((2048, D), F32),
             VMEM((1152, 3 * D), BF), VMEM((1152, 3 * D), BF), VMEM((4, 3 * D, FF), BF),
             VMEM((4, 1024, 3 * D), BF), VMEM((4, 3 * D, 1024), BF), VMEM((4, 1024, FF), BF), VMEM((2048, FC), BF),
-            VMEM((2048, D), F32), VMEM((4, 1152, 3 * D), F32), VMEM((PACK1, D), F32),
+            VMEM((2048, D), F32), VMEM((4, 1152, 3 * D), F32), VMEM((PACK1, D), F32), VMEM(SPLIT, BF),
         ],
         flops=16 * 10**9, name="feed", vmem=44,
     )
 
 
 def back(place, kept, mgrad, gains, wq, wsr, wkv, wout):
-    x, normed, query, prob, att, _, pat, pooled, kv = kept
+    _, normed, query, prob, att, _, pat, pooled, kv = kept
     return call(
         back_kernel,
         (place,),
-        (x, normed, query, prob, att, mgrad, pat, pooled, kv, gains, wq, wsr, wkv, wout),
-        [(CHUNK, BF)] * 4 + [((PACK2 // 2, D), BF), ((PACK2 // 2, D), BF)],
-        [
-            VMEM((PACK2, D), F32), VMEM((1024, D), BF), VMEM((1024, D), BF), VMEM((1024, D), BF),
-            VMEM((2048, D), BF), VMEM((2048, D), F32),
-        ],
+        (normed, query, prob, att, mgrad, pat, pooled, kv, gains, wq, wsr, wkv, wout),
+        [(FLAT, BF), ((128, D), BF), ((PACK2 // 2, D), BF), ((PACK2 // 2, D), BF)],
+        [VMEM((PACK2, D), F32)],
         flops=2 * 10**9, name="back",
+    )
+
+
+def input_gradient(place, x, query_grad, pooled_low, mgrad, gains, wq, wsr):
+    return call(
+        input_kernel,
+        (place,),
+        (x, query_grad, pooled_low, mgrad, gains, wq, wsr),
+        [(CHUNK, BF)] * 4,
+        [VMEM((2048, D), F32), VMEM((2, 16, 64, D), BF)],
+        flops=10**9, name="input_gradient",
     )
 
 
@@ -678,62 +710,79 @@
     ]
 
 
-def first_sum(parts):
-    got = {k: over_four(parts[k], k, 0) for k in (3, 2, 1)}
-    return plus(parts[0], got[1], got[2], got[3])
-
-
-def second_sum(mine, got):
-    got = [g.astype(F32) for g in got]
-    return ((mine.astype(F32) + got[0]) + (got[1] + got[2])).astype(BF)
-
-
-def to_four(value, phase):
-    got = {k: over_four(value, k, phase) for k in (3, 2, 1)}
-    return got[1], got[2], got[3]
-
-
-def finish_kernel(place, *refs):
-    pieces, (q, sr, kv, out, fc1, fc2, dw, ln1, ln2, srg, stage1, stage2, sems) = refs[:8], refs[8:]
-    rows1, rows2 = PACK1 // 8, PACK2 // 8
-    for j, piece in enumerate(pieces):
+def to_four(values, phase):
+    return [over_four(values[k], k, phase) for k in (1, 2, 3)]
+
+
+def finish_kernel(half, place, *refs):
+    pieces, refs = refs[: 4 * (half + 1)], refs[4 * (half + 1) :]
+    if half:
+        refs = refs[6:]
+    (q, sr, kv, out, fc1, fc2), refs = refs[:6], refs[6:]
+    stage, small_dw, small_ln1, small_ln2, small_srg, sems = refs[-6:]
+    copies = []
+
+    def move(source, target):
+        copies.append(pltpu.make_async_copy(source, target, sems.at[len(copies)]))
+        copies[-1].start()
+
+    def chunk_of(j):
         core, first = (place[1], place[2]) if j < 4 else (1 - place[1], place[3])
-        spot = core * 4 + (first ^ (j % 4))
-        stage1[pl.ds(pl.multiple_of(spot * rows1, 16), rows1), :] = piece[pl.ds(0, rows1), :].astype(F32)
-        stage2[pl.ds(pl.multiple_of(spot * rows2, 16), rows2), :] = piece[pl.ds(rows1, rows2), :].astype(F32)
-    moves = [
-        (stage2.at[pl.ds(0, 2048)], sr),
-        (stage1.at[pl.ds(FF, FF)], fc2),
-        *((stage1.at[pl.ds(j * D, D)], fc1.at[:, pl.ds(j * D, D)]) for j in range(8)),
-        *((stage2.at[pl.ds(2048 + j * D, D)], kv.at[:, pl.ds(j * D, D)]) for j in range(2)),
-        (stage2.at[pl.ds(2304, D)], q),
-        (stage2.at[pl.ds(2432, D)], out),
-    ]
-    copies = [pltpu.make_async_copy(a, b, sems.at[n]) for n, (a, b) in enumerate(moves)]
-    for copy in copies:
-        copy.start()
-    for tap in range(9):
-        for j in range(8):
-            dw[tap // 3, pl.ds(tap % 3, 1), pl.ds(j * D, D)] = stage1[pl.ds(2 * FF + tap * 8 + j, 1), :]
-    ln2[...] = stage1[pl.ds(2 * FF + 72, 1), :].reshape(D)
-    ln1[...] = stage2[pl.ds(2560, 1), :].reshape(D)
-    srg[...] = stage2[pl.ds(2561, 1), :].reshape(D)
+        return core * 4 + (first ^ (j % 4))
+
+    for k in range(4):
+        c = chunk_of(4 * half + k)
+        stage[k] = pieces[4 * half + k][...].astype(F32)
+        chan = pl.ds(pl.multiple_of(c * D, D), D)
+        move(stage.at[k, pl.ds(0, D)], fc1.at[:, chan])
+        move(stage.at[k, pl.ds(D, D)], fc2.at[chan])
+        move(stage.at[k, pl.ds(272, 256)], sr.at[pl.ds(pl.multiple_of(c * 256, 256), 256)])
+        row = pl.ds(pl.multiple_of((c % 4) * 32, 32), 32)
+        move(stage.at[k, pl.ds(528, 32)], kv.at[row, pl.ds(pl.multiple_of((c // 4) * D, D), D)])
+        row = pl.ds(pl.multiple_of(c * 16, 16), 16)
+        move(stage.at[k, pl.ds(560, 16)], q.at[row])
+        move(stage.at[k, pl.ds(576, 16)], out.at[row])
+    if half:
+        sums = [jnp.zeros((1, D), F32)] * 3
+        for j, piece in enumerate(pieces):
+            chan = pl.ds(pl.multiple_of(chunk_of(j) * D, D), D)
+            small = piece[pl.ds(256, 16), :].astype(F32)
+            for tap in range(9):
+                small_dw[tap // 3, pl.ds(tap % 3, 1), chan] = small[tap : tap + 1]
+            last = piece[pl.ds(592, 16), :].astype(F32)
+            rows = (last[0:1], small[9:10], last[1:2])
+            sums = [total + row for total, row in zip(sums, rows)]
+        move(small_dw, refs[0])
+        for ref, small, total in zip(refs[1:4], (small_ln1, small_ln2, small_srg), sums):
+            small[...] = total.reshape(D)
+            move(small, ref)
     for copy in copies:
         copy.wait()
 
 
-def finish(place, pieces):
+def finish(place, pieces, earlier=()):
     far, near = pl.BlockSpec(memory_space=pl.ANY), pl.BlockSpec(memory_space=VMEM)
-    shapes = [(D, D), (2048, D), (D, 2 * D), (D, D), (D, FF), (FF, D), (3, 3, FF), (D,), (D,), (D,)]
+    half = 1 if earlier else 0
+    shapes = [((D, D), F32), ((2048, D), F32), ((D, 2 * D), F32), ((D, D), F32), ((D, FF), F32), ((FF, D), F32)]
+    specs, n = [far] * 6, len(shapes)
+    if half:
+        shapes += [((3, 3, FF), F32), ((D,), F32), ((D,), F32), ((D,), F32)]
+        specs += [far] * 4
+    before = 1 + len(pieces)
     return pl.pallas_call(
-        finish_kernel,
-        out_shape=[jax.ShapeDtypeStruct(shape, F32) for shape in shapes],
-        in_specs=[pl.BlockSpec(memory_space=pltpu.SMEM)] + [near] * 8,
-        out_specs=[far] * 6 + [near] * 4,
-        scratch_shapes=[VMEM((PACK1, D), F32), VMEM((PACK2, D), F32), pltpu.SemaphoreType.DMA((14,))],
-        compiler_params=pltpu.CompilerParams(vmem_limit_bytes=12 * 2**20),
+        functools.partial(finish_kernel, half),
+        out_shape=[jax.ShapeDtypeStruct(*each) for each in shapes],
+        in_specs=[pl.BlockSpec(memory_space=pltpu.SMEM)] + [near] * (before - 1) + [far] * len(earlier),
+        out_specs=specs,
+        scratch_shapes=[
+            VMEM((4, 608, D), F32), VMEM((3, 3, FF), F32), VMEM((D,), F32), VMEM((D,), F32), VMEM((D,), F32),
+            pltpu.SemaphoreType.DMA((28,)),
+        ],
+        input_output_aliases={before + i: i for i in range(n)} if half else {},
+        compiler_params=pltpu.CompilerParams(vmem_limit_bytes=8 * 2**20),
+        cost_estimate=pl.CostEstimate(flops=0, bytes_accessed=4 * 2**20, transcendentals=0),
         name="finish",
-    )(place, *pieces)
+    )(place, *pieces, *earlier)
 
 
 def gather_kernel(place, part0, part1, part2, part3, out, sems):
@@ -779,7 +828,7 @@
 
     def returned(parts):
         near = {k: over_rows(parts[k], k) for k in (3, 2, 1)}
-        return parts[0], near[1], near[2], near[3]
+        return [parts[0], near[1], near[2], near[3]]
 
     gains = jnp.stack([ln1_gain, sr_gain, ln2_gain])
     row0, row1, row2 = dw_weight.astype(F32)
@@ -787,29 +836,34 @@
         [row0, 0.5 * (row0 + row1 + row2), 0.5 * (row0 - row1 + row2), row2, jnp.zeros((4, FF), F32)]
     )
     token_parts = spread(tokens)
-    cotangent, _ = lax.optimization_barrier((cotangent, token_parts[3]))
+    cotangent, _ = lax.optimization_barrier((cotangent, token_parts[1]))
     kept = attend(
         place, token_parts, gains, q_weight, sr_weight, kv_weight, out_weight
     )
     *block_parts, mgrad, send1, keep1 = feed(
-        place, kept[5].reshape(2048, D), spread(cotangent), gains, fc1_weight, taps, fc2_weight
-    )
-    *input_parts, send2, keep2 = back(
-        place, kept, mgrad.reshape(JOINT), gains, q_weight, sr_weight, kv_weight, out_weight
+        place, kept[5].reshape(SPLIT), spread(cotangent), gains, fc1_weight, taps, fc2_weight
+    )
+    mgrad = mgrad.reshape(FLAT)
+    query_grad, pooled_low, send2, keep2 = back(
+        place, kept, mgrad, gains, q_weight, sr_weight, kv_weight, out_weight
     )
     parts = plane_parts([(send1, keep1), (send2, keep2)])
-    parts, block_parts = lax.optimization_barrier((parts, returned(block_parts)))
-    mine = first_sum(parts)
-    got, block_out, input_parts = lax.optimization_barrier(
-        (to_four(mine, 1), gather_rows(place, block_parts, tokens.shape), returned(input_parts))
-    )
-    total = second_sum(mine, got)
-    got, input_grad = lax.optimization_barrier(
-        (to_four(total, 0), gather_rows(place, input_parts, tokens.shape))
-    )
-    pieces = [total, *got]
-    pieces += [over_rows(piece, 1) for piece in pieces]
-    q, sr, kv, out, fc1, fc2, dw, ln1_sum, ln2_sum, srg_sum = finish(place, pieces)
+    block = returned(block_parts)
+    parts, block[2] = lax.optimization_barrier((parts, block[2]))
+    inputs = input_gradient(place, kept[0], query_grad, pooled_low, mgrad, gains, q_weight, sr_weight)
+    mine, inputs = lax.optimization_barrier((plus(parts[0], *to_four(parts, 0)), list(inputs)))
+    inputs = returned(inputs)
+    got = [g.astype(F32) for g in to_four([mine] * 4, 1)]
+    got, block_out = lax.optimization_barrier((got, gather_rows(place, block, tokens.shape)))
+    got, block[3] = lax.optimization_barrier((got, block[3]))
+    total = ((mine.astype(F32) + got[0]) + (got[1] + got[2])).astype(BF)
+    got = to_four([total] * 4, 0)
+    got, inputs[2], inputs[3] = lax.optimization_barrier((got, inputs[2], inputs[3]))
+    got, input_grad = lax.optimization_barrier((got, gather_rows(place, inputs, tokens.shape)))
+    pieces = (total, *got)
+    others = tuple(over_rows(piece, 1) for piece in pieces)
+    half = finish(place, pieces)
+    q, sr, kv, out, fc1, fc2, dw, ln1_sum, ln2_sum, srg_sum = finish(place, pieces + others, half)
     return block_out, input_grad, ln1_sum, q, sr, srg_sum, kv, out, ln2_sum, fc1, dw, fc2
 
 

time: 87.7 us -> 82.2 us (0.937)
  Pallas kernels: 39 us -> 34.1 us
    ppermute x18, waiting for transfers between devices: 11.6 us -> 17.4 us  [over_rows(): return lax.ppermute(value, 'rows', [(i, i ^ k) for i in range(4)])]
    pallas_call x3 -> x4, Pallas kernels: 33.4 us -> 27.8 us  [call(): pl.pallas_call(kernel, out_shape=[jax.ShapeDtypeStruct(shape, kind) for s...]
    ppermute x9, waiting for transfers between devices: 8.68 us -> 3.14 us  [over_four(): return lax.ppermute(value, ('rows', 'batch'), pairs)]
    pallas_call x1 -> x2, Pallas kernels: 2.84 us -> 3.65 us  [finish(): pl.pallas_call(functools.partial(finish_kernel, half), out_shape=[jax.Sha...]
  transfers between devices with their start and end apart: 27 -> 27, of which waited for: 13 -> 10; matrix products, arithmetic and copies ran while one was open for 1% -> 1% of each run, Pallas kernels for 17% -> 16%
where the time goes in v3:
time: 82.2 us; the launch traced here: 82 us
  Pallas kernels  34.1 us (41%)
  starting transfers between devices  24 us (29%)
  waiting for transfers between devices  20.5 us (25%)
  local copies, waits for them, and re-layouts  1.68 us (2%)
  between operations  1.24 us (2%)
    pallas_call x4, Pallas kernels, call(): pl.pallas_call(kernel, out_shape=[jax.ShapeDtypeStruct(shape, kind) for s...  27.8 us
    ppermute x18, waiting for transfers between devices, over_rows(): return lax.ppermute(value, 'rows', [(i, i ^ k) for i in range(4)])  17.4 us
    ppermute x18, starting transfers between devices, over_rows(): return lax.ppermute(value, 'rows', [(i, i ^ k) for i in range(4)])  12.4 us
    ppermute x9, starting transfers between devices, over_four(): return lax.ppermute(value, ('rows', 'batch'), pairs)  11.6 us
    pallas_call x2, Pallas kernels, finish(): pl.pallas_call(functools.partial(finish_kernel, half), out_shape=[jax.Sha...  3.65 us
    ppermute x9, waiting for transfers between devices, over_four(): return lax.ppermute(value, ('rows', 'batch'), pairs)  3.14 us
    pallas_call x2, Pallas kernels, gather_rows(): pl.pallas_call(gather_kernel, out_shape=jax.ShapeDtypeStruct(shape, BF),...  2.72 us
  transfers between devices with their start and end apart: 27, of which 10 were waited for; matrix products, arithmetic and copies ran while one was open for 1% of the time, Pallas kernels for 16%

profile of v3, /device:TPU:0, one launch (start us, length us, event | category | flops | bytes accessed | tf_op | source)
XLA Modules:
  0.0 82.0 jit_solution(18163095183160339212)
XLA Ops:
  0.7 1.1 %constant_dynamic-slice_fusion.3 = (bf16[2,4,64,128]{3,2,1,0:T(8,128)(2,1)S(1)}, bf16[2,4,64,128]{3,2,1,0:T(8,128)(2,1)S(1)}, bf16[2,4,64,128]{3,2,1,0:T(8,128)(2,1)S(1)}) fusion(bf16[8,4,64,128]{3,2,1,0:T(8,128)(2,1)} %own.1, s32[]{:T(128)S(6)} %select_n.28, s32[]{:T(128)S(6)} %select_n.27, s32[]{:T(128)S(6)} %select_n.26), kind=kLoop, calls=%fused_computation.17 | loop fusion | bytes 786444 | tf_op jit(solution)/shard_map/dynamic_slice | solution.py:825
  1.8 2.5 %collective-permute-start.2 = (bf16[2,4,64,128]{3,2,1,0:T(8,128)(2,1)S(1)}, bf16[2,4,64,128]{3,2,1,0:T(8,128)(2,1)S(1)}, u32[]{:S(2)}, u32[]{:S(2)}) collective-permute-start(bf16[2,4,64,128]{3,2,1,0:T(8,128)(2,1)S(1)} %get-tuple-element.149), channel_id=1, source_target_pairs={{0,24},{8,16},{16,8},{24,0},{1,25},{9,17},{17,9},{25,1},{2,26},{10... | collective-permute-start | bytes 393224 | tf_op jit(solution)/shard_map/ppermute | solution.py:692
  4.3 0.6 collective-permute-start.1
  5.1 1.2 %collective-permute-done.near1 = bf16[2,4,64,128]{3,2,1,0:T(8,128)(2,1)S(1)} collective-permute-done((bf16[2,4,64,128]{3,2,1,0:T(8,128)(2,1)S(1)}, bf16[2,4,64,128]{3,2,1,0:T(8,128)(2,1)S(1)}, u32[]{:S(2)}, u32[]{:S(2)}) %collective-permute-start) | collective-permute-done | bytes 131104 | tf_op jit(solution)/shard_map/ppermute | solution.py:692
  6.3 1.5 %collective-permute-start.5 = (bf16[2,4,64,128]{3,2,1,0:T(8,128)(2,1)S(1)}, bf16[2,4,64,128]{3,2,1,0:T(8,128)(2,1)S(1)}, u32[]{:S(2)}, u32[]{:S(2)}) collective-permute-start(bf16[2,4,64,128]{3,2,1,0:T(8,128)(2,1)S(1)} %get-tuple-element.146), channel_id=1, source_target_pairs={{0,24},{8,16},{16,8},{24,0},{1,25},{9,17},{17,9},{25,1},{2,26},{10... | collective-permute-start | bytes 393224 | tf_op jit(solution)/shard_map/ppermute | solution.py:692
  7.8 0.4 collective-permute-start.4
  8.2 0.1 collective-permute-start.3
  8.3 0.1 dynamic_slice.24
  8.4 0.1 dynamic_slice.25
  8.4 0.2 concatenate.19.taps
  8.6 0.1 concatenate.18.place
  8.7 3.2 %collective-permute-done.1.near2 = bf16[2,4,64,128]{3,2,1,0:T(8,128)(2,1)S(1)} collective-permute-done((bf16[2,4,64,128]{3,2,1,0:T(8,128)(2,1)S(1)}, bf16[2,4,64,128]{3,2,1,0:T(8,128)(2,1)S(1)}, u32[]{:S(2)}, u32[]{:S(2)}) %collective-permute-start.1) | collective-permute-done | bytes 131104 | tf_op jit(solution)/shard_map/ppermute | solution.py:692
  11.9 3.5 %attend.1 = (bf16[2048,128]{1,0:T(8,128)(2,1)S(1)}, bf16[2048,128]{1,0:T(8,128)(2,1)S(1)}, bf16[2048,128]{1,0:T(8,128)(2,1)S(1)}, f32[2048,128]{1,0:T(8,128)S(1)...) custom-call(s32[8]{0:T(128)S(1)} %concatenate.18.place, ...), custom_call_target="tpu_custom_call" | custom-call | flops 1000000000 | bytes 4194304 | tf_op jit(solution)/shard_map/attend/pallas_call | solution.py:617
  15.4 1.3 %collective-permute-done.4.cot2 = bf16[2,4,64,128]{3,2,1,0:T(8,128)(2,1)S(1)} collective-permute-done((bf16[2,4,64,128]{3,2,1,0:T(8,128)(2,1)S(1)}, bf16[2,4,64,128]{3,2,1,0:T(8,128)(2,1)S(1)}, u32[]{:S(2)}, u32[]{:S(2)}) %collective-permute-start.4) | collective-permute-done | bytes 131104 | tf_op jit(solution)/shard_map/ppermute | solution.py:692
  16.8 19.5 %feed.1 = (bf16[2,4,64,128]{3,2,1,0:T(8,128)(2,1)S(1)}, bf16[2,4,64,128]{3,2,1,0:T(8,128)(2,1)S(1)}, bf16[2,4,64,128]{3,2,1,0:T(8,128)(2,1)S(1)}, bf16[2,4,64,12...) custom-call(s32[8]{0:T(128)S(1)} %concatenate.18.place, ...), custom_call_target="tpu_custom_call" | custom-call | flops 16000000000 | bytes 4194304 | tf_op jit(solution)/shard_map/feed/pallas_call | solution.py:617
  36.3 0.1 collective-permute-start.6
  36.3 2.4 %collective-permute-start.8 = (bf16[2,4,64,128]{3,2,1,0:T(8,128)(2,1)S(1)}, bf16[2,4,64,128]{3,2,1,0:T(8,128)(2,1)S(1)}, u32[]{:S(2)}, u32[]{:S(2)}) collective-permute-start(bf16[2,4,64,128]{3,2,1,0:T(8,128)(2,1)S(1)} %get-tuple-element.93), channel_id=1, source_target_pairs={{0,16},{8,24},{16,0},{24,8},{1,17},{9,25},{17,1},{25,9},{2,18},{10... | collective-permute-start | bytes 393224 | tf_op jit(solution)/shard_map/ppermute | solution.py:692
  38.7 2.9 %back.1 = (bf16[2048,128]{1,0:T(8,128)(2,1)S(1)}, bf16[128,128]{1,0:T(8,128)(2,1)S(1)}, bf16[1344,128]{1,0:T(8,128)(2,1)S(1)}, bf16[1344,128]{1,0:T(8,128)(2,1)S(1)}) custom-call(s32[8]{0:T(128)S(1)} %concatenate.18.place, bf16[2048,128]{1,0:T(8,128)(2,1)S(1)} %get-tuple-element.83.normed, bf16[2048,128]{1,0:T(8,128)(2,1)S(1)} %get-tuple-element.84.query, ...), custom_call_target="tpu_custom_call" | custom-call | flops 2000000000 | bytes 4194304 | tf_op jit(solution)/shard_map/back/pallas_call | solution.py:617
  41.7 0.2 collective-permute-start.7
  41.9 0.1 add_convert_fusion.1
  42.0 1.4 %collective-permute-done.7 = bf16[1344,128]{1,0:T(8,128)(2,1)S(1)} collective-permute-done((bf16[1344,128]{1,0:T(8,128)(2,1)S(1)}, bf16[1344,128]{1,0:T(8,128)(2,1)S(1)}, u32[]{:S(2)}, u32[]{:S(2)}) %collective-permute-start.7) | collective-permute-done | bytes 344096 | tf_op jit(solution)/shard_map/ppermute | solution.py:692
  43.4 0.1 add_convert_fusion
  43.6 1.5 %collective-permute-start.9 = (bf16[608,128]{1,0:T(8,128)(2,1)S(1)}, bf16[608,128]{1,0:T(8,128)(2,1)S(1)}, u32[]{:S(2)}, u32[]{:S(2)}) collective-permute-start(bf16[608,128]{1,0:T(8,128)(2,1)S(1)} %get-tuple-element.95), channel_id=1, source_target_pairs={{0,1},{1,0},{2,3},{3,2},{4,5},{5,4},{6,7},{7,6},{8,10},{9,11},{10,... | collective-permute-start | bytes 466952 | tf_op jit(solution)/shard_map/ppermute | solution.py:698
  45.1 0.9 %collective-permute-start.10 = (bf16[608,128]{1,0:T(8,128)(2,1)S(1)}, bf16[608,128]{1,0:T(8,128)(2,1)S(1)}, u32[]{:S(2)}, u32[]{:S(2)}) collective-permute-start(bf16[608,128]{1,0:T(8,128)(2,1)S(1)} %get-tuple-element.96), channel_id=1, source_target_pairs={{0,16},{1,17},{2,18},{3,19},{4,20},{5,21},{6,22},{7,23},{8,12},{9,... | collective-permute-start | bytes 466952 | tf_op jit(solution)/shard_map/ppermute | solution.py:698
  46.0 1.1 %collective-permute-start.11 = (bf16[608,128]{1,0:T(8,128)(2,1)S(1)}, bf16[608,128]{1,0:T(8,128)(2,1)S(1)}, u32[]{:S(2)}, u32[]{:S(2)}) collective-permute-start(bf16[608,128]{1,0:T(8,128)(2,1)S(1)} %get-tuple-element.97), channel_id=1, source_target_pairs={{0,17},{1,16},{2,19},{3,18},{4,21},{5,20},{6,23},{7,22},{8,14},{9,... | collective-permute-start | bytes 466952 | tf_op jit(solution)/shard_map/ppermute | solution.py:698
  47.1 1.9 %input_gradient.1 = (bf16[2,4,64,128]{3,2,1,0:T(8,128)(2,1)S(1)}, bf16[2,4,64,128]{3,2,1,0:T(8,128)(2,1)S(1)}, bf16[2,4,64,128]{3,2,1,0:T(8,128)(2,1)S(1)}, bf16[2,4,64,128]{3,2,1,0:T(8,128)(2,1)S(1)}) custom-call(s32[8]{0:T(128)S(1)} %concatenate.18.place, bf16[2048,128]{1,0:T(8,128)(2,1)S(1)} %get-tuple-element.98.x, ...), custom_call_target="tpu_custom_call" | custom-call | flops 1000000000 | bytes 4194304 | tf_op jit(solution)/shard_map/input_gradient/pallas_call | solution.py:617
  49.0 1.3 %collective-permute-done.10 = bf16[608,128]{1,0:T(8,128)(2,1)S(1)} collective-permute-done((bf16[608,128]{1,0:T(8,128)(2,1)S(1)}, bf16[608,128]{1,0:T(8,128)(2,1)S(1)}, u32[]{:S(2)}, u32[]{:S(2)}) %collective-permute-start.10) | collective-permute-done | bytes 155680 | tf_op jit(solution)/shard_map/ppermute | solution.py:698
  50.4 1.8 %collective-permute-done.11 = bf16[608,128]{1,0:T(8,128)(2,1)S(1)} collective-permute-done((bf16[608,128]{1,0:T(8,128)(2,1)S(1)}, bf16[608,128]{1,0:T(8,128)(2,1)S(1)}, u32[]{:S(2)}, u32[]{:S(2)}) %collective-permute-start.11) | collective-permute-done | bytes 155680 | tf_op jit(solution)/shard_map/ppermute | solution.py:698
  52.2 0.1 add_convert_fusion.3
  52.3 3.7 %collective-permute-start.14 = (bf16[608,128]{1,0:T(8,128)(2,1)S(1)}, bf16[608,128]{1,0:T(8,128)(2,1)S(1)}, u32[]{:S(2)}, u32[]{:S(2)}) collective-permute-start(bf16[608,128]{1,0:T(8,128)(2,1)S(1)} %add_convert_fusion.3), channel_id=1, source_target_pairs={{0,6},{1,7},{2,4},{3,5},{4,2},{5,3},{6,0},{7,1},{8,25},{9,24},{10,... | collective-permute-start | bytes 466952 | tf_op jit(solution)/shard_map/ppermute | solution.py:698
  55.9 0.8 collective-permute-start.12
  56.7 1.2 %collective-permute-start.16 = (bf16[2,4,64,128]{3,2,1,0:T(8,128)(2,1)S(1)}, bf16[2,4,64,128]{3,2,1,0:T(8,128)(2,1)S(1)}, u32[]{:S(2)}, u32[]{:S(2)}) collective-permute-start(bf16[2,4,64,128]{3,2,1,0:T(8,128)(2,1)S(1)} %get-tuple-element.109), channel_id=1, source_target_pairs={{0,24},{8,16},{16,8},{24,0},{1,25},{9,17},{17,9},{25,1},{2,26},{10... | collective-permute-start | bytes 393224 | tf_op jit(solution)/shard_map/ppermute | solution.py:692
  57.9 0.1 collective-permute-done.15.part1
  58.1 5.1 %collective-permute-done.16.part3 = bf16[2,4,64,128]{3,2,1,0:T(8,128)(2,1)S(1)} collective-permute-done((bf16[2,4,64,128]{3,2,1,0:T(8,128)(2,1)S(1)}, bf16[2,4,64,128]{3,2,1,0:T(8,128)(2,1)S(1)}, u32[]{:S(2)}, u32[]{:S(2)}) %collective-permute-start.16) | collective-permute-done | bytes 131104 | tf_op jit(solution)/shard_map/ppermute | solution.py:692
  63.1 1.4 %gather_rows.2 = bf16[8,4,64,128]{3,2,1,0:T(8,128)(2,1)} custom-call(s32[8]{0:T(128)S(1)} %concatenate.18.place, bf16[2,4,64,128]{3,2,1,0:T(8,128)(2,1)S(1)} %get-tuple-element.106.part0, bf16[2,4,64,128]{3,2,1,0:T(8,128)(2,1)S(1)} %collective-permute-done.15.part1, bf16[2,4,64,128]{3,2,1,0:T(8,128)(2,1)S(1)} %collective-permute-done.8.part2, ...), custom_call_target="tpu_custom_call" | custom-call | tf_op jit(solution)/shard_map/gather_rows/pallas_call | solution.py:801
  64.5 0.1 collective-permute-start.20
  64.8 2.4 %collective-permute-start.19 = (bf16[608,128]{1,0:T(8,128)(2,1)S(1)}, bf16[608,128]{1,0:T(8,128)(2,1)S(1)}, u32[]{:S(2)}, u32[]{:S(2)}) collective-permute-start(bf16[608,128]{1,0:T(8,128)(2,1)S(1)} %add_convert_fusion.2.refs_0_), channel_id=1, source_target_pairs={{0,17},{1,16},{2,19},{3,18},{4,21},{5,20},{6,23},{7,22},{8,14},{9,... | collective-permute-start | bytes 466952 | tf_op jit(solution)/shard_map/ppermute | solution.py:698
  67.1 1.2 %collective-permute-start.18 = (bf16[608,128]{1,0:T(8,128)(2,1)S(1)}, bf16[608,128]{1,0:T(8,128)(2,1)S(1)}, u32[]{:S(2)}, u32[]{:S(2)}) collective-permute-start(bf16[608,128]{1,0:T(8,128)(2,1)S(1)} %add_convert_fusion.2.refs_0_), channel_id=1, source_target_pairs={{0,16},{1,17},{2,18},{3,19},{4,20},{5,21},{6,22},{7,23},{8,12},{9,... | collective-permute-start | bytes 466952 | tf_op jit(solution)/shard_map/ppermute | solution.py:698
  68.3 1.6 %collective-permute-start.21 = (bf16[2,4,64,128]{3,2,1,0:T(8,128)(2,1)S(1)}, bf16[2,4,64,128]{3,2,1,0:T(8,128)(2,1)S(1)}, u32[]{:S(2)}, u32[]{:S(2)}) collective-permute-start(bf16[2,4,64,128]{3,2,1,0:T(8,128)(2,1)S(1)} %get-tuple-element.118), channel_id=1, source_target_pairs={{0,24},{8,16},{16,8},{24,0},{1,25},{9,17},{17,9},{25,1},{2,26},{10... | collective-permute-start | bytes 393224 | tf_op jit(solution)/shard_map/ppermute | solution.py:692
  69.9 2.3 %collective-permute-done.20.part2 = bf16[2,4,64,128]{3,2,1,0:T(8,128)(2,1)S(1)} collective-permute-done((bf16[2,4,64,128]{3,2,1,0:T(8,128)(2,1)S(1)}, bf16[2,4,64,128]{3,2,1,0:T(8,128)(2,1)S(1)}, u32[]{:S(2)}, u32[]{:S(2)}) %collective-permute-start.20) | collective-permute-done | bytes 131104 | tf_op jit(solution)/shard_map/ppermute | solution.py:692
  72.2 2.7 %collective-permute-done.21.part3 = bf16[2,4,64,128]{3,2,1,0:T(8,128)(2,1)S(1)} collective-permute-done((bf16[2,4,64,128]{3,2,1,0:T(8,128)(2,1)S(1)}, bf16[2,4,64,128]{3,2,1,0:T(8,128)(2,1)S(1)}, u32[]{:S(2)}, u32[]{:S(2)}) %collective-permute-start.21) | collective-permute-done | bytes 131104 | tf_op jit(solution)/shard_map/ppermute | solution.py:692
  75.0 1.2 %collective-permute-start.23 = (bf16[608,128]{1,0:T(8,128)(2,1)S(1)}, bf16[608,128]{1,0:T(8,128)(2,1)S(1)}, u32[]{:S(2)}, u32[]{:S(2)}) collective-permute-start(bf16[608,128]{1,0:T(8,128)(2,1)S(1)} %add_convert_fusion.2.refs_0_), channel_id=1, source_target_pairs={{0,8},{8,0},{16,24},{24,16},{1,9},{9,1},{17,25},{25,17},{2,10},{10... | collective-permute-start | bytes 466952 | tf_op jit(solution)/shard_map/ppermute | solution.py:692
  76.1 1.4 %gather_rows.3 = bf16[8,4,64,128]{3,2,1,0:T(8,128)(2,1)} custom-call(s32[8]{0:T(128)S(1)} %concatenate.18.place, bf16[2,4,64,128]{3,2,1,0:T(8,128)(2,1)S(1)} %get-tuple-element.122.part0, bf16[2,4,64,128]{3,2,1,0:T(8,128)(2,1)S(1)} %collective-permute-done.22.part1, bf16[2,4,64,128]{3,2,1,0:T(8,128)(2,1)S(1)} %collective-permute-done.20.part2, ...), custom_call_target="tpu_custom_call" | custom-call | tf_op jit(solution)/shard_map/gather_rows/pallas_call | solution.py:801
  77.5 0.1 collective-permute-start.24
  77.6 0.5 collective-permute-start.25
  78.1 0.1 collective-permute-start.26
  78.2 1.8 %finish.2 = (f32[128,128]{1,0:T(8,128)}, f32[2048,128]{1,0:T(8,128)}, f32[128,256]{1,0:T(8,128)}, f32[128,128]{1,0:T(8,128)}, f32[128,1024]{1,0:T(8,128)}, /*index=5*/f32[1024,128]{1,0:T(8,128)}) custom-call(s32[8]{0:T(128)S(1)} %concatenate.18.place, bf16[608,128]{1,0:T(8,128)(2,1)S(1)} %add_convert_fusion.2.refs_0_, ...), custom_call_target="tpu_custom_call" | custom-call | bytes 4194304 | tf_op jit(solution)/shard_map/finish/pallas_call | solution.py:772
  80.0 1.8 %finish.3 = (f32[128,128]{1,0:T(8,128)}, f32[2048,128]{1,0:T(8,128)}, f32[128,256]{1,0:T(8,128)}, f32[128,128]{1,0:T(8,128)}, f32[128,1024]{1,0:T(8,128)}, /*ind...) custom-call(s32[8]{0:T(128)S(1)} %concatenate.18.place, ...), custom_call_target="tpu_custom_call", output_to_operand_aliasing={{0}: (9, {}), {1}: (10, {}), {2}: (11, {}), {3}: (12, {}), ... | custom-call | bytes 4194304 | tf_op jit(solution)/shard_map/finish/pallas_call | solution.py:772
  (64 shorter events, 0.5 us)
Async XLA Ops:
  0.6 5.6 %copy-start.1 = (bf16[8,4,64,128]{3,2,1,0:T(8,128)(2,1)S(1)}, bf16[8,4,64,128]{3,2,1,0:T(8,128)(2,1)}, u32[]{:S(2)}) copy-start(bf16[8,4,64,128]{3,2,1,0:T(8,128)(2,1)} %cot) | copy-start | bytes 1572868
  0.7 4.3 %copy-start.8 = (bf16[3,3,1024]{2,1,0:T(4,128)(2,1)S(1)}, bf16[3,3,1024]{2,1,0:T(4,128)(2,1)}, u32[]{:S(2)}) copy-start(bf16[3,3,1024]{2,1,0:T(4,128)(2,1)} %param.25) | copy-start | bytes 55300
  1.8 6.9 %collective-permute-start.2 = (bf16[2,4,64,128]{3,2,1,0:T(8,128)(2,1)S(1)}, bf16[2,4,64,128]{3,2,1,0:T(8,128)(2,1)S(1)}, u32[]{:S(2)}, u32[]{:S(2)}) collective-permute-start(bf16[2,4,64,128]{3,2,1,0:T(8,128)(2,1)S(1)} %get-tuple-element.149), channel_id=1, source_target_pairs={{0,24},{8,16},{16,8},{24,0},{1,25},{9,17},{17,9},{25,1},{2,26},{10... | collective-permute-start | bytes 393224 | tf_op jit(solution)/shard_map/ppermute | solution.py:692
  4.3 7.6 %collective-permute-start.1 = (bf16[2,4,64,128]{3,2,1,0:T(8,128)(2,1)S(1)}, bf16[2,4,64,128]{3,2,1,0:T(8,128)(2,1)S(1)}, u32[]{:S(2)}, u32[]{:S(2)}) collective-permute-start(bf16[2,4,64,128]{3,2,1,0:T(8,128)(2,1)S(1)} %get-tuple-element.150), channel_id=1, source_target_pairs={{0,16},{8,24},{16,0},{24,8},{1,17},{9,25},{17,1},{25,9},{2,18},{10... | collective-permute-start | bytes 393224 | tf_op jit(solution)/shard_map/ppermute | solution.py:692
  4.9 1.3 %collective-permute-start = (bf16[2,4,64,128]{3,2,1,0:T(8,128)(2,1)S(1)}, bf16[2,4,64,128]{3,2,1,0:T(8,128)(2,1)S(1)}, u32[]{:S(2)}, u32[]{:S(2)}) collective-permute-start(bf16[2,4,64,128]{3,2,1,0:T(8,128)(2,1)S(1)} %get-tuple-element.151), channel_id=1, source_target_pairs={{0,8},{8,0},{16,24},{24,16},{1,9},{9,1},{17,25},{25,17},{2,10},{10... | collective-permute-start | bytes 393224 | tf_op jit(solution)/shard_map/ppermute | solution.py:692
  5.0 6.9 %copy-start.7 = (bf16[128,128]{1,0:T(8,128)(2,1)S(1)}, bf16[128,128]{1,0:T(8,128)(2,1)}, u32[]{:S(2)}) copy-start(bf16[128,128]{1,0:T(8,128)(2,1)} %wq.5) | copy-start | bytes 98308
  5.0 6.9 %copy-start.5 = (bf16[128,256]{1,0:T(8,128)(2,1)S(1)}, bf16[128,256]{1,0:T(8,128)(2,1)}, u32[]{:S(2)}) copy-start(bf16[128,256]{1,0:T(8,128)(2,1)} %wkv.3) | copy-start | bytes 196612
  5.0 3.2 %copy-start.9 = (f32[128]{0:T(128)S(1)}, f32[128]{0:T(128)}, u32[]{:S(2)}) copy-start(f32[128]{0:T(128)} %param.23) | copy-start | bytes 1540
  5.0 3.2 %copy-start.10 = (f32[128]{0:T(128)S(1)}, f32[128]{0:T(128)}, u32[]{:S(2)}) copy-start(f32[128]{0:T(128)} %param.20) | copy-start | bytes 1540
  5.0 3.2 %copy-start.11 = (f32[128]{0:T(128)S(1)}, f32[128]{0:T(128)}, u32[]{:S(2)}) copy-start(f32[128]{0:T(128)} %param.17) | copy-start | bytes 1540
  5.0 3.2 %copy-start.12 = (s32[8]{0:T(128)S(1)}, s32[8]{0:T(128)}, u32[]{:S(2)}) copy-start(s32[8]{0:T(128)} %param.15) | copy-start | bytes 100
  5.0 3.3 %copy-start.13 = (s32[8]{0:T(128)S(1)}, s32[8]{0:T(128)}, u32[]{:S(2)}) copy-start(s32[8]{0:T(128)} %param.16) | copy-start | bytes 100
  5.1 6.9 %copy-start.2 = (bf16[2048,128]{1,0:T(8,128)(2,1)S(1)}, bf16[2048,128]{1,0:T(8,128)(2,1)}, u32[]{:S(2)}) copy-start(bf16[2048,128]{1,0:T(8,128)(2,1)} %wsr.5) | copy-start | bytes 1572868
  5.1 6.8 %copy-start = (bf16[8,4,64,128]{3,2,1,0:T(8,128)(2,1)S(1)}, bf16[8,4,64,128]{3,2,1,0:T(8,128)(2,1)}, u32[]{:S(2)}) copy-start(bf16[8,4,64,128]{3,2,1,0:T(8,128)(2,1)} %own.1) | copy-start | bytes 1572868
  6.3 9.1 %collective-permute-start.5 = (bf16[2,4,64,128]{3,2,1,0:T(8,128)(2,1)S(1)}, bf16[2,4,64,128]{3,2,1,0:T(8,128)(2,1)S(1)}, u32[]{:S(2)}, u32[]{:S(2)}) collective-permute-start(bf16[2,4,64,128]{3,2,1,0:T(8,128)(2,1)S(1)} %get-tuple-element.146), channel_id=1, source_target_pairs={{0,24},{8,16},{16,8},{24,0},{1,25},{9,17},{17,9},{25,1},{2,26},{10... | collective-permute-start | bytes 393224 | tf_op jit(solution)/shard_map/ppermute | solution.py:692
  7.8 9.0 %collective-permute-start.4 = (bf16[2,4,64,128]{3,2,1,0:T(8,128)(2,1)S(1)}, bf16[2,4,64,128]{3,2,1,0:T(8,128)(2,1)S(1)}, u32[]{:S(2)}, u32[]{:S(2)}) collective-permute-start(bf16[2,4,64,128]{3,2,1,0:T(8,128)(2,1)S(1)} %get-tuple-element.147), channel_id=1, source_target_pairs={{0,16},{8,24},{16,0},{24,8},{1,17},{9,25},{17,1},{25,9},{2,18},{10... | collective-permute-start | bytes 393224 | tf_op jit(solution)/shard_map/ppermute | solution.py:692
  8.2 8.6 %collective-permute-start.3 = (bf16[2,4,64,128]{3,2,1,0:T(8,128)(2,1)S(1)}, bf16[2,4,64,128]{3,2,1,0:T(8,128)(2,1)S(1)}, u32[]{:S(2)}, u32[]{:S(2)}) collective-permute-start(bf16[2,4,64,128]{3,2,1,0:T(8,128)(2,1)S(1)} %get-tuple-element.148), channel_id=1, source_target_pairs={{0,8},{8,0},{16,24},{24,16},{1,9},{9,1},{17,25},{25,17},{2,10},{10... | collective-permute-start | bytes 393224 | tf_op jit(solution)/shard_map/ppermute | solution.py:692
  8.4 3.5 %copy-start.6 = (bf16[128,128]{1,0:T(8,128)(2,1)S(1)}, bf16[128,128]{1,0:T(8,128)(2,1)}, u32[]{:S(2)}) copy-start(bf16[128,128]{1,0:T(8,128)(2,1)} %wout.3) | copy-start | bytes 98308
  8.7 8.1 %copy-start.3 = (bf16[128,1024]{1,0:T(8,128)(2,1)S(1)}, bf16[128,1024]{1,0:T(8,128)(2,1)}, u32[]{:S(2)}) copy-start(bf16[128,1024]{1,0:T(8,128)(2,1)} %wfc1.1) | copy-start | bytes 786436
  8.7 8.1 %copy-start.4 = (bf16[1024,128]{1,0:T(8,128)(2,1)S(1)}, bf16[1024,128]{1,0:T(8,128)(2,1)}, u32[]{:S(2)}) copy-start(bf16[1024,128]{1,0:T(8,128)(2,1)} %wfc2.1) | copy-start | bytes 786436
  36.3 5.6 %collective-permute-start.6 = (bf16[1088,128]{1,0:T(8,128)(2,1)S(1)}, bf16[1088,128]{1,0:T(8,128)(2,1)S(1)}, u32[]{:S(2)}, u32[]{:S(2)}) collective-permute-start(bf16[1088,128]{1,0:T(8,128)(2,1)S(1)} %get-tuple-element.82), channel_id=1, source_target_pairs={{0,8},{8,0},{16,24},{24,16},{1,9},{9,1},{17,25},{25,17},{2,10},{10... | collective-permute-start | bytes 835592 | tf_op jit(solution)/shard_map/ppermute | solution.py:692
  36.3 7.2 %collective-permute-start.8 = (bf16[2,4,64,128]{3,2,1,0:T(8,128)(2,1)S(1)}, bf16[2,4,64,128]{3,2,1,0:T(8,128)(2,1)S(1)}, u32[]{:S(2)}, u32[]{:S(2)}) collective-permute-start(bf16[2,4,64,128]{3,2,1,0:T(8,128)(2,1)S(1)} %get-tuple-element.93), channel_id=1, source_target_pairs={{0,16},{8,24},{16,0},{24,8},{1,17},{9,25},{17,1},{25,9},{2,18},{10... | collective-permute-start | bytes 393224 | tf_op jit(solution)/shard_map/ppermute | solution.py:692
  41.7 1.7 %collective-permute-start.7 = (bf16[1344,128]{1,0:T(8,128)(2,1)S(1)}, bf16[1344,128]{1,0:T(8,128)(2,1)S(1)}, u32[]{:S(2)}, u32[]{:S(2)}) collective-permute-start(bf16[1344,128]{1,0:T(8,128)(2,1)S(1)} %get-tuple-element.92), channel_id=1, source_target_pairs={{0,8},{8,0},{16,24},{24,16},{1,9},{9,1},{17,25},{25,17},{2,10},{10... | collective-permute-start | bytes 1032200 | tf_op jit(solution)/shard_map/ppermute | solution.py:692
  43.6 5.4 %collective-permute-start.9 = (bf16[608,128]{1,0:T(8,128)(2,1)S(1)}, bf16[608,128]{1,0:T(8,128)(2,1)S(1)}, u32[]{:S(2)}, u32[]{:S(2)}) collective-permute-start(bf16[608,128]{1,0:T(8,128)(2,1)S(1)} %get-tuple-element.95), channel_id=1, source_target_pairs={{0,1},{1,0},{2,3},{3,2},{4,5},{5,4},{6,7},{7,6},{8,10},{9,11},{10,... | collective-permute-start | bytes 466952 | tf_op jit(solution)/shard_map/ppermute | solution.py:698
  45.1 5.2 %collective-permute-start.10 = (bf16[608,128]{1,0:T(8,128)(2,1)S(1)}, bf16[608,128]{1,0:T(8,128)(2,1)S(1)}, u32[]{:S(2)}, u32[]{:S(2)}) collective-permute-start(bf16[608,128]{1,0:T(8,128)(2,1)S(1)} %get-tuple-element.96), channel_id=1, source_target_pairs={{0,16},{1,17},{2,18},{3,19},{4,20},{5,21},{6,22},{7,23},{8,12},{9,... | collective-permute-start | bytes 466952 | tf_op jit(solution)/shard_map/ppermute | solution.py:698
  46.0 6.1 %collective-permute-start.11 = (bf16[608,128]{1,0:T(8,128)(2,1)S(1)}, bf16[608,128]{1,0:T(8,128)(2,1)S(1)}, u32[]{:S(2)}, u32[]{:S(2)}) collective-permute-start(bf16[608,128]{1,0:T(8,128)(2,1)S(1)} %get-tuple-element.97), channel_id=1, source_target_pairs={{0,17},{1,16},{2,19},{3,18},{4,21},{5,20},{6,23},{7,22},{8,14},{9,... | collective-permute-start | bytes 466952 | tf_op jit(solution)/shard_map/ppermute | solution.py:698
  52.3 12.3 %collective-permute-start.14 = (bf16[608,128]{1,0:T(8,128)(2,1)S(1)}, bf16[608,128]{1,0:T(8,128)(2,1)S(1)}, u32[]{:S(2)}, u32[]{:S(2)}) collective-permute-start(bf16[608,128]{1,0:T(8,128)(2,1)S(1)} %add_convert_fusion.3), channel_id=1, source_target_pairs={{0,6},{1,7},{2,4},{3,5},{4,2},{5,3},{6,0},{7,1},{8,25},{9,24},{10,... | collective-permute-start | bytes 466952 | tf_op jit(solution)/shard_map/ppermute | solution.py:698
  55.9 8.7 %collective-permute-start.13 = (bf16[608,128]{1,0:T(8,128)(2,1)S(1)}, bf16[608,128]{1,0:T(8,128)(2,1)S(1)}, u32[]{:S(2)}, u32[]{:S(2)}) collective-permute-start(bf16[608,128]{1,0:T(8,128)(2,1)S(1)} %add_convert_fusion.3), channel_id=1, source_target_pairs={{0,4},{1,5},{2,6},{3,7},{4,0},{5,1},{6,2},{7,3},{8,24},{9,25},{10,... | collective-permute-start | bytes 466952 | tf_op jit(solution)/shard_map/ppermute | solution.py:698
  55.9 8.7 %collective-permute-start.12 = (bf16[608,128]{1,0:T(8,128)(2,1)S(1)}, bf16[608,128]{1,0:T(8,128)(2,1)S(1)}, u32[]{:S(2)}, u32[]{:S(2)}) collective-permute-start(bf16[608,128]{1,0:T(8,128)(2,1)S(1)} %add_convert_fusion.3), channel_id=1, source_target_pairs={{0,2},{1,3},{2,0},{3,1},{4,6},{5,7},{6,4},{7,5},{8,9},{9,8},{10,11... | collective-permute-start | bytes 466952 | tf_op jit(solution)/shard_map/ppermute | solution.py:698
  56.7 1.3 %collective-permute-start.15 = (bf16[2,4,64,128]{3,2,1,0:T(8,128)(2,1)S(1)}, bf16[2,4,64,128]{3,2,1,0:T(8,128)(2,1)S(1)}, u32[]{:S(2)}, u32[]{:S(2)}) collective-permute-start(bf16[2,4,64,128]{3,2,1,0:T(8,128)(2,1)S(1)} %get-tuple-element.107), channel_id=1, source_target_pairs={{0,8},{8,0},{16,24},{24,16},{1,9},{9,1},{17,25},{25,17},{2,10},{10... | collective-permute-start | bytes 393224 | tf_op jit(solution)/shard_map/ppermute | solution.py:692
  56.7 6.4 %collective-permute-start.16 = (bf16[2,4,64,128]{3,2,1,0:T(8,128)(2,1)S(1)}, bf16[2,4,64,128]{3,2,1,0:T(8,128)(2,1)S(1)}, u32[]{:S(2)}, u32[]{:S(2)}) collective-permute-start(bf16[2,4,64,128]{3,2,1,0:T(8,128)(2,1)S(1)} %get-tuple-element.109), channel_id=1, source_target_pairs={{0,24},{8,16},{16,8},{24,0},{1,25},{9,17},{17,9},{25,1},{2,26},{10... | collective-permute-start | bytes 393224 | tf_op jit(solution)/shard_map/ppermute | solution.py:692
  64.5 7.7 %collective-permute-start.20 = (bf16[2,4,64,128]{3,2,1,0:T(8,128)(2,1)S(1)}, bf16[2,4,64,128]{3,2,1,0:T(8,128)(2,1)S(1)}, u32[]{:S(2)}, u32[]{:S(2)}) collective-permute-start(bf16[2,4,64,128]{3,2,1,0:T(8,128)(2,1)S(1)} %get-tuple-element.117), channel_id=1, source_target_pairs={{0,16},{8,24},{16,0},{24,8},{1,17},{9,25},{17,1},{25,9},{2,18},{10... | collective-permute-start | bytes 393224 | tf_op jit(solution)/shard_map/ppermute | solution.py:692
  64.8 11.4 %collective-permute-start.19 = (bf16[608,128]{1,0:T(8,128)(2,1)S(1)}, bf16[608,128]{1,0:T(8,128)(2,1)S(1)}, u32[]{:S(2)}, u32[]{:S(2)}) collective-permute-start(bf16[608,128]{1,0:T(8,128)(2,1)S(1)} %add_convert_fusion.2.refs_0_), channel_id=1, source_target_pairs={{0,17},{1,16},{2,19},{3,18},{4,21},{5,20},{6,23},{7,22},{8,14},{9,... | collective-permute-start | bytes 466952 | tf_op jit(solution)/shard_map/ppermute | solution.py:698
  67.1 9.0 %collective-permute-start.18 = (bf16[608,128]{1,0:T(8,128)(2,1)S(1)}, bf16[608,128]{1,0:T(8,128)(2,1)S(1)}, u32[]{:S(2)}, u32[]{:S(2)}) collective-permute-start(bf16[608,128]{1,0:T(8,128)(2,1)S(1)} %add_convert_fusion.2.refs_0_), channel_id=1, source_target_pairs={{0,16},{1,17},{2,18},{3,19},{4,20},{5,21},{6,22},{7,23},{8,12},{9,... | collective-permute-start | bytes 466952 | tf_op jit(solution)/shard_map/ppermute | solution.py:698
  68.3 7.8 %collective-permute-start.17 = (bf16[608,128]{1,0:T(8,128)(2,1)S(1)}, bf16[608,128]{1,0:T(8,128)(2,1)S(1)}, u32[]{:S(2)}, u32[]{:S(2)}) collective-permute-start(bf16[608,128]{1,0:T(8,128)(2,1)S(1)} %add_convert_fusion.2.refs_0_), channel_id=1, source_target_pairs={{0,1},{1,0},{2,3},{3,2},{4,5},{5,4},{6,7},{7,6},{8,10},{9,11},{10,... | collective-permute-start | bytes 466952 | tf_op jit(solution)/shard_map/ppermute | solution.py:698
  68.3 6.6 %collective-permute-start.21 = (bf16[2,4,64,128]{3,2,1,0:T(8,128)(2,1)S(1)}, bf16[2,4,64,128]{3,2,1,0:T(8,128)(2,1)S(1)}, u32[]{:S(2)}, u32[]{:S(2)}) collective-permute-start(bf16[2,4,64,128]{3,2,1,0:T(8,128)(2,1)S(1)} %get-tuple-element.118), channel_id=1, source_target_pairs={{0,24},{8,16},{16,8},{24,0},{1,25},{9,17},{17,9},{25,1},{2,26},{10... | collective-permute-start | bytes 393224 | tf_op jit(solution)/shard_map/ppermute | solution.py:692
  72.2 3.9 %collective-permute-start.22 = (bf16[2,4,64,128]{3,2,1,0:T(8,128)(2,1)S(1)}, bf16[2,4,64,128]{3,2,1,0:T(8,128)(2,1)S(1)}, u32[]{:S(2)}, u32[]{:S(2)}) collective-permute-start(bf16[2,4,64,128]{3,2,1,0:T(8,128)(2,1)S(1)} %get-tuple-element.123), channel_id=1, source_target_pairs={{0,8},{8,0},{16,24},{24,16},{1,9},{9,1},{17,25},{25,17},{2,10},{10... | collective-permute-start | bytes 393224 | tf_op jit(solution)/shard_map/ppermute | solution.py:692
  75.0 5.0 %collective-permute-start.23 = (bf16[608,128]{1,0:T(8,128)(2,1)S(1)}, bf16[608,128]{1,0:T(8,128)(2,1)S(1)}, u32[]{:S(2)}, u32[]{:S(2)}) collective-permute-start(bf16[608,128]{1,0:T(8,128)(2,1)S(1)} %add_convert_fusion.2.refs_0_), channel_id=1, source_target_pairs={{0,8},{8,0},{16,24},{24,16},{1,9},{9,1},{17,25},{25,17},{2,10},{10... | collective-permute-start | bytes 466952 | tf_op jit(solution)/shard_map/ppermute | solution.py:692
  77.5 2.5 %collective-permute-start.24 = (bf16[608,128]{1,0:T(8,128)(2,1)S(1)}, bf16[608,128]{1,0:T(8,128)(2,1)S(1)}, u32[]{:S(2)}, u32[]{:S(2)}) collective-permute-start(bf16[608,128]{1,0:T(8,128)(2,1)S(1)} %collective-permute-done.17.refs_1_), channel_id=1, source_target_pairs={{0,8},{8,0},{16,24},{24,16},{1,9},{9,1},{17,25},{25,17},{2,10},{10... | collective-permute-start | bytes 466952 | tf_op jit(solution)/shard_map/ppermute | solution.py:692
  77.6 2.4 %collective-permute-start.25 = (bf16[608,128]{1,0:T(8,128)(2,1)S(1)}, bf16[608,128]{1,0:T(8,128)(2,1)S(1)}, u32[]{:S(2)}, u32[]{:S(2)}) collective-permute-start(bf16[608,128]{1,0:T(8,128)(2,1)S(1)} %collective-permute-done.18.refs_2_), channel_id=1, source_target_pairs={{0,8},{8,0},{16,24},{24,16},{1,9},{9,1},{17,25},{25,17},{2,10},{10... | collective-permute-start | bytes 466952 | tf_op jit(solution)/shard_map/ppermute | solution.py:692
  78.1 1.9 %collective-permute-start.26 = (bf16[608,128]{1,0:T(8,128)(2,1)S(1)}, bf16[608,128]{1,0:T(8,128)(2,1)S(1)}, u32[]{:S(2)}, u32[]{:S(2)}) collective-permute-start(bf16[608,128]{1,0:T(8,128)(2,1)S(1)} %collective-permute-done.19.refs_3_), channel_id=1, source_target_pairs={{0,8},{8,0},{16,24},{24,16},{1,9},{9,1},{17,25},{25,17},{2,10},{10... | collective-permute-start | bytes 466952 | tf_op jit(solution)/shard_map/ppermute | solution.py:692

commit v4 on v3

--- a/solution.py
+++ b/solution.py
@@ -386,7 +386,7 @@
 def feed_kernel(
     place, mid, cot, cot1, cot2, cot3, gains, wfc1, taps, wfc2,
     bo0, bo1, bo2, bo3, mg_out, send_out, keep_out,
-    cj, br, br_t, mask, even, odd, mix, pairs, pairs_t, cg, act, acc, back, stage, result,
+    cj, br, br_t, mask, even, odd, mix, pairs, pairs_t, cg, act, acc, back, stage, result, unit2, scale2,
 ):
     me = place[0]
     edge = jnp.zeros((64, 3 * D), jnp.bfloat16)
@@ -415,7 +415,9 @@
     def by_parity():
         return jnp.concatenate([mid[:, :, e].reshape(1024, D) for e in range(2)], axis=0)
 
-    unit, _ = norm_parts(by_parity())
+    unit, scale = norm_parts(by_parity())
+    unit2[...] = unit
+    scale2[...] = jnp.broadcast_to(scale, (2048, D))
     normed = ((unit * gains[pl.ds(2, 1), :]).astype(jnp.bfloat16)).astype(jnp.float32) * mask[...]
     before = jnp.where(col == 0, 0.0, pltpu.roll(normed, 1, 0))
     after = jnp.where(col == 63, 0.0, pltpu.roll(normed, 2047, 0))
@@ -494,7 +496,7 @@
     before = jnp.where(col == 0, 0.0, pltpu.roll(spread[:, 2 * D :], 1, 0))
     normed_grad = (spread[:, D : 2 * D] + before + after) * mask[...]
     middle = by_parity()
-    unit, scale = norm_parts(middle)
+    unit, scale = unit2[...], scale2[...]
     gain_grad = jnp.sum(normed_grad * unit, axis=0, keepdims=True)
     total = cj[...].astype(jnp.float32) + norm_back(normed_grad, gains[pl.ds(2, 1), :], unit, scale)
     final = (middle + acc[...] * mask[...]).astype(jnp.bfloat16)
@@ -659,7 +661,7 @@
             VMEM((2048, D), BF), VMEM((2048, D), BF), VMEM((D, 2048), BF), VMEM((2048, D), F32),
             VMEM((1152, 3 * D), BF), VMEM((1152, 3 * D), BF), VMEM((4, 3 * D, FF), BF),
             VMEM((4, 1024, 3 * D), BF), VMEM((4, 3 * D, 1024), BF), VMEM((4, 1024, FF), BF), VMEM((2048, FC), BF),
-            VMEM((2048, D), F32), VMEM((4, 1152, 3 * D), F32), VMEM((PACK1, D), F32), VMEM(SPLIT, BF),
+            VMEM((2048, D), F32), VMEM((4, 1152, 3 * D), F32), VMEM((PACK1, D), F32), VMEM(SPLIT, BF), VMEM(FLAT, F32), VMEM(FLAT, F32),
         ],
         flops=16 * 10**9, name="feed", vmem=44,
     )
@@ -849,10 +851,10 @@
     )
     parts = plane_parts([(send1, keep1), (send2, keep2)])
     block = returned(block_parts)
-    parts, block[2] = lax.optimization_barrier((parts, block[2]))
     inputs = input_gradient(place, kept[0], query_grad, pooled_low, mgrad, gains, q_weight, sr_weight)
     mine, inputs = lax.optimization_barrier((plus(parts[0], *to_four(parts, 0)), list(inputs)))
     inputs = returned(inputs)
+    mine, block[2] = lax.optimization_barrier((mine, block[2]))
     got = [g.astype(F32) for g in to_four([mine] * 4, 1)]
     got, block_out = lax.optimization_barrier((got, gather_rows(place, block, tokens.shape)))
     got, block[3] = lax.optimization_barrier((got, block[3]))

time: 82.2 us -> 81.5 us (level)
  waiting for transfers between devices: 20.5 us -> 17.8 us
  starting transfers between devices: 24 us -> 26.3 us
    ppermute x18, waiting for transfers between devices: 17.4 us -> 15.4 us  [over_rows(): return lax.ppermute(value, 'rows', [(i, i ^ k) for i in range(4)])]
    ppermute x18, starting transfers between devices: 12.4 us -> 14.3 us  [over_rows(): return lax.ppermute(value, 'rows', [(i, i ^ k) for i in range(4)])]
  transfers between devices with their start and end apart: 27 -> 27, of which waited for: 10 -> 8; matrix products, arithmetic and copies ran while one was open for 1% -> 1% of each run, Pallas kernels for 16% -> 16%
where the time goes in v4:
time: 81.5 us; the launch traced here: 81.3 us
  Pallas kernels  33.9 us (42%)
  starting transfers between devices  26.3 us (32%)
  waiting for transfers between devices  17.8 us (22%)
  local copies, waits for them, and re-layouts  1.68 us (2%)
  between operations  1.24 us (2%)
    pallas_call x4, Pallas kernels, call(): pl.pallas_call(kernel, out_shape=[jax.ShapeDtypeStruct(shape, kind) for s...  27.6 us
    ppermute x18, waiting for transfers between devices, over_rows(): return lax.ppermute(value, 'rows', [(i, i ^ k) for i in range(4)])  15.4 us
    ppermute x18, starting transfers between devices, over_rows(): return lax.ppermute(value, 'rows', [(i, i ^ k) for i in range(4)])  14.3 us
    ppermute x9, starting transfers between devices, over_four(): return lax.ppermute(value, ('rows', 'batch'), pairs)  11.9 us
    pallas_call x2, Pallas kernels, finish(): pl.pallas_call(functools.partial(finish_kernel, half), out_shape=[jax.Sha...  3.65 us
    pallas_call x2, Pallas kernels, gather_rows(): pl.pallas_call(gather_kernel, out_shape=jax.ShapeDtypeStruct(shape, BF),...  2.72 us
    ppermute x9, waiting for transfers between devices, over_four(): return lax.ppermute(value, ('rows', 'batch'), pairs)  2.35 us
  transfers between devices with their start and end apart: 27, of which 8 were waited for; matrix products, arithmetic and copies ran while one was open for 1% of the time, Pallas kernels for 16%

profile of v4, /device:TPU:0, one launch (start us, length us, event | category | flops | bytes accessed | tf_op | source)
XLA Modules:
  0.0 81.3 jit_solution(13199015374315716557)
XLA Ops:
  0.7 1.1 %constant_dynamic-slice_fusion.3 = (bf16[2,4,64,128]{3,2,1,0:T(8,128)(2,1)S(1)}, bf16[2,4,64,128]{3,2,1,0:T(8,128)(2,1)S(1)}, bf16[2,4,64,128]{3,2,1,0:T(8,128)(2,1)S(1)}) fusion(bf16[8,4,64,128]{3,2,1,0:T(8,128)(2,1)} %own.1, s32[]{:T(128)S(6)} %select_n.28, s32[]{:T(128)S(6)} %select_n.27, s32[]{:T(128)S(6)} %select_n.26), kind=kLoop, calls=%fused_computation.16 | loop fusion | bytes 786444 | tf_op jit(solution)/shard_map/dynamic_slice | solution.py:827
  1.8 2.5 %collective-permute-start.2 = (bf16[2,4,64,128]{3,2,1,0:T(8,128)(2,1)S(1)}, bf16[2,4,64,128]{3,2,1,0:T(8,128)(2,1)S(1)}, u32[]{:S(2)}, u32[]{:S(2)}) collective-permute-start(bf16[2,4,64,128]{3,2,1,0:T(8,128)(2,1)S(1)} %get-tuple-element.143), channel_id=1, source_target_pairs={{0,24},{8,16},{16,8},{24,0},{1,25},{9,17},{17,9},{25,1},{2,26},{10... | collective-permute-start | bytes 393224 | tf_op jit(solution)/shard_map/ppermute | solution.py:694
  4.3 0.6 collective-permute-start.1
  5.1 1.2 %collective-permute-done.near1 = bf16[2,4,64,128]{3,2,1,0:T(8,128)(2,1)S(1)} collective-permute-done((bf16[2,4,64,128]{3,2,1,0:T(8,128)(2,1)S(1)}, bf16[2,4,64,128]{3,2,1,0:T(8,128)(2,1)S(1)}, u32[]{:S(2)}, u32[]{:S(2)}) %collective-permute-start) | collective-permute-done | bytes 131104 | tf_op jit(solution)/shard_map/ppermute | solution.py:694
  6.3 1.5 %collective-permute-start.5 = (bf16[2,4,64,128]{3,2,1,0:T(8,128)(2,1)S(1)}, bf16[2,4,64,128]{3,2,1,0:T(8,128)(2,1)S(1)}, u32[]{:S(2)}, u32[]{:S(2)}) collective-permute-start(bf16[2,4,64,128]{3,2,1,0:T(8,128)(2,1)S(1)} %get-tuple-element.140), channel_id=1, source_target_pairs={{0,24},{8,16},{16,8},{24,0},{1,25},{9,17},{17,9},{25,1},{2,26},{10... | collective-permute-start | bytes 393224 | tf_op jit(solution)/shard_map/ppermute | solution.py:694
  7.8 0.4 collective-permute-start.4
  8.2 0.1 collective-permute-start.3
  8.3 0.1 dynamic_slice.24
  8.4 0.1 dynamic_slice.25
  8.4 0.2 concatenate.19.taps
  8.6 0.1 concatenate.18.place
  8.7 3.2 %collective-permute-done.1.near2 = bf16[2,4,64,128]{3,2,1,0:T(8,128)(2,1)S(1)} collective-permute-done((bf16[2,4,64,128]{3,2,1,0:T(8,128)(2,1)S(1)}, bf16[2,4,64,128]{3,2,1,0:T(8,128)(2,1)S(1)}, u32[]{:S(2)}, u32[]{:S(2)}) %collective-permute-start.1) | collective-permute-done | bytes 131104 | tf_op jit(solution)/shard_map/ppermute | solution.py:694
  11.9 3.5 %attend.1 = (bf16[2048,128]{1,0:T(8,128)(2,1)S(1)}, bf16[2048,128]{1,0:T(8,128)(2,1)S(1)}, bf16[2048,128]{1,0:T(8,128)(2,1)S(1)}, f32[2048,128]{1,0:T(8,128)S(1)...) custom-call(s32[8]{0:T(128)S(1)} %concatenate.18.place, ...), custom_call_target="tpu_custom_call" | custom-call | flops 1000000000 | bytes 4194304 | tf_op jit(solution)/shard_map/attend/pallas_call | solution.py:619
  15.4 1.3 %collective-permute-done.4.cot2 = bf16[2,4,64,128]{3,2,1,0:T(8,128)(2,1)S(1)} collective-permute-done((bf16[2,4,64,128]{3,2,1,0:T(8,128)(2,1)S(1)}, bf16[2,4,64,128]{3,2,1,0:T(8,128)(2,1)S(1)}, u32[]{:S(2)}, u32[]{:S(2)}) %collective-permute-start.4) | collective-permute-done | bytes 131104 | tf_op jit(solution)/shard_map/ppermute | solution.py:694
  16.8 19.3 %feed.1 = (bf16[2,4,64,128]{3,2,1,0:T(8,128)(2,1)S(1)}, bf16[2,4,64,128]{3,2,1,0:T(8,128)(2,1)S(1)}, bf16[2,4,64,128]{3,2,1,0:T(8,128)(2,1)S(1)}, bf16[2,4,64,12...) custom-call(s32[8]{0:T(128)S(1)} %concatenate.18.place, ...), custom_call_target="tpu_custom_call" | custom-call | flops 16000000000 | bytes 4194304 | tf_op jit(solution)/shard_map/feed/pallas_call | solution.py:619
  36.0 0.1 collective-permute-start.6
  36.1 2.9 %back.1 = (bf16[2048,128]{1,0:T(8,128)(2,1)S(1)}, bf16[128,128]{1,0:T(8,128)(2,1)S(1)}, bf16[1344,128]{1,0:T(8,128)(2,1)S(1)}, bf16[1344,128]{1,0:T(8,128)(2,1)S(1)}) custom-call(s32[8]{0:T(128)S(1)} %concatenate.18.place, bf16[2048,128]{1,0:T(8,128)(2,1)S(1)} %get-tuple-element.80.normed, bf16[2048,128]{1,0:T(8,128)(2,1)S(1)} %get-tuple-element.81.query, ...), custom_call_target="tpu_custom_call" | custom-call | flops 2000000000 | bytes 4194304 | tf_op jit(solution)/shard_map/back/pallas_call | solution.py:619
  39.1 0.6 collective-permute-start.7
  39.6 0.1 add_convert_fusion.1
  39.7 1.2 %collective-permute-done.7 = bf16[1344,128]{1,0:T(8,128)(2,1)S(1)} collective-permute-done((bf16[1344,128]{1,0:T(8,128)(2,1)S(1)}, bf16[1344,128]{1,0:T(8,128)(2,1)S(1)}, u32[]{:S(2)}, u32[]{:S(2)}) %collective-permute-start.7) | collective-permute-done | bytes 344096 | tf_op jit(solution)/shard_map/ppermute | solution.py:694
  40.9 0.1 add_convert_fusion
  41.1 2.3 %collective-permute-start.8 = (bf16[608,128]{1,0:T(8,128)(2,1)S(1)}, bf16[608,128]{1,0:T(8,128)(2,1)S(1)}, u32[]{:S(2)}, u32[]{:S(2)}) collective-permute-start(bf16[608,128]{1,0:T(8,128)(2,1)S(1)} %pad_maximum_fusion), channel_id=1, source_target_pairs={{0,1},{1,0},{2,3},{3,2},{4,5},{5,4},{6,7},{7,6},{8,10},{9,11},{10,... | collective-permute-start | bytes 466952 | tf_op jit(solution)/shard_map/ppermute | solution.py:700
  43.4 1.6 %collective-permute-start.9 = (bf16[608,128]{1,0:T(8,128)(2,1)S(1)}, bf16[608,128]{1,0:T(8,128)(2,1)S(1)}, u32[]{:S(2)}, u32[]{:S(2)}) collective-permute-start(bf16[608,128]{1,0:T(8,128)(2,1)S(1)} %pad_maximum_fusion.1), channel_id=1, source_target_pairs={{0,16},{1,17},{2,18},{3,19},{4,20},{5,21},{6,22},{7,23},{8,12},{9,... | collective-permute-start | bytes 466952 | tf_op jit(solution)/shard_map/ppermute | solution.py:700
  45.0 0.1 collective-permute-start.10
  45.1 2.0 %collective-permute-start.11 = (bf16[2,4,64,128]{3,2,1,0:T(8,128)(2,1)S(1)}, bf16[2,4,64,128]{3,2,1,0:T(8,128)(2,1)S(1)}, u32[]{:S(2)}, u32[]{:S(2)}) collective-permute-start(bf16[2,4,64,128]{3,2,1,0:T(8,128)(2,1)S(1)} %get-tuple-element.98), channel_id=1, source_target_pairs={{0,16},{8,24},{16,0},{24,8},{1,17},{9,25},{17,1},{25,9},{2,18},{10... | collective-permute-start | bytes 393224 | tf_op jit(solution)/shard_map/ppermute | solution.py:694
  47.1 1.9 %input_gradient.1 = (bf16[2,4,64,128]{3,2,1,0:T(8,128)(2,1)S(1)}, bf16[2,4,64,128]{3,2,1,0:T(8,128)(2,1)S(1)}, bf16[2,4,64,128]{3,2,1,0:T(8,128)(2,1)S(1)}, bf16[2,4,64,128]{3,2,1,0:T(8,128)(2,1)S(1)}) custom-call(s32[8]{0:T(128)S(1)} %concatenate.18.place, bf16[2048,128]{1,0:T(8,128)(2,1)S(1)} %get-tuple-element.90.x, ...), custom_call_target="tpu_custom_call" | custom-call | flops 1000000000 | bytes 4194304 | tf_op jit(solution)/shard_map/input_gradient/pallas_call | solution.py:619
  49.0 2.3 %collective-permute-done.10 = bf16[608,128]{1,0:T(8,128)(2,1)S(1)} collective-permute-done((bf16[608,128]{1,0:T(8,128)(2,1)S(1)}, bf16[608,128]{1,0:T(8,128)(2,1)S(1)}, u32[]{:S(2)}, u32[]{:S(2)}) %collective-permute-start.10) | collective-permute-done | bytes 155680 | tf_op jit(solution)/shard_map/ppermute | solution.py:700
  51.3 0.1 add_convert_fusion.3
  51.4 1.8 %collective-permute-done.11.part2 = bf16[2,4,64,128]{3,2,1,0:T(8,128)(2,1)S(1)} collective-permute-done((bf16[2,4,64,128]{3,2,1,0:T(8,128)(2,1)S(1)}, bf16[2,4,64,128]{3,2,1,0:T(8,128)(2,1)S(1)}, u32[]{:S(2)}, u32[]{:S(2)}) %collective-permute-start.11) | collective-permute-done | bytes 131104 | tf_op jit(solution)/shard_map/ppermute | solution.py:694
  53.2 3.6 %collective-permute-start.14 = (bf16[608,128]{1,0:T(8,128)(2,1)S(1)}, bf16[608,128]{1,0:T(8,128)(2,1)S(1)}, u32[]{:S(2)}, u32[]{:S(2)}) collective-permute-start(bf16[608,128]{1,0:T(8,128)(2,1)S(1)} %add_convert_fusion.3), channel_id=1, source_target_pairs={{0,6},{1,7},{2,4},{3,5},{4,2},{5,3},{6,0},{7,1},{8,25},{9,24},{10,... | collective-permute-start | bytes 466952 | tf_op jit(solution)/shard_map/ppermute | solution.py:700
  56.8 0.8 collective-permute-start.12
  57.6 1.6 %collective-permute-start.16 = (bf16[2,4,64,128]{3,2,1,0:T(8,128)(2,1)S(1)}, bf16[2,4,64,128]{3,2,1,0:T(8,128)(2,1)S(1)}, u32[]{:S(2)}, u32[]{:S(2)}) collective-permute-start(bf16[2,4,64,128]{3,2,1,0:T(8,128)(2,1)S(1)} %get-tuple-element.103), channel_id=1, source_target_pairs={{0,24},{8,16},{16,8},{24,0},{1,25},{9,17},{17,9},{25,1},{2,26},{10... | collective-permute-start | bytes 393224 | tf_op jit(solution)/shard_map/ppermute | solution.py:694
  59.2 1.2 %collective-permute-start.20 = (bf16[2,4,64,128]{3,2,1,0:T(8,128)(2,1)S(1)}, bf16[2,4,64,128]{3,2,1,0:T(8,128)(2,1)S(1)}, u32[]{:S(2)}, u32[]{:S(2)}) collective-permute-start(bf16[2,4,64,128]{3,2,1,0:T(8,128)(2,1)S(1)} %get-tuple-element.111), channel_id=1, source_target_pairs={{0,16},{8,24},{16,0},{24,8},{1,17},{9,25},{17,1},{25,9},{2,18},{10... | collective-permute-start | bytes 393224 | tf_op jit(solution)/shard_map/ppermute | solution.py:694
  60.4 2.6 %collective-permute-done.16.part3 = bf16[2,4,64,128]{3,2,1,0:T(8,128)(2,1)S(1)} collective-permute-done((bf16[2,4,64,128]{3,2,1,0:T(8,128)(2,1)S(1)}, bf16[2,4,64,128]{3,2,1,0:T(8,128)(2,1)S(1)}, u32[]{:S(2)}, u32[]{:S(2)}) %collective-permute-start.16) | collective-permute-done | bytes 131104 | tf_op jit(solution)/shard_map/ppermute | solution.py:694
  63.1 1.4 %gather_rows.2 = bf16[8,4,64,128]{3,2,1,0:T(8,128)(2,1)} custom-call(s32[8]{0:T(128)S(1)} %concatenate.18.place, bf16[2,4,64,128]{3,2,1,0:T(8,128)(2,1)S(1)} %get-tuple-element.100.part0, bf16[2,4,64,128]{3,2,1,0:T(8,128)(2,1)S(1)} %collective-permute-done.15.part1, bf16[2,4,64,128]{3,2,1,0:T(8,128)(2,1)S(1)} %collective-permute-done.11.part2, ...), custom_call_target="tpu_custom_call" | custom-call | tf_op jit(solution)/shard_map/gather_rows/pallas_call | solution.py:803
  64.5 0.1 add_convert_fusion.2.refs_0_
  64.6 1.5 %collective-permute-start.19 = (bf16[608,128]{1,0:T(8,128)(2,1)S(1)}, bf16[608,128]{1,0:T(8,128)(2,1)S(1)}, u32[]{:S(2)}, u32[]{:S(2)}) collective-permute-start(bf16[608,128]{1,0:T(8,128)(2,1)S(1)} %add_convert_fusion.2.refs_0_), channel_id=1, source_target_pairs={{0,17},{1,16},{2,19},{3,18},{4,21},{5,20},{6,23},{7,22},{8,14},{9,... | collective-permute-start | bytes 466952 | tf_op jit(solution)/shard_map/ppermute | solution.py:700
  66.1 1.1 %collective-permute-start.18 = (bf16[608,128]{1,0:T(8,128)(2,1)S(1)}, bf16[608,128]{1,0:T(8,128)(2,1)S(1)}, u32[]{:S(2)}, u32[]{:S(2)}) collective-permute-start(bf16[608,128]{1,0:T(8,128)(2,1)S(1)} %add_convert_fusion.2.refs_0_), channel_id=1, source_target_pairs={{0,16},{1,17},{2,18},{3,19},{4,20},{5,21},{6,22},{7,23},{8,12},{9,... | collective-permute-start | bytes 466952 | tf_op jit(solution)/shard_map/ppermute | solution.py:700
  67.2 1.0 %collective-permute-start.17 = (bf16[608,128]{1,0:T(8,128)(2,1)S(1)}, bf16[608,128]{1,0:T(8,128)(2,1)S(1)}, u32[]{:S(2)}, u32[]{:S(2)}) collective-permute-start(bf16[608,128]{1,0:T(8,128)(2,1)S(1)} %add_convert_fusion.2.refs_0_), channel_id=1, source_target_pairs={{0,1},{1,0},{2,3},{3,2},{4,5},{5,4},{6,7},{7,6},{8,10},{9,11},{10,... | collective-permute-start | bytes 466952 | tf_op jit(solution)/shard_map/ppermute | solution.py:700
  68.2 2.3 %collective-permute-start.21 = (bf16[2,4,64,128]{3,2,1,0:T(8,128)(2,1)S(1)}, bf16[2,4,64,128]{3,2,1,0:T(8,128)(2,1)S(1)}, u32[]{:S(2)}, u32[]{:S(2)}) collective-permute-start(bf16[2,4,64,128]{3,2,1,0:T(8,128)(2,1)S(1)} %get-tuple-element.112), channel_id=1, source_target_pairs={{0,24},{8,16},{16,8},{24,0},{1,25},{9,17},{17,9},{25,1},{2,26},{10... | collective-permute-start | bytes 393224 | tf_op jit(solution)/shard_map/ppermute | solution.py:694
  70.4 4.1 %collective-permute-done.21.part3 = bf16[2,4,64,128]{3,2,1,0:T(8,128)(2,1)S(1)} collective-permute-done((bf16[2,4,64,128]{3,2,1,0:T(8,128)(2,1)S(1)}, bf16[2,4,64,128]{3,2,1,0:T(8,128)(2,1)S(1)}, u32[]{:S(2)}, u32[]{:S(2)}) %collective-permute-start.21) | collective-permute-done | bytes 131104 | tf_op jit(solution)/shard_map/ppermute | solution.py:694
  74.5 0.6 collective-permute-start.23
  75.1 1.4 %gather_rows.3 = bf16[8,4,64,128]{3,2,1,0:T(8,128)(2,1)} custom-call(s32[8]{0:T(128)S(1)} %concatenate.18.place, bf16[2,4,64,128]{3,2,1,0:T(8,128)(2,1)S(1)} %get-tuple-element.116.part0, bf16[2,4,64,128]{3,2,1,0:T(8,128)(2,1)S(1)} %collective-permute-done.22.part1, bf16[2,4,64,128]{3,2,1,0:T(8,128)(2,1)S(1)} %collective-permute-done.20.part2, ...), custom_call_target="tpu_custom_call" | custom-call | tf_op jit(solution)/shard_map/gather_rows/pallas_call | solution.py:803
  76.5 0.5 collective-permute-start.24
  77.0 0.1 collective-permute-start.25
  77.1 0.4 collective-permute-start.26
  77.5 1.8 %finish.2 = (f32[128,128]{1,0:T(8,128)}, f32[2048,128]{1,0:T(8,128)}, f32[128,256]{1,0:T(8,128)}, f32[128,128]{1,0:T(8,128)}, f32[128,1024]{1,0:T(8,128)}, /*index=5*/f32[1024,128]{1,0:T(8,128)}) custom-call(s32[8]{0:T(128)S(1)} %concatenate.18.place, bf16[608,128]{1,0:T(8,128)(2,1)S(1)} %add_convert_fusion.2.refs_0_, ...), custom_call_target="tpu_custom_call" | custom-call | bytes 4194304 | tf_op jit(solution)/shard_map/finish/pallas_call | solution.py:774
  79.3 1.8 %finish.3 = (f32[128,128]{1,0:T(8,128)}, f32[2048,128]{1,0:T(8,128)}, f32[128,256]{1,0:T(8,128)}, f32[128,128]{1,0:T(8,128)}, f32[128,1024]{1,0:T(8,128)}, /*ind...) custom-call(s32[8]{0:T(128)S(1)} %concatenate.18.place, ...), custom_call_target="tpu_custom_call", output_to_operand_aliasing={{0}: (9, {}), {1}: (10, {}), {2}: (11, {}), {3}: (12, {}), ... | custom-call | bytes 4194304 | tf_op jit(solution)/shard_map/finish/pallas_call | solution.py:774
  (65 shorter events, 0.4 us)
Async XLA Ops:
  0.6 5.6 %copy-start.1 = (bf16[8,4,64,128]{3,2,1,0:T(8,128)(2,1)S(1)}, bf16[8,4,64,128]{3,2,1,0:T(8,128)(2,1)}, u32[]{:S(2)}) copy-start(bf16[8,4,64,128]{3,2,1,0:T(8,128)(2,1)} %cot) | copy-start | bytes 1572868
  0.7 4.3 %copy-start.8 = (bf16[3,3,1024]{2,1,0:T(4,128)(2,1)S(1)}, bf16[3,3,1024]{2,1,0:T(4,128)(2,1)}, u32[]{:S(2)}) copy-start(bf16[3,3,1024]{2,1,0:T(4,128)(2,1)} %param.25) | copy-start | bytes 55300
  1.8 6.9 %collective-permute-start.2 = (bf16[2,4,64,128]{3,2,1,0:T(8,128)(2,1)S(1)}, bf16[2,4,64,128]{3,2,1,0:T(8,128)(2,1)S(1)}, u32[]{:S(2)}, u32[]{:S(2)}) collective-permute-start(bf16[2,4,64,128]{3,2,1,0:T(8,128)(2,1)S(1)} %get-tuple-element.143), channel_id=1, source_target_pairs={{0,24},{8,16},{16,8},{24,0},{1,25},{9,17},{17,9},{25,1},{2,26},{10... | collective-permute-start | bytes 393224 | tf_op jit(solution)/shard_map/ppermute | solution.py:694
  4.3 7.6 %collective-permute-start.1 = (bf16[2,4,64,128]{3,2,1,0:T(8,128)(2,1)S(1)}, bf16[2,4,64,128]{3,2,1,0:T(8,128)(2,1)S(1)}, u32[]{:S(2)}, u32[]{:S(2)}) collective-permute-start(bf16[2,4,64,128]{3,2,1,0:T(8,128)(2,1)S(1)} %get-tuple-element.144), channel_id=1, source_target_pairs={{0,16},{8,24},{16,0},{24,8},{1,17},{9,25},{17,1},{25,9},{2,18},{10... | collective-permute-start | bytes 393224 | tf_op jit(solution)/shard_map/ppermute | solution.py:694
  4.9 1.3 %collective-permute-start = (bf16[2,4,64,128]{3,2,1,0:T(8,128)(2,1)S(1)}, bf16[2,4,64,128]{3,2,1,0:T(8,128)(2,1)S(1)}, u32[]{:S(2)}, u32[]{:S(2)}) collective-permute-start(bf16[2,4,64,128]{3,2,1,0:T(8,128)(2,1)S(1)} %get-tuple-element.145), channel_id=1, source_target_pairs={{0,8},{8,0},{16,24},{24,16},{1,9},{9,1},{17,25},{25,17},{2,10},{10... | collective-permute-start | bytes 393224 | tf_op jit(solution)/shard_map/ppermute | solution.py:694
  5.0 6.9 %copy-start.7 = (bf16[128,128]{1,0:T(8,128)(2,1)S(1)}, bf16[128,128]{1,0:T(8,128)(2,1)}, u32[]{:S(2)}) copy-start(bf16[128,128]{1,0:T(8,128)(2,1)} %wq.5) | copy-start | bytes 98308
  5.0 6.9 %copy-start.5 = (bf16[128,256]{1,0:T(8,128)(2,1)S(1)}, bf16[128,256]{1,0:T(8,128)(2,1)}, u32[]{:S(2)}) copy-start(bf16[128,256]{1,0:T(8,128)(2,1)} %wkv.3) | copy-start | bytes 196612
  5.0 3.2 %copy-start.9 = (f32[128]{0:T(128)S(1)}, f32[128]{0:T(128)}, u32[]{:S(2)}) copy-start(f32[128]{0:T(128)} %param.23) | copy-start | bytes 1540
  5.0 3.2 %copy-start.10 = (f32[128]{0:T(128)S(1)}, f32[128]{0:T(128)}, u32[]{:S(2)}) copy-start(f32[128]{0:T(128)} %param.20) | copy-start | bytes 1540
  5.0 3.2 %copy-start.11 = (f32[128]{0:T(128)S(1)}, f32[128]{0:T(128)}, u32[]{:S(2)}) copy-start(f32[128]{0:T(128)} %param.17) | copy-start | bytes 1540
  5.0 3.2 %copy-start.12 = (s32[8]{0:T(128)S(1)}, s32[8]{0:T(128)}, u32[]{:S(2)}) copy-start(s32[8]{0:T(128)} %param.15) | copy-start | bytes 100
  5.0 3.3 %copy-start.13 = (s32[8]{0:T(128)S(1)}, s32[8]{0:T(128)}, u32[]{:S(2)}) copy-start(s32[8]{0:T(128)} %param.16) | copy-start | bytes 100
  5.1 6.9 %copy-start.2 = (bf16[2048,128]{1,0:T(8,128)(2,1)S(1)}, bf16[2048,128]{1,0:T(8,128)(2,1)}, u32[]{:S(2)}) copy-start(bf16[2048,128]{1,0:T(8,128)(2,1)} %wsr.5) | copy-start | bytes 1572868
  5.1 6.8 %copy-start = (bf16[8,4,64,128]{3,2,1,0:T(8,128)(2,1)S(1)}, bf16[8,4,64,128]{3,2,1,0:T(8,128)(2,1)}, u32[]{:S(2)}) copy-start(bf16[8,4,64,128]{3,2,1,0:T(8,128)(2,1)} %own.1) | copy-start | bytes 1572868
  6.3 9.1 %collective-permute-start.5 = (bf16[2,4,64,128]{3,2,1,0:T(8,128)(2,1)S(1)}, bf16[2,4,64,128]{3,2,1,0:T(8,128)(2,1)S(1)}, u32[]{:S(2)}, u32[]{:S(2)}) collective-permute-start(bf16[2,4,64,128]{3,2,1,0:T(8,128)(2,1)S(1)} %get-tuple-element.140), channel_id=1, source_target_pairs={{0,24},{8,16},{16,8},{24,0},{1,25},{9,17},{17,9},{25,1},{2,26},{10... | collective-permute-start | bytes 393224 | tf_op jit(solution)/shard_map/ppermute | solution.py:694
  7.8 9.0 %collective-permute-start.4 = (bf16[2,4,64,128]{3,2,1,0:T(8,128)(2,1)S(1)}, bf16[2,4,64,128]{3,2,1,0:T(8,128)(2,1)S(1)}, u32[]{:S(2)}, u32[]{:S(2)}) collective-permute-start(bf16[2,4,64,128]{3,2,1,0:T(8,128)(2,1)S(1)} %get-tuple-element.141), channel_id=1, source_target_pairs={{0,16},{8,24},{16,0},{24,8},{1,17},{9,25},{17,1},{25,9},{2,18},{10... | collective-permute-start | bytes 393224 | tf_op jit(solution)/shard_map/ppermute | solution.py:694
  8.2 8.6 %collective-permute-start.3 = (bf16[2,4,64,128]{3,2,1,0:T(8,128)(2,1)S(1)}, bf16[2,4,64,128]{3,2,1,0:T(8,128)(2,1)S(1)}, u32[]{:S(2)}, u32[]{:S(2)}) collective-permute-start(bf16[2,4,64,128]{3,2,1,0:T(8,128)(2,1)S(1)} %get-tuple-element.142), channel_id=1, source_target_pairs={{0,8},{8,0},{16,24},{24,16},{1,9},{9,1},{17,25},{25,17},{2,10},{10... | collective-permute-start | bytes 393224 | tf_op jit(solution)/shard_map/ppermute | solution.py:694
  8.4 3.5 %copy-start.6 = (bf16[128,128]{1,0:T(8,128)(2,1)S(1)}, bf16[128,128]{1,0:T(8,128)(2,1)}, u32[]{:S(2)}) copy-start(bf16[128,128]{1,0:T(8,128)(2,1)} %wout.3) | copy-start | bytes 98308
  8.7 8.1 %copy-start.3 = (bf16[128,1024]{1,0:T(8,128)(2,1)S(1)}, bf16[128,1024]{1,0:T(8,128)(2,1)}, u32[]{:S(2)}) copy-start(bf16[128,1024]{1,0:T(8,128)(2,1)} %wfc1.1) | copy-start | bytes 786436
  8.7 8.1 %copy-start.4 = (bf16[1024,128]{1,0:T(8,128)(2,1)S(1)}, bf16[1024,128]{1,0:T(8,128)(2,1)}, u32[]{:S(2)}) copy-start(bf16[1024,128]{1,0:T(8,128)(2,1)} %wfc2.1) | copy-start | bytes 786436
  36.0 3.6 %collective-permute-start.6 = (bf16[1088,128]{1,0:T(8,128)(2,1)S(1)}, bf16[1088,128]{1,0:T(8,128)(2,1)S(1)}, u32[]{:S(2)}, u32[]{:S(2)}) collective-permute-start(bf16[1088,128]{1,0:T(8,128)(2,1)S(1)} %get-tuple-element.79), channel_id=1, source_target_pairs={{0,8},{8,0},{16,24},{24,16},{1,9},{9,1},{17,25},{25,17},{2,10},{10... | collective-permute-start | bytes 835592 | tf_op jit(solution)/shard_map/ppermute | solution.py:694
  39.1 1.8 %collective-permute-start.7 = (bf16[1344,128]{1,0:T(8,128)(2,1)S(1)}, bf16[1344,128]{1,0:T(8,128)(2,1)S(1)}, u32[]{:S(2)}, u32[]{:S(2)}) collective-permute-start(bf16[1344,128]{1,0:T(8,128)(2,1)S(1)} %get-tuple-element.89), channel_id=1, source_target_pairs={{0,8},{8,0},{16,24},{24,16},{1,9},{9,1},{17,25},{25,17},{2,10},{10... | collective-permute-start | bytes 1032200 | tf_op jit(solution)/shard_map/ppermute | solution.py:694
  41.1 7.9 %collective-permute-start.8 = (bf16[608,128]{1,0:T(8,128)(2,1)S(1)}, bf16[608,128]{1,0:T(8,128)(2,1)S(1)}, u32[]{:S(2)}, u32[]{:S(2)}) collective-permute-start(bf16[608,128]{1,0:T(8,128)(2,1)S(1)} %pad_maximum_fusion), channel_id=1, source_target_pairs={{0,1},{1,0},{2,3},{3,2},{4,5},{5,4},{6,7},{7,6},{8,10},{9,11},{10,... | collective-permute-start | bytes 466952 | tf_op jit(solution)/shard_map/ppermute | solution.py:700
  43.4 5.6 %collective-permute-start.9 = (bf16[608,128]{1,0:T(8,128)(2,1)S(1)}, bf16[608,128]{1,0:T(8,128)(2,1)S(1)}, u32[]{:S(2)}, u32[]{:S(2)}) collective-permute-start(bf16[608,128]{1,0:T(8,128)(2,1)S(1)} %pad_maximum_fusion.1), channel_id=1, source_target_pairs={{0,16},{1,17},{2,18},{3,19},{4,20},{5,21},{6,22},{7,23},{8,12},{9,... | collective-permute-start | bytes 466952 | tf_op jit(solution)/shard_map/ppermute | solution.py:700
  45.0 6.3 %collective-permute-start.10 = (bf16[608,128]{1,0:T(8,128)(2,1)S(1)}, bf16[608,128]{1,0:T(8,128)(2,1)S(1)}, u32[]{:S(2)}, u32[]{:S(2)}) collective-permute-start(bf16[608,128]{1,0:T(8,128)(2,1)S(1)} %pad_maximum_fusion.2), channel_id=1, source_target_pairs={{0,17},{1,16},{2,19},{3,18},{4,21},{5,20},{6,23},{7,22},{8,14},{9,... | collective-permute-start | bytes 466952 | tf_op jit(solution)/shard_map/ppermute | solution.py:700
  45.1 8.1 %collective-permute-start.11 = (bf16[2,4,64,128]{3,2,1,0:T(8,128)(2,1)S(1)}, bf16[2,4,64,128]{3,2,1,0:T(8,128)(2,1)S(1)}, u32[]{:S(2)}, u32[]{:S(2)}) collective-permute-start(bf16[2,4,64,128]{3,2,1,0:T(8,128)(2,1)S(1)} %get-tuple-element.98), channel_id=1, source_target_pairs={{0,16},{8,24},{16,0},{24,8},{1,17},{9,25},{17,1},{25,9},{2,18},{10... | collective-permute-start | bytes 393224 | tf_op jit(solution)/shard_map/ppermute | solution.py:694
  53.2 11.2 %collective-permute-start.14 = (bf16[608,128]{1,0:T(8,128)(2,1)S(1)}, bf16[608,128]{1,0:T(8,128)(2,1)S(1)}, u32[]{:S(2)}, u32[]{:S(2)}) collective-permute-start(bf16[608,128]{1,0:T(8,128)(2,1)S(1)} %add_convert_fusion.3), channel_id=1, source_target_pairs={{0,6},{1,7},{2,4},{3,5},{4,2},{5,3},{6,0},{7,1},{8,25},{9,24},{10,... | collective-permute-start | bytes 466952 | tf_op jit(solution)/shard_map/ppermute | solution.py:700
  56.8 7.7 %collective-permute-start.13 = (bf16[608,128]{1,0:T(8,128)(2,1)S(1)}, bf16[608,128]{1,0:T(8,128)(2,1)S(1)}, u32[]{:S(2)}, u32[]{:S(2)}) collective-permute-start(bf16[608,128]{1,0:T(8,128)(2,1)S(1)} %add_convert_fusion.3), channel_id=1, source_target_pairs={{0,4},{1,5},{2,6},{3,7},{4,0},{5,1},{6,2},{7,3},{8,24},{9,25},{10,... | collective-permute-start | bytes 466952 | tf_op jit(solution)/shard_map/ppermute | solution.py:700
  56.8 7.7 %collective-permute-start.12 = (bf16[608,128]{1,0:T(8,128)(2,1)S(1)}, bf16[608,128]{1,0:T(8,128)(2,1)S(1)}, u32[]{:S(2)}, u32[]{:S(2)}) collective-permute-start(bf16[608,128]{1,0:T(8,128)(2,1)S(1)} %add_convert_fusion.3), channel_id=1, source_target_pairs={{0,2},{1,3},{2,0},{3,1},{4,6},{5,7},{6,4},{7,5},{8,9},{9,8},{10,11... | collective-permute-start | bytes 466952 | tf_op jit(solution)/shard_map/ppermute | solution.py:700
  57.6 1.6 %collective-permute-start.15 = (bf16[2,4,64,128]{3,2,1,0:T(8,128)(2,1)S(1)}, bf16[2,4,64,128]{3,2,1,0:T(8,128)(2,1)S(1)}, u32[]{:S(2)}, u32[]{:S(2)}) collective-permute-start(bf16[2,4,64,128]{3,2,1,0:T(8,128)(2,1)S(1)} %get-tuple-element.101), channel_id=1, source_target_pairs={{0,8},{8,0},{16,24},{24,16},{1,9},{9,1},{17,25},{25,17},{2,10},{10... | collective-permute-start | bytes 393224 | tf_op jit(solution)/shard_map/ppermute | solution.py:694
  57.6 5.5 %collective-permute-start.16 = (bf16[2,4,64,128]{3,2,1,0:T(8,128)(2,1)S(1)}, bf16[2,4,64,128]{3,2,1,0:T(8,128)(2,1)S(1)}, u32[]{:S(2)}, u32[]{:S(2)}) collective-permute-start(bf16[2,4,64,128]{3,2,1,0:T(8,128)(2,1)S(1)} %get-tuple-element.103), channel_id=1, source_target_pairs={{0,24},{8,16},{16,8},{24,0},{1,25},{9,17},{17,9},{25,1},{2,26},{10... | collective-permute-start | bytes 393224 | tf_op jit(solution)/shard_map/ppermute | solution.py:694
  59.2 11.2 %collective-permute-start.20 = (bf16[2,4,64,128]{3,2,1,0:T(8,128)(2,1)S(1)}, bf16[2,4,64,128]{3,2,1,0:T(8,128)(2,1)S(1)}, u32[]{:S(2)}, u32[]{:S(2)}) collective-permute-start(bf16[2,4,64,128]{3,2,1,0:T(8,128)(2,1)S(1)} %get-tuple-element.111), channel_id=1, source_target_pairs={{0,16},{8,24},{16,0},{24,8},{1,17},{9,25},{17,1},{25,9},{2,18},{10... | collective-permute-start | bytes 393224 | tf_op jit(solution)/shard_map/ppermute | solution.py:694
  64.6 10.5 %collective-permute-start.19 = (bf16[608,128]{1,0:T(8,128)(2,1)S(1)}, bf16[608,128]{1,0:T(8,128)(2,1)S(1)}, u32[]{:S(2)}, u32[]{:S(2)}) collective-permute-start(bf16[608,128]{1,0:T(8,128)(2,1)S(1)} %add_convert_fusion.2.refs_0_), channel_id=1, source_target_pairs={{0,17},{1,16},{2,19},{3,18},{4,21},{5,20},{6,23},{7,22},{8,14},{9,... | collective-permute-start | bytes 466952 | tf_op jit(solution)/shard_map/ppermute | solution.py:700
  66.1 9.0 %collective-permute-start.18 = (bf16[608,128]{1,0:T(8,128)(2,1)S(1)}, bf16[608,128]{1,0:T(8,128)(2,1)S(1)}, u32[]{:S(2)}, u32[]{:S(2)}) collective-permute-start(bf16[608,128]{1,0:T(8,128)(2,1)S(1)} %add_convert_fusion.2.refs_0_), channel_id=1, source_target_pairs={{0,16},{1,17},{2,18},{3,19},{4,20},{5,21},{6,22},{7,23},{8,12},{9,... | collective-permute-start | bytes 466952 | tf_op jit(solution)/shard_map/ppermute | solution.py:700
  67.2 7.9 %collective-permute-start.17 = (bf16[608,128]{1,0:T(8,128)(2,1)S(1)}, bf16[608,128]{1,0:T(8,128)(2,1)S(1)}, u32[]{:S(2)}, u32[]{:S(2)}) collective-permute-start(bf16[608,128]{1,0:T(8,128)(2,1)S(1)} %add_convert_fusion.2.refs_0_), channel_id=1, source_target_pairs={{0,1},{1,0},{2,3},{3,2},{4,5},{5,4},{6,7},{7,6},{8,10},{9,11},{10,... | collective-permute-start | bytes 466952 | tf_op jit(solution)/shard_map/ppermute | solution.py:700
  68.2 6.4 %collective-permute-start.21 = (bf16[2,4,64,128]{3,2,1,0:T(8,128)(2,1)S(1)}, bf16[2,4,64,128]{3,2,1,0:T(8,128)(2,1)S(1)}, u32[]{:S(2)}, u32[]{:S(2)}) collective-permute-start(bf16[2,4,64,128]{3,2,1,0:T(8,128)(2,1)S(1)} %get-tuple-element.112), channel_id=1, source_target_pairs={{0,24},{8,16},{16,8},{24,0},{1,25},{9,17},{17,9},{25,1},{2,26},{10... | collective-permute-start | bytes 393224 | tf_op jit(solution)/shard_map/ppermute | solution.py:694
  70.4 4.7 %collective-permute-start.22 = (bf16[2,4,64,128]{3,2,1,0:T(8,128)(2,1)S(1)}, bf16[2,4,64,128]{3,2,1,0:T(8,128)(2,1)S(1)}, u32[]{:S(2)}, u32[]{:S(2)}) collective-permute-start(bf16[2,4,64,128]{3,2,1,0:T(8,128)(2,1)S(1)} %get-tuple-element.117), channel_id=1, source_target_pairs={{0,8},{8,0},{16,24},{24,16},{1,9},{9,1},{17,25},{25,17},{2,10},{10... | collective-permute-start | bytes 393224 | tf_op jit(solution)/shard_map/ppermute | solution.py:694
  74.5 4.7 %collective-permute-start.23 = (bf16[608,128]{1,0:T(8,128)(2,1)S(1)}, bf16[608,128]{1,0:T(8,128)(2,1)S(1)}, u32[]{:S(2)}, u32[]{:S(2)}) collective-permute-start(bf16[608,128]{1,0:T(8,128)(2,1)S(1)} %add_convert_fusion.2.refs_0_), channel_id=1, source_target_pairs={{0,8},{8,0},{16,24},{24,16},{1,9},{9,1},{17,25},{25,17},{2,10},{10... | collective-permute-start | bytes 466952 | tf_op jit(solution)/shard_map/ppermute | solution.py:694
  76.5 2.8 %collective-permute-start.24 = (bf16[608,128]{1,0:T(8,128)(2,1)S(1)}, bf16[608,128]{1,0:T(8,128)(2,1)S(1)}, u32[]{:S(2)}, u32[]{:S(2)}) collective-permute-start(bf16[608,128]{1,0:T(8,128)(2,1)S(1)} %collective-permute-done.17.refs_1_), channel_id=1, source_target_pairs={{0,8},{8,0},{16,24},{24,16},{1,9},{9,1},{17,25},{25,17},{2,10},{10... | collective-permute-start | bytes 466952 | tf_op jit(solution)/shard_map/ppermute | solution.py:694
  77.0 2.3 %collective-permute-start.25 = (bf16[608,128]{1,0:T(8,128)(2,1)S(1)}, bf16[608,128]{1,0:T(8,128)(2,1)S(1)}, u32[]{:S(2)}, u32[]{:S(2)}) collective-permute-start(bf16[608,128]{1,0:T(8,128)(2,1)S(1)} %collective-permute-done.18.refs_2_), channel_id=1, source_target_pairs={{0,8},{8,0},{16,24},{24,16},{1,9},{9,1},{17,25},{25,17},{2,10},{10... | collective-permute-start | bytes 466952 | tf_op jit(solution)/shard_map/ppermute | solution.py:694
  77.1 2.2 %collective-permute-start.26 = (bf16[608,128]{1,0:T(8,128)(2,1)S(1)}, bf16[608,128]{1,0:T(8,128)(2,1)S(1)}, u32[]{:S(2)}, u32[]{:S(2)}) collective-permute-start(bf16[608,128]{1,0:T(8,128)(2,1)S(1)} %collective-permute-done.19.refs_3_), channel_id=1, source_target_pairs={{0,8},{8,0},{16,24},{24,16},{1,9},{9,1},{17,25},{25,17},{2,10},{10... | collective-permute-start | bytes 466952 | tf_op jit(solution)/shard_map/ppermute | solution.py:694

commit v5 on v4

--- a/solution.py
+++ b/solution.py
@@ -720,6 +720,8 @@
     pieces, refs = refs[: 4 * (half + 1)], refs[4 * (half + 1) :]
     if half:
         refs = refs[6:]
+    else:
+        grads, refs = refs[:4], refs[4:]
     (q, sr, kv, out, fc1, fc2), refs = refs[:6], refs[6:]
     stage, small_dw, small_ln1, small_ln2, small_srg, sems = refs[-6:]
     copies = []
@@ -732,6 +734,9 @@
         core, first = (place[1], place[2]) if j < 4 else (1 - place[1], place[3])
         return core * 4 + (first ^ (j % 4))
 
+    if not half:
+        for k in range(4):
+            move(grads[k], refs[0].at[pl.ds(2 * (place[0] ^ k), 2)])
     for k in range(4):
         c = chunk_of(4 * half + k)
         stage[k] = pieces[4 * half + k][...].astype(F32)
@@ -762,7 +767,7 @@
         copy.wait()
 
 
-def finish(place, pieces, earlier=()):
+def finish(place, pieces, earlier=(), grads=(), shape=None):
     far, near = pl.BlockSpec(memory_space=pl.ANY), pl.BlockSpec(memory_space=VMEM)
     half = 1 if earlier else 0
     shapes = [((D, D), F32), ((2048, D), F32), ((D, 2 * D), F32), ((D, D), F32), ((D, FF), F32), ((FF, D), F32)]
@@ -770,7 +775,10 @@
     if half:
         shapes += [((3, 3, FF), F32), ((D,), F32), ((D,), F32), ((D,), F32)]
         specs += [far] * 4
-    before = 1 + len(pieces)
+    else:
+        shapes += [(shape, BF)]
+        specs += [far]
+    before = 1 + len(pieces) + len(grads)
     return pl.pallas_call(
         functools.partial(finish_kernel, half),
         out_shape=[jax.ShapeDtypeStruct(*each) for each in shapes],
@@ -784,7 +792,7 @@
         compiler_params=pltpu.CompilerParams(vmem_limit_bytes=8 * 2**20),
         cost_estimate=pl.CostEstimate(flops=0, bytes_accessed=4 * 2**20, transcendentals=0),
         name="finish",
-    )(place, *pieces, *earlier)
+    )(place, *pieces, *grads, *earlier)
 
 
 def gather_kernel(place, part0, part1, part2, part3, out, sems):
@@ -857,14 +865,13 @@
     mine, block[2] = lax.optimization_barrier((mine, block[2]))
     got = [g.astype(F32) for g in to_four([mine] * 4, 1)]
     got, block_out = lax.optimization_barrier((got, gather_rows(place, block, tokens.shape)))
-    got, block[3] = lax.optimization_barrier((got, block[3]))
+    got, inputs[1], inputs[2] = lax.optimization_barrier((got, inputs[1], inputs[2]))
     total = ((mine.astype(F32) + got[0]) + (got[1] + got[2])).astype(BF)
     got = to_four([total] * 4, 0)
-    got, inputs[2], inputs[3] = lax.optimization_barrier((got, inputs[2], inputs[3]))
-    got, input_grad = lax.optimization_barrier((got, gather_rows(place, inputs, tokens.shape)))
+    got, inputs[3] = lax.optimization_barrier((got, inputs[3]))
     pieces = (total, *got)
     others = tuple(over_rows(piece, 1) for piece in pieces)
-    half = finish(place, pieces)
+    *half, input_grad = finish(place, pieces, (), inputs, tokens.shape)
     q, sr, kv, out, fc1, fc2, dw, ln1_sum, ln2_sum, srg_sum = finish(place, pieces + others, half)
     return block_out, input_grad, ln1_sum, q, sr, srg_sum, kv, out, ln2_sum, fc1, dw, fc2
 

time: 81.5 us -> 80.4 us (0.987)
  waiting for transfers between devices: 17.8 us -> 19.7 us
  starting transfers between devices: 26.3 us -> 24.6 us
  Pallas kernels: 33.9 us -> 32.7 us
    ppermute x9, waiting for transfers between devices: 2.35 us -> 6.62 us  [over_four(): return lax.ppermute(value, ('rows', 'batch'), pairs)]
    ppermute x18, waiting for transfers between devices: 15.4 us -> 13 us  [over_rows(): return lax.ppermute(value, 'rows', [(i, i ^ k) for i in range(4)])]
    ppermute x18, starting transfers between devices: 14.3 us -> 12.5 us  [over_rows(): return lax.ppermute(value, 'rows', [(i, i ^ k) for i in range(4)])]
    pallas_call x2 -> x1, Pallas kernels: 2.72 us -> 1.36 us  [gather_rows(): pl.pallas_call(gather_kernel, out_shape=jax.ShapeDtypeStruct(shape, BF),...]
  transfers between devices with their start and end apart: 27 -> 27, of which waited for: 8 -> 8; matrix products, arithmetic and copies ran while one was open for 1% -> 1% of each run, Pallas kernels for 16% -> 14%
where the time goes in v5:
time: 80.4 us; the launch traced here: 80.3 us
  Pallas kernels  32.7 us (41%)
  starting transfers between devices  24.6 us (31%)
  waiting for transfers between devices  19.7 us (25%)
  local copies, waits for them, and re-layouts  1.68 us (2%)
  between operations  1.22 us (2%)
    pallas_call x4, Pallas kernels, call(): pl.pallas_call(kernel, out_shape=[jax.ShapeDtypeStruct(shape, kind) for s...  27.6 us
    ppermute x18, waiting for transfers between devices, over_rows(): return lax.ppermute(value, 'rows', [(i, i ^ k) for i in range(4)])  13 us
    ppermute x18, starting transfers between devices, over_rows(): return lax.ppermute(value, 'rows', [(i, i ^ k) for i in range(4)])  12.5 us
    ppermute x9, starting transfers between devices, over_four(): return lax.ppermute(value, ('rows', 'batch'), pairs)  12 us
    ppermute x9, waiting for transfers between devices, over_four(): return lax.ppermute(value, ('rows', 'batch'), pairs)  6.62 us
    pallas_call x2, Pallas kernels, finish(): pl.pallas_call(functools.partial(finish_kernel, half), out_shape=[jax.Sha...  3.8 us
  transfers between devices with their start and end apart: 27, of which 8 were waited for; matrix products, arithmetic and copies ran while one was open for 1% of the time, Pallas kernels for 14%

profile of v5, /device:TPU:0, one launch (start us, length us, event | category | flops | bytes accessed | tf_op | source)
XLA Modules:
  0.0 80.3 jit_solution(12112505316539835015)
XLA Ops:
  0.7 1.1 %constant_dynamic-slice_fusion.3 = (bf16[2,4,64,128]{3,2,1,0:T(8,128)(2,1)S(1)}, bf16[2,4,64,128]{3,2,1,0:T(8,128)(2,1)S(1)}, bf16[2,4,64,128]{3,2,1,0:T(8,128)(2,1)S(1)}) fusion(bf16[8,4,64,128]{3,2,1,0:T(8,128)(2,1)} %own.1, s32[]{:T(128)S(6)} %select_n.28, s32[]{:T(128)S(6)} %select_n.27, s32[]{:T(128)S(6)} %select_n.26), kind=kLoop, calls=%fused_computation.16 | loop fusion | bytes 786444 | tf_op jit(solution)/shard_map/dynamic_slice | solution.py:835
  1.8 2.5 %collective-permute-start.2 = (bf16[2,4,64,128]{3,2,1,0:T(8,128)(2,1)S(1)}, bf16[2,4,64,128]{3,2,1,0:T(8,128)(2,1)S(1)}, u32[]{:S(2)}, u32[]{:S(2)}) collective-permute-start(bf16[2,4,64,128]{3,2,1,0:T(8,128)(2,1)S(1)} %get-tuple-element.139), channel_id=1, source_target_pairs={{0,24},{8,16},{16,8},{24,0},{1,25},{9,17},{17,9},{25,1},{2,26},{10... | collective-permute-start | bytes 393224 | tf_op jit(solution)/shard_map/ppermute | solution.py:694
  4.3 0.6 collective-permute-start.1
  5.1 1.2 %collective-permute-done.near1 = bf16[2,4,64,128]{3,2,1,0:T(8,128)(2,1)S(1)} collective-permute-done((bf16[2,4,64,128]{3,2,1,0:T(8,128)(2,1)S(1)}, bf16[2,4,64,128]{3,2,1,0:T(8,128)(2,1)S(1)}, u32[]{:S(2)}, u32[]{:S(2)}) %collective-permute-start) | collective-permute-done | bytes 131104 | tf_op jit(solution)/shard_map/ppermute | solution.py:694
  6.3 1.5 %collective-permute-start.5 = (bf16[2,4,64,128]{3,2,1,0:T(8,128)(2,1)S(1)}, bf16[2,4,64,128]{3,2,1,0:T(8,128)(2,1)S(1)}, u32[]{:S(2)}, u32[]{:S(2)}) collective-permute-start(bf16[2,4,64,128]{3,2,1,0:T(8,128)(2,1)S(1)} %get-tuple-element.136), channel_id=1, source_target_pairs={{0,24},{8,16},{16,8},{24,0},{1,25},{9,17},{17,9},{25,1},{2,26},{10... | collective-permute-start | bytes 393224 | tf_op jit(solution)/shard_map/ppermute | solution.py:694
  7.8 0.4 collective-permute-start.4
  8.2 0.1 collective-permute-start.3
  8.3 0.1 dynamic_slice.24
  8.4 0.1 dynamic_slice.25
  8.4 0.2 concatenate.19.taps
  8.6 0.1 concatenate.18.place
  8.7 3.2 %collective-permute-done.1.near2 = bf16[2,4,64,128]{3,2,1,0:T(8,128)(2,1)S(1)} collective-permute-done((bf16[2,4,64,128]{3,2,1,0:T(8,128)(2,1)S(1)}, bf16[2,4,64,128]{3,2,1,0:T(8,128)(2,1)S(1)}, u32[]{:S(2)}, u32[]{:S(2)}) %collective-permute-start.1) | collective-permute-done | bytes 131104 | tf_op jit(solution)/shard_map/ppermute | solution.py:694
  11.9 3.5 %attend.1 = (bf16[2048,128]{1,0:T(8,128)(2,1)S(1)}, bf16[2048,128]{1,0:T(8,128)(2,1)S(1)}, bf16[2048,128]{1,0:T(8,128)(2,1)S(1)}, f32[2048,128]{1,0:T(8,128)S(1)...) custom-call(s32[8]{0:T(128)S(1)} %concatenate.18.place, ...), custom_call_target="tpu_custom_call" | custom-call | flops 1000000000 | bytes 4194304 | tf_op jit(solution)/shard_map/attend/pallas_call | solution.py:619
  15.4 1.3 %collective-permute-done.4.cot2 = bf16[2,4,64,128]{3,2,1,0:T(8,128)(2,1)S(1)} collective-permute-done((bf16[2,4,64,128]{3,2,1,0:T(8,128)(2,1)S(1)}, bf16[2,4,64,128]{3,2,1,0:T(8,128)(2,1)S(1)}, u32[]{:S(2)}, u32[]{:S(2)}) %collective-permute-start.4) | collective-permute-done | bytes 131104 | tf_op jit(solution)/shard_map/ppermute | solution.py:694
  16.8 19.3 %feed.1 = (bf16[2,4,64,128]{3,2,1,0:T(8,128)(2,1)S(1)}, bf16[2,4,64,128]{3,2,1,0:T(8,128)(2,1)S(1)}, bf16[2,4,64,128]{3,2,1,0:T(8,128)(2,1)S(1)}, bf16[2,4,64,12...) custom-call(s32[8]{0:T(128)S(1)} %concatenate.18.place, ...), custom_call_target="tpu_custom_call" | custom-call | flops 16000000000 | bytes 4194304 | tf_op jit(solution)/shard_map/feed/pallas_call | solution.py:619
  36.0 0.1 collective-permute-start.6
  36.1 2.9 %back.1 = (bf16[2048,128]{1,0:T(8,128)(2,1)S(1)}, bf16[128,128]{1,0:T(8,128)(2,1)S(1)}, bf16[1344,128]{1,0:T(8,128)(2,1)S(1)}, bf16[1344,128]{1,0:T(8,128)(2,1)S(1)}) custom-call(s32[8]{0:T(128)S(1)} %concatenate.18.place, bf16[2048,128]{1,0:T(8,128)(2,1)S(1)} %get-tuple-element.78.normed, bf16[2048,128]{1,0:T(8,128)(2,1)S(1)} %get-tuple-element.79.query, ...), custom_call_target="tpu_custom_call" | custom-call | flops 2000000000 | bytes 4194304 | tf_op jit(solution)/shard_map/back/pallas_call | solution.py:619
  39.1 0.6 collective-permute-start.7
  39.6 0.1 add_convert_fusion.1
  39.7 1.2 %collective-permute-done.7 = bf16[1344,128]{1,0:T(8,128)(2,1)S(1)} collective-permute-done((bf16[1344,128]{1,0:T(8,128)(2,1)S(1)}, bf16[1344,128]{1,0:T(8,128)(2,1)S(1)}, u32[]{:S(2)}, u32[]{:S(2)}) %collective-permute-start.7) | collective-permute-done | bytes 344096 | tf_op jit(solution)/shard_map/ppermute | solution.py:694
  40.9 0.1 add_convert_fusion
  41.1 2.3 %collective-permute-start.8 = (bf16[608,128]{1,0:T(8,128)(2,1)S(1)}, bf16[608,128]{1,0:T(8,128)(2,1)S(1)}, u32[]{:S(2)}, u32[]{:S(2)}) collective-permute-start(bf16[608,128]{1,0:T(8,128)(2,1)S(1)} %pad_maximum_fusion), channel_id=1, source_target_pairs={{0,1},{1,0},{2,3},{3,2},{4,5},{5,4},{6,7},{7,6},{8,10},{9,11},{10,... | collective-permute-start | bytes 466952 | tf_op jit(solution)/shard_map/ppermute | solution.py:700
  43.4 1.6 %collective-permute-start.9 = (bf16[608,128]{1,0:T(8,128)(2,1)S(1)}, bf16[608,128]{1,0:T(8,128)(2,1)S(1)}, u32[]{:S(2)}, u32[]{:S(2)}) collective-permute-start(bf16[608,128]{1,0:T(8,128)(2,1)S(1)} %pad_maximum_fusion.1), channel_id=1, source_target_pairs={{0,16},{1,17},{2,18},{3,19},{4,20},{5,21},{6,22},{7,23},{8,12},{9,... | collective-permute-start | bytes 466952 | tf_op jit(solution)/shard_map/ppermute | solution.py:700
  45.0 0.1 collective-permute-start.10
  45.1 2.0 %collective-permute-start.11 = (bf16[2,4,64,128]{3,2,1,0:T(8,128)(2,1)S(1)}, bf16[2,4,64,128]{3,2,1,0:T(8,128)(2,1)S(1)}, u32[]{:S(2)}, u32[]{:S(2)}) collective-permute-start(bf16[2,4,64,128]{3,2,1,0:T(8,128)(2,1)S(1)} %get-tuple-element.96), channel_id=1, source_target_pairs={{0,16},{8,24},{16,0},{24,8},{1,17},{9,25},{17,1},{25,9},{2,18},{10... | collective-permute-start | bytes 393224 | tf_op jit(solution)/shard_map/ppermute | solution.py:694
  47.1 0.3 collective-permute-start.15
  47.4 1.9 %input_gradient.1 = (bf16[2,4,64,128]{3,2,1,0:T(8,128)(2,1)S(1)}, bf16[2,4,64,128]{3,2,1,0:T(8,128)(2,1)S(1)}, bf16[2,4,64,128]{3,2,1,0:T(8,128)(2,1)S(1)}, bf16[2,4,64,128]{3,2,1,0:T(8,128)(2,1)S(1)}) custom-call(s32[8]{0:T(128)S(1)} %concatenate.18.place, bf16[2048,128]{1,0:T(8,128)(2,1)S(1)} %get-tuple-element.88.x, ...), custom_call_target="tpu_custom_call" | custom-call | flops 1000000000 | bytes 4194304 | tf_op jit(solution)/shard_map/input_gradient/pallas_call | solution.py:619
  49.2 0.2 collective-permute-start.16
  49.4 1.9 %collective-permute-done.10 = bf16[608,128]{1,0:T(8,128)(2,1)S(1)} collective-permute-done((bf16[608,128]{1,0:T(8,128)(2,1)S(1)}, bf16[608,128]{1,0:T(8,128)(2,1)S(1)}, u32[]{:S(2)}, u32[]{:S(2)}) %collective-permute-start.10) | collective-permute-done | bytes 155680 | tf_op jit(solution)/shard_map/ppermute | solution.py:700
  51.3 0.1 add_convert_fusion.3
  51.4 1.8 %collective-permute-done.11.part2 = bf16[2,4,64,128]{3,2,1,0:T(8,128)(2,1)S(1)} collective-permute-done((bf16[2,4,64,128]{3,2,1,0:T(8,128)(2,1)S(1)}, bf16[2,4,64,128]{3,2,1,0:T(8,128)(2,1)S(1)}, u32[]{:S(2)}, u32[]{:S(2)}) %collective-permute-start.11) | collective-permute-done | bytes 131104 | tf_op jit(solution)/shard_map/ppermute | solution.py:694
  53.2 3.9 %collective-permute-start.14 = (bf16[608,128]{1,0:T(8,128)(2,1)S(1)}, bf16[608,128]{1,0:T(8,128)(2,1)S(1)}, u32[]{:S(2)}, u32[]{:S(2)}) collective-permute-start(bf16[608,128]{1,0:T(8,128)(2,1)S(1)} %add_convert_fusion.3), channel_id=1, source_target_pairs={{0,6},{1,7},{2,4},{3,5},{4,2},{5,3},{6,0},{7,1},{8,25},{9,24},{10,... | collective-permute-start | bytes 466952 | tf_op jit(solution)/shard_map/ppermute | solution.py:700
  57.1 0.2 collective-permute-start.13
  57.3 0.4 collective-permute-start.12
  57.7 1.5 %collective-permute-start.18 = (bf16[2,4,64,128]{3,2,1,0:T(8,128)(2,1)S(1)}, bf16[2,4,64,128]{3,2,1,0:T(8,128)(2,1)S(1)}, u32[]{:S(2)}, u32[]{:S(2)}) collective-permute-start(bf16[2,4,64,128]{3,2,1,0:T(8,128)(2,1)S(1)} %get-tuple-element.107), channel_id=1, source_target_pairs={{0,16},{8,24},{16,0},{24,8},{1,17},{9,25},{17,1},{25,9},{2,18},{10... | collective-permute-start | bytes 393224 | tf_op jit(solution)/shard_map/ppermute | solution.py:694
  59.2 1.4 %gather_rows.1 = bf16[8,4,64,128]{3,2,1,0:T(8,128)(2,1)} custom-call(s32[8]{0:T(128)S(1)} %concatenate.18.place, bf16[2,4,64,128]{3,2,1,0:T(8,128)(2,1)S(1)} %get-tuple-element.98.part0, bf16[2,4,64,128]{3,2,1,0:T(8,128)(2,1)S(1)} %collective-permute-done.15.part1, bf16[2,4,64,128]{3,2,1,0:T(8,128)(2,1)S(1)} %collective-permute-done.11.part2, ...), custom_call_target="tpu_custom_call" | custom-call | tf_op jit(solution)/shard_map/gather_rows/pallas_call | solution.py:811
  60.6 4.7 %collective-permute-done.13 = bf16[608,128]{1,0:T(8,128)(2,1)S(1)} collective-permute-done((bf16[608,128]{1,0:T(8,128)(2,1)S(1)}, bf16[608,128]{1,0:T(8,128)(2,1)S(1)}, u32[]{:S(2)}, u32[]{:S(2)}) %collective-permute-start.13) | collective-permute-done | bytes 155680 | tf_op jit(solution)/shard_map/ppermute | solution.py:700
  65.4 0.1 add_convert_fusion.2.refs_0_
  65.5 0.7 collective-permute-start.21
  66.2 0.9 %collective-permute-start.20 = (bf16[608,128]{1,0:T(8,128)(2,1)S(1)}, bf16[608,128]{1,0:T(8,128)(2,1)S(1)}, u32[]{:S(2)}, u32[]{:S(2)}) collective-permute-start(bf16[608,128]{1,0:T(8,128)(2,1)S(1)} %add_convert_fusion.2.refs_0_), channel_id=1, source_target_pairs={{0,16},{1,17},{2,18},{3,19},{4,20},{5,21},{6,22},{7,23},{8,12},{9,... | collective-permute-start | bytes 466952 | tf_op jit(solution)/shard_map/ppermute | solution.py:700
  67.0 2.0 %collective-permute-start.19 = (bf16[608,128]{1,0:T(8,128)(2,1)S(1)}, bf16[608,128]{1,0:T(8,128)(2,1)S(1)}, u32[]{:S(2)}, u32[]{:S(2)}) collective-permute-start(bf16[608,128]{1,0:T(8,128)(2,1)S(1)} %add_convert_fusion.2.refs_0_), channel_id=1, source_target_pairs={{0,1},{1,0},{2,3},{3,2},{4,5},{5,4},{6,7},{7,6},{8,10},{9,11},{10,... | collective-permute-start | bytes 466952 | tf_op jit(solution)/shard_map/ppermute | solution.py:700
  69.0 1.5 %collective-permute-start.23 = (bf16[608,128]{1,0:T(8,128)(2,1)S(1)}, bf16[608,128]{1,0:T(8,128)(2,1)S(1)}, u32[]{:S(2)}, u32[]{:S(2)}) collective-permute-start(bf16[608,128]{1,0:T(8,128)(2,1)S(1)} %add_convert_fusion.2.refs_0_), channel_id=1, source_target_pairs={{0,8},{8,0},{16,24},{24,16},{1,9},{9,1},{17,25},{25,17},{2,10},{10... | collective-permute-start | bytes 466952 | tf_op jit(solution)/shard_map/ppermute | solution.py:694
  70.6 4.3 %collective-permute-done.22.refs_7_ = bf16[2,4,64,128]{3,2,1,0:T(8,128)(2,1)S(1)} collective-permute-done((bf16[2,4,64,128]{3,2,1,0:T(8,128)(2,1)S(1)}, bf16[2,4,64,128]{3,2,1,0:T(8,128)(2,1)S(1)}, u32[]{:S(2)}, u32[]{:S(2)}) %collective-permute-start.22) | collective-permute-done | bytes 131104 | tf_op jit(solution)/shard_map/ppermute | solution.py:694
  74.9 0.8 %collective-permute-start.24 = (bf16[608,128]{1,0:T(8,128)(2,1)S(1)}, bf16[608,128]{1,0:T(8,128)(2,1)S(1)}, u32[]{:S(2)}, u32[]{:S(2)}) collective-permute-start(bf16[608,128]{1,0:T(8,128)(2,1)S(1)} %collective-permute-done.19.refs_1_), channel_id=1, source_target_pairs={{0,8},{8,0},{16,24},{24,16},{1,9},{9,1},{17,25},{25,17},{2,10},{10... | collective-permute-start | bytes 466952 | tf_op jit(solution)/shard_map/ppermute | solution.py:694
  75.8 0.1 collective-permute-start.25
  75.8 0.4 collective-permute-start.26
  76.3 2.0 %finish.2 = (f32[128,128]{1,0:T(8,128)}, f32[2048,128]{1,0:T(8,128)}, f32[128,256]{1,0:T(8,128)}, f32[128,128]{1,0:T(8,128)}, f32[128,1024]{1,0:T(8,128)}, /*ind...) custom-call(s32[8]{0:T(128)S(1)} %concatenate.18.place, bf16[608,128]{1,0:T(8,128)(2,1)S(1)} %add_convert_fusion.2.refs_0_, ...), custom_call_target="tpu_custom_call" | custom-call | bytes 4194304 | tf_op jit(solution)/shard_map/finish/pallas_call | solution.py:782
  78.3 1.8 %finish.3 = (f32[128,128]{1,0:T(8,128)}, f32[2048,128]{1,0:T(8,128)}, f32[128,256]{1,0:T(8,128)}, f32[128,128]{1,0:T(8,128)}, f32[128,1024]{1,0:T(8,128)}, /*ind...) custom-call(s32[8]{0:T(128)S(1)} %concatenate.18.place, ...), custom_call_target="tpu_custom_call", output_to_operand_aliasing={{0}: (9, {}), {1}: (10, {}), {2}: (11, {}), {3}: (12, {}), ... | custom-call | bytes 4194304 | tf_op jit(solution)/shard_map/finish/pallas_call | solution.py:782
  (64 shorter events, 0.4 us)
Async XLA Ops:
  0.6 5.6 %copy-start.1 = (bf16[8,4,64,128]{3,2,1,0:T(8,128)(2,1)S(1)}, bf16[8,4,64,128]{3,2,1,0:T(8,128)(2,1)}, u32[]{:S(2)}) copy-start(bf16[8,4,64,128]{3,2,1,0:T(8,128)(2,1)} %cot) | copy-start | bytes 1572868
  0.7 4.3 %copy-start.8 = (bf16[3,3,1024]{2,1,0:T(4,128)(2,1)S(1)}, bf16[3,3,1024]{2,1,0:T(4,128)(2,1)}, u32[]{:S(2)}) copy-start(bf16[3,3,1024]{2,1,0:T(4,128)(2,1)} %param.25) | copy-start | bytes 55300
  1.8 6.9 %collective-permute-start.2 = (bf16[2,4,64,128]{3,2,1,0:T(8,128)(2,1)S(1)}, bf16[2,4,64,128]{3,2,1,0:T(8,128)(2,1)S(1)}, u32[]{:S(2)}, u32[]{:S(2)}) collective-permute-start(bf16[2,4,64,128]{3,2,1,0:T(8,128)(2,1)S(1)} %get-tuple-element.139), channel_id=1, source_target_pairs={{0,24},{8,16},{16,8},{24,0},{1,25},{9,17},{17,9},{25,1},{2,26},{10... | collective-permute-start | bytes 393224 | tf_op jit(solution)/shard_map/ppermute | solution.py:694
  4.3 7.6 %collective-permute-start.1 = (bf16[2,4,64,128]{3,2,1,0:T(8,128)(2,1)S(1)}, bf16[2,4,64,128]{3,2,1,0:T(8,128)(2,1)S(1)}, u32[]{:S(2)}, u32[]{:S(2)}) collective-permute-start(bf16[2,4,64,128]{3,2,1,0:T(8,128)(2,1)S(1)} %get-tuple-element.140), channel_id=1, source_target_pairs={{0,16},{8,24},{16,0},{24,8},{1,17},{9,25},{17,1},{25,9},{2,18},{10... | collective-permute-start | bytes 393224 | tf_op jit(solution)/shard_map/ppermute | solution.py:694
  4.9 1.3 %collective-permute-start = (bf16[2,4,64,128]{3,2,1,0:T(8,128)(2,1)S(1)}, bf16[2,4,64,128]{3,2,1,0:T(8,128)(2,1)S(1)}, u32[]{:S(2)}, u32[]{:S(2)}) collective-permute-start(bf16[2,4,64,128]{3,2,1,0:T(8,128)(2,1)S(1)} %get-tuple-element.141), channel_id=1, source_target_pairs={{0,8},{8,0},{16,24},{24,16},{1,9},{9,1},{17,25},{25,17},{2,10},{10... | collective-permute-start | bytes 393224 | tf_op jit(solution)/shard_map/ppermute | solution.py:694
  5.0 6.9 %copy-start.7 = (bf16[128,128]{1,0:T(8,128)(2,1)S(1)}, bf16[128,128]{1,0:T(8,128)(2,1)}, u32[]{:S(2)}) copy-start(bf16[128,128]{1,0:T(8,128)(2,1)} %wq.5) | copy-start | bytes 98308
  5.0 6.9 %copy-start.5 = (bf16[128,256]{1,0:T(8,128)(2,1)S(1)}, bf16[128,256]{1,0:T(8,128)(2,1)}, u32[]{:S(2)}) copy-start(bf16[128,256]{1,0:T(8,128)(2,1)} %wkv.3) | copy-start | bytes 196612
  5.0 3.2 %copy-start.9 = (f32[128]{0:T(128)S(1)}, f32[128]{0:T(128)}, u32[]{:S(2)}) copy-start(f32[128]{0:T(128)} %param.23) | copy-start | bytes 1540
  5.0 3.2 %copy-start.10 = (f32[128]{0:T(128)S(1)}, f32[128]{0:T(128)}, u32[]{:S(2)}) copy-start(f32[128]{0:T(128)} %param.20) | copy-start | bytes 1540
  5.0 3.2 %copy-start.11 = (f32[128]{0:T(128)S(1)}, f32[128]{0:T(128)}, u32[]{:S(2)}) copy-start(f32[128]{0:T(128)} %param.17) | copy-start | bytes 1540
  5.0 3.2 %copy-start.12 = (s32[8]{0:T(128)S(1)}, s32[8]{0:T(128)}, u32[]{:S(2)}) copy-start(s32[8]{0:T(128)} %param.15) | copy-start | bytes 100
  5.0 3.3 %copy-start.13 = (s32[8]{0:T(128)S(1)}, s32[8]{0:T(128)}, u32[]{:S(2)}) copy-start(s32[8]{0:T(128)} %param.16) | copy-start | bytes 100
  5.1 6.9 %copy-start.2 = (bf16[2048,128]{1,0:T(8,128)(2,1)S(1)}, bf16[2048,128]{1,0:T(8,128)(2,1)}, u32[]{:S(2)}) copy-start(bf16[2048,128]{1,0:T(8,128)(2,1)} %wsr.5) | copy-start | bytes 1572868
  5.1 6.8 %copy-start = (bf16[8,4,64,128]{3,2,1,0:T(8,128)(2,1)S(1)}, bf16[8,4,64,128]{3,2,1,0:T(8,128)(2,1)}, u32[]{:S(2)}) copy-start(bf16[8,4,64,128]{3,2,1,0:T(8,128)(2,1)} %own.1) | copy-start | bytes 1572868
  6.3 9.1 %collective-permute-start.5 = (bf16[2,4,64,128]{3,2,1,0:T(8,128)(2,1)S(1)}, bf16[2,4,64,128]{3,2,1,0:T(8,128)(2,1)S(1)}, u32[]{:S(2)}, u32[]{:S(2)}) collective-permute-start(bf16[2,4,64,128]{3,2,1,0:T(8,128)(2,1)S(1)} %get-tuple-element.136), channel_id=1, source_target_pairs={{0,24},{8,16},{16,8},{24,0},{1,25},{9,17},{17,9},{25,1},{2,26},{10... | collective-permute-start | bytes 393224 | tf_op jit(solution)/shard_map/ppermute | solution.py:694
  7.8 9.0 %collective-permute-start.4 = (bf16[2,4,64,128]{3,2,1,0:T(8,128)(2,1)S(1)}, bf16[2,4,64,128]{3,2,1,0:T(8,128)(2,1)S(1)}, u32[]{:S(2)}, u32[]{:S(2)}) collective-permute-start(bf16[2,4,64,128]{3,2,1,0:T(8,128)(2,1)S(1)} %get-tuple-element.137), channel_id=1, source_target_pairs={{0,16},{8,24},{16,0},{24,8},{1,17},{9,25},{17,1},{25,9},{2,18},{10... | collective-permute-start | bytes 393224 | tf_op jit(solution)/shard_map/ppermute | solution.py:694
  8.2 8.6 %collective-permute-start.3 = (bf16[2,4,64,128]{3,2,1,0:T(8,128)(2,1)S(1)}, bf16[2,4,64,128]{3,2,1,0:T(8,128)(2,1)S(1)}, u32[]{:S(2)}, u32[]{:S(2)}) collective-permute-start(bf16[2,4,64,128]{3,2,1,0:T(8,128)(2,1)S(1)} %get-tuple-element.138), channel_id=1, source_target_pairs={{0,8},{8,0},{16,24},{24,16},{1,9},{9,1},{17,25},{25,17},{2,10},{10... | collective-permute-start | bytes 393224 | tf_op jit(solution)/shard_map/ppermute | solution.py:694
  8.4 3.5 %copy-start.6 = (bf16[128,128]{1,0:T(8,128)(2,1)S(1)}, bf16[128,128]{1,0:T(8,128)(2,1)}, u32[]{:S(2)}) copy-start(bf16[128,128]{1,0:T(8,128)(2,1)} %wout.3) | copy-start | bytes 98308
  8.7 8.1 %copy-start.3 = (bf16[128,1024]{1,0:T(8,128)(2,1)S(1)}, bf16[128,1024]{1,0:T(8,128)(2,1)}, u32[]{:S(2)}) copy-start(bf16[128,1024]{1,0:T(8,128)(2,1)} %wfc1.1) | copy-start | bytes 786436
  8.7 8.1 %copy-start.4 = (bf16[1024,128]{1,0:T(8,128)(2,1)S(1)}, bf16[1024,128]{1,0:T(8,128)(2,1)}, u32[]{:S(2)}) copy-start(bf16[1024,128]{1,0:T(8,128)(2,1)} %wfc2.1) | copy-start | bytes 786436
  36.0 3.6 %collective-permute-start.6 = (bf16[1088,128]{1,0:T(8,128)(2,1)S(1)}, bf16[1088,128]{1,0:T(8,128)(2,1)S(1)}, u32[]{:S(2)}, u32[]{:S(2)}) collective-permute-start(bf16[1088,128]{1,0:T(8,128)(2,1)S(1)} %get-tuple-element.77), channel_id=1, source_target_pairs={{0,8},{8,0},{16,24},{24,16},{1,9},{9,1},{17,25},{25,17},{2,10},{10... | collective-permute-start | bytes 835592 | tf_op jit(solution)/shard_map/ppermute | solution.py:694
  39.1 1.8 %collective-permute-start.7 = (bf16[1344,128]{1,0:T(8,128)(2,1)S(1)}, bf16[1344,128]{1,0:T(8,128)(2,1)S(1)}, u32[]{:S(2)}, u32[]{:S(2)}) collective-permute-start(bf16[1344,128]{1,0:T(8,128)(2,1)S(1)} %get-tuple-element.87), channel_id=1, source_target_pairs={{0,8},{8,0},{16,24},{24,16},{1,9},{9,1},{17,25},{25,17},{2,10},{10... | collective-permute-start | bytes 1032200 | tf_op jit(solution)/shard_map/ppermute | solution.py:694
  41.1 8.2 %collective-permute-start.8 = (bf16[608,128]{1,0:T(8,128)(2,1)S(1)}, bf16[608,128]{1,0:T(8,128)(2,1)S(1)}, u32[]{:S(2)}, u32[]{:S(2)}) collective-permute-start(bf16[608,128]{1,0:T(8,128)(2,1)S(1)} %pad_maximum_fusion), channel_id=1, source_target_pairs={{0,1},{1,0},{2,3},{3,2},{4,5},{5,4},{6,7},{7,6},{8,10},{9,11},{10,... | collective-permute-start | bytes 466952 | tf_op jit(solution)/shard_map/ppermute | solution.py:700
  43.4 6.0 %collective-permute-start.9 = (bf16[608,128]{1,0:T(8,128)(2,1)S(1)}, bf16[608,128]{1,0:T(8,128)(2,1)S(1)}, u32[]{:S(2)}, u32[]{:S(2)}) collective-permute-start(bf16[608,128]{1,0:T(8,128)(2,1)S(1)} %pad_maximum_fusion.1), channel_id=1, source_target_pairs={{0,16},{1,17},{2,18},{3,19},{4,20},{5,21},{6,22},{7,23},{8,12},{9,... | collective-permute-start | bytes 466952 | tf_op jit(solution)/shard_map/ppermute | solution.py:700
  45.0 6.3 %collective-permute-start.10 = (bf16[608,128]{1,0:T(8,128)(2,1)S(1)}, bf16[608,128]{1,0:T(8,128)(2,1)S(1)}, u32[]{:S(2)}, u32[]{:S(2)}) collective-permute-start(bf16[608,128]{1,0:T(8,128)(2,1)S(1)} %pad_maximum_fusion.2), channel_id=1, source_target_pairs={{0,17},{1,16},{2,19},{3,18},{4,21},{5,20},{6,23},{7,22},{8,14},{9,... | collective-permute-start | bytes 466952 | tf_op jit(solution)/shard_map/ppermute | solution.py:700
  45.1 8.1 %collective-permute-start.11 = (bf16[2,4,64,128]{3,2,1,0:T(8,128)(2,1)S(1)}, bf16[2,4,64,128]{3,2,1,0:T(8,128)(2,1)S(1)}, u32[]{:S(2)}, u32[]{:S(2)}) collective-permute-start(bf16[2,4,64,128]{3,2,1,0:T(8,128)(2,1)S(1)} %get-tuple-element.96), channel_id=1, source_target_pairs={{0,16},{8,24},{16,0},{24,8},{1,17},{9,25},{17,1},{25,9},{2,18},{10... | collective-permute-start | bytes 393224 | tf_op jit(solution)/shard_map/ppermute | solution.py:694
  47.1 10.6 %collective-permute-start.15 = (bf16[2,4,64,128]{3,2,1,0:T(8,128)(2,1)S(1)}, bf16[2,4,64,128]{3,2,1,0:T(8,128)(2,1)S(1)}, u32[]{:S(2)}, u32[]{:S(2)}) collective-permute-start(bf16[2,4,64,128]{3,2,1,0:T(8,128)(2,1)S(1)} %get-tuple-element.99), channel_id=1, source_target_pairs={{0,8},{8,0},{16,24},{24,16},{1,9},{9,1},{17,25},{25,17},{2,10},{10... | collective-permute-start | bytes 393224 | tf_op jit(solution)/shard_map/ppermute | solution.py:694
  49.2 8.5 %collective-permute-start.16 = (bf16[2,4,64,128]{3,2,1,0:T(8,128)(2,1)S(1)}, bf16[2,4,64,128]{3,2,1,0:T(8,128)(2,1)S(1)}, u32[]{:S(2)}, u32[]{:S(2)}) collective-permute-start(bf16[2,4,64,128]{3,2,1,0:T(8,128)(2,1)S(1)} %get-tuple-element.101), channel_id=1, source_target_pairs={{0,24},{8,16},{16,8},{24,0},{1,25},{9,17},{17,9},{25,1},{2,26},{10... | collective-permute-start | bytes 393224 | tf_op jit(solution)/shard_map/ppermute | solution.py:694
  53.2 7.4 %collective-permute-start.14 = (bf16[608,128]{1,0:T(8,128)(2,1)S(1)}, bf16[608,128]{1,0:T(8,128)(2,1)S(1)}, u32[]{:S(2)}, u32[]{:S(2)}) collective-permute-start(bf16[608,128]{1,0:T(8,128)(2,1)S(1)} %add_convert_fusion.3), channel_id=1, source_target_pairs={{0,6},{1,7},{2,4},{3,5},{4,2},{5,3},{6,0},{7,1},{8,25},{9,24},{10,... | collective-permute-start | bytes 466952 | tf_op jit(solution)/shard_map/ppermute | solution.py:700
  57.1 8.2 %collective-permute-start.13 = (bf16[608,128]{1,0:T(8,128)(2,1)S(1)}, bf16[608,128]{1,0:T(8,128)(2,1)S(1)}, u32[]{:S(2)}, u32[]{:S(2)}) collective-permute-start(bf16[608,128]{1,0:T(8,128)(2,1)S(1)} %add_convert_fusion.3), channel_id=1, source_target_pairs={{0,4},{1,5},{2,6},{3,7},{4,0},{5,1},{6,2},{7,3},{8,24},{9,25},{10,... | collective-permute-start | bytes 466952 | tf_op jit(solution)/shard_map/ppermute | solution.py:700
  57.3 8.1 %collective-permute-start.12 = (bf16[608,128]{1,0:T(8,128)(2,1)S(1)}, bf16[608,128]{1,0:T(8,128)(2,1)S(1)}, u32[]{:S(2)}, u32[]{:S(2)}) collective-permute-start(bf16[608,128]{1,0:T(8,128)(2,1)S(1)} %add_convert_fusion.3), channel_id=1, source_target_pairs={{0,2},{1,3},{2,0},{3,1},{4,6},{5,7},{6,4},{7,5},{8,9},{9,8},{10,11... | collective-permute-start | bytes 466952 | tf_op jit(solution)/shard_map/ppermute | solution.py:700
  57.7 7.7 %collective-permute-start.17 = (bf16[2,4,64,128]{3,2,1,0:T(8,128)(2,1)S(1)}, bf16[2,4,64,128]{3,2,1,0:T(8,128)(2,1)S(1)}, u32[]{:S(2)}, u32[]{:S(2)}) collective-permute-start(bf16[2,4,64,128]{3,2,1,0:T(8,128)(2,1)S(1)} %get-tuple-element.106), channel_id=1, source_target_pairs={{0,8},{8,0},{16,24},{24,16},{1,9},{9,1},{17,25},{25,17},{2,10},{10... | collective-permute-start | bytes 393224 | tf_op jit(solution)/shard_map/ppermute | solution.py:694
  57.7 7.7 %collective-permute-start.18 = (bf16[2,4,64,128]{3,2,1,0:T(8,128)(2,1)S(1)}, bf16[2,4,64,128]{3,2,1,0:T(8,128)(2,1)S(1)}, u32[]{:S(2)}, u32[]{:S(2)}) collective-permute-start(bf16[2,4,64,128]{3,2,1,0:T(8,128)(2,1)S(1)} %get-tuple-element.107), channel_id=1, source_target_pairs={{0,16},{8,24},{16,0},{24,8},{1,17},{9,25},{17,1},{25,9},{2,18},{10... | collective-permute-start | bytes 393224 | tf_op jit(solution)/shard_map/ppermute | solution.py:694
  65.5 9.4 %collective-permute-start.21 = (bf16[608,128]{1,0:T(8,128)(2,1)S(1)}, bf16[608,128]{1,0:T(8,128)(2,1)S(1)}, u32[]{:S(2)}, u32[]{:S(2)}) collective-permute-start(bf16[608,128]{1,0:T(8,128)(2,1)S(1)} %add_convert_fusion.2.refs_0_), channel_id=1, source_target_pairs={{0,17},{1,16},{2,19},{3,18},{4,21},{5,20},{6,23},{7,22},{8,14},{9,... | collective-permute-start | bytes 466952 | tf_op jit(solution)/shard_map/ppermute | solution.py:700
  66.2 8.8 %collective-permute-start.20 = (bf16[608,128]{1,0:T(8,128)(2,1)S(1)}, bf16[608,128]{1,0:T(8,128)(2,1)S(1)}, u32[]{:S(2)}, u32[]{:S(2)}) collective-permute-start(bf16[608,128]{1,0:T(8,128)(2,1)S(1)} %add_convert_fusion.2.refs_0_), channel_id=1, source_target_pairs={{0,16},{1,17},{2,18},{3,19},{4,20},{5,21},{6,22},{7,23},{8,12},{9,... | collective-permute-start | bytes 466952 | tf_op jit(solution)/shard_map/ppermute | solution.py:700
  67.0 7.9 %collective-permute-start.19 = (bf16[608,128]{1,0:T(8,128)(2,1)S(1)}, bf16[608,128]{1,0:T(8,128)(2,1)S(1)}, u32[]{:S(2)}, u32[]{:S(2)}) collective-permute-start(bf16[608,128]{1,0:T(8,128)(2,1)S(1)} %add_convert_fusion.2.refs_0_), channel_id=1, source_target_pairs={{0,1},{1,0},{2,3},{3,2},{4,5},{5,4},{6,7},{7,6},{8,10},{9,11},{10,... | collective-permute-start | bytes 466952 | tf_op jit(solution)/shard_map/ppermute | solution.py:700
  69.0 5.9 %collective-permute-start.22 = (bf16[2,4,64,128]{3,2,1,0:T(8,128)(2,1)S(1)}, bf16[2,4,64,128]{3,2,1,0:T(8,128)(2,1)S(1)}, u32[]{:S(2)}, u32[]{:S(2)}) collective-permute-start(bf16[2,4,64,128]{3,2,1,0:T(8,128)(2,1)S(1)} %get-tuple-element.111), channel_id=1, source_target_pairs={{0,24},{8,16},{16,8},{24,0},{1,25},{9,17},{17,9},{25,1},{2,26},{10... | collective-permute-start | bytes 393224 | tf_op jit(solution)/shard_map/ppermute | solution.py:694
  69.0 9.2 %collective-permute-start.23 = (bf16[608,128]{1,0:T(8,128)(2,1)S(1)}, bf16[608,128]{1,0:T(8,128)(2,1)S(1)}, u32[]{:S(2)}, u32[]{:S(2)}) collective-permute-start(bf16[608,128]{1,0:T(8,128)(2,1)S(1)} %add_convert_fusion.2.refs_0_), channel_id=1, source_target_pairs={{0,8},{8,0},{16,24},{24,16},{1,9},{9,1},{17,25},{25,17},{2,10},{10... | collective-permute-start | bytes 466952 | tf_op jit(solution)/shard_map/ppermute | solution.py:694
  74.9 3.3 %collective-permute-start.24 = (bf16[608,128]{1,0:T(8,128)(2,1)S(1)}, bf16[608,128]{1,0:T(8,128)(2,1)S(1)}, u32[]{:S(2)}, u32[]{:S(2)}) collective-permute-start(bf16[608,128]{1,0:T(8,128)(2,1)S(1)} %collective-permute-done.19.refs_1_), channel_id=1, source_target_pairs={{0,8},{8,0},{16,24},{24,16},{1,9},{9,1},{17,25},{25,17},{2,10},{10... | collective-permute-start | bytes 466952 | tf_op jit(solution)/shard_map/ppermute | solution.py:694
  75.8 2.5 %collective-permute-start.25 = (bf16[608,128]{1,0:T(8,128)(2,1)S(1)}, bf16[608,128]{1,0:T(8,128)(2,1)S(1)}, u32[]{:S(2)}, u32[]{:S(2)}) collective-permute-start(bf16[608,128]{1,0:T(8,128)(2,1)S(1)} %collective-permute-done.20.refs_2_), channel_id=1, source_target_pairs={{0,8},{8,0},{16,24},{24,16},{1,9},{9,1},{17,25},{25,17},{2,10},{10... | collective-permute-start | bytes 466952 | tf_op jit(solution)/shard_map/ppermute | solution.py:694
  75.8 2.4 %collective-permute-start.26 = (bf16[608,128]{1,0:T(8,128)(2,1)S(1)}, bf16[608,128]{1,0:T(8,128)(2,1)S(1)}, u32[]{:S(2)}, u32[]{:S(2)}) collective-permute-start(bf16[608,128]{1,0:T(8,128)(2,1)S(1)} %collective-permute-done.21.refs_3_), channel_id=1, source_target_pairs={{0,8},{8,0},{16,24},{24,16},{1,9},{9,1},{17,25},{25,17},{2,10},{10... | collective-permute-start | bytes 466952 | tf_op jit(solution)/shard_map/ppermute | solution.py:694

commit v6 on v5

--- a/solution.py
+++ b/solution.py
@@ -695,6 +695,8 @@
 
 
 def over_four(value, k, phase):
+    if phase == 1:
+        k = 4 - k
     plane, line = (k >> 1) * 16 + (k & 1), 2 * k
     pairs = [(i, i ^ (plane if (i >> 3) & 1 == phase else line)) for i in range(32)]
     return lax.ppermute(value, ("rows", "batch"), pairs)
@@ -866,7 +868,7 @@
     got = [g.astype(F32) for g in to_four([mine] * 4, 1)]
     got, block_out = lax.optimization_barrier((got, gather_rows(place, block, tokens.shape)))
     got, inputs[1], inputs[2] = lax.optimization_barrier((got, inputs[1], inputs[2]))
-    total = ((mine.astype(F32) + got[0]) + (got[1] + got[2])).astype(BF)
+    total = ((mine.astype(F32) + got[2]) + (got[1] + got[0])).astype(BF)
     got = to_four([total] * 4, 0)
     got, inputs[3] = lax.optimization_barrier((got, inputs[3]))
     pieces = (total, *got)

time: 80.4 us -> 80.4 us (level)
  waiting for transfers between devices: 19.7 us -> 18.8 us
where the time goes in v6:
time: 80.4 us; the launch traced here: 80.3 us
  Pallas kernels  32.7 us (41%)
  starting transfers between devices  25.4 us (32%)
  waiting for transfers between devices  18.8 us (23%)
  local copies, waits for them, and re-layouts  1.68 us (2%)
  between operations  1.22 us (2%)
    pallas_call x4, Pallas kernels, call(): pl.pallas_call(kernel, out_shape=[jax.ShapeDtypeStruct(shape, kind) for s...  27.6 us
    ppermute x18, waiting for transfers between devices, over_rows(): return lax.ppermute(value, 'rows', [(i, i ^ k) for i in range(4)])  12.9 us
    ppermute x18, starting transfers between devices, over_rows(): return lax.ppermute(value, 'rows', [(i, i ^ k) for i in range(4)])  12.7 us
    ppermute x9, starting transfers between devices, over_four(): return lax.ppermute(value, ('rows', 'batch'), pairs)  12.7 us
    ppermute x9, waiting for transfers between devices, over_four(): return lax.ppermute(value, ('rows', 'batch'), pairs)  5.86 us
    pallas_call x2, Pallas kernels, finish(): pl.pallas_call(functools.partial(finish_kernel, half), out_shape=[jax.Sha...  3.8 us
  transfers between devices with their start and end apart: 27, of which 8 were waited for; matrix products, arithmetic and copies ran while one was open for 1% of the time, Pallas kernels for 14%

profile of v6, /device:TPU:0, one launch (start us, length us, event | category | flops | bytes accessed | tf_op | source)
XLA Modules:
  0.0 80.3 jit_solution(14398996215632612075)
XLA Ops:
  0.7 1.1 %constant_dynamic-slice_fusion.3 = (bf16[2,4,64,128]{3,2,1,0:T(8,128)(2,1)S(1)}, bf16[2,4,64,128]{3,2,1,0:T(8,128)(2,1)S(1)}, bf16[2,4,64,128]{3,2,1,0:T(8,128)(2,1)S(1)}) fusion(bf16[8,4,64,128]{3,2,1,0:T(8,128)(2,1)} %own.1, s32[]{:T(128)S(6)} %select_n.28, s32[]{:T(128)S(6)} %select_n.27, s32[]{:T(128)S(6)} %select_n.26), kind=kLoop, calls=%fused_computation.16 | loop fusion | bytes 786444 | tf_op jit(solution)/shard_map/dynamic_slice | solution.py:837
  1.8 2.5 %collective-permute-start.2 = (bf16[2,4,64,128]{3,2,1,0:T(8,128)(2,1)S(1)}, bf16[2,4,64,128]{3,2,1,0:T(8,128)(2,1)S(1)}, u32[]{:S(2)}, u32[]{:S(2)}) collective-permute-start(bf16[2,4,64,128]{3,2,1,0:T(8,128)(2,1)S(1)} %get-tuple-element.139), channel_id=1, source_target_pairs={{0,24},{8,16},{16,8},{24,0},{1,25},{9,17},{17,9},{25,1},{2,26},{10... | collective-permute-start | bytes 393224 | tf_op jit(solution)/shard_map/ppermute | solution.py:694
  4.3 0.6 collective-permute-start.1
  5.1 1.2 %collective-permute-done.near1 = bf16[2,4,64,128]{3,2,1,0:T(8,128)(2,1)S(1)} collective-permute-done((bf16[2,4,64,128]{3,2,1,0:T(8,128)(2,1)S(1)}, bf16[2,4,64,128]{3,2,1,0:T(8,128)(2,1)S(1)}, u32[]{:S(2)}, u32[]{:S(2)}) %collective-permute-start) | collective-permute-done | bytes 131104 | tf_op jit(solution)/shard_map/ppermute | solution.py:694
  6.3 1.5 %collective-permute-start.5 = (bf16[2,4,64,128]{3,2,1,0:T(8,128)(2,1)S(1)}, bf16[2,4,64,128]{3,2,1,0:T(8,128)(2,1)S(1)}, u32[]{:S(2)}, u32[]{:S(2)}) collective-permute-start(bf16[2,4,64,128]{3,2,1,0:T(8,128)(2,1)S(1)} %get-tuple-element.136), channel_id=1, source_target_pairs={{0,24},{8,16},{16,8},{24,0},{1,25},{9,17},{17,9},{25,1},{2,26},{10... | collective-permute-start | bytes 393224 | tf_op jit(solution)/shard_map/ppermute | solution.py:694
  7.8 0.4 collective-permute-start.4
  8.2 0.1 collective-permute-start.3
  8.3 0.1 dynamic_slice.24
  8.4 0.1 dynamic_slice.25
  8.4 0.2 concatenate.19.taps
  8.6 0.1 concatenate.18.place
  8.7 3.2 %collective-permute-done.1.near2 = bf16[2,4,64,128]{3,2,1,0:T(8,128)(2,1)S(1)} collective-permute-done((bf16[2,4,64,128]{3,2,1,0:T(8,128)(2,1)S(1)}, bf16[2,4,64,128]{3,2,1,0:T(8,128)(2,1)S(1)}, u32[]{:S(2)}, u32[]{:S(2)}) %collective-permute-start.1) | collective-permute-done | bytes 131104 | tf_op jit(solution)/shard_map/ppermute | solution.py:694
  11.9 3.5 %attend.1 = (bf16[2048,128]{1,0:T(8,128)(2,1)S(1)}, bf16[2048,128]{1,0:T(8,128)(2,1)S(1)}, bf16[2048,128]{1,0:T(8,128)(2,1)S(1)}, f32[2048,128]{1,0:T(8,128)S(1)...) custom-call(s32[8]{0:T(128)S(1)} %concatenate.18.place, ...), custom_call_target="tpu_custom_call" | custom-call | flops 1000000000 | bytes 4194304 | tf_op jit(solution)/shard_map/attend/pallas_call | solution.py:619
  15.4 1.3 %collective-permute-done.4.cot2 = bf16[2,4,64,128]{3,2,1,0:T(8,128)(2,1)S(1)} collective-permute-done((bf16[2,4,64,128]{3,2,1,0:T(8,128)(2,1)S(1)}, bf16[2,4,64,128]{3,2,1,0:T(8,128)(2,1)S(1)}, u32[]{:S(2)}, u32[]{:S(2)}) %collective-permute-start.4) | collective-permute-done | bytes 131104 | tf_op jit(solution)/shard_map/ppermute | solution.py:694
  16.8 19.3 %feed.1 = (bf16[2,4,64,128]{3,2,1,0:T(8,128)(2,1)S(1)}, bf16[2,4,64,128]{3,2,1,0:T(8,128)(2,1)S(1)}, bf16[2,4,64,128]{3,2,1,0:T(8,128)(2,1)S(1)}, bf16[2,4,64,12...) custom-call(s32[8]{0:T(128)S(1)} %concatenate.18.place, ...), custom_call_target="tpu_custom_call" | custom-call | flops 16000000000 | bytes 4194304 | tf_op jit(solution)/shard_map/feed/pallas_call | solution.py:619
  36.0 0.1 collective-permute-start.6
  36.1 2.9 %back.1 = (bf16[2048,128]{1,0:T(8,128)(2,1)S(1)}, bf16[128,128]{1,0:T(8,128)(2,1)S(1)}, bf16[1344,128]{1,0:T(8,128)(2,1)S(1)}, bf16[1344,128]{1,0:T(8,128)(2,1)S(1)}) custom-call(s32[8]{0:T(128)S(1)} %concatenate.18.place, bf16[2048,128]{1,0:T(8,128)(2,1)S(1)} %get-tuple-element.78.normed, bf16[2048,128]{1,0:T(8,128)(2,1)S(1)} %get-tuple-element.79.query, ...), custom_call_target="tpu_custom_call" | custom-call | flops 2000000000 | bytes 4194304 | tf_op jit(solution)/shard_map/back/pallas_call | solution.py:619
  39.1 0.6 collective-permute-start.7
  39.6 0.1 add_convert_fusion.1
  39.7 1.2 %collective-permute-done.7 = bf16[1344,128]{1,0:T(8,128)(2,1)S(1)} collective-permute-done((bf16[1344,128]{1,0:T(8,128)(2,1)S(1)}, bf16[1344,128]{1,0:T(8,128)(2,1)S(1)}, u32[]{:S(2)}, u32[]{:S(2)}) %collective-permute-start.7) | collective-permute-done | bytes 344096 | tf_op jit(solution)/shard_map/ppermute | solution.py:694
  40.9 0.1 add_convert_fusion
  41.1 2.3 %collective-permute-start.8 = (bf16[608,128]{1,0:T(8,128)(2,1)S(1)}, bf16[608,128]{1,0:T(8,128)(2,1)S(1)}, u32[]{:S(2)}, u32[]{:S(2)}) collective-permute-start(bf16[608,128]{1,0:T(8,128)(2,1)S(1)} %pad_maximum_fusion), channel_id=1, source_target_pairs={{0,1},{1,0},{2,3},{3,2},{4,5},{5,4},{6,7},{7,6},{8,10},{9,11},{10,... | collective-permute-start | bytes 466952 | tf_op jit(solution)/shard_map/ppermute | solution.py:702
  43.4 1.6 %collective-permute-start.9 = (bf16[608,128]{1,0:T(8,128)(2,1)S(1)}, bf16[608,128]{1,0:T(8,128)(2,1)S(1)}, u32[]{:S(2)}, u32[]{:S(2)}) collective-permute-start(bf16[608,128]{1,0:T(8,128)(2,1)S(1)} %pad_maximum_fusion.1), channel_id=1, source_target_pairs={{0,16},{1,17},{2,18},{3,19},{4,20},{5,21},{6,22},{7,23},{8,12},{9,... | collective-permute-start | bytes 466952 | tf_op jit(solution)/shard_map/ppermute | solution.py:702
  45.0 0.1 collective-permute-start.10
  45.1 2.0 %collective-permute-start.11 = (bf16[2,4,64,128]{3,2,1,0:T(8,128)(2,1)S(1)}, bf16[2,4,64,128]{3,2,1,0:T(8,128)(2,1)S(1)}, u32[]{:S(2)}, u32[]{:S(2)}) collective-permute-start(bf16[2,4,64,128]{3,2,1,0:T(8,128)(2,1)S(1)} %get-tuple-element.96), channel_id=1, source_target_pairs={{0,16},{8,24},{16,0},{24,8},{1,17},{9,25},{17,1},{25,9},{2,18},{10... | collective-permute-start | bytes 393224 | tf_op jit(solution)/shard_map/ppermute | solution.py:694
  47.1 0.3 collective-permute-start.15
  47.4 1.9 %input_gradient.1 = (bf16[2,4,64,128]{3,2,1,0:T(8,128)(2,1)S(1)}, bf16[2,4,64,128]{3,2,1,0:T(8,128)(2,1)S(1)}, bf16[2,4,64,128]{3,2,1,0:T(8,128)(2,1)S(1)}, bf16[2,4,64,128]{3,2,1,0:T(8,128)(2,1)S(1)}) custom-call(s32[8]{0:T(128)S(1)} %concatenate.18.place, bf16[2048,128]{1,0:T(8,128)(2,1)S(1)} %get-tuple-element.88.x, ...), custom_call_target="tpu_custom_call" | custom-call | flops 1000000000 | bytes 4194304 | tf_op jit(solution)/shard_map/input_gradient/pallas_call | solution.py:619
  49.2 0.2 collective-permute-start.16
  49.4 1.9 %collective-permute-done.10 = bf16[608,128]{1,0:T(8,128)(2,1)S(1)} collective-permute-done((bf16[608,128]{1,0:T(8,128)(2,1)S(1)}, bf16[608,128]{1,0:T(8,128)(2,1)S(1)}, u32[]{:S(2)}, u32[]{:S(2)}) %collective-permute-start.10) | collective-permute-done | bytes 155680 | tf_op jit(solution)/shard_map/ppermute | solution.py:702
  51.3 0.1 add_convert_fusion.3
  51.4 1.8 %collective-permute-done.11.part2 = bf16[2,4,64,128]{3,2,1,0:T(8,128)(2,1)S(1)} collective-permute-done((bf16[2,4,64,128]{3,2,1,0:T(8,128)(2,1)S(1)}, bf16[2,4,64,128]{3,2,1,0:T(8,128)(2,1)S(1)}, u32[]{:S(2)}, u32[]{:S(2)}) %collective-permute-start.11) | collective-permute-done | bytes 131104 | tf_op jit(solution)/shard_map/ppermute | solution.py:694
  53.2 2.6 %collective-permute-start.14 = (bf16[608,128]{1,0:T(8,128)(2,1)S(1)}, bf16[608,128]{1,0:T(8,128)(2,1)S(1)}, u32[]{:S(2)}, u32[]{:S(2)}) collective-permute-start(bf16[608,128]{1,0:T(8,128)(2,1)S(1)} %add_convert_fusion.3), channel_id=1, source_target_pairs={{0,2},{1,3},{2,0},{3,1},{4,6},{5,7},{6,4},{7,5},{8,9},{9,8},{10,11... | collective-permute-start | bytes 466952 | tf_op jit(solution)/shard_map/ppermute | solution.py:702
  55.8 1.9 %collective-permute-start.13 = (bf16[608,128]{1,0:T(8,128)(2,1)S(1)}, bf16[608,128]{1,0:T(8,128)(2,1)S(1)}, u32[]{:S(2)}, u32[]{:S(2)}) collective-permute-start(bf16[608,128]{1,0:T(8,128)(2,1)S(1)} %add_convert_fusion.3), channel_id=1, source_target_pairs={{0,4},{1,5},{2,6},{3,7},{4,0},{5,1},{6,2},{7,3},{8,24},{9,25},{10,... | collective-permute-start | bytes 466952 | tf_op jit(solution)/shard_map/ppermute | solution.py:702
  57.7 0.6 collective-permute-start.12
  58.3 1.6 %collective-permute-start.18 = (bf16[2,4,64,128]{3,2,1,0:T(8,128)(2,1)S(1)}, bf16[2,4,64,128]{3,2,1,0:T(8,128)(2,1)S(1)}, u32[]{:S(2)}, u32[]{:S(2)}) collective-permute-start(bf16[2,4,64,128]{3,2,1,0:T(8,128)(2,1)S(1)} %get-tuple-element.107), channel_id=1, source_target_pairs={{0,16},{8,24},{16,0},{24,8},{1,17},{9,25},{17,1},{25,9},{2,18},{10... | collective-permute-start | bytes 393224 | tf_op jit(solution)/shard_map/ppermute | solution.py:694
  59.9 1.4 %gather_rows.1 = bf16[8,4,64,128]{3,2,1,0:T(8,128)(2,1)} custom-call(s32[8]{0:T(128)S(1)} %concatenate.18.place, bf16[2,4,64,128]{3,2,1,0:T(8,128)(2,1)S(1)} %get-tuple-element.98.part0, bf16[2,4,64,128]{3,2,1,0:T(8,128)(2,1)S(1)} %collective-permute-done.15.part1, bf16[2,4,64,128]{3,2,1,0:T(8,128)(2,1)S(1)} %collective-permute-done.11.part2, ...), custom_call_target="tpu_custom_call" | custom-call | tf_op jit(solution)/shard_map/gather_rows/pallas_call | solution.py:813
  61.3 4.0 %collective-permute-done.13 = bf16[608,128]{1,0:T(8,128)(2,1)S(1)} collective-permute-done((bf16[608,128]{1,0:T(8,128)(2,1)S(1)}, bf16[608,128]{1,0:T(8,128)(2,1)S(1)}, u32[]{:S(2)}, u32[]{:S(2)}) %collective-permute-start.13) | collective-permute-done | bytes 155680 | tf_op jit(solution)/shard_map/ppermute | solution.py:702
  65.4 0.1 add_convert_fusion.2.refs_0_
  65.4 0.7 collective-permute-start.21
  66.1 1.4 %collective-permute-start.20 = (bf16[608,128]{1,0:T(8,128)(2,1)S(1)}, bf16[608,128]{1,0:T(8,128)(2,1)S(1)}, u32[]{:S(2)}, u32[]{:S(2)}) collective-permute-start(bf16[608,128]{1,0:T(8,128)(2,1)S(1)} %add_convert_fusion.2.refs_0_), channel_id=1, source_target_pairs={{0,16},{1,17},{2,18},{3,19},{4,20},{5,21},{6,22},{7,23},{8,12},{9,... | collective-permute-start | bytes 466952 | tf_op jit(solution)/shard_map/ppermute | solution.py:702
  67.5 1.5 %collective-permute-start.19 = (bf16[608,128]{1,0:T(8,128)(2,1)S(1)}, bf16[608,128]{1,0:T(8,128)(2,1)S(1)}, u32[]{:S(2)}, u32[]{:S(2)}) collective-permute-start(bf16[608,128]{1,0:T(8,128)(2,1)S(1)} %add_convert_fusion.2.refs_0_), channel_id=1, source_target_pairs={{0,1},{1,0},{2,3},{3,2},{4,5},{5,4},{6,7},{7,6},{8,10},{9,11},{10,... | collective-permute-start | bytes 466952 | tf_op jit(solution)/shard_map/ppermute | solution.py:702
  69.0 1.6 %collective-permute-start.23 = (bf16[608,128]{1,0:T(8,128)(2,1)S(1)}, bf16[608,128]{1,0:T(8,128)(2,1)S(1)}, u32[]{:S(2)}, u32[]{:S(2)}) collective-permute-start(bf16[608,128]{1,0:T(8,128)(2,1)S(1)} %add_convert_fusion.2.refs_0_), channel_id=1, source_target_pairs={{0,8},{8,0},{16,24},{24,16},{1,9},{9,1},{17,25},{25,17},{2,10},{10... | collective-permute-start | bytes 466952 | tf_op jit(solution)/shard_map/ppermute | solution.py:694
  70.6 4.2 %collective-permute-done.22.refs_7_ = bf16[2,4,64,128]{3,2,1,0:T(8,128)(2,1)S(1)} collective-permute-done((bf16[2,4,64,128]{3,2,1,0:T(8,128)(2,1)S(1)}, bf16[2,4,64,128]{3,2,1,0:T(8,128)(2,1)S(1)}, u32[]{:S(2)}, u32[]{:S(2)}) %collective-permute-start.22) | collective-permute-done | bytes 131104 | tf_op jit(solution)/shard_map/ppermute | solution.py:694
  74.9 0.9 %collective-permute-start.24 = (bf16[608,128]{1,0:T(8,128)(2,1)S(1)}, bf16[608,128]{1,0:T(8,128)(2,1)S(1)}, u32[]{:S(2)}, u32[]{:S(2)}) collective-permute-start(bf16[608,128]{1,0:T(8,128)(2,1)S(1)} %collective-permute-done.19.refs_1_), channel_id=1, source_target_pairs={{0,8},{8,0},{16,24},{24,16},{1,9},{9,1},{17,25},{25,17},{2,10},{10... | collective-permute-start | bytes 466952 | tf_op jit(solution)/shard_map/ppermute | solution.py:694
  75.8 0.1 collective-permute-start.25
  75.8 0.4 collective-permute-start.26
  76.3 2.0 %finish.2 = (f32[128,128]{1,0:T(8,128)}, f32[2048,128]{1,0:T(8,128)}, f32[128,256]{1,0:T(8,128)}, f32[128,128]{1,0:T(8,128)}, f32[128,1024]{1,0:T(8,128)}, /*ind...) custom-call(s32[8]{0:T(128)S(1)} %concatenate.18.place, bf16[608,128]{1,0:T(8,128)(2,1)S(1)} %add_convert_fusion.2.refs_0_, ...), custom_call_target="tpu_custom_call" | custom-call | bytes 4194304 | tf_op jit(solution)/shard_map/finish/pallas_call | solution.py:784
  78.3 1.8 %finish.3 = (f32[128,128]{1,0:T(8,128)}, f32[2048,128]{1,0:T(8,128)}, f32[128,256]{1,0:T(8,128)}, f32[128,128]{1,0:T(8,128)}, f32[128,1024]{1,0:T(8,128)}, /*ind...) custom-call(s32[8]{0:T(128)S(1)} %concatenate.18.place, ...), custom_call_target="tpu_custom_call", output_to_operand_aliasing={{0}: (9, {}), {1}: (10, {}), {2}: (11, {}), {3}: (12, {}), ... | custom-call | bytes 4194304 | tf_op jit(solution)/shard_map/finish/pallas_call | solution.py:784
  (64 shorter events, 0.4 us)
Async XLA Ops:
  0.6 5.6 %copy-start.1 = (bf16[8,4,64,128]{3,2,1,0:T(8,128)(2,1)S(1)}, bf16[8,4,64,128]{3,2,1,0:T(8,128)(2,1)}, u32[]{:S(2)}) copy-start(bf16[8,4,64,128]{3,2,1,0:T(8,128)(2,1)} %cot) | copy-start | bytes 1572868
  0.7 4.3 %copy-start.8 = (bf16[3,3,1024]{2,1,0:T(4,128)(2,1)S(1)}, bf16[3,3,1024]{2,1,0:T(4,128)(2,1)}, u32[]{:S(2)}) copy-start(bf16[3,3,1024]{2,1,0:T(4,128)(2,1)} %param.25) | copy-start | bytes 55300
  1.8 6.9 %collective-permute-start.2 = (bf16[2,4,64,128]{3,2,1,0:T(8,128)(2,1)S(1)}, bf16[2,4,64,128]{3,2,1,0:T(8,128)(2,1)S(1)}, u32[]{:S(2)}, u32[]{:S(2)}) collective-permute-start(bf16[2,4,64,128]{3,2,1,0:T(8,128)(2,1)S(1)} %get-tuple-element.139), channel_id=1, source_target_pairs={{0,24},{8,16},{16,8},{24,0},{1,25},{9,17},{17,9},{25,1},{2,26},{10... | collective-permute-start | bytes 393224 | tf_op jit(solution)/shard_map/ppermute | solution.py:694
  4.3 7.6 %collective-permute-start.1 = (bf16[2,4,64,128]{3,2,1,0:T(8,128)(2,1)S(1)}, bf16[2,4,64,128]{3,2,1,0:T(8,128)(2,1)S(1)}, u32[]{:S(2)}, u32[]{:S(2)}) collective-permute-start(bf16[2,4,64,128]{3,2,1,0:T(8,128)(2,1)S(1)} %get-tuple-element.140), channel_id=1, source_target_pairs={{0,16},{8,24},{16,0},{24,8},{1,17},{9,25},{17,1},{25,9},{2,18},{10... | collective-permute-start | bytes 393224 | tf_op jit(solution)/shard_map/ppermute | solution.py:694
  4.9 1.3 %collective-permute-start = (bf16[2,4,64,128]{3,2,1,0:T(8,128)(2,1)S(1)}, bf16[2,4,64,128]{3,2,1,0:T(8,128)(2,1)S(1)}, u32[]{:S(2)}, u32[]{:S(2)}) collective-permute-start(bf16[2,4,64,128]{3,2,1,0:T(8,128)(2,1)S(1)} %get-tuple-element.141), channel_id=1, source_target_pairs={{0,8},{8,0},{16,24},{24,16},{1,9},{9,1},{17,25},{25,17},{2,10},{10... | collective-permute-start | bytes 393224 | tf_op jit(solution)/shard_map/ppermute | solution.py:694
  5.0 6.9 %copy-start.7 = (bf16[128,128]{1,0:T(8,128)(2,1)S(1)}, bf16[128,128]{1,0:T(8,128)(2,1)}, u32[]{:S(2)}) copy-start(bf16[128,128]{1,0:T(8,128)(2,1)} %wq.5) | copy-start | bytes 98308
  5.0 6.9 %copy-start.5 = (bf16[128,256]{1,0:T(8,128)(2,1)S(1)}, bf16[128,256]{1,0:T(8,128)(2,1)}, u32[]{:S(2)}) copy-start(bf16[128,256]{1,0:T(8,128)(2,1)} %wkv.3) | copy-start | bytes 196612
  5.0 3.2 %copy-start.9 = (f32[128]{0:T(128)S(1)}, f32[128]{0:T(128)}, u32[]{:S(2)}) copy-start(f32[128]{0:T(128)} %param.23) | copy-start | bytes 1540
  5.0 3.2 %copy-start.10 = (f32[128]{0:T(128)S(1)}, f32[128]{0:T(128)}, u32[]{:S(2)}) copy-start(f32[128]{0:T(128)} %param.20) | copy-start | bytes 1540
  5.0 3.2 %copy-start.11 = (f32[128]{0:T(128)S(1)}, f32[128]{0:T(128)}, u32[]{:S(2)}) copy-start(f32[128]{0:T(128)} %param.17) | copy-start | bytes 1540
  5.0 3.2 %copy-start.12 = (s32[8]{0:T(128)S(1)}, s32[8]{0:T(128)}, u32[]{:S(2)}) copy-start(s32[8]{0:T(128)} %param.15) | copy-start | bytes 100
  5.0 3.3 %copy-start.13 = (s32[8]{0:T(128)S(1)}, s32[8]{0:T(128)}, u32[]{:S(2)}) copy-start(s32[8]{0:T(128)} %param.16) | copy-start | bytes 100
  5.1 6.9 %copy-start.2 = (bf16[2048,128]{1,0:T(8,128)(2,1)S(1)}, bf16[2048,128]{1,0:T(8,128)(2,1)}, u32[]{:S(2)}) copy-start(bf16[2048,128]{1,0:T(8,128)(2,1)} %wsr.5) | copy-start | bytes 1572868
  5.1 6.8 %copy-start = (bf16[8,4,64,128]{3,2,1,0:T(8,128)(2,1)S(1)}, bf16[8,4,64,128]{3,2,1,0:T(8,128)(2,1)}, u32[]{:S(2)}) copy-start(bf16[8,4,64,128]{3,2,1,0:T(8,128)(2,1)} %own.1) | copy-start | bytes 1572868
  6.3 9.1 %collective-permute-start.5 = (bf16[2,4,64,128]{3,2,1,0:T(8,128)(2,1)S(1)}, bf16[2,4,64,128]{3,2,1,0:T(8,128)(2,1)S(1)}, u32[]{:S(2)}, u32[]{:S(2)}) collective-permute-start(bf16[2,4,64,128]{3,2,1,0:T(8,128)(2,1)S(1)} %get-tuple-element.136), channel_id=1, source_target_pairs={{0,24},{8,16},{16,8},{24,0},{1,25},{9,17},{17,9},{25,1},{2,26},{10... | collective-permute-start | bytes 393224 | tf_op jit(solution)/shard_map/ppermute | solution.py:694
  7.8 9.0 %collective-permute-start.4 = (bf16[2,4,64,128]{3,2,1,0:T(8,128)(2,1)S(1)}, bf16[2,4,64,128]{3,2,1,0:T(8,128)(2,1)S(1)}, u32[]{:S(2)}, u32[]{:S(2)}) collective-permute-start(bf16[2,4,64,128]{3,2,1,0:T(8,128)(2,1)S(1)} %get-tuple-element.137), channel_id=1, source_target_pairs={{0,16},{8,24},{16,0},{24,8},{1,17},{9,25},{17,1},{25,9},{2,18},{10... | collective-permute-start | bytes 393224 | tf_op jit(solution)/shard_map/ppermute | solution.py:694
  8.2 8.6 %collective-permute-start.3 = (bf16[2,4,64,128]{3,2,1,0:T(8,128)(2,1)S(1)}, bf16[2,4,64,128]{3,2,1,0:T(8,128)(2,1)S(1)}, u32[]{:S(2)}, u32[]{:S(2)}) collective-permute-start(bf16[2,4,64,128]{3,2,1,0:T(8,128)(2,1)S(1)} %get-tuple-element.138), channel_id=1, source_target_pairs={{0,8},{8,0},{16,24},{24,16},{1,9},{9,1},{17,25},{25,17},{2,10},{10... | collective-permute-start | bytes 393224 | tf_op jit(solution)/shard_map/ppermute | solution.py:694
  8.4 3.5 %copy-start.6 = (bf16[128,128]{1,0:T(8,128)(2,1)S(1)}, bf16[128,128]{1,0:T(8,128)(2,1)}, u32[]{:S(2)}) copy-start(bf16[128,128]{1,0:T(8,128)(2,1)} %wout.3) | copy-start | bytes 98308
  8.7 8.1 %copy-start.3 = (bf16[128,1024]{1,0:T(8,128)(2,1)S(1)}, bf16[128,1024]{1,0:T(8,128)(2,1)}, u32[]{:S(2)}) copy-start(bf16[128,1024]{1,0:T(8,128)(2,1)} %wfc1.1) | copy-start | bytes 786436
  8.7 8.1 %copy-start.4 = (bf16[1024,128]{1,0:T(8,128)(2,1)S(1)}, bf16[1024,128]{1,0:T(8,128)(2,1)}, u32[]{:S(2)}) copy-start(bf16[1024,128]{1,0:T(8,128)(2,1)} %wfc2.1) | copy-start | bytes 786436
  36.0 3.6 %collective-permute-start.6 = (bf16[1088,128]{1,0:T(8,128)(2,1)S(1)}, bf16[1088,128]{1,0:T(8,128)(2,1)S(1)}, u32[]{:S(2)}, u32[]{:S(2)}) collective-permute-start(bf16[1088,128]{1,0:T(8,128)(2,1)S(1)} %get-tuple-element.77), channel_id=1, source_target_pairs={{0,8},{8,0},{16,24},{24,16},{1,9},{9,1},{17,25},{25,17},{2,10},{10... | collective-permute-start | bytes 835592 | tf_op jit(solution)/shard_map/ppermute | solution.py:694
  39.1 1.8 %collective-permute-start.7 = (bf16[1344,128]{1,0:T(8,128)(2,1)S(1)}, bf16[1344,128]{1,0:T(8,128)(2,1)S(1)}, u32[]{:S(2)}, u32[]{:S(2)}) collective-permute-start(bf16[1344,128]{1,0:T(8,128)(2,1)S(1)} %get-tuple-element.87), channel_id=1, source_target_pairs={{0,8},{8,0},{16,24},{24,16},{1,9},{9,1},{17,25},{25,17},{2,10},{10... | collective-permute-start | bytes 1032200 | tf_op jit(solution)/shard_map/ppermute | solution.py:694
  41.1 8.2 %collective-permute-start.8 = (bf16[608,128]{1,0:T(8,128)(2,1)S(1)}, bf16[608,128]{1,0:T(8,128)(2,1)S(1)}, u32[]{:S(2)}, u32[]{:S(2)}) collective-permute-start(bf16[608,128]{1,0:T(8,128)(2,1)S(1)} %pad_maximum_fusion), channel_id=1, source_target_pairs={{0,1},{1,0},{2,3},{3,2},{4,5},{5,4},{6,7},{7,6},{8,10},{9,11},{10,... | collective-permute-start | bytes 466952 | tf_op jit(solution)/shard_map/ppermute | solution.py:702
  43.4 6.0 %collective-permute-start.9 = (bf16[608,128]{1,0:T(8,128)(2,1)S(1)}, bf16[608,128]{1,0:T(8,128)(2,1)S(1)}, u32[]{:S(2)}, u32[]{:S(2)}) collective-permute-start(bf16[608,128]{1,0:T(8,128)(2,1)S(1)} %pad_maximum_fusion.1), channel_id=1, source_target_pairs={{0,16},{1,17},{2,18},{3,19},{4,20},{5,21},{6,22},{7,23},{8,12},{9,... | collective-permute-start | bytes 466952 | tf_op jit(solution)/shard_map/ppermute | solution.py:702
  45.0 6.3 %collective-permute-start.10 = (bf16[608,128]{1,0:T(8,128)(2,1)S(1)}, bf16[608,128]{1,0:T(8,128)(2,1)S(1)}, u32[]{:S(2)}, u32[]{:S(2)}) collective-permute-start(bf16[608,128]{1,0:T(8,128)(2,1)S(1)} %pad_maximum_fusion.2), channel_id=1, source_target_pairs={{0,17},{1,16},{2,19},{3,18},{4,21},{5,20},{6,23},{7,22},{8,14},{9,... | collective-permute-start | bytes 466952 | tf_op jit(solution)/shard_map/ppermute | solution.py:702
  45.1 8.1 %collective-permute-start.11 = (bf16[2,4,64,128]{3,2,1,0:T(8,128)(2,1)S(1)}, bf16[2,4,64,128]{3,2,1,0:T(8,128)(2,1)S(1)}, u32[]{:S(2)}, u32[]{:S(2)}) collective-permute-start(bf16[2,4,64,128]{3,2,1,0:T(8,128)(2,1)S(1)} %get-tuple-element.96), channel_id=1, source_target_pairs={{0,16},{8,24},{16,0},{24,8},{1,17},{9,25},{17,1},{25,9},{2,18},{10... | collective-permute-start | bytes 393224 | tf_op jit(solution)/shard_map/ppermute | solution.py:694
  47.1 11.3 %collective-permute-start.15 = (bf16[2,4,64,128]{3,2,1,0:T(8,128)(2,1)S(1)}, bf16[2,4,64,128]{3,2,1,0:T(8,128)(2,1)S(1)}, u32[]{:S(2)}, u32[]{:S(2)}) collective-permute-start(bf16[2,4,64,128]{3,2,1,0:T(8,128)(2,1)S(1)} %get-tuple-element.99), channel_id=1, source_target_pairs={{0,8},{8,0},{16,24},{24,16},{1,9},{9,1},{17,25},{25,17},{2,10},{10... | collective-permute-start | bytes 393224 | tf_op jit(solution)/shard_map/ppermute | solution.py:694
  49.2 9.1 %collective-permute-start.16 = (bf16[2,4,64,128]{3,2,1,0:T(8,128)(2,1)S(1)}, bf16[2,4,64,128]{3,2,1,0:T(8,128)(2,1)S(1)}, u32[]{:S(2)}, u32[]{:S(2)}) collective-permute-start(bf16[2,4,64,128]{3,2,1,0:T(8,128)(2,1)S(1)} %get-tuple-element.101), channel_id=1, source_target_pairs={{0,24},{8,16},{16,8},{24,0},{1,25},{9,17},{17,9},{25,1},{2,26},{10... | collective-permute-start | bytes 393224 | tf_op jit(solution)/shard_map/ppermute | solution.py:694
  53.2 8.1 %collective-permute-start.14 = (bf16[608,128]{1,0:T(8,128)(2,1)S(1)}, bf16[608,128]{1,0:T(8,128)(2,1)S(1)}, u32[]{:S(2)}, u32[]{:S(2)}) collective-permute-start(bf16[608,128]{1,0:T(8,128)(2,1)S(1)} %add_convert_fusion.3), channel_id=1, source_target_pairs={{0,2},{1,3},{2,0},{3,1},{4,6},{5,7},{6,4},{7,5},{8,9},{9,8},{10,11... | collective-permute-start | bytes 466952 | tf_op jit(solution)/shard_map/ppermute | solution.py:702
  55.8 9.5 %collective-permute-start.13 = (bf16[608,128]{1,0:T(8,128)(2,1)S(1)}, bf16[608,128]{1,0:T(8,128)(2,1)S(1)}, u32[]{:S(2)}, u32[]{:S(2)}) collective-permute-start(bf16[608,128]{1,0:T(8,128)(2,1)S(1)} %add_convert_fusion.3), channel_id=1, source_target_pairs={{0,4},{1,5},{2,6},{3,7},{4,0},{5,1},{6,2},{7,3},{8,24},{9,25},{10,... | collective-permute-start | bytes 466952 | tf_op jit(solution)/shard_map/ppermute | solution.py:702
  57.7 7.6 %collective-permute-start.12 = (bf16[608,128]{1,0:T(8,128)(2,1)S(1)}, bf16[608,128]{1,0:T(8,128)(2,1)S(1)}, u32[]{:S(2)}, u32[]{:S(2)}) collective-permute-start(bf16[608,128]{1,0:T(8,128)(2,1)S(1)} %add_convert_fusion.3), channel_id=1, source_target_pairs={{0,6},{1,7},{2,4},{3,5},{4,2},{5,3},{6,0},{7,1},{8,25},{9,24},{10,... | collective-permute-start | bytes 466952 | tf_op jit(solution)/shard_map/ppermute | solution.py:702
  58.3 7.0 %collective-permute-start.17 = (bf16[2,4,64,128]{3,2,1,0:T(8,128)(2,1)S(1)}, bf16[2,4,64,128]{3,2,1,0:T(8,128)(2,1)S(1)}, u32[]{:S(2)}, u32[]{:S(2)}) collective-permute-start(bf16[2,4,64,128]{3,2,1,0:T(8,128)(2,1)S(1)} %get-tuple-element.106), channel_id=1, source_target_pairs={{0,8},{8,0},{16,24},{24,16},{1,9},{9,1},{17,25},{25,17},{2,10},{10... | collective-permute-start | bytes 393224 | tf_op jit(solution)/shard_map/ppermute | solution.py:694
  58.3 7.0 %collective-permute-start.18 = (bf16[2,4,64,128]{3,2,1,0:T(8,128)(2,1)S(1)}, bf16[2,4,64,128]{3,2,1,0:T(8,128)(2,1)S(1)}, u32[]{:S(2)}, u32[]{:S(2)}) collective-permute-start(bf16[2,4,64,128]{3,2,1,0:T(8,128)(2,1)S(1)} %get-tuple-element.107), channel_id=1, source_target_pairs={{0,16},{8,24},{16,0},{24,8},{1,17},{9,25},{17,1},{25,9},{2,18},{10... | collective-permute-start | bytes 393224 | tf_op jit(solution)/shard_map/ppermute | solution.py:694
  65.4 9.4 %collective-permute-start.21 = (bf16[608,128]{1,0:T(8,128)(2,1)S(1)}, bf16[608,128]{1,0:T(8,128)(2,1)S(1)}, u32[]{:S(2)}, u32[]{:S(2)}) collective-permute-start(bf16[608,128]{1,0:T(8,128)(2,1)S(1)} %add_convert_fusion.2.refs_0_), channel_id=1, source_target_pairs={{0,17},{1,16},{2,19},{3,18},{4,21},{5,20},{6,23},{7,22},{8,14},{9,... | collective-permute-start | bytes 466952 | tf_op jit(solution)/shard_map/ppermute | solution.py:702
  66.1 8.7 %collective-permute-start.20 = (bf16[608,128]{1,0:T(8,128)(2,1)S(1)}, bf16[608,128]{1,0:T(8,128)(2,1)S(1)}, u32[]{:S(2)}, u32[]{:S(2)}) collective-permute-start(bf16[608,128]{1,0:T(8,128)(2,1)S(1)} %add_convert_fusion.2.refs_0_), channel_id=1, source_target_pairs={{0,16},{1,17},{2,18},{3,19},{4,20},{5,21},{6,22},{7,23},{8,12},{9,... | collective-permute-start | bytes 466952 | tf_op jit(solution)/shard_map/ppermute | solution.py:702
  67.5 7.4 %collective-permute-start.19 = (bf16[608,128]{1,0:T(8,128)(2,1)S(1)}, bf16[608,128]{1,0:T(8,128)(2,1)S(1)}, u32[]{:S(2)}, u32[]{:S(2)}) collective-permute-start(bf16[608,128]{1,0:T(8,128)(2,1)S(1)} %add_convert_fusion.2.refs_0_), channel_id=1, source_target_pairs={{0,1},{1,0},{2,3},{3,2},{4,5},{5,4},{6,7},{7,6},{8,10},{9,11},{10,... | collective-permute-start | bytes 466952 | tf_op jit(solution)/shard_map/ppermute | solution.py:702
  69.0 5.9 %collective-permute-start.22 = (bf16[2,4,64,128]{3,2,1,0:T(8,128)(2,1)S(1)}, bf16[2,4,64,128]{3,2,1,0:T(8,128)(2,1)S(1)}, u32[]{:S(2)}, u32[]{:S(2)}) collective-permute-start(bf16[2,4,64,128]{3,2,1,0:T(8,128)(2,1)S(1)} %get-tuple-element.111), channel_id=1, source_target_pairs={{0,24},{8,16},{16,8},{24,0},{1,25},{9,17},{17,9},{25,1},{2,26},{10... | collective-permute-start | bytes 393224 | tf_op jit(solution)/shard_map/ppermute | solution.py:694
  69.0 9.2 %collective-permute-start.23 = (bf16[608,128]{1,0:T(8,128)(2,1)S(1)}, bf16[608,128]{1,0:T(8,128)(2,1)S(1)}, u32[]{:S(2)}, u32[]{:S(2)}) collective-permute-start(bf16[608,128]{1,0:T(8,128)(2,1)S(1)} %add_convert_fusion.2.refs_0_), channel_id=1, source_target_pairs={{0,8},{8,0},{16,24},{24,16},{1,9},{9,1},{17,25},{25,17},{2,10},{10... | collective-permute-start | bytes 466952 | tf_op jit(solution)/shard_map/ppermute | solution.py:694
  74.9 3.4 %collective-permute-start.24 = (bf16[608,128]{1,0:T(8,128)(2,1)S(1)}, bf16[608,128]{1,0:T(8,128)(2,1)S(1)}, u32[]{:S(2)}, u32[]{:S(2)}) collective-permute-start(bf16[608,128]{1,0:T(8,128)(2,1)S(1)} %collective-permute-done.19.refs_1_), channel_id=1, source_target_pairs={{0,8},{8,0},{16,24},{24,16},{1,9},{9,1},{17,25},{25,17},{2,10},{10... | collective-permute-start | bytes 466952 | tf_op jit(solution)/shard_map/ppermute | solution.py:694
  75.8 2.5 %collective-permute-start.25 = (bf16[608,128]{1,0:T(8,128)(2,1)S(1)}, bf16[608,128]{1,0:T(8,128)(2,1)S(1)}, u32[]{:S(2)}, u32[]{:S(2)}) collective-permute-start(bf16[608,128]{1,0:T(8,128)(2,1)S(1)} %collective-permute-done.20.refs_2_), channel_id=1, source_target_pairs={{0,8},{8,0},{16,24},{24,16},{1,9},{9,1},{17,25},{25,17},{2,10},{10... | collective-permute-start | bytes 466952 | tf_op jit(solution)/shard_map/ppermute | solution.py:694
  75.8 2.4 %collective-permute-start.26 = (bf16[608,128]{1,0:T(8,128)(2,1)S(1)}, bf16[608,128]{1,0:T(8,128)(2,1)S(1)}, u32[]{:S(2)}, u32[]{:S(2)}) collective-permute-start(bf16[608,128]{1,0:T(8,128)(2,1)S(1)} %collective-permute-done.21.refs_3_), channel_id=1, source_target_pairs={{0,8},{8,0},{16,24},{24,16},{1,9},{9,1},{17,25},{25,17},{2,10},{10... | collective-permute-start | bytes 466952 | tf_op jit(solution)/shard_map/ppermute | solution.py:694
